TPU v7x, 32 devices: a whole 2x2x4 slice. The times are simulated.
32 devices in a mesh: dp: 16 (over z, x, core), tensor: 2 (over y).
Axes of the slice: x: 2, y: 2, z: 4, core: 2. Of those that a mesh axis runs over, the one named last changes fastest.
Arguments:
- inputs: bfloat16 [16, 1024, 1536], P('dp', 'tensor'), may hold values from -6 to 6
- encoder_text_states: bfloat16 [16, 64, 1536], P('dp'), may hold values from -6 to 6
- cotangent: bfloat16 [16, 1024, 1536], P('dp', 'tensor'), may hold values from -1.5 to 1.5
- clip_adapter_index: int32 [16, 10], P('dp'), may hold values from 0 to 7
- self_norm_gain: float32 [1536], replicated, may hold values from 0.25 to 1.75
- cross_norm_gain: float32 [1536], replicated, may hold values from 0.25 to 1.75
- feed_norm_gain: float32 [1536], replicated, may hold values from 0.25 to 1.75
- self_query_key_value_weight: bfloat16 [3, 1536, 1536], P(None, None, 'tensor'), may hold values from -0.15625 to 0.15625
- self_output_weight: bfloat16 [1536, 1536], P('tensor'), may hold values from -0.625 to 0.625
- cross_query_weight: bfloat16 [1536, 1536], P(None, 'tensor'), may hold values from -0.15625 to 0.15625
- cross_key_value_weight: bfloat16 [2, 1536, 1536], P(None, None, 'tensor'), may hold values from -0.15625 to 0.15625
- cross_output_weight: bfloat16 [1536, 1536], P('tensor'), may hold values from -0.4375 to 0.4375
- up_weight: bfloat16 [1536, 6144], P(None, 'tensor'), may hold values from -0.15625 to 0.15625
- down_weight: bfloat16 [6144, 1536], P('tensor'), may hold values from -0.078125 to 0.078125
- self_first_factors: bfloat16 [3, 8, 16, 1536], replicated, may hold values from -0.15625 to 0.15625
- self_second_factors: bfloat16 [3, 8, 16, 1536], P(None, None, None, 'tensor'), may hold values from -0.375 to 0.375
- cross_first_factors: bfloat16 [3, 8, 16, 1536], replicated, may hold values from -0.15625 to 0.15625
- cross_second_factors: bfloat16 [3, 8, 16, 1536], P(None, None, None, 'tensor'), may hold values from -0.375 to 0.375
- attention_first_factors: bfloat16 [2, 8, 16, 1536], P(None, None, None, 'tensor'), may hold values from -0.15625 to 0.15625
- attention_second_factors: bfloat16 [2, 8, 16, 1536], replicated, may hold values from -0.75 to 0.75
- input_first_factors: bfloat16 [8, 16, 1536], replicated, may hold values from -0.15625 to 0.15625
- input_second_factors: bfloat16 [8, 16, 6144], P(None, None, 'tensor'), may hold values from -0.375 to 0.375
- output_first_factors: bfloat16 [8, 16, 6144], P(None, None, 'tensor'), may hold values from -0.078125 to 0.078125
- output_second_factors: bfloat16 [8, 16, 1536], replicated, may hold values from -0.375 to 0.375
Outputs:
- output: bfloat16 [16, 1024, 1536], P('dp', 'tensor')
- input_grad: float32 [16, 1024, 1536], P('dp', 'tensor')
- text_grad: float32 [16, 64, 1536], P('dp', None, 'tensor')
- grad_lora_self_a: float32 [3, 8, 16, 1536], P(None, None, None, 'tensor')
- grad_lora_self_b: float32 [3, 8, 16, 1536], P(None, None, None, 'tensor')
- grad_lora_cross_a: float32 [3, 8, 16, 1536], P(None, None, None, 'tensor')
- grad_lora_cross_b: float32 [3, 8, 16, 1536], P(None, None, None, 'tensor')
- grad_lora_out_a: float32 [2, 8, 16, 1536], P(None, None, None, 'tensor')
- grad_lora_out_b: float32 [2, 8, 16, 1536], P(None, None, None, 'tensor')
- grad_lora_up_a: float32 [8, 16, 1536], P(None, None, 'tensor')
- grad_lora_up_b: float32 [8, 16, 6144], P(None, None, 'tensor')
- grad_lora_down_a: float32 [8, 16, 6144], P(None, None, 'tensor')
- grad_lora_down_b: float32 [8, 16, 1536], P(None, None, 'tensor')
Inputs may be any that keep to these rules, and one draw needn't show every extreme that they name: `clip_adapter_index`: the adapter, of 8, that clip c uses for projection j.
All inputs are finite; a program needn't handle non-finite values.
Results may differ from a plain program's by a relative error of at most 0.035.
Values may be sent and summed in bfloat16 or wider, within the bound.
No kernel may reach another device: no remote copies, remote signals or barrier semaphores. Data moves between devices by JAX's collectives and lax.ppermute only.
A program may use at most 384 MiB of HBM per device.

v0:
```python
import jax
import jax.numpy as jnp
from jax import lax
from jax.sharding import PartitionSpec as P

HEAD_DIM = 64


epsilon = 1e-05


def split_dot(form, wide_part, narrow_part):
    high_part = wide_part.astype(jnp.bfloat16)
    rest_part = (wide_part - high_part.astype(jnp.float32)).astype(jnp.bfloat16)
    first = jnp.einsum(form, high_part, narrow_part, preferred_element_type=jnp.float32)
    return first + jnp.einsum(form, rest_part, narrow_part, preferred_element_type=jnp.float32)


def layer_norm(stream, gain_vec):
    centred = stream - jnp.mean(stream, axis=-1, keepdims=True)
    inverse = lax.rsqrt(jnp.mean(centred * centred, axis=-1, keepdims=True) + epsilon)
    normed = centred * inverse
    return (normed * gain_vec, normed, inverse)


def norm_back(grad_out, gain_vec, normed, inverse):
    grad_norm = grad_out * gain_vec
    mean_grad = jnp.mean(grad_norm, axis=-1, keepdims=True)
    mean_cross = jnp.mean(grad_norm * normed, axis=-1, keepdims=True)
    return inverse * (grad_norm - mean_grad - normed * mean_cross)


def spread_rows(local_rows):
    return lax.all_gather(local_rows.astype(jnp.bfloat16), "tensor", axis=1, tiled=True)


def reduce_grads(partial_sum):
    return lax.psum_scatter(
        partial_sum.astype(jnp.bfloat16), "tensor", scatter_dimension=1, tiled=True
    ).astype(jnp.float32)


def project_rows(act_rows, weight, output_choice, input_choice):
    low_rank = jnp.einsum(
        "ctd,crd->ctr", act_rows, output_choice, preferred_element_type=jnp.float32
    )
    result = jnp.einsum("ctd,de->cte", act_rows, weight, preferred_element_type=jnp.float32)
    result = result + split_dot("ctr,cre->cte", low_rank, input_choice)
    return (result, low_rank)


def project_back(grad_low, act_rows, weight, output_choice, input_choice, low_rank):
    grad_rank = jnp.einsum(
        "cte,cre->ctr", grad_low, input_choice, preferred_element_type=jnp.float32
    )
    grad_rows = jnp.einsum("cte,de->ctd", grad_low, weight, preferred_element_type=jnp.float32)
    grad_rows = grad_rows + split_dot("ctr,crd->ctd", grad_rank, output_choice)
    grad_down = split_dot("ctr,ctd->crd", grad_rank, act_rows)
    grad_up = split_dot("ctr,cte->cre", low_rank, grad_low)
    return (grad_rows, grad_down, grad_up)


def causal_keep(first_row, block_rows, key_count):
    query_at = first_row + jnp.arange(block_rows, dtype=jnp.int32)[:, None]
    key_at = jnp.arange(key_count, dtype=jnp.int32)[None, :]
    return key_at <= query_at


def attention_forward(queries, key_rows, value_rows, causal):
    frames = queries.shape[1]
    key_count = key_rows.shape[1]
    block_rows = min(512, frames)
    score_scale = HEAD_DIM ** (-0.5)
    outputs = []
    log_totals = []
    for first_row in range(0, frames, block_rows):
        key_end = first_row + block_rows if causal else key_count
        query_block = queries[:, first_row : first_row + block_rows]
        scores = (
            jnp.einsum(
                "cbhe,ckhe->chbk",
                query_block,
                key_rows[:, :key_end],
                preferred_element_type=jnp.float32,
            )
            * score_scale
        )
        if causal:
            scores = jnp.where(causal_keep(first_row, block_rows, key_end), scores, -1e30)
        largest = jnp.max(scores, axis=-1, keepdims=True)
        exponent = jnp.exp(scores - largest)
        summed = jnp.sum(exponent, axis=-1, keepdims=True)
        prob_low = (exponent / summed).astype(jnp.bfloat16)
        outputs.append(
            jnp.einsum(
                "chbk,ckhe->cbhe",
                prob_low,
                value_rows[:, :key_end],
                preferred_element_type=jnp.float32,
            )
        )
        log_totals.append(largest + jnp.log(summed))
    return (jnp.concatenate(outputs, axis=1), jnp.concatenate(log_totals, axis=2))


def attention_back(queries, key_rows, value_rows, log_totals, grad_mixed, causal):
    frames = queries.shape[1]
    key_count = key_rows.shape[1]
    block_rows = min(512, frames)
    score_scale = HEAD_DIM ** (-0.5)
    grad_keys = jnp.zeros(key_rows.shape, jnp.float32)
    grad_values = jnp.zeros(value_rows.shape, jnp.float32)
    grad_queries = []
    for first_row in range(0, frames, block_rows):
        key_end = first_row + block_rows if causal else key_count
        key_part = key_rows[:, :key_end]
        value_part = value_rows[:, :key_end]
        query_block = queries[:, first_row : first_row + block_rows]
        grad_block = grad_mixed[:, first_row : first_row + block_rows]
        scores = (
            jnp.einsum("cbhe,ckhe->chbk", query_block, key_part, preferred_element_type=jnp.float32)
            * score_scale
        )
        if causal:
            scores = jnp.where(causal_keep(first_row, block_rows, key_end), scores, -1e30)
        probs = jnp.exp(scores - log_totals[:, :, first_row : first_row + block_rows])
        grad_values = grad_values.at[:, :key_end].add(
            jnp.einsum(
                "chbk,cbhe->ckhe",
                probs.astype(jnp.bfloat16),
                grad_block,
                preferred_element_type=jnp.float32,
            )
        )
        grad_probs = jnp.einsum(
            "cbhe,ckhe->chbk", grad_block, value_part, preferred_element_type=jnp.float32
        )
        inner_sum = jnp.sum(probs * grad_probs, axis=-1, keepdims=True)
        grad_scores = (probs * (grad_probs - inner_sum)).astype(jnp.bfloat16)
        grad_queries.append(
            jnp.einsum("chbk,ckhe->cbhe", grad_scores, key_part, preferred_element_type=jnp.float32)
            * score_scale
        )
        grad_keys = grad_keys.at[:, :key_end].add(
            jnp.einsum(
                "chbk,cbhe->ckhe", grad_scores, query_block, preferred_element_type=jnp.float32
            )
            * score_scale
        )
    return (jnp.concatenate(grad_queries, axis=1), grad_keys, grad_values)


def gelu_exact(pre_act):
    return jax.nn.gelu(pre_act, approximate=False)


def on_device(
    inputs,
    encoder_text_states,
    cotangent,
    clip_adapter_index,
    self_norm_gain,
    cross_norm_gain,
    feed_norm_gain,
    self_query_key_value_weight,
    self_output_weight,
    cross_query_weight,
    cross_key_value_weight,
    cross_output_weight,
    up_weight,
    down_weight,
    self_first_factors,
    self_second_factors,
    cross_first_factors,
    cross_second_factors,
    attention_first_factors,
    attention_second_factors,
    input_first_factors,
    input_second_factors,
    output_first_factors,
    output_second_factors,
):
    adapter_slot_count = input_first_factors.shape[0]
    chooser = (
        clip_adapter_index[:, :, None]
        == jnp.arange(adapter_slot_count, dtype=jnp.int32)[None, None, :]
    ).astype(jnp.bfloat16)
    local_heads = self_output_weight.shape[0] // HEAD_DIM

    def choose_adapter_slot(adapter_slot_table, column_index):
        return jnp.einsum(
            "cn,npq->cpq",
            chooser[:, column_index],
            adapter_slot_table,
            preferred_element_type=jnp.float32,
        ).astype(jnp.bfloat16)

    def slot_grads(grad_pick, column_index):
        return split_dot("cpq,cn->npq", grad_pick, chooser[:, column_index])

    def split_heads(stacked):
        return stacked.reshape(stacked.shape[0], stacked.shape[1], local_heads, HEAD_DIM)

    def join_heads(stacked):
        return stacked.reshape(stacked.shape[0], stacked.shape[1], local_heads * HEAD_DIM)

    def out_forward(mixed_in, inner_layer):
        column_index = 3 + 4 * inner_layer
        input_choice = choose_adapter_slot(attention_second_factors[inner_layer], column_index)
        weight = self_output_weight if inner_layer == 0 else cross_output_weight
        output_choice = choose_adapter_slot(attention_first_factors[inner_layer], column_index)
        partial_out, low_rank = project_rows(mixed_in, weight, output_choice, input_choice)
        branch = lax.psum_scatter(
            partial_out.astype(jnp.bfloat16), "tensor", scatter_dimension=1, tiled=True
        ).astype(jnp.float32)
        kept_data = (mixed_in, weight, output_choice, input_choice, low_rank)
        return (branch, kept_data)

    def out_back(grad_stream, kept_data):
        mixed_in, weight, output_choice, input_choice, low_rank = kept_data
        grad_low = grad_stream.astype(jnp.bfloat16)
        grad_full = lax.all_gather(grad_low, "tensor", axis=1, tiled=True)
        grad_rows, grad_down, grad_up = project_back(
            grad_full, mixed_in, weight, output_choice, input_choice, low_rank
        )
        grad_mixed = grad_rows.astype(jnp.bfloat16)
        return (grad_mixed, grad_down, grad_up)

    stream = inputs.astype(jnp.float32)
    normed_value, normed_one, inverse_one = layer_norm(stream, self_norm_gain)
    rows_one = spread_rows(normed_value)
    self_down_factor = [
        choose_adapter_slot(self_first_factors[slot_number], slot_number)
        for slot_number in range(3)
    ]
    self_up_factor = [
        choose_adapter_slot(self_second_factors[slot_number], slot_number)
        for slot_number in range(3)
    ]
    self_parts = [
        project_rows(
            rows_one,
            self_query_key_value_weight[slot_number],
            self_down_factor[slot_number],
            self_up_factor[slot_number],
        )
        for slot_number in range(3)
    ]
    self_heads = [
        split_heads(self_parts[slot_number][0].astype(jnp.bfloat16)) for slot_number in range(3)
    ]
    mixed_one, totals_one = attention_forward(self_heads[0], self_heads[1], self_heads[2], True)
    mixed_one = join_heads(mixed_one).astype(jnp.bfloat16)
    branch_one, kept_one = out_forward(mixed_one, 0)
    stream_one = stream + branch_one
    normed_value, normed_two, inverse_two = layer_norm(stream_one, cross_norm_gain)
    rows_two = spread_rows(normed_value)
    cross_down_factor = [
        choose_adapter_slot(cross_first_factors[slot_number], 4 + slot_number)
        for slot_number in range(3)
    ]
    cross_up_factor = [
        choose_adapter_slot(cross_second_factors[slot_number], 4 + slot_number)
        for slot_number in range(3)
    ]
    query_full, query_rank = project_rows(
        rows_two, cross_query_weight, cross_down_factor[0], cross_up_factor[0]
    )
    key_full, key_rank = project_rows(
        encoder_text_states, cross_key_value_weight[0], cross_down_factor[1], cross_up_factor[1]
    )
    value_full, value_rank = project_rows(
        encoder_text_states, cross_key_value_weight[1], cross_down_factor[2], cross_up_factor[2]
    )
    query_two = split_heads(query_full.astype(jnp.bfloat16))
    key_two = split_heads(key_full.astype(jnp.bfloat16))
    value_two = split_heads(value_full.astype(jnp.bfloat16))
    mixed_two, totals_two = attention_forward(query_two, key_two, value_two, False)
    mixed_two = join_heads(mixed_two).astype(jnp.bfloat16)
    branch_two, kept_two = out_forward(mixed_two, 1)
    stream_two = stream_one + branch_two
    normed_value, normed_three, inverse_three = layer_norm(stream_two, feed_norm_gain)
    rows_three = spread_rows(normed_value)
    input_second_choice = choose_adapter_slot(input_first_factors, 8)
    input_first_choice = choose_adapter_slot(input_second_factors, 8)
    before, up_rank = project_rows(rows_three, up_weight, input_second_choice, input_first_choice)
    gelu_value, gelu_pull = jax.vjp(gelu_exact, before)
    hidden = gelu_value.astype(jnp.bfloat16)
    output_second_choice = choose_adapter_slot(output_first_factors, 9)
    output_first_choice = choose_adapter_slot(output_second_factors, 9)
    partial_out, down_rank = project_rows(
        hidden, down_weight, output_second_choice, output_first_choice
    )
    branch_three = lax.psum_scatter(
        partial_out.astype(jnp.bfloat16), "tensor", scatter_dimension=1, tiled=True
    ).astype(jnp.float32)
    output = (stream_two + branch_three).astype(jnp.bfloat16)
    grad_full = lax.all_gather(cotangent, "tensor", axis=1, tiled=True)
    grad_hidden, grad_down_a, grad_down_b = project_back(
        grad_full, hidden, down_weight, output_second_choice, output_first_choice, down_rank
    )
    grad_before = gelu_pull(grad_hidden)[0].astype(jnp.bfloat16)
    grad_rows, grad_up_a, grad_up_b = project_back(
        grad_before, rows_three, up_weight, input_second_choice, input_first_choice, up_rank
    )
    grad_stream = cotangent.astype(jnp.float32) + norm_back(
        reduce_grads(grad_rows), feed_norm_gain, normed_three, inverse_three
    )
    grad_mixed, grad_out_a_two, grad_out_b_two = out_back(grad_stream, kept_two)
    grad_query, grad_key, grad_value = attention_back(
        query_two, key_two, value_two, totals_two, split_heads(grad_mixed), False
    )
    grad_query = join_heads(grad_query).astype(jnp.bfloat16)
    grad_key = join_heads(grad_key).astype(jnp.bfloat16)
    grad_value = join_heads(grad_value).astype(jnp.bfloat16)
    grad_rows_query, cross_grad_a_zero, cross_grad_b_zero = project_back(
        grad_query,
        rows_two,
        cross_query_weight,
        cross_down_factor[0],
        cross_up_factor[0],
        query_rank,
    )
    grad_text_key, cross_grad_a_one, cross_grad_b_one = project_back(
        grad_key,
        encoder_text_states,
        cross_key_value_weight[0],
        cross_down_factor[1],
        cross_up_factor[1],
        key_rank,
    )
    grad_text_value, cross_grad_a_two, cross_grad_b_two = project_back(
        grad_value,
        encoder_text_states,
        cross_key_value_weight[1],
        cross_down_factor[2],
        cross_up_factor[2],
        value_rank,
    )
    normed_grad, text_grad = (
        lax.psum_scatter(
            grad_rows_query.astype(jnp.bfloat16), "tensor", scatter_dimension=1, tiled=True
        ).astype(jnp.float32),
        lax.psum_scatter(
            (grad_text_key + grad_text_value).astype(jnp.bfloat16),
            "tensor",
            scatter_dimension=2,
            tiled=True,
        ).astype(jnp.float32),
    )
    grad_stream = grad_stream + norm_back(normed_grad, cross_norm_gain, normed_two, inverse_two)
    grad_mixed, grad_out_a_one, grad_out_b_one = out_back(grad_stream, kept_one)
    grad_query, grad_key, grad_value = attention_back(
        self_heads[0], self_heads[1], self_heads[2], totals_one, split_heads(grad_mixed), True
    )
    self_grads = [
        join_heads(grad_query).astype(jnp.bfloat16),
        join_heads(grad_key).astype(jnp.bfloat16),
        join_heads(grad_value).astype(jnp.bfloat16),
    ]
    self_rows_total = jnp.zeros(rows_one.shape, jnp.float32)
    self_grad_a = []
    self_grad_b = []
    for slot_number in range(3):
        grad_rows, grad_a_part, grad_b_part = project_back(
            self_grads[slot_number],
            rows_one,
            self_query_key_value_weight[slot_number],
            self_down_factor[slot_number],
            self_up_factor[slot_number],
            self_parts[slot_number][1],
        )
        self_rows_total = self_rows_total + grad_rows
        self_grad_a.append(slot_grads(grad_a_part, slot_number))
        self_grad_b.append(slot_grads(grad_b_part, slot_number))
    input_grad = grad_stream + norm_back(
        reduce_grads(self_rows_total), self_norm_gain, normed_one, inverse_one
    )
    sum_self_a = jnp.stack(self_grad_a)
    sum_self_b = jnp.stack(self_grad_b)
    sum_cross_a = jnp.stack(
        [
            slot_grads(cross_grad_a_zero, 4),
            slot_grads(cross_grad_a_one, 5),
            slot_grads(cross_grad_a_two, 6),
        ]
    )
    sum_cross_b = jnp.stack(
        [
            slot_grads(cross_grad_b_zero, 4),
            slot_grads(cross_grad_b_one, 5),
            slot_grads(cross_grad_b_two, 6),
        ]
    )
    sum_out_a = jnp.stack([slot_grads(grad_out_a_one, 3), slot_grads(grad_out_a_two, 7)])
    sum_out_b = jnp.stack([slot_grads(grad_out_b_one, 3), slot_grads(grad_out_b_two, 7)])
    sum_up_a = slot_grads(grad_up_a, 8)
    sum_up_b = slot_grads(grad_up_b, 8)
    sum_down_a = slot_grads(grad_down_a, 9)
    sum_down_b = slot_grads(grad_down_b, 9)
    sum_self_a, sum_cross_a, sum_out_b, sum_up_a, sum_down_b = (
        lax.psum_scatter(
            sum_self_a.astype(jnp.bfloat16), "tensor", scatter_dimension=3, tiled=True
        ).astype(jnp.float32),
        lax.psum_scatter(
            sum_cross_a.astype(jnp.bfloat16), "tensor", scatter_dimension=3, tiled=True
        ).astype(jnp.float32),
        lax.psum_scatter(
            sum_out_b.astype(jnp.bfloat16), "tensor", scatter_dimension=3, tiled=True
        ).astype(jnp.float32),
        lax.psum_scatter(
            sum_up_a.astype(jnp.bfloat16), "tensor", scatter_dimension=2, tiled=True
        ).astype(jnp.float32),
        lax.psum_scatter(
            sum_down_b.astype(jnp.bfloat16), "tensor", scatter_dimension=2, tiled=True
        ).astype(jnp.float32),
    )
    totals = (
        lax.psum(sum_self_a.astype(jnp.bfloat16), "dp").astype(jnp.float32),
        lax.psum(sum_self_b.astype(jnp.bfloat16), "dp").astype(jnp.float32),
        lax.psum(sum_cross_a.astype(jnp.bfloat16), "dp").astype(jnp.float32),
        lax.psum(sum_cross_b.astype(jnp.bfloat16), "dp").astype(jnp.float32),
        lax.psum(sum_out_a.astype(jnp.bfloat16), "dp").astype(jnp.float32),
        lax.psum(sum_out_b.astype(jnp.bfloat16), "dp").astype(jnp.float32),
        lax.psum(sum_up_a.astype(jnp.bfloat16), "dp").astype(jnp.float32),
        lax.psum(sum_up_b.astype(jnp.bfloat16), "dp").astype(jnp.float32),
        lax.psum(sum_down_a.astype(jnp.bfloat16), "dp").astype(jnp.float32),
        lax.psum(sum_down_b.astype(jnp.bfloat16), "dp").astype(jnp.float32),
    )
    return (
        output,
        input_grad,
        text_grad,
        totals[0],
        totals[1],
        totals[2],
        totals[3],
        totals[4],
        totals[5],
        totals[6],
        totals[7],
        totals[8],
        totals[9],
    )


def solution(mesh):
    in_specs = (
        P("dp", "tensor", None),
        P("dp", None, None),
        P("dp", "tensor", None),
        P("dp", None),
        P(),
        P(),
        P(),
        P(None, None, "tensor"),
        P("tensor", None),
        P(None, "tensor"),
        P(None, None, "tensor"),
        P("tensor", None),
        P(None, "tensor"),
        P("tensor", None),
        P(),
        P(None, None, None, "tensor"),
        P(),
        P(None, None, None, "tensor"),
        P(None, None, None, "tensor"),
        P(),
        P(),
        P(None, None, "tensor"),
        P(None, None, "tensor"),
        P(),
    )
    out_specs = (
        P("dp", "tensor", None),
        P("dp", "tensor", None),
        P("dp", None, "tensor"),
        P(None, None, None, "tensor"),
        P(None, None, None, "tensor"),
        P(None, None, None, "tensor"),
        P(None, None, None, "tensor"),
        P(None, None, None, "tensor"),
        P(None, None, None, "tensor"),
        P(None, None, "tensor"),
        P(None, None, "tensor"),
        P(None, None, "tensor"),
        P(None, None, "tensor"),
    )
    return jax.shard_map(
        on_device, mesh=mesh, in_specs=in_specs, out_specs=out_specs, check_vma=False
    )
```

profile of v0, /device:TPU:0, one launch (start us, length us, event | category | flops | bytes accessed | tf_op | source)
XLA Modules:
  0.0 1097.2 jit_solution(13654833760634249941)
XLA Ops:
  24.0 37.3 %all-gather.7.cloned.1.call-done = bf16[1,1024,1536]{2,1,0:T(8,128)(2,1)} async-done(((bf16[1,512,1536]{2,1,0:T(8,128)(2,1)}), bf16[1,1024,1536]{2,1,0:T(8,128)(2,1)}) %all-gather.7.cloned.1.call-update) | async-done | bytes 3145744 | tf_op jit(solution)/shard_map/all_gather | solution.py:34
  103.1 12.3 %fusion = f32[12,512]{1,0:T(8,128)S(1)} fusion(f32[12,512]{1,0:T(8,128)S(1)} %get-tuple-element.208, f32[12,512,1024]{2,1,0:T(8,128)} %get-tuple-element.209, pred[512,1024]{1,0:T(8,128)(4,1)S(1)} %iota_compare_fusion), kind=kLoop, calls=%fused_computation.6 | loop fusion | flops 25159680 | bytes 25739264 | tf_op jit(solution)/shard_map/reduce_sum | solution.py:92
  141.1 38.3 %reduce-scatter.13.cloned.1.call-done = bf16[1,512,1536]{2,1,0:T(8,128)(2,1)} async-done(((bf16[1,1024,1536]{2,1,0:T(8,128)(2,1)}), bf16[1,512,1536]{2,1,0:T(8,128)(2,1)}) %reduce-scatter.13.cloned.1.call-update) | async-done | bytes 1572880 | tf_op jit(solution)/shard_map/reduce_scatter | solution.py:213
  197.7 32.2 %all-gather.9.cloned.1.call-done = bf16[1,1024,1536]{2,1,0:T(8,128)(2,1)} async-done(((bf16[1,512,1536]{2,1,0:T(8,128)(2,1)}), bf16[1,1024,1536]{2,1,0:T(8,128)(2,1)}) %all-gather.9.cloned.1.call-update) | async-done | bytes 3145744 | tf_op jit(solution)/shard_map/all_gather | solution.py:34
  249.5 40.9 %reduce-scatter.15.cloned.1.call-done = bf16[1,512,1536]{2,1,0:T(8,128)(2,1)} async-done(((bf16[1,1024,1536]{2,1,0:T(8,128)(2,1)}), bf16[1,512,1536]{2,1,0:T(8,128)(2,1)}) %reduce-scatter.15.cloned.1.call-update) | async-done | bytes 1572880 | tf_op jit(solution)/shard_map/reduce_scatter | solution.py:213
  300.0 36.8 %all-gather.13.cloned.1.call-done = bf16[1,1024,1536]{2,1,0:T(8,128)(2,1)} async-done(((bf16[1,512,1536]{2,1,0:T(8,128)(2,1)}), bf16[1,1024,1536]{2,1,0:T(8,128)(2,1)}) %all-gather.13.cloned.1.call-update) | async-done | bytes 3145744 | tf_op jit(solution)/shard_map/all_gather | solution.py:298
  347.3 15.5 %fusion.61 = f32[1024,3072]{1,0:T(8,128)} fusion(bf16[3072,1536]{1,0:T(8,128)(2,1)} %param.65, bf16[1,1024,1536]{2,1,0:T(8,128)(2,1)S(1)} %copy-done.31), kind=kOutput, calls=%fused_computation.96 | convolution fusion | flops 9663676416 | bytes 25165824 | tf_op jit(solution)/shard_map/cte,de->ctd/dot_general | solution.py:56
  362.8 20.9 %all-gather.11.cloned.1.call-done = bf16[1,1024,1536]{2,1,0:T(8,128)(2,1)} async-done(((bf16[1,512,1536]{2,1,0:T(8,128)(2,1)}), bf16[1,1024,1536]{2,1,0:T(8,128)(2,1)}) %all-gather.11.cloned.1.call-update) | async-done | bytes 3145744 | tf_op jit(solution)/shard_map/all_gather | solution.py:34
  388.4 15.1 %fusion.69 = f32[1024,3072]{1,0:T(8,128)} fusion(bf16[1536,3072]{1,0:T(8,128)(2,1)} %param.64, bf16[1,1024,1536]{2,1,0:T(8,128)(2,1)S(1)} %copy-done.22), kind=kOutput, calls=%fused_computation.104 | convolution fusion | flops 9663676416 | bytes 25165824 | tf_op jit(solution)/shard_map/ctd,de->cte/dot_general | solution.py:47
  403.5 32.7 %multiply_convert_fusion.2 = (bf16[1024,3072]{1,0:T(8,128)(2,1)}, f32[1024,3072]{1,0:T(8,128)}, f32[1024,3072]{1,0:T(8,128)}) fusion(f32[1024,3072]{1,0:T(8,128)} %fusion.69, f32[1024,3072]{1,0:T(8,128)S(1)} %fusion.417, bf16[1,16,3072]{2,0,1:T(2,128)(2,1)S(1)} %fusion.207, f32[1024,16]{0,1:T(8,128)S(1)} %fusion.67), kind=kOutput, calls=%fused_computation.16 | convolution fusion | flops 311492608 | bytes 56786944 | tf_op jit(solution)/shard_map/ctr,cre->cte/dot_general | solution.py:16
  436.2 18.1 %add_convert_fusion = bf16[1024,3072]{1,0:T(8,128)(2,1)S(1)} fusion(f32[1024,3072]{1,0:T(8,128)} %get-tuple-element.178, f32[1024,3072]{1,0:T(8,128)} %fusion.61, f32[1024,3072]{1,0:T(8,128)} %fusion.410, f32[1024,3072]{1,0:T(8,128)} %get-tuple-element.216, f32[1024,16]{0,1:T(8,128)S(1)} %copy-done.67, bf16[1,16,3072]{2,0,1:T(2,128)(2,1)S(1)} %copy-done.75), kind=kOutput, calls=%fused_computation.15 | convolution fusion | flops 151060480 | bytes 56786944 | tf_op jit(solution)/shard_map/ctr,crd->ctd/dot_general | solution.py:16
  457.0 12.5 %fusion.472 = f32[1024,1536]{1,0:T(8,128)S(1)} fusion(bf16[1024,3072]{1,0:T(8,128)(2,1)S(1)} %add_convert_fusion, bf16[1536,3072]{1,0:T(8,128)(2,1)} %param.64), kind=kOutput, calls=%fused_computation.671 | convolution fusion | flops 9663676416 | bytes 22020096 | tf_op jit(solution)/shard_map/cte,de->ctd/dot_general | solution.py:56
  478.8 15.0 %fusion.471 = f32[1024,1536]{1,0:T(8,128)S(1)} fusion(bf16[1024,3072]{1,0:T(8,128)(2,1)} %get-tuple-element.177, bf16[3072,1536]{1,0:T(8,128)(2,1)} %param.65), kind=kOutput, calls=%fused_computation.670 | convolution fusion | flops 9663676416 | bytes 22020096 | tf_op jit(solution)/shard_map/ctd,de->cte/dot_general | solution.py:47
  496.7 20.0 %reduce-scatter.19.cloned.1.call-done = bf16[1,512,1536]{2,1,0:T(8,128)(2,1)} async-done(((bf16[1,1024,1536]{2,1,0:T(8,128)(2,1)}), bf16[1,512,1536]{2,1,0:T(8,128)(2,1)}) %reduce-scatter.19.cloned.1.call-update) | async-done | bytes 1572880 | tf_op jit(solution)/shard_map/reduce_scatter | solution.py:38
  520.0 42.4 %reduce-scatter.17.cloned.1.call-done = bf16[1,512,1536]{2,1,0:T(8,128)(2,1)} async-done(((bf16[1,1024,1536]{2,1,0:T(8,128)(2,1)}), bf16[1,512,1536]{2,1,0:T(8,128)(2,1)}) %reduce-scatter.17.cloned.1.call-update) | async-done | bytes 1572880 | tf_op jit(solution)/shard_map/reduce_scatter | solution.py:294
  568.8 44.6 %all-gather.15.cloned.1.call-done = bf16[1,1024,1536]{2,1,0:T(8,128)(2,1)} async-done(((bf16[1,512,1536]{2,1,0:T(8,128)(2,1)}), bf16[1,1024,1536]{2,1,0:T(8,128)(2,1)}) %all-gather.15.cloned.1.call-update) | async-done | bytes 3145744 | tf_op jit(solution)/shard_map/all_gather | solution.py:222
  643.4 33.9 %reduce-scatter.21.cloned.1.call-done = bf16[1,512,1536]{2,1,0:T(8,128)(2,1)} async-done(((bf16[1,1024,1536]{2,1,0:T(8,128)(2,1)}), bf16[1,512,1536]{2,1,0:T(8,128)(2,1)}) %reduce-scatter.21.cloned.1.call-update) | async-done | bytes 1572880 | tf_op jit(solution)/shard_map/reduce_scatter | solution.py:341
  751.8 18.9 %multiply_reduce_fusion = (f32[12,512]{1,0:T(8,128)}, f32[12,512,1024]{2,1,0:T(8,128)}) fusion(f32[12,512]{1,0:T(8,128)} %log_add_fusion, f32[12,512,1024]{2,1,0:T(8,128)} %get-tuple-element.209, pred[512,1024]{1,0:T(8,128)(4,1)S(1)} %copy-done.42, bf16[1024,12,64]{0,2,1:T(8,128)(2,1)} %bitcast.673, bf16[1,1024,12,64]{1,3,2,0:T(8,128)(2,1)} %bitcast.678), kind=kOutput, calls=%fused_computation.1 | convolution fusion | flops 836757504 | bytes 53272576 | tf_op jit(solution)/shard_map/cbhe,ckhe->chbk/dot_general | solution.py:135
  770.6 12.5 %fusion.37 = bf16[1,1024,12,64]{1,3,2,0:T(8,128)(2,1)S(1)} fusion(f32[1,512,12,64]{1,3,2,0:T(8,128)} %fusion.175, f32[12,512]{1,0:T(8,128)} %log_add_fusion, f32[12,512,1024]{2,1,0:T(8,128)} %get-tuple-element.209, pred[512,1024]{1,0:T(8,128)(4,1)S(1)} %copy-done.42, bf16[1,1024,12,64]{1,3,2,0:T(8,128)(2,1)} %bitcast.679), kind=kOutput, calls=%fused_computation.71 | convolution fusion | flops 832045056 | bytes 29655040 | tf_op jit(solution)/shard_map/chbk,cbhe->ckhe/dot_general | solution.py:128
  784.4 14.1 %multiply_convert_fusion.1 = bf16[12,512,512]{1,2,0:T(8,128)(2,1)} fusion(f32[12,512,512]{1,2,0:T(8,128)} %get-tuple-element.222, f32[12,512]{1,0:T(8,128)S(1)} %copy-done.177, f32[12,512]{1,0:T(8,128)S(1)} %copy-done.157, f32[12,512,512]{1,2,0:T(8,128)} %copy-done.4, pred[512,512]{0,1:T(8,128)(4,1)S(1)} %copy-done.50), kind=kLoop, calls=%fused_computation.12 | loop fusion | flops 18874368 | bytes 31768576 | tf_op jit(solution)/shard_map/convert_element_type | solution.py:139
  807.6 15.8 %multiply_convert_fusion = bf16[12,512,1024]{2,1,0:T(8,128)(2,1)} fusion(f32[12,512,1024]{2,1,0:T(8,128)} %get-tuple-element.224, f32[12,512]{1,0:T(8,128)S(1)} %copy-done.170, f32[12,512]{1,0:T(8,128)S(1)} %copy-done.151, f32[12,512,1024]{2,1,0:T(8,128)S(1)} %bitcast.643, pred[512,1024]{1,0:T(8,128)(4,1)S(1)} %copy-done.42), kind=kLoop, calls=%fused_computation | loop fusion | flops 37748736 | bytes 63488000 | tf_op jit(solution)/shard_map/convert_element_type | solution.py:139
  914.1 19.6 %fusion.30 = bf16[1,1024,1536]{2,1,0:T(8,128)(2,1)} fusion(f32[1024,1536]{1,0:T(8,128)} %fusion.121, f32[1024,1536]{1,0:T(8,128)} %fusion.386, f32[1024,1536]{1,0:T(8,128)} %fusion.115, f32[1024,1536]{1,0:T(8,128)} %fusion.389, f32[1024,1536]{1,0:T(8,128)} %fusion.391, f32[1024,1536]{1,0:T(8,128)} %fusion.118, f32[1024,1536]{1,0:T(8,128)} %fusion.393, ...), kind=kOutput, calls=%fused_computation.63 | convolution fusion | flops 64552960 | bytes 53592064 | tf_op jit(solution)/shard_map/ctr,crd->ctd/dot_general | solution.py:16
  935.3 101.5 %all-reduce.5.cloned.1.call-done = (bf16[3,8,16,768]{3,2,1,0:T(8,128)(2,1)}, bf16[3,8,16,768]{3,2,1,0:T(8,128)(2,1)}, bf16[3,8,16,768]{3,2,1,0:T(8,128)(2,1)}, b...) async-done(((bf16[3,8,16,768]{3,2,1,0:T(8,128)(2,1)}, ...) | async-done | bytes 5111824 | tf_op jit(solution)/shard_map/psum | solution.py:419
  1050.6 32.1 %reduce-scatter.23.cloned.1.call-done = bf16[1,512,1536]{2,1,0:T(8,128)(2,1)} async-done(((bf16[1,1024,1536]{2,1,0:T(8,128)(2,1)}), bf16[1,512,1536]{2,1,0:T(8,128)(2,1)}) %reduce-scatter.23.cloned.1.call-update) | async-done | bytes 1572880 | tf_op jit(solution)/shard_map/reduce_scatter | solution.py:38
  (748 shorter events, 397.6 us)
Async XLA Ops:
  7.2 232.6 %copy-start = (bf16[768,1536]{1,0:T(8,128)(2,1)S(1)}, bf16[768,1536]{1,0:T(8,128)(2,1)}, u32[]{:S(2)}) copy-start(bf16[768,1536]{1,0:T(8,128)(2,1)} %param.63) | copy-start | bytes 7077892
  7.2 54.1 %all-gather.7.cloned.1.call-start = ((), (), s32[]{:S(2)}) async-start(), calls=%async_computation.12 | async-start | bytes 4718592 | tf_op jit(solution)/shard_map/all_gather | solution.py:34
  13.5 165.9 %reduce-scatter.13.cloned.1.call-start = ((), (), s32[]{:S(2)}) async-start(), calls=%async_computation.13 | async-start | bytes 4718592 | tf_op jit(solution)/shard_map/reduce_scatter | solution.py:213
  13.7 285.6 %copy-start.139 = (pred[1,10,8]{2,1,0:T(8,128)(4,1)}, pred[1,10,8]{2,1,0:T(8,128)(4,1)S(1)}, u32[]{:S(2)}) copy-start(pred[1,10,8]{2,1,0:T(8,128)(4,1)S(1)} %iota_compare_fusion.2) | copy-start | bytes 244
  21.1 112.1 %copy-start.114 = (bf16[1,16,1536]{2,0,1:T(2,128)(2,1)}, bf16[1,16,1536]{2,0,1:T(2,128)(2,1)S(1)}, u32[]{:S(2)}) copy-start(bf16[1,16,1536]{2,0,1:T(2,128)(2,1)S(1)} %fusion.244) | copy-start | bytes 147460
  24.0 91.4 %copy-start.41 = (pred[512,1024]{1,0:T(8,128)(4,1)}, pred[512,1024]{1,0:T(8,128)(4,1)S(1)}, u32[]{:S(2)}) copy-start(pred[512,1024]{1,0:T(8,128)(4,1)S(1)} %iota_compare_fusion) | copy-start | bytes 1572868
  135.9 94.0 %all-gather.9.cloned.1.call-start = ((), (), s32[]{:S(2)}) async-start(), calls=%async_computation.14 | async-start | bytes 4718592 | tf_op jit(solution)/shard_map/all_gather | solution.py:34
  184.8 105.6 %reduce-scatter.15.cloned.1.call-start = ((), (), s32[]{:S(2)}) async-start(), calls=%async_computation.15 | async-start | bytes 4718592 | tf_op jit(solution)/shard_map/reduce_scatter | solution.py:213
  246.9 89.9 %all-gather.13.cloned.1.call-start = ((), (), s32[]{:S(2)}) async-start(), calls=%async_computation.18 | async-start | bytes 4718592 | tf_op jit(solution)/shard_map/all_gather | solution.py:298
  247.5 136.3 %all-gather.11.cloned.1.call-start = ((), (), s32[]{:S(2)}) async-start(), calls=%async_computation.16 | async-start | bytes 4718592 | tf_op jit(solution)/shard_map/all_gather | solution.py:34
  297.3 219.4 %reduce-scatter.19.cloned.1.call-start = ((), (), s32[]{:S(2)}) async-start(), calls=%async_computation.19 | async-start | bytes 4718592 | tf_op jit(solution)/shard_map/reduce_scatter | solution.py:38
  473.2 89.2 %reduce-scatter.17.cloned.1.call-start = ((), (), s32[]{:S(2)}) async-start(), calls=%async_computation.17 | async-start | bytes 4718592 | tf_op jit(solution)/shard_map/reduce_scatter | solution.py:294
  496.6 116.7 %all-gather.15.cloned.1.call-start = ((), (), s32[]{:S(2)}) async-start(), calls=%async_computation.20 | async-start | bytes 4718592 | tf_op jit(solution)/shard_map/all_gather | solution.py:222
  568.3 109.0 %reduce-scatter.21.cloned.1.call-start = ((), (), s32[]{:S(2)}) async-start(), calls=%async_computation.21 | async-start | bytes 4718592 | tf_op jit(solution)/shard_map/reduce_scatter | solution.py:341
  616.3 91.3 %copy-start.88 = (f32[1024,16]{0,1:T(8,128)}, f32[1024,16]{0,1:T(8,128)S(1)}, u32[]{:S(2)}) copy-start(f32[1024,16]{0,1:T(8,128)S(1)} %fusion.51) | copy-start | bytes 196612
  633.8 97.0 %all-gather.17.cloned.1.call-start = ((), (), s32[]{:S(2)}) async-start(), calls=%async_computation.22 | async-start | bytes 4718592 | tf_op jit(solution)/shard_map/all_gather | solution.py:222
  685.7 218.1 %reduce-scatter.35.cloned.1.call-start = ((), (), s32[]{:S(2)}) async-start(), calls=%async_computation.29 | async-start | bytes 589824 | tf_op jit(solution)/shard_map/reduce_scatter | solution.py:414
  702.7 201.1 %reduce-scatter.33.cloned.1.call-start = ((), (), s32[]{:S(2)}) async-start(), calls=%async_computation.28 | async-start | bytes 589824 | tf_op jit(solution)/shard_map/reduce_scatter | solution.py:411
  707.5 196.3 %reduce-scatter.29.cloned.1.call-start = ((), (), s32[]{:S(2)}) async-start(), calls=%async_computation.26 | async-start | bytes 1769472 | tf_op jit(solution)/shard_map/reduce_scatter | solution.py:405
  726.3 177.5 %reduce-scatter.31.cloned.1.call-start = ((), (), s32[]{:S(2)}) async-start(), calls=%async_computation.27 | async-start | bytes 1179648 | tf_op jit(solution)/shard_map/reduce_scatter | solution.py:408
  848.8 55.0 %reduce-scatter.27.cloned.1.call-start = ((), (), s32[]{:S(2)}) async-start(), calls=%async_computation.25 | async-start | bytes 1769472 | tf_op jit(solution)/shard_map/reduce_scatter | solution.py:402
  856.5 77.2 %reduce-scatter.25.cloned.1.call-start = ((), (), s32[]{:S(2)}) async-start(), calls=%async_computation.24 | async-start | bytes 294912 | tf_op jit(solution)/shard_map/reduce_scatter | solution.py:344
  867.8 169.1 %all-reduce.5.cloned.1.call-start = ((), (), s32[]{:S(2)}) async-start(), calls=%async_computation.30 | async-start | bytes 10223616 | tf_op jit(solution)/shard_map/psum | solution.py:419
  903.9 178.8 %reduce-scatter.23.cloned.1.call-start = ((), (), s32[]{:S(2)}) async-start(), calls=%async_computation.23 | async-start | bytes 4718592 | tf_op jit(solution)/shard_map/reduce_scatter | solution.py:38
  (223 other events, 1979.8 us)
Sparse Core Ops, SparseCore 0:
  13.6 47.6 all-gather.6
  136.0 43.3 reduce-scatter.12
  184.9 44.9 all-gather.8
  247.0 43.3 reduce-scatter.14
  291.8 44.9 all-gather.12
  338.8 44.9 all-gather.10
  473.3 43.3 reduce-scatter.18
  519.0 43.3 reduce-scatter.16
  568.4 44.9 all-gather.14
  633.9 43.3 reduce-scatter.20
  685.8 44.9 all-gather.16
  733.0 13.1 reduce-scatter.34
  748.4 13.1 reduce-scatter.32
  764.3 21.7 reduce-scatter.28
  849.0 17.7 reduce-scatter.30
  869.5 21.7 reduce-scatter.26
  894.0 10.9 reduce-scatter.24
  910.3 126.4 all-reduce.4
  1039.1 43.5 reduce-scatter.22
where the time goes:
time: 1120 us; the launch traced here: 1100 us
  waiting for transfers between devices  486 us (43%)
  matrix products  438 us (39%)
  other arithmetic  126 us (11%)
  local copies, waits for them, and re-layouts  28.2 us (3%)
  between operations  16.7 us (1%)
    dot_general x40, matrix products, split_dot(): jnp.einsum(form, rest_part, narrow_part, preferred_element_type=jnp.float32)  119 us
    psum x1, waiting for transfers between devices, on_device(): lax.psum(sum_self_a.astype(jnp.bfloat16), 'dp').astype(jnp.float32)  101 us
    all_gather x3, waiting for transfers between devices, spread_rows(): lax.all_gather(local_rows.astype(jnp.bfloat16), 'tensor', axis=1, tiled=T...  90.4 us
    reduce_scatter x2, waiting for transfers between devices, out_forward(): lax.psum_scatter(partial_out.astype(jnp.bfloat16), 'tensor', scatter_dime...  79.2 us
    dot_general x10, matrix products, project_back(): jnp.einsum('cte,de->ctd', grad_low, weight, preferred_element_type=jnp.fl...  62.6 us
    dot_general x40, matrix products, split_dot(): jnp.einsum(form, high_part, narrow_part, preferred_element_type=jnp.float32)  54.8 us
    reduce_scatter x2, waiting for transfers between devices, reduce_grads(): lax.psum_scatter(partial_sum.astype(jnp.bfloat16), 'tensor', scatter_dime...  52.1 us
    dot_general x10, matrix products, project_rows(): jnp.einsum('ctd,de->cte', act_rows, weight, preferred_element_type=jnp.fl...  51.3 us
  transfers between devices with their start and end apart: 19, of which 13 were waited for; matrix products, arithmetic and copies ran while one was open for 32% of the time, Pallas kernels for 0%

commit v1 on v0

--- a/solution.py
+++ b/solution.py
@@ -1,6 +1,8 @@
 import jax
 import jax.numpy as jnp
 from jax import lax
+from jax.experimental import pallas as pl
+from jax.experimental.pallas import tpu as pltpu
 from jax.sharding import PartitionSpec as P
 
 HEAD_DIM = 64
@@ -444,6 +446,1213 @@
     )
 
 
+LOW = jnp.bfloat16
+WIDE = jnp.float32
+VMEM_BYTES = 58 * 1024 * 1024
+RANK_UNIT = 16
+
+
+def mm(left, right, left_dim=1, right_dim=0):
+    return lax.dot_general(
+        left, right, (((left_dim,), (right_dim,)), ((), ())), preferred_element_type=WIDE
+    )
+
+
+def mm_nt(left, right):
+    return mm(left, right, 1, 1)
+
+
+def mm_tn(left, right):
+    return mm(left, right, 0, 0)
+
+
+def norm_rows(rows, gain):
+    centred = rows - jnp.mean(rows, axis=-1, keepdims=True)
+    inverse = lax.rsqrt(jnp.mean(centred * centred, axis=-1, keepdims=True) + epsilon)
+    normed = centred * inverse
+    return normed * gain, normed, inverse
+
+
+def lane_halves():
+    lane = lax.broadcasted_iota(jnp.int32, (1, 2 * HEAD_DIM), 1)
+    return lane < HEAD_DIM
+
+
+def half_masks():
+    left = lane_halves()
+    first = jnp.where(left, 1.0, 0.0)
+    return first.astype(LOW), (1.0 - first).astype(LOW)
+
+
+def gelu_parts(pre):
+    bell = jnp.exp(-0.5 * pre * pre)
+    step = 1.0 / (1.0 + (0.3275911 * 0.7071067811865476) * jnp.abs(pre))
+    tail = step * (
+        0.5 * 0.254829592
+        + step
+        * (
+            0.5 * -0.284496736
+            + step
+            * (0.5 * 1.421413741 + step * (0.5 * -1.453152027 + step * (0.5 * 1.061405429)))
+        )
+    )
+    tail = tail * bell
+    phi = jnp.where(pre >= 0.0, 1.0 - tail, tail)
+    return pre * phi, phi + pre * bell * 0.3989422804014327
+
+
+def whole(shape, where=None):
+    place = (0,) * len(shape) if where is None else where
+    return pl.BlockSpec(shape, lambda *_: place, pipeline_mode=pl.Buffered(1))
+
+
+def call(body, grid, in_specs, out_specs, out_shape, scratch, flops, moved, name, args):
+    return pl.pallas_call(
+        body,
+        grid_spec=pltpu.PrefetchScalarGridSpec(
+            num_scalar_prefetch=1,
+            grid=grid,
+            in_specs=in_specs,
+            out_specs=out_specs,
+            scratch_shapes=scratch,
+        ),
+        out_shape=out_shape,
+        compiler_params=pltpu.CompilerParams(
+            dimension_semantics=("arbitrary",) * len(grid), vmem_limit_bytes=VMEM_BYTES
+        ),
+        cost_estimate=pl.CostEstimate(flops=flops, bytes_accessed=moved, transcendentals=0),
+        name=name,
+    )(*args)
+
+
+def shaped(shape, dtype):
+    return jax.ShapeDtypeStruct(shape, dtype)
+
+
+def first_norm_body(_, x_ref, gain_ref, out_ref):
+    rows, _, _ = norm_rows(x_ref[...].astype(WIDE), gain_ref[...])
+    out_ref[...] = rows.astype(LOW)
+
+
+def first_norm(meta, x, gain):
+    frames, width = x.shape
+    block = min(256, frames)
+    rows = pl.BlockSpec((block, width), lambda t, _: (t, 0))
+    return call(
+        first_norm_body,
+        (frames // block,),
+        [rows, whole((1, width))],
+        rows,
+        shaped(x.shape, LOW),
+        [],
+        10 * x.size,
+        4 * x.size,
+        "first_norm",
+        (meta, x, gain),
+    )
+
+
+def project_body(_, act_ref, weight_ref, down_ref, up_ref, out_ref):
+    act = act_ref[...]
+    rank = mm_nt(act, down_ref[0, 0]).astype(LOW)
+    out_ref[0] = (mm(act, weight_ref[0]) + mm(rank, up_ref[0, 0])).astype(LOW)
+
+
+def project_heads(meta, act, weights, down, up, slots, skip, name):
+    rows, width = act.shape
+    count, _, local = weights.shape
+    first_slot = slots
+    return call(
+        project_body,
+        (count,),
+        [
+            whole((rows, width)),
+            pl.BlockSpec((1, width, local), lambda j, m: (j, 0, 0)),
+            pl.BlockSpec((1, 1, RANK_UNIT, width), lambda j, m: (j + skip, m[first_slot + j], 0, 0)),
+            pl.BlockSpec((1, 1, RANK_UNIT, local), lambda j, m: (j + skip, m[first_slot + j], 0, 0)),
+        ],
+        pl.BlockSpec((1, rows, local), lambda j, m: (j, 0, 0)),
+        shaped((count, rows, local), LOW),
+        [],
+        2 * rows * width * local * count,
+        2 * (weights.size + act.size + count * rows * local),
+        name,
+        (meta, act, weights, down, up),
+    )
+
+
+def project_back_body(
+    _, last, act_ref, grad_ref, weight_ref, down_ref, up_ref, out_ref, ga_ref, gb_ref, total_ref
+):
+    step = pl.program_id(0)
+    act = act_ref[...]
+    grad = grad_ref[0]
+    down = down_ref[0, 0]
+    rank = mm_nt(act, down).astype(LOW)
+    grad_rank = mm_nt(grad, up_ref[0, 0]).astype(LOW)
+    ga_ref[0] = mm_tn(grad_rank, act)
+    gb_ref[0] = mm_tn(rank, grad)
+    part = mm_nt(grad, weight_ref[0]) + mm(grad_rank, down)
+
+    @pl.when(step == 0)
+    def _():
+        total_ref[...] = part
+
+    @pl.when(step > 0)
+    def _():
+        total_ref[...] += part
+
+    @pl.when(step == last)
+    def _():
+        out_ref[...] = total_ref[...].astype(out_ref.dtype)
+
+
+def project_back_heads(meta, act, grads, weights, down, up, slots, skip, kind, name):
+    rows, width = act.shape
+    count, _, local = weights.shape
+    first_slot = slots
+    return call(
+        lambda m, *refs: project_back_body(m, count - 1, *refs),
+        (count,),
+        [
+            whole((rows, width)),
+            pl.BlockSpec((1, rows, local), lambda j, m: (j, 0, 0)),
+            pl.BlockSpec((1, width, local), lambda j, m: (j, 0, 0)),
+            pl.BlockSpec((1, 1, RANK_UNIT, width), lambda j, m: (j + skip, m[first_slot + j], 0, 0)),
+            pl.BlockSpec((1, 1, RANK_UNIT, local), lambda j, m: (j + skip, m[first_slot + j], 0, 0)),
+        ],
+        (
+            whole((rows, width)),
+            pl.BlockSpec((1, RANK_UNIT, width), lambda j, m: (j, 0, 0)),
+            pl.BlockSpec((1, RANK_UNIT, local), lambda j, m: (j, 0, 0)),
+        ),
+        (
+            shaped((rows, width), kind),
+            shaped((count, RANK_UNIT, width), WIDE),
+            shaped((count, RANK_UNIT, local), WIDE),
+        ),
+        [pltpu.VMEM((rows, width), WIDE)],
+        2 * rows * width * local * count,
+        2 * (weights.size + act.size + count * rows * local) + 4 * rows * width,
+        name,
+        (meta, act, grads, weights, down, up),
+    )
+
+
+ROW_BLOCK = 256
+
+
+def order_frames(is_first, own, other, low_part, high_part):
+    @pl.when(is_first)
+    def _():
+        low_part[...] = own[...]
+        high_part[...] = other[...]
+
+    @pl.when(jnp.logical_not(is_first))
+    def _():
+        low_part[...] = other[...]
+        high_part[...] = own[...]
+
+
+def self_forward_body(meta, own_ref, other_ref, out_own_ref, out_other_ref, held, result):
+    half = own_ref.shape[1]
+    is_first = meta[10] == 0
+    order_frames(is_first, own_ref, other_ref, held.at[:, :half], held.at[:, half:])
+    left = lane_halves()
+    masks = half_masks()
+    scale = HEAD_DIM**-0.5
+    query_at = lax.broadcasted_iota(jnp.int32, (ROW_BLOCK, ROW_BLOCK), 0)
+    key_at = lax.broadcasted_iota(jnp.int32, (ROW_BLOCK, ROW_BLOCK), 1)
+    keep = key_at <= query_at
+    for first in range(0, 2 * half, ROW_BLOCK):
+        end = first + ROW_BLOCK
+        query = held[0, first:end] * jnp.asarray(scale, LOW)
+        keys = held[1, :end]
+        values = held[2, :end]
+        parts = []
+        for which in (0, 1):
+            one_query = query * masks[which]
+            near = jnp.where(keep, mm_nt(one_query, keys[first:]), -1e30)
+            largest = jnp.max(near, axis=-1, keepdims=True)
+            spread = values * masks[which] + masks[1 - which]
+            if first > 0:
+                far = mm_nt(one_query, keys[:first])
+                largest = jnp.maximum(largest, jnp.max(far, axis=-1, keepdims=True))
+                mixed = mm(jnp.exp(far - largest).astype(LOW), spread[:first])
+                mixed = mixed + mm(jnp.exp(near - largest).astype(LOW), spread[first:])
+            else:
+                mixed = mm(jnp.exp(near - largest).astype(LOW), spread)
+            parts.append(mixed)
+        mixed = jnp.where(left, parts[0], parts[1])
+        summed = pltpu.roll(jnp.where(left, parts[1], parts[0]), HEAD_DIM, 1)
+        result[first:end] = (mixed / summed).astype(LOW)
+
+    @pl.when(is_first)
+    def _():
+        out_own_ref[...] = result[:half]
+        out_other_ref[...] = result[half:]
+
+    @pl.when(jnp.logical_not(is_first))
+    def _():
+        out_own_ref[...] = result[half:]
+        out_other_ref[...] = result[:half]
+
+
+def self_forward(meta, own, other):
+    _, half, local = own.shape
+    pair = 2 * HEAD_DIM
+    three = pl.BlockSpec((3, half, pair), lambda p, m: (0, 0, p))
+    one = pl.BlockSpec((half, pair), lambda p, m: (0, p))
+    return call(
+        self_forward_body,
+        (local // pair,),
+        [three, three],
+        (one, one),
+        (shaped((half, local), LOW), shaped((half, local), LOW)),
+        [pltpu.VMEM((3, 2 * half, pair), LOW), pltpu.VMEM((2 * half, pair), LOW)],
+        20 * half * half * local,
+        16 * half * local,
+        "self_forward",
+        (meta, own, other),
+    )
+
+
+def self_back_body(
+    meta,
+    own_ref,
+    other_ref,
+    grad_own_ref,
+    grad_other_ref,
+    out_own_ref,
+    out_other_ref,
+    held,
+    grads,
+    key_total,
+    value_total,
+    result,
+):
+    half = own_ref.shape[1]
+    is_first = meta[10] == 0
+    order_frames(is_first, own_ref, other_ref, held.at[:, :half], held.at[:, half:])
+    order_frames(is_first, grad_own_ref, grad_other_ref, grads.at[:half], grads.at[half:])
+    masks = half_masks()
+    scale = HEAD_DIM**-0.5
+    query_at = lax.broadcasted_iota(jnp.int32, (ROW_BLOCK, ROW_BLOCK), 1)
+    key_at = lax.broadcasted_iota(jnp.int32, (ROW_BLOCK, ROW_BLOCK), 0)
+    keep = key_at <= query_at
+    key_total[...] = jnp.zeros_like(key_total)
+    value_total[...] = jnp.zeros_like(value_total)
+    for first in range(0, 2 * half, ROW_BLOCK):
+        end = first + ROW_BLOCK
+        query = held[0, first:end] * jnp.asarray(scale, LOW)
+        grad = grads[first:end]
+        spans = [(first, end)] + ([(0, first)] if first > 0 else [])
+        query_grad = None
+        for which in (0, 1):
+            mask = masks[which]
+            one_query = query * mask
+            one_grad = grad * mask
+            scores = []
+            for low_key, high_key in spans:
+                score = mm_nt(held[1, low_key:high_key], one_query)
+                if low_key == first:
+                    score = jnp.where(keep, score, -1e30)
+                scores.append(score)
+            largest = jnp.max(scores[0], axis=0, keepdims=True)
+            for score in scores[1:]:
+                largest = jnp.maximum(largest, jnp.max(score, axis=0, keepdims=True))
+            probs = [jnp.exp(score - largest) for score in scores]
+            summed = jnp.sum(probs[0], axis=0, keepdims=True)
+            for prob in probs[1:]:
+                summed = summed + jnp.sum(prob, axis=0, keepdims=True)
+            inverse = 1.0 / summed
+            probs = [prob * inverse for prob in probs]
+            prob_grads = [
+                mm_nt(held[2, low_key:high_key], one_grad) for low_key, high_key in spans
+            ]
+            inner = jnp.sum(probs[0] * prob_grads[0], axis=0, keepdims=True)
+            for prob, prob_grad in zip(probs[1:], prob_grads[1:]):
+                inner = inner + jnp.sum(prob * prob_grad, axis=0, keepdims=True)
+            for (low_key, high_key), prob, prob_grad in zip(spans, probs, prob_grads):
+                score_grad = (prob * (prob_grad - inner)).astype(LOW)
+                value_total[low_key:high_key] += mm(prob.astype(LOW), one_grad)
+                key_total[low_key:high_key] += mm(score_grad, one_query)
+                part = mm_tn(score_grad, held[1, low_key:high_key] * mask)
+                query_grad = part if query_grad is None else query_grad + part
+        result[0, first:end] = (query_grad * scale).astype(LOW)
+    result[1] = key_total[...].astype(LOW)
+    result[2] = value_total[...].astype(LOW)
+
+    @pl.when(is_first)
+    def _():
+        out_own_ref[...] = result[:, :half]
+        out_other_ref[...] = result[:, half:]
+
+    @pl.when(jnp.logical_not(is_first))
+    def _():
+        out_own_ref[...] = result[:, half:]
+        out_other_ref[...] = result[:, :half]
+
+
+def self_back(meta, own, other, grad_own, grad_other):
+    _, half, local = own.shape
+    pair = 2 * HEAD_DIM
+    three = pl.BlockSpec((3, half, pair), lambda p, m: (0, 0, p))
+    one = pl.BlockSpec((half, pair), lambda p, m: (0, p))
+    return call(
+        self_back_body,
+        (local // pair,),
+        [three, three, one, one],
+        (three, three),
+        (shaped(own.shape, LOW), shaped(own.shape, LOW)),
+        [
+            pltpu.VMEM((3, 2 * half, pair), LOW),
+            pltpu.VMEM((2 * half, pair), LOW),
+            pltpu.VMEM((2 * half, pair), WIDE),
+            pltpu.VMEM((2 * half, pair), WIDE),
+            pltpu.VMEM((3, 2 * half, pair), LOW),
+        ],
+        50 * half * half * local,
+        30 * half * local,
+        "self_back",
+        (meta, own, other, grad_own, grad_other),
+    )
+
+
+def halves_of(ref, local):
+    step = ref.shape[2] // 2
+    return (
+        ref[:, 0, :step, :].reshape(local, ref.shape[3]),
+        ref[:, 0, step:, :].reshape(local, ref.shape[3]),
+    )
+
+
+def full_of(ref):
+    return ref[:, 0].reshape(ref.shape[0] * ref.shape[2], ref.shape[3])
+
+
+def pair_tiles(keys, values, pair, masks):
+    span = slice(2 * HEAD_DIM * pair, 2 * HEAD_DIM * (pair + 1))
+    key_part = keys[:, span]
+    value_part = values[:, span]
+    key_tile = jnp.concatenate([key_part * masks[0], key_part * masks[1]], axis=0)
+    value_tile = jnp.concatenate([value_part * masks[0], value_part * masks[1]], axis=0)
+    return key_tile, value_tile
+
+
+def both_halves(left, values, reduce, empty):
+    first = reduce(jnp.where(left, values, empty), axis=-1, keepdims=True)
+    second = reduce(jnp.where(left, empty, values), axis=-1, keepdims=True)
+    return jnp.where(left, first, second)
+
+
+def text_weights(left, query, key_tile):
+    scores = mm_nt(query, key_tile)
+    return jnp.exp(scores - both_halves(left, scores, jnp.max, -1e30))
+
+
+def mix_text(query, keys, values, left, masks):
+    mixed = []
+    ones = jnp.concatenate(
+        [jnp.broadcast_to(masks[0], (HEAD_DIM, 2 * HEAD_DIM)), jnp.broadcast_to(masks[1], (HEAD_DIM, 2 * HEAD_DIM))],
+        axis=0,
+    )
+    for pair in range(query.shape[1] // (2 * HEAD_DIM)):
+        key_tile, value_tile = pair_tiles(keys, values, pair, masks)
+        one_query = query[:, 2 * HEAD_DIM * pair : 2 * HEAD_DIM * (pair + 1)]
+        weights = text_weights(left, one_query * jnp.asarray(HEAD_DIM**-0.5, LOW), key_tile)
+        weights = weights.astype(LOW)
+        mixed.append((mm(weights, value_tile) / mm(weights, ones)).astype(LOW))
+    return jnp.concatenate(mixed, axis=1)
+
+
+def middle_forward_body(
+    _,
+    x_ref,
+    z_own_ref,
+    z_other_ref,
+    out_own_ref,
+    out_other_ref,
+    query_own_ref,
+    query_other_ref,
+    cross_own_ref,
+    cross_other_ref,
+    down3_ref,
+    down3_other_ref,
+    up3_ref,
+    down4_ref,
+    up4_ref,
+    up4_other_ref,
+    down7_ref,
+    down7_other_ref,
+    up7_ref,
+    text_own_ref,
+    text_other_ref,
+    gain_two_ref,
+    gain_three_ref,
+    stream_one_ref,
+    stream_two_ref,
+    rows_three_ref,
+    query_out_own_ref,
+    query_out_other_ref,
+    z2_own_ref,
+    z2_other_ref,
+):
+    local = z_own_ref.shape[1]
+    left = lane_halves()
+    masks = half_masks()
+
+    def out_product(own, other, weight_own, weight_other_ref, down, down_other, up):
+        rank = (mm_nt(own, down) + mm_nt(other, down_other)).astype(LOW)
+        first, second = halves_of(weight_other_ref, local)
+        product = mm(own, weight_own[...]) + mm(rank, up)
+        return product + jnp.concatenate([mm(other, first), mm(other, second)], axis=1)
+
+    stream = x_ref[...].astype(WIDE) + out_product(
+        z_own_ref[...],
+        z_other_ref[...],
+        out_own_ref,
+        out_other_ref,
+        down3_ref[0, 0],
+        down3_other_ref[...],
+        up3_ref[0, 0],
+    )
+    stream_one_ref[...] = stream
+    rows_two = norm_rows(stream, gain_two_ref[...])[0].astype(LOW)
+    rank = mm_nt(rows_two, down4_ref[0, 0]).astype(LOW)
+    query_own = (mm(rows_two, query_own_ref[...]) + mm(rank, up4_ref[0, 0])).astype(LOW)
+    query_other = (
+        mm(rows_two, full_of(query_other_ref)) + mm(rank, up4_other_ref[...])
+    ).astype(LOW)
+    query_out_own_ref[...] = query_own
+    query_out_other_ref[...] = query_other
+    z2_own = mix_text(query_own, text_own_ref[0], text_own_ref[1], left, masks)
+    z2_other = mix_text(query_other, text_other_ref[0], text_other_ref[1], left, masks)
+    z2_own_ref[...] = z2_own
+    z2_other_ref[...] = z2_other
+    stream = stream + out_product(
+        z2_own,
+        z2_other,
+        cross_own_ref,
+        cross_other_ref,
+        down7_ref[0, 0],
+        down7_other_ref[...],
+        up7_ref[0, 0],
+    )
+    stream_two_ref[...] = stream
+    rows_three_ref[...] = norm_rows(stream, gain_three_ref[...])[0].astype(LOW)
+
+
+def chosen(table, entry, slot):
+    shape = (1, 1) + table.shape[2:]
+    return pl.BlockSpec(
+        shape, lambda t, m: (entry, m[slot], 0, 0), pipeline_mode=pl.Buffered(1)
+    )
+
+
+def middle_specs(weights, gathered, tables, packed):
+    out_weight, query_weight, cross_weight = weights
+    attention_down, attention_up, cross_down, cross_up = tables
+    shards, _, depth, local = gathered.shape
+    one = (shards, 1, depth, local)
+    rank = (RANK_UNIT, local)
+    specs = [
+        whole(out_weight.shape),
+        whole(one, (0, 0, 0, 0)),
+        whole(query_weight.shape),
+        whole(one, (0, 1, 0, 0)),
+        whole(cross_weight.shape),
+        whole(one, (0, 2, 0, 0)),
+        chosen(attention_down, 0, 3),
+        whole(rank, (0, 0)),
+        chosen(attention_up, 0, 3),
+        chosen(cross_down, 0, 4),
+        chosen(cross_up, 0, 4),
+        whole(rank, (0, 2)),
+        chosen(attention_down, 1, 7),
+        whole(rank, (0, 1)),
+        chosen(attention_up, 1, 7),
+    ]
+    args = (
+        out_weight,
+        gathered,
+        query_weight,
+        gathered,
+        cross_weight,
+        gathered,
+        attention_down,
+        packed,
+        attention_up,
+        cross_down,
+        cross_up,
+        packed,
+        attention_down,
+        packed,
+        attention_up,
+    )
+    return specs, args
+
+
+def middle_forward(meta, x, z_own, z_other, weights, gathered, tables, packed, text_own, text_other, gains):
+    frames, width = x.shape
+    local = z_own.shape[1]
+    block = min(256, frames)
+    wide = pl.BlockSpec((block, width), lambda t, m: (t, 0))
+    narrow = pl.BlockSpec((block, local), lambda t, m: (t, 0))
+    specs, args = middle_specs(weights, gathered, tables, packed)
+    return call(
+        middle_forward_body,
+        (frames // block,),
+        [wide, narrow, narrow]
+        + specs
+        + [whole(text_own.shape), whole(text_other.shape), whole((1, width)), whole((1, width))],
+        (wide, wide, wide, narrow, narrow, narrow, narrow),
+        (
+            shaped((frames, width), WIDE),
+            shaped((frames, width), WIDE),
+            shaped((frames, width), LOW),
+            shaped((frames, local), LOW),
+            shaped((frames, local), LOW),
+            shaped((frames, local), LOW),
+            shaped((frames, local), LOW),
+        ),
+        [],
+        6 * frames * width * width,
+        6 * width * width + 20 * frames * width,
+        "middle_forward",
+        (meta, x, z_own, z_other) + args + (text_own, text_other) + gains,
+    )
+
+
+def middle_back_body(
+    _,
+    last,
+    grad_ref,
+    stream_one_ref,
+    z_own_ref,
+    z_other_ref,
+    query_in_own_ref,
+    query_in_other_ref,
+    z2_own_ref,
+    z2_other_ref,
+    out_own_ref,
+    out_other_ref,
+    query_own_ref,
+    query_other_ref,
+    cross_own_ref,
+    cross_other_ref,
+    down3_ref,
+    down3_other_ref,
+    up3_ref,
+    down4_ref,
+    up4_ref,
+    up4_other_ref,
+    down7_ref,
+    down7_other_ref,
+    up7_ref,
+    text_own_ref,
+    text_other_ref,
+    gain_two_ref,
+    grad_one_ref,
+    dz_own_ref,
+    dz_other_ref,
+    text_grad_own_ref,
+    text_grad_other_ref,
+    ga3_ref,
+    gb3_ref,
+    ga4_ref,
+    gb4_ref,
+    ga7_ref,
+    gb7_ref,
+    key_total,
+    value_total,
+):
+    step = pl.program_id(0)
+    local = z_own_ref.shape[1]
+    pairs = local // (2 * HEAD_DIM)
+    left = lane_halves()
+    masks = half_masks()
+    scale = jnp.asarray(HEAD_DIM**-0.5, LOW)
+
+    @pl.when(step == 0)
+    def _():
+        key_total[...] = jnp.zeros_like(key_total)
+        value_total[...] = jnp.zeros_like(value_total)
+        for ref in (ga3_ref, gb3_ref, ga4_ref, gb4_ref, ga7_ref, gb7_ref):
+            ref[...] = jnp.zeros_like(ref)
+
+    def out_back(grad, own, other, weight_own, weight_other_ref, down, down_other, up, ga_ref, gb_ref):
+        rank = (mm_nt(own, down) + mm_nt(other, down_other)).astype(LOW)
+        grad_rank = mm_nt(grad, up).astype(LOW)
+        ga_ref[:, :local] += mm_tn(grad_rank, own)
+        ga_ref[:, local:] += mm_tn(grad_rank, other)
+        gb_ref[...] += mm_tn(rank, grad)
+        first, second = halves_of(weight_other_ref, local)
+        middle = grad.shape[1] // 2
+        grad_own = mm_nt(grad, weight_own[...]) + mm(grad_rank, down)
+        grad_other = (
+            mm_nt(grad[:, :middle], first)
+            + mm_nt(grad[:, middle:], second)
+            + mm(grad_rank, down_other)
+        )
+        return grad_own.astype(LOW), grad_other.astype(LOW)
+
+    grad = grad_ref[...]
+    dz2_own, dz2_other = out_back(
+        grad.astype(LOW),
+        z2_own_ref[...],
+        z2_other_ref[...],
+        cross_own_ref,
+        cross_other_ref,
+        down7_ref[0, 0],
+        down7_other_ref[...],
+        up7_ref[0, 0],
+        ga7_ref,
+        gb7_ref,
+    )
+
+    ones = jnp.concatenate(
+        [jnp.broadcast_to(masks[0], (HEAD_DIM, 2 * HEAD_DIM)), jnp.broadcast_to(masks[1], (HEAD_DIM, 2 * HEAD_DIM))],
+        axis=0,
+    )
+
+    def text_back(query, dz2, keys, values, part):
+        query_grads = []
+        for pair in range(pairs):
+            span = slice(2 * HEAD_DIM * pair, 2 * HEAD_DIM * (pair + 1))
+            key_tile, value_tile = pair_tiles(keys, values, pair, masks)
+            one_query = query[:, span] * scale
+            one_grad = dz2[:, span]
+            weights = text_weights(left, one_query, key_tile)
+            probs = weights / mm(weights.astype(LOW), ones)
+            prob_grads = mm_nt(one_grad, value_tile)
+            inner = both_halves(left, probs * prob_grads, jnp.sum, 0.0)
+            score_grads = (probs * (prob_grads - inner)).astype(LOW)
+            query_grads.append(
+                (mm(score_grads, key_tile) * HEAD_DIM**-0.5).astype(LOW)
+            )
+            key_total[part, pair] += mm_tn(score_grads, one_query)
+            value_total[part, pair] += mm_tn(probs.astype(LOW), one_grad)
+        return jnp.concatenate(query_grads, axis=1)
+
+    dq_own = text_back(query_in_own_ref[...], dz2_own, text_own_ref[0], text_own_ref[1], 0)
+    dq_other = text_back(query_in_other_ref[...], dz2_other, text_other_ref[0], text_other_ref[1], 1)
+
+    rows_two, normed, inverse = norm_rows(stream_one_ref[...], gain_two_ref[...])
+    rows_two = rows_two.astype(LOW)
+    rank = mm_nt(rows_two, down4_ref[0, 0]).astype(LOW)
+    grad_rank = (mm_nt(dq_own, up4_ref[0, 0]) + mm_nt(dq_other, up4_other_ref[...])).astype(LOW)
+    ga4_ref[...] += mm_tn(grad_rank, rows_two)
+    gb4_ref[:, :local] += mm_tn(rank, dq_own)
+    gb4_ref[:, local:] += mm_tn(rank, dq_other)
+    grad_rows = (
+        mm_nt(dq_own, query_own_ref[...])
+        + mm_nt(dq_other, full_of(query_other_ref))
+        + mm(grad_rank, down4_ref[0, 0])
+    )
+    grad = grad + norm_back(grad_rows, gain_two_ref[...], normed, inverse)
+    grad_one_ref[...] = grad
+    dz_own, dz_other = out_back(
+        grad.astype(LOW),
+        z_own_ref[...],
+        z_other_ref[...],
+        out_own_ref,
+        out_other_ref,
+        down3_ref[0, 0],
+        down3_other_ref[...],
+        up3_ref[0, 0],
+        ga3_ref,
+        gb3_ref,
+    )
+    dz_own_ref[...] = dz_own
+    dz_other_ref[...] = dz_other
+
+    @pl.when(step == last)
+    def _():
+        for total, slot in ((key_total, 0), (value_total, 1)):
+            for part, ref in ((0, text_grad_own_ref), (1, text_grad_other_ref)):
+                for pair in range(pairs):
+                    span = slice(2 * HEAD_DIM * pair, 2 * HEAD_DIM * (pair + 1))
+                    tile = total[part, pair]
+                    ref[slot, :, span] = jnp.where(left, tile[:HEAD_DIM], tile[HEAD_DIM:])
+
+
+def middle_back(
+    meta, grad, stream_one, z_own, z_other, q_own, q_other, z2_own, z2_other,
+    weights, gathered, tables, packed, text_own, text_other, gain,
+):
+    frames, width = grad.shape
+    local = z_own.shape[1]
+    pairs = local // (2 * HEAD_DIM)
+    block = min(256, frames)
+    wide = pl.BlockSpec((block, width), lambda t, m: (t, 0))
+    narrow = pl.BlockSpec((block, local), lambda t, m: (t, 0))
+    specs, args = middle_specs(weights, gathered, tables, packed)
+    rank = (RANK_UNIT, width)
+    steps = frames // block
+    return call(
+        lambda m, *refs: middle_back_body(m, steps - 1, *refs),
+        (steps,),
+        [wide, wide] + [narrow] * 6 + specs + [whole(text_own.shape), whole(text_other.shape), whole((1, width))],
+        (wide, narrow, narrow, whole(text_own.shape), whole(text_own.shape)) + (whole(rank),) * 6,
+        (
+            shaped((frames, width), WIDE),
+            shaped((frames, local), LOW),
+            shaped((frames, local), LOW),
+            shaped(text_own.shape, WIDE),
+            shaped(text_own.shape, WIDE),
+        )
+        + (shaped(rank, WIDE),) * 6,
+        [
+            pltpu.VMEM((2, pairs, 2 * HEAD_DIM, 2 * HEAD_DIM), WIDE),
+            pltpu.VMEM((2, pairs, 2 * HEAD_DIM, 2 * HEAD_DIM), WIDE),
+        ],
+        6 * frames * width * width,
+        6 * width * width + 24 * frames * width,
+        "middle_back",
+        (meta, grad, stream_one, z_own, z_other, q_own, q_other, z2_own, z2_other)
+        + args
+        + (text_own, text_other, gain),
+    )
+
+
+def feed_tile(
+    rows_ref, cot_ref, up_weight, down_weight, up_rank, down_rank,
+    ga9_ref, gb8_ref, branch, grad_rows, rank9, grad_rank8, rank8, grad_rank9,
+):
+    frames = rows_ref.shape[0]
+    block = min(256, frames)
+    ga9 = None
+    gb8 = None
+    for first in range(0, frames, block):
+        span = slice(first, first + block)
+        rows = rows_ref[span]
+        cot = cot_ref[span]
+        pre = mm(rows, up_weight) + mm(rank8[span], up_rank)
+        grad_hidden = mm_nt(cot, down_weight) + mm(grad_rank9[span], down_rank)
+        hidden, slope = gelu_parts(pre)
+        hidden = hidden.astype(LOW)
+        grad_pre = (grad_hidden * slope).astype(LOW)
+        branch[span] += mm(hidden, down_weight)
+        rank9[span] += mm_nt(hidden, down_rank)
+        grad_rows[span] += mm_nt(grad_pre, up_weight)
+        grad_rank8[span] += mm_nt(grad_pre, up_rank)
+        one = mm_tn(grad_rank9[span], hidden)
+        two = mm_tn(rank8[span], grad_pre)
+        ga9 = one if ga9 is None else ga9 + one
+        gb8 = two if gb8 is None else gb8 + two
+    ga9_ref[...] = ga9
+    gb8_ref[...] = gb8
+
+
+def feed_own_body(
+    _, rows_ref, cot_ref, up_weight_ref, down_weight_ref, up_rank_ref, down_rank_ref,
+    down8_ref, up9_ref,
+    branch_ref, grad_rows_ref, rank9_ref, grad_rank8_ref, ga9_ref, gb8_ref,
+    rank8, grad_rank9,
+):
+    @pl.when(pl.program_id(0) == 0)
+    def _():
+        rank8[...] = mm_nt(rows_ref[...], down8_ref[0]).astype(LOW)
+        grad_rank9[...] = mm_nt(cot_ref[...], up9_ref[0]).astype(LOW)
+        for ref in (branch_ref, grad_rows_ref, rank9_ref, grad_rank8_ref):
+            ref[...] = jnp.zeros_like(ref)
+
+    feed_tile(
+        rows_ref, cot_ref, up_weight_ref[...], down_weight_ref[...], up_rank_ref[0], down_rank_ref[0],
+        ga9_ref, gb8_ref, branch_ref, grad_rows_ref, rank9_ref, grad_rank8_ref, rank8, grad_rank9,
+    )
+
+
+def table_tile(tile, slot):
+    return pl.BlockSpec((1, RANK_UNIT, tile), lambda t, m: (m[slot], 0, t))
+
+
+def feed_own(meta, rows, cot, up_weight, down_weight, input_down, input_up, output_down, output_up, tile):
+    frames, width = rows.shape
+    hidden = up_weight.shape[1]
+    grads = pl.BlockSpec((RANK_UNIT, tile), lambda t, m: (0, t))
+    picked = pl.BlockSpec((1, RANK_UNIT, width), lambda t, m: (m[8], 0, 0))
+    picked_out = pl.BlockSpec((1, RANK_UNIT, width), lambda t, m: (m[9], 0, 0))
+    rank = (frames, RANK_UNIT)
+    return call(
+        feed_own_body,
+        (hidden // tile,),
+        [
+            whole((frames, width)),
+            whole((frames, width)),
+            pl.BlockSpec((width, tile), lambda t, m: (0, t)),
+            pl.BlockSpec((tile, width), lambda t, m: (t, 0)),
+            table_tile(tile, 8),
+            table_tile(tile, 9),
+            picked,
+            picked_out,
+        ],
+        (whole((frames, width)), whole((frames, width)), whole(rank), whole(rank), grads, grads),
+        (
+            shaped((frames, width), WIDE),
+            shaped((frames, width), WIDE),
+            shaped(rank, WIDE),
+            shaped(rank, WIDE),
+            shaped((RANK_UNIT, hidden), WIDE),
+            shaped((RANK_UNIT, hidden), WIDE),
+        ),
+        [pltpu.VMEM(rank, LOW), pltpu.VMEM(rank, LOW)],
+        8 * frames * width * hidden,
+        4 * width * hidden + 12 * frames * width,
+        "feed_own",
+        (meta, rows, cot, up_weight, down_weight, input_up, output_down, input_down, output_up),
+    )
+
+
+def feed_other_body(
+    _, last, rows_ref, cot_ref, up_weight_ref, down_weight_ref, up_rank_ref, down_rank_ref,
+    down8_ref, up9_ref, branch_in_ref, grad_rows_in_ref, rank9_in_ref, grad_rank8_in_ref,
+    stream_ref, gain_ref,
+    out_ref, grad_ref, ga9_ref, gb8_ref, ga8_ref, gb9_ref,
+    branch, grad_rows, rank9, grad_rank8, rank8, grad_rank9,
+):
+    step = pl.program_id(0)
+
+    @pl.when(step == 0)
+    def _():
+        rank8[...] = mm_nt(rows_ref[...], down8_ref[0]).astype(LOW)
+        grad_rank9[...] = mm_nt(cot_ref[...], up9_ref[0]).astype(LOW)
+        branch[...] = branch_in_ref[...]
+        grad_rows[...] = grad_rows_in_ref[...]
+        rank9[...] = rank9_in_ref[...]
+        grad_rank8[...] = grad_rank8_in_ref[...]
+
+    shards, _, depth, tile = up_weight_ref.shape
+    up_weight = up_weight_ref[...].reshape(shards * depth, tile)
+    down_weight = down_weight_ref[...].reshape(tile, down_weight_ref.shape[3])
+    feed_tile(
+        rows_ref, cot_ref, up_weight, down_weight, up_rank_ref[...], down_rank_ref[...],
+        ga9_ref, gb8_ref, branch, grad_rows, rank9, grad_rank8, rank8, grad_rank9,
+    )
+
+    @pl.when(step == last)
+    def _():
+        frames = rows_ref.shape[0]
+        block = min(128, frames)
+        last8 = grad_rank8[...].astype(LOW)
+        last9 = rank9[...].astype(LOW)
+        ga8_ref[...] = mm_tn(last8, rows_ref[...])
+        gb9_ref[...] = mm_tn(last9, cot_ref[...])
+        for first in range(0, frames, block):
+            span = slice(first, first + block)
+            stream = stream_ref[span]
+            out = stream + branch[span] + mm(last9[span], up9_ref[0])
+            out_ref[span] = out.astype(LOW)
+            _, normed, inverse = norm_rows(stream, gain_ref[...])
+            grad = grad_rows[span] + mm(last8[span], down8_ref[0])
+            grad_ref[span] = cot_ref[span].astype(WIDE) + norm_back(
+                grad, gain_ref[...], normed, inverse
+            )
+
+
+def feed_other(
+    meta, rows, cot, gathered, packed, first_pack, input_down, output_up, carried, stream, gain, tile
+):
+    frames, width = rows.shape
+    shards, quarters, depth, _ = gathered.shape
+    hidden = quarters // 2 * width
+    per_half = width // tile
+    own_shards = tile // (quarters // 2 * depth)
+    down_first = quarters // 2
+    grads = pl.BlockSpec((RANK_UNIT, tile), lambda t, m: (0, t))
+    picked = pl.BlockSpec((1, RANK_UNIT, width), lambda t, m: (m[8], 0, 0))
+    picked_out = pl.BlockSpec((1, RANK_UNIT, width), lambda t, m: (m[9], 0, 0))
+    rank = (frames, RANK_UNIT)
+    steps = hidden // tile
+    full = whole((frames, width))
+    return call(
+        lambda m, *refs: feed_other_body(m, steps - 1, *refs),
+        (steps,),
+        [
+            full,
+            full,
+            pl.BlockSpec(
+                (shards, 1, depth, tile),
+                lambda t, m: (0, down_first + t // per_half, 0, t % per_half),
+            ),
+            pl.BlockSpec((own_shards, down_first, depth, width), lambda t, m: (t, 0, 0, 0)),
+            pl.BlockSpec((RANK_UNIT, tile), lambda t, m: (0, first_pack // tile + t)),
+            pl.BlockSpec((RANK_UNIT, tile), lambda t, m: (0, (first_pack + hidden) // tile + t)),
+            picked,
+            picked_out,
+            full,
+            full,
+            whole(rank),
+            whole(rank),
+            full,
+            whole((1, width)),
+        ],
+        (full, full, grads, grads, whole((RANK_UNIT, width)), whole((RANK_UNIT, width))),
+        (
+            shaped((frames, width), LOW),
+            shaped((frames, width), WIDE),
+            shaped((RANK_UNIT, hidden), WIDE),
+            shaped((RANK_UNIT, hidden), WIDE),
+            shaped((RANK_UNIT, width), WIDE),
+            shaped((RANK_UNIT, width), WIDE),
+        ),
+        [
+            pltpu.VMEM((frames, width), WIDE),
+            pltpu.VMEM((frames, width), WIDE),
+            pltpu.VMEM(rank, WIDE),
+            pltpu.VMEM(rank, WIDE),
+            pltpu.VMEM(rank, LOW),
+            pltpu.VMEM(rank, LOW),
+        ],
+        8 * frames * width * hidden,
+        4 * width * hidden + 24 * frames * width,
+        "feed_other",
+        (meta, rows, cot, gathered, gathered, packed, packed, input_down, output_up)
+        + tuple(carried)
+        + (stream, gain),
+    )
+
+
+def last_norm_body(_, x_ref, own_ref, other_ref, grad_ref, gain_ref, out_ref):
+    _, normed, inverse = norm_rows(x_ref[...].astype(WIDE), gain_ref[...])
+    total = own_ref[...] + other_ref[...].astype(WIDE)
+    out_ref[...] = grad_ref[...] + norm_back(total, gain_ref[...], normed, inverse)
+
+
+def last_norm(meta, x, own, other, grad, gain):
+    frames, width = x.shape
+    block = min(256, frames)
+    rows = pl.BlockSpec((block, width), lambda t, _: (t, 0))
+    return call(
+        last_norm_body,
+        (frames // block,),
+        [rows, rows, rows, rows, whole((1, width))],
+        rows,
+        shaped(x.shape, WIDE),
+        [],
+        20 * x.size,
+        16 * x.size,
+        "last_norm",
+        (meta, x, own, other, grad, gain),
+    )
+
+
+def on_pair(
+    inputs,
+    encoder_text_states,
+    cotangent,
+    clip_adapter_index,
+    self_norm_gain,
+    cross_norm_gain,
+    feed_norm_gain,
+    self_query_key_value_weight,
+    self_output_weight,
+    cross_query_weight,
+    cross_key_value_weight,
+    cross_output_weight,
+    up_weight,
+    down_weight,
+    self_first_factors,
+    self_second_factors,
+    cross_first_factors,
+    cross_second_factors,
+    attention_first_factors,
+    attention_second_factors,
+    input_first_factors,
+    input_second_factors,
+    output_first_factors,
+    output_second_factors,
+):
+    x = inputs[0]
+    text = encoder_text_states[0]
+    cot = cotangent[0]
+    width = x.shape[1]
+    local = self_output_weight.shape[0]
+    hidden = up_weight.shape[1]
+    slots = input_first_factors.shape[0]
+    group_count = lax.axis_size("dp")
+    place = lax.axis_index("dp")
+    side = lax.axis_index("tensor")
+    picks = clip_adapter_index[0]
+    meta = jnp.concatenate([picks, side[None].astype(jnp.int32)])
+    gain_one, gain_two, gain_three = (
+        vec.reshape(1, width) for vec in (self_norm_gain, cross_norm_gain, feed_norm_gain)
+    )
+
+    def swap(array):
+        return lax.ppermute(array, "tensor", [(0, 1), (1, 0)])
+
+    depth = width // group_count
+    step = local // group_count
+
+    def share(weight, size):
+        return lax.dynamic_slice_in_dim(weight, place * size, size, axis=0)
+
+    def side_by_side(rows, count):
+        return rows.reshape(rows.shape[0], count, -1).transpose(1, 0, 2)
+
+    out_share = side_by_side(share(self_output_weight, step), 2).reshape(depth, local)
+    query_share = share(cross_query_weight, depth)
+    cross_share = side_by_side(share(cross_output_weight, step), 2).reshape(depth, local)
+    share_one = swap(jnp.stack([out_share, query_share, cross_share]))
+    gathered_one = lax.all_gather(share_one, "dp", axis=0)
+
+    rows_one = first_norm(meta, x, gain_one)
+    rows_one_other = swap(rows_one)
+
+    def pick(table, slot):
+        return lax.dynamic_index_in_dim(table, picks[slot], axis=0, keepdims=False)
+
+    packed = swap(
+        jnp.concatenate(
+            [
+                pick(attention_first_factors[0], 3),
+                pick(attention_first_factors[1], 7),
+                pick(cross_second_factors[0], 4),
+                jnp.zeros((RANK_UNIT, local), LOW),
+                pick(input_second_factors, 8),
+                pick(output_first_factors, 9),
+            ],
+            axis=1,
+        )
+    )
+    first_pack = 4 * local
+
+    parts = hidden // width
+    down_share = share(down_weight, parts * depth).reshape(parts, depth, width)
+    up_share = side_by_side(share(up_weight, depth), parts)
+    share_two = swap(jnp.concatenate([down_share, up_share], axis=0))
+    gathered_two = lax.all_gather(share_two, "dp", axis=0)
+
+    text_own = project_heads(
+        meta, text, cross_key_value_weight, cross_first_factors, cross_second_factors, 5, 1, "text_heads"
+    )
+    text_other = swap(text_own)
+    heads_own = project_heads(
+        meta, rows_one, self_query_key_value_weight, self_first_factors, self_second_factors, 0, 0, "own_heads"
+    )
+    heads_other = project_heads(
+        meta, rows_one_other, self_query_key_value_weight, self_first_factors, self_second_factors, 0, 0, "other_heads"
+    )
+    z_own_frames, z_other_frames = self_forward(meta, heads_own, heads_other)
+    z_other_heads = swap(z_other_frames)
+    weights = (self_output_weight, cross_query_weight, cross_output_weight)
+    tables = (attention_first_factors, attention_second_factors, cross_first_factors, cross_second_factors)
+    stream_one, stream_two, rows_three, q_own, q_other, z2_own, z2_other = middle_forward(
+        meta, x, z_own_frames, z_other_heads, weights, gathered_one, tables, packed,
+        text_own, text_other, (gain_two, gain_three),
+    )
+    tile = local
+    branch, grad_rows, rank9, grad_rank8, ga9_own, gb8_own = feed_own(
+        meta, rows_three, cot, up_weight, down_weight, input_first_factors, input_second_factors,
+        output_first_factors, output_second_factors, tile,
+    )
+    output, grad_two, ga9_other, gb8_other, ga8, gb9 = feed_other(
+        meta, rows_three, cot, gathered_two, packed, first_pack, input_first_factors,
+        output_second_factors, (branch, grad_rows, rank9, grad_rank8), stream_two, gain_three, tile,
+    )
+
+    (
+        grad_one, dz_own_heads, dz_other_heads, text_grad_own, text_grad_other,
+        ga3, gb3, ga4, gb4, ga7, gb7,
+    ) = middle_back(
+        meta, grad_two, stream_one, z_own_frames, z_other_heads, q_own, q_other, z2_own, z2_other,
+        weights, gathered_one, tables, packed, text_own, text_other, gain_two,
+    )
+    dz_other_frames = swap(dz_other_heads)
+    text_heads_grad = (text_grad_own + swap(text_grad_other.astype(LOW)).astype(WIDE)).astype(LOW)
+    text_rows, ga56, gb56 = project_back_heads(
+        meta, text, text_heads_grad, cross_key_value_weight, cross_first_factors, cross_second_factors,
+        5, 1, WIDE, "text_back",
+    )
+    grads_own, grads_other = self_back(meta, heads_own, heads_other, dz_own_heads, dz_other_frames)
+    partial_other, ga012_other, gb012_other = project_back_heads(
+        meta, rows_one_other, grads_other, self_query_key_value_weight, self_first_factors,
+        self_second_factors, 0, 0, LOW, "other_back",
+    )
+    received = swap(partial_other)
+    partial_own, ga012_own, gb012_own = project_back_heads(
+        meta, rows_one, grads_own, self_query_key_value_weight, self_first_factors,
+        self_second_factors, 0, 0, WIDE, "own_back",
+    )
+    input_grad = last_norm(meta, x, partial_own, received, grad_one, gain_one)
+
+    def my_half(array):
+        return lax.dynamic_slice_in_dim(array, side * (array.shape[1] // 2), array.shape[1] // 2, axis=1)
+
+    def other_half(array):
+        return lax.dynamic_slice_in_dim(
+            array, (1 - side) * (array.shape[1] // 2), array.shape[1] // 2, axis=1
+        )
+
+    def over_clips(mine, theirs, ready, columns):
+        received_part = swap(jnp.concatenate(theirs, axis=1).astype(LOW)).astype(WIDE)
+        both = jnp.concatenate(mine, axis=1) + received_part
+        labels = jnp.zeros((RANK_UNIT, 2 * HEAD_DIM), WIDE).at[0, : picks.shape[0]].set(picks.astype(WIDE))
+        payload = jnp.concatenate([both] + ready + [labels], axis=1).astype(LOW)
+        everyone = lax.all_gather(payload, "dp", axis=0)
+        names = everyone[:, 0, -2 * HEAD_DIM :][:, : picks.shape[0]].astype(jnp.int32)
+        results = []
+        first = 0
+        for column, size in columns:
+            choose = (names[:, column, None] == jnp.arange(slots, dtype=jnp.int32)[None]).astype(LOW)
+            results.append(
+                jnp.einsum(
+                    "cn,cpq->npq", choose, everyone[:, :, first : first + size],
+                    preferred_element_type=WIDE,
+                )
+            )
+            first += size
+        return results
+
+    def text_half(which):
+        return text_rows[:, : width // 2] if which == 0 else text_rows[:, width // 2 :]
+
+    text_mine = jnp.where(side == 0, text_half(0), text_half(1))
+    text_theirs = jnp.where(side == 0, text_half(1), text_half(0))
+    text_grad = text_mine + swap(text_theirs.astype(LOW)).astype(WIDE)
+
+    half_width = width // 2
+    early = over_clips(
+        [my_half(ga8), my_half(gb9), my_half(gb3), my_half(gb7), my_half(ga4), my_half(ga56[0]), my_half(ga56[1])]
+        + [ga9_own, gb8_own, ga3[:, :local], ga7[:, :local], gb4[:, :local]],
+        [other_half(ga8), other_half(gb9), other_half(gb3), other_half(gb7), other_half(ga4), other_half(ga56[0]), other_half(ga56[1])]
+        + [ga9_other, gb8_other, ga3[:, local:], ga7[:, local:], gb4[:, local:]],
+        [gb56[0], gb56[1]],
+        [
+            (8, half_width), (9, half_width), (3, half_width), (7, half_width), (4, half_width),
+            (5, half_width), (6, half_width), (9, hidden), (8, hidden), (3, local), (7, local), (4, local),
+            (5, local), (6, local),
+        ],
+    )
+    ga8_sum, gb9_sum, gb3_sum, gb7_sum, ga4_sum, ga5_sum, ga6_sum = early[:7]
+    ga9_sum, gb8_sum, ga3_sum, ga7_sum, gb4_sum, gb5_sum, gb6_sum = early[7:]
+    ga012 = ga012_own + ga012_other
+    gb012 = gb012_own + gb012_other
+    late = over_clips(
+        [my_half(ga012[j]) for j in range(3)],
+        [other_half(ga012[j]) for j in range(3)],
+        [gb012[j] for j in range(3)],
+        [(j, half_width) for j in range(3)] + [(j, local) for j in range(3)],
+    )
+    return (
+        output[None],
+        input_grad[None],
+        text_grad[None],
+        jnp.stack(late[:3]),
+        jnp.stack(late[3:]),
+        jnp.stack([ga4_sum, ga5_sum, ga6_sum]),
+        jnp.stack([gb4_sum, gb5_sum, gb6_sum]),
+        jnp.stack([ga3_sum, ga7_sum]),
+        jnp.stack([gb3_sum, gb7_sum]),
+        ga8_sum,
+        gb8_sum,
+        ga9_sum,
+        gb9_sum,
+    )
+
+
 def solution(mesh):
     in_specs = (
         P("dp", "tensor", None),
@@ -486,6 +1695,7 @@
         P(None, None, "tensor"),
         P(None, None, "tensor"),
     )
+    layer = on_pair if mesh.shape["tensor"] == 2 else on_device
     return jax.shard_map(
-        on_device, mesh=mesh, in_specs=in_specs, out_specs=out_specs, check_vma=False
-    )
+        layer, mesh=mesh, in_specs=in_specs, out_specs=out_specs, check_vma=False
+    )

time: 1120 us -> 562 us (0.50); the launches traced: 1100 us -> 555 us
  matrix products: 438 us -> 7.61 us
  waiting for transfers between devices: 486 us -> 171 us
  Pallas kernels: 0 us -> 286 us
  other arithmetic: 126 us -> 6.7 us
  local copies, waits for them, and re-layouts: 28.2 us -> 42.5 us
  starting transfers between devices: 2.14 us -> 16 us
    dot_general x164 -> x20, matrix products: 438 us -> 7.61 us  [over_clips(): jnp.einsum('cn,cpq->npq', choose, everyone[:, :, first:first + size], pre...]
    pallas_call x0 -> x14, Pallas kernels: none -> 286 us  [call(): pl.pallas_call(body, grid_spec=pltpu.PrefetchScalarGridSpec(num_scalar_pr...]
    reduce_scatter x12 -> x0, waiting for transfers between devices: 208 us -> none  [the longest x2 79.2 us: out_forward(): lax.psum_scatter(partial_out.astype(jnp.bfloat16), 'tensor', scatter_dime...]
    all_gather x6 -> x4, waiting for transfers between devices: 176 us -> 67.8 us  [the longest x2 67.7 us: over_clips(): everyone = lax.all_gather(payload, 'dp', axis=0)]
    ppermute x0 -> x12, waiting for transfers between devices: none -> 104 us  [swap(): return lax.ppermute(array, 'tensor', [(0, 1), (1, 0)])]
    psum x1 -> x0, waiting for transfers between devices: 101 us -> none  [on_device(): lax.psum(sum_self_a.astype(jnp.bfloat16), 'dp').astype(jnp.float32)]
    convert_element_type x24 -> x6, other arithmetic: 66.4 us -> 1.82 us  [the longest x1 1.07 us: on_pair(): text_grad_other.astype(LOW)]
    reduce_sum x13 -> x0, other arithmetic: 36 us -> none  [the longest x4 15.4 us: attention_forward(): summed = jnp.sum(exponent, axis=-1, keepdims=True)]
  transfers between devices with their start and end apart: 19 -> 16, of which waited for: 13 -> 10; matrix products, arithmetic and copies ran while one was open for 32% -> 4% of each run, Pallas kernels for 0% -> 37%
where the time goes in v1:
time: 562 us; the launch traced here: 555 us
  Pallas kernels  286 us (51%)
  waiting for transfers between devices  171 us (30%)
  local copies, waits for them, and re-layouts  42.5 us (8%)
  between operations  24.4 us (4%)
  starting transfers between devices  16 us (3%)
  matrix products  7.61 us (1%)
  other arithmetic  6.7 us (1%)
    pallas_call x14, Pallas kernels, call(): pl.pallas_call(body, grid_spec=pltpu.PrefetchScalarGridSpec(num_scalar_pr...  286 us
    ppermute x12, waiting for transfers between devices, swap(): return lax.ppermute(array, 'tensor', [(0, 1), (1, 0)])  104 us
    all_gather x2, waiting for transfers between devices, over_clips(): everyone = lax.all_gather(payload, 'dp', axis=0)  67.7 us
    unnamed x94, local copies, waits for them, and re-layouts  25 us
    ppermute x12, starting transfers between devices, swap(): return lax.ppermute(array, 'tensor', [(0, 1), (1, 0)])  15.8 us
  transfers between devices with their start and end apart: 16, of which 10 were waited for; matrix products, arithmetic and copies ran while one was open for 4% of the time, Pallas kernels for 37%

profile of v1, /device:TPU:0, one launch (start us, length us, event | category | flops | bytes accessed | tf_op | source)
XLA Modules:
  0.0 554.6 jit_solution(16892770397529301258)
XLA Ops:
  9.4 3.0 collective-permute-start.2
  12.4 10.2 %collective-permute-done.2 = bf16[3,96,768]{2,1,0:T(8,128)(2,1)S(1)} collective-permute-done((bf16[3,96,768]{2,1,0:T(8,128)(2,1)S(1)}, bf16[3,96,768]{2,1,0:T(8,128)(2,1)S(1)}, u32[]{:S(2)}, u32[]{:S(2)}) %collective-permute-start.2) | collective-permute-done | bytes 442400 | tf_op jit(solution)/shard_map/ppermute | solution.py:1484
  27.6 25.4 %collective-permute-done.5 = bf16[4,96,1536]{2,1,0:T(8,128)(2,1)S(1)} collective-permute-done((bf16[4,96,1536]{2,1,0:T(8,128)(2,1)S(1)}, bf16[4,96,1536]{2,1,0:T(8,128)(2,1)S(1)}, u32[]{:S(2)}, u32[]{:S(2)}) %collective-permute-start.5) | collective-permute-done | bytes 1179680 | tf_op jit(solution)/shard_map/ppermute | solution.py:1484
  55.4 3.9 first_norm.1.act_ref.refs_0_
  69.4 12.3 %own_heads.1.own_ref = bf16[3,512,768]{2,1,0:T(8,128)(2,1)} custom-call(s32[11]{0:T(128)} %pad_add_fusion._.meta.m, bf16[512,1536]{1,0:T(8,128)(2,1)} %first_norm.1.act_ref.refs_0_, bf16[3,1536,768]{2,1,0:T(8,128)(2,1)} %refs_2_.4, bf16[3,8,16,1536]{3,2,1,0:T(8,128)(2,1)} %refs_3_.4, bf16[3,8,16,768]{3,2,1,0:T(8,128)(2,1)} %refs_4_.4), custom_call_target="tpu_custom_call" | custom-call | flops 3623878656 | bytes 11010048 | tf_op jit(solution)/shard_map/own_heads/pallas_call | solution.py:510
  81.7 12.5 %collective-permute-done.act_ref.refs_0_ = bf16[512,1536]{1,0:T(8,128)(2,1)} collective-permute-done((bf16[512,1536]{1,0:T(8,128)(2,1)}, bf16[512,1536]{1,0:T(8,128)(2,1)}, u32[]{:S(2)}, u32[]{:S(2)}) %collective-permute-start) | collective-permute-done | bytes 1572896 | tf_op jit(solution)/shard_map/ppermute | solution.py:1484
  94.2 12.3 %other_heads.1.other_ref = bf16[3,512,768]{2,1,0:T(8,128)(2,1)} custom-call(s32[11]{0:T(128)} %pad_add_fusion._.meta.m, bf16[512,1536]{1,0:T(8,128)(2,1)} %collective-permute-done.act_ref.refs_0_, bf16[3,1536,768]{2,1,0:T(8,128)(2,1)} %refs_2_.4, bf16[3,8,16,1536]{3,2,1,0:T(8,128)(2,1)} %refs_3_.4, bf16[3,8,16,768]{3,2,1,0:T(8,128)(2,1)} %refs_4_.4), custom_call_target="tpu_custom_call" | custom-call | flops 3623878656 | bytes 11010048 | tf_op jit(solution)/shard_map/other_heads/pallas_call | solution.py:510
  106.5 22.1 %self_forward.1 = (bf16[512,768]{1,0:T(8,128)(2,1)}, bf16[512,768]{1,0:T(8,128)(2,1)}) custom-call(s32[11]{0:T(128)} %pad_add_fusion._.meta.m, bf16[3,512,768]{2,1,0:T(8,128)(2,1)} %own_heads.1.own_ref, bf16[3,512,768]{2,1,0:T(8,128)(2,1)} %other_heads.1.other_ref), custom_call_target="tpu_custom_call" | custom-call | flops 4026531840 | bytes 6291456 | tf_op jit(solution)/shard_map/self_forward/pallas_call | solution.py:510
  134.4 4.8 text_heads.1.text_own_ref.refs_23_
  141.6 14.6 %collective-permute-done.4.text_other_ref.refs_24_ = bf16[2,64,768]{2,1,0:T(8,128)(2,1)S(1)} collective-permute-done((bf16[2,64,768]{2,1,0:T(8,128)(2,1)}, bf16[2,64,768]{2,1,0:T(8,128)(2,1)S(1)}, u32[]{:S(2)}, u32[]{:S(2)}) %collective-permute-start.4) | collective-permute-done | bytes 196640 | tf_op jit(solution)/shard_map/ppermute | solution.py:1484
  157.3 32.7 %middle_forward.1 = (f32[512,1536]{1,0:T(8,128)}, f32[512,1536]{1,0:T(8,128)}, bf16[512,1536]{1,0:T(8,128)(2,1)}, bf16[512,768]{1,0:T(8,128)(2,1)}, bf16[512,768...) custom-call(s32[11]{0:T(128)} %pad_add_fusion._.meta.m, bf16[512,1536]{1,0:T(8,128)(2,1)} %bitcast.159, ...), custom_call_target="tpu_custom_call" | custom-call | flops 7247757312 | bytes 29884416 | tf_op jit(solution)/shard_map/middle_forward/pallas_call | solution.py:510
  190.0 34.5 %feed_own.1 = (f32[512,1536]{1,0:T(8,128)}, f32[512,1536]{1,0:T(8,128)}, f32[512,16]{1,0:T(8,128)}, f32[512,16]{1,0:T(8,128)}, f32[16,3072]{1,0:T(8,128)}, /*index=5*/f32[16,3072]{1,0:T(8,128)}) custom-call(s32[11]{0:T(128)} %pad_add_fusion._.meta.m, bf16[512,1536]{1,0:T(8,128)(2,1)} %get-tuple-element.78.rows_ref.refs_0_, bf16[512,1536]{1,0:T(8,128)(2,1)} %bitcast.176, ...), custom_call_target="tpu_custom_call" | custom-call | flops 19327352832 | bytes 28311552 | tf_op jit(solution)/shard_map/feed_own/pallas_call | solution.py:510
  224.6 40.5 %feed_other.1 = (bf16[512,1536]{1,0:T(8,128)(2,1)}, f32[512,1536]{1,0:T(8,128)}, f32[16,3072]{1,0:T(8,128)}, f32[16,3072]{1,0:T(8,128)}, f32[16,1536]{1,0:T(8,128)}, /*index=5*/f32[16,1536]{1,0:T(8,128)}) custom-call(s32[11]{0:T(128)} %pad_add_fusion._.meta.m, bf16[512,1536]{1,0:T(8,128)(2,1)} %get-tuple-element.78.rows_ref.refs_0_, ...), custom_call_target="tpu_custom_call" | custom-call | flops 19327352832 | bytes 37748736 | tf_op jit(solution)/shard_map/feed_other/pallas_call | solution.py:510
  265.1 39.4 %middle_back.1 = (f32[512,1536]{1,0:T(8,128)}, bf16[512,768]{1,0:T(8,128)(2,1)}, bf16[512,768]{1,0:T(8,128)(2,1)}, f32[2,64,768]{2,1,0:T(8,128)}, f32[2,64,768]{...) custom-call(s32[11]{0:T(128)} %pad_add_fusion._.meta.m, ...), custom_call_target="tpu_custom_call" | custom-call | flops 7247757312 | bytes 33030144 | tf_op jit(solution)/shard_map/middle_back/pallas_call | solution.py:510
  314.2 6.9 %text_back.1 = (f32[64,1536]{1,0:T(8,128)}, f32[2,16,1536]{2,1,0:T(8,128)}, f32[2,16,768]{2,1,0:T(8,128)}) custom-call(s32[11]{0:T(128)} %pad_add_fusion._.meta.m, bf16[64,1536]{1,0:T(8,128)(2,1)} %bitcast.166, bf16[2,64,768]{2,1,0:T(8,128)(2,1)} %add_convert_fusion.1.refs_1_, bf16[2,1536,768]{2,1,0:T(8,128)(2,1)} %refs_2_.5, ...), custom_call_target="tpu_custom_call" | custom-call | flops 301989888 | bytes 5505024 | tf_op jit(solution)/shard_map/text_back/pallas_call | solution.py:510
  323.6 6.6 %collective-permute-done.6.grad_other_ref = bf16[512,768]{1,0:T(8,128)(2,1)S(1)} collective-permute-done((bf16[512,768]{1,0:T(8,128)(2,1)}, bf16[512,768]{1,0:T(8,128)(2,1)S(1)}, u32[]{:S(2)}, u32[]{:S(2)}) %collective-permute-start.6) | collective-permute-done | bytes 786464 | tf_op jit(solution)/shard_map/ppermute | solution.py:1484
  331.1 40.0 %self_back.1 = (bf16[3,512,768]{2,1,0:T(8,128)(2,1)}, bf16[3,512,768]{2,1,0:T(8,128)(2,1)}) custom-call(s32[11]{0:T(128)} %pad_add_fusion._.meta.m, bf16[3,512,768]{2,1,0:T(8,128)(2,1)} %own_heads.1.own_ref, bf16[3,512,768]{2,1,0:T(8,128)(2,1)} %other_heads.1.other_ref, bf16[512,768]{1,0:T(8,128)(2,1)} %get-tuple-element.91.grad_own_ref, ...), custom_call_target="tpu_custom_call" | custom-call | flops 10066329600 | bytes 11796480 | tf_op jit(solution)/shard_map/self_back/pallas_call | solution.py:510
  371.1 15.0 %own_back.1 = (f32[512,1536]{1,0:T(8,128)}, f32[3,16,1536]{2,1,0:T(8,128)}, f32[3,16,768]{2,1,0:T(8,128)}) custom-call(s32[11]{0:T(128)} %pad_add_fusion._.meta.m, bf16[512,1536]{1,0:T(8,128)(2,1)} %first_norm.1.act_ref.refs_0_, bf16[3,512,768]{2,1,0:T(8,128)(2,1)} %get-tuple-element.93.refs_1_, bf16[3,1536,768]{2,1,0:T(8,128)(2,1)} %refs_2_.4, ...), custom_call_target="tpu_custom_call" | custom-call | flops 3623878656 | bytes 14155776 | tf_op jit(solution)/shard_map/own_back/pallas_call | solution.py:510
  386.1 14.5 %other_back.1 = (bf16[512,1536]{1,0:T(8,128)(2,1)}, f32[3,16,1536]{2,1,0:T(8,128)}, f32[3,16,768]{2,1,0:T(8,128)}) custom-call(s32[11]{0:T(128)} %pad_add_fusion._.meta.m, bf16[512,1536]{1,0:T(8,128)(2,1)} %collective-permute-done.act_ref.refs_0_, bf16[3,512,768]{2,1,0:T(8,128)(2,1)} %get-tuple-element.95.refs_1_, bf16[3,1536,768]{2,1,0:T(8,128)(2,1)} %refs_2_.4, ...), custom_call_target="tpu_custom_call" | custom-call | flops 3623878656 | bytes 14155776 | tf_op jit(solution)/shard_map/other_back/pallas_call | solution.py:510
  403.4 3.7 collective-permute-done.10
  411.0 29.8 %collective-permute-done.9 = bf16[64,768]{1,0:T(8,128)(2,1)S(1)} collective-permute-done((bf16[64,768]{1,0:T(8,128)(2,1)S(1)}, bf16[64,768]{1,0:T(8,128)(2,1)S(1)}, u32[]{:S(2)}, u32[]{:S(2)}) %collective-permute-start.9) | collective-permute-done | bytes 98336 | tf_op jit(solution)/shard_map/ppermute | solution.py:1484
  442.6 7.0 %last_norm.1 = f32[512,1536]{1,0:T(8,128)} custom-call(s32[11]{0:T(128)} %pad_add_fusion._.meta.m, bf16[512,1536]{1,0:T(8,128)(2,1)} %bitcast.160, f32[512,1536]{1,0:T(8,128)} %get-tuple-element.94.own_ref, bf16[512,1536]{1,0:T(8,128)(2,1)} %copy-done.3, f32[512,1536]{1,0:T(8,128)} %get-tuple-element.97.grad_ref, f32[1,1536]{1,0:T(1,128)} %reshape.234.gain_ref), custom_call_target="tpu_custom_call" | custom-call | flops 15728640 | bytes 12582912 | tf_op jit(solution)/shard_map/last_norm/pallas_call | solution.py:510
  458.2 66.3 %all-gather.9.cloned.1.call-done = bf16[16,16,15488]{2,1,0:T(8,128)(2,1)} async-done(((bf16[1,16,15488]{2,1,0:T(8,128)(2,1)}), bf16[16,16,15488]{2,1,0:T(8,128)(2,1)}) %all-gather.9.cloned.1.call-update) | async-done | bytes 7929872 | tf_op jit(solution)/shard_map/all_gather | solution.py:1594
  525.6 2.6 fusion.83
  (202 shorter events, 69.4 us)
Async XLA Ops:
  7.2 149.1 %all-gather.11.cloned.1.call-start = ((), (), s32[]{:S(2)}) async-start(), calls=%async_computation.2 | async-start | bytes 7520256 | tf_op jit(solution)/shard_map/all_gather | solution.py:1499
  9.4 13.2 %collective-permute-start.2 = (bf16[3,96,768]{2,1,0:T(8,128)(2,1)S(1)}, bf16[3,96,768]{2,1,0:T(8,128)(2,1)S(1)}, u32[]{:S(2)}, u32[]{:S(2)}) collective-permute-start(bf16[3,96,768]{2,1,0:T(8,128)(2,1)S(1)} %pad_maximum_fusion.8), channel_id=1, source_target_pairs={{0,1},{1,0},{2,3},{3,2},{4,5},{5,4},{6,7},{7,6},{8,9},{9,8},{10,11... | collective-permute-start | bytes 1327112 | tf_op jit(solution)/shard_map/ppermute | solution.py:1484
  23.4 201.2 %all-gather.13.cloned.1.call-start = ((), (), s32[]{:S(2)}) async-start(), calls=%async_computation.3 | async-start | bytes 20054016 | tf_op jit(solution)/shard_map/all_gather | solution.py:1526
  25.7 28.5 %copy-start.23 = (f32[1536]{0:T(1024)S(1)}, f32[1536]{0:T(1024)}, u32[]{:S(2)}) copy-start(f32[1536]{0:T(1024)} %param.32) | copy-start | bytes 18436
  25.7 29.0 %copy-start.22 = (s32[1,10]{1,0:T(1,128)S(1)}, s32[1,10]{1,0:T(1,128)}, u32[]{:S(2)}) copy-start(s32[1,10]{1,0:T(1,128)} %param.31) | copy-start | bytes 124
  25.8 27.2 %collective-permute-start.5 = (bf16[4,96,1536]{2,1,0:T(8,128)(2,1)S(1)}, bf16[4,96,1536]{2,1,0:T(8,128)(2,1)S(1)}, u32[]{:S(2)}, u32[]{:S(2)}) collective-permute-start(bf16[4,96,1536]{2,1,0:T(8,128)(2,1)S(1)} %pad_maximum_fusion), channel_id=1, source_target_pairs={{0,1},{1,0},{2,3},{3,2},{4,5},{5,4},{6,7},{7,6},{8,9},{9,8},{10,11... | collective-permute-start | bytes 3538952 | tf_op jit(solution)/shard_map/ppermute | solution.py:1484
  54.1 397.0 %all-gather.7.cloned.1.call-start = ((), (), s32[]{:S(2)}) async-start(), calls=%async_computation | async-start | bytes 2576384 | tf_op jit(solution)/shard_map/all_gather | solution.py:1594
  55.4 13.9 %copy-start.1 = (bf16[2,8,16,768]{3,2,1,0:T(8,128)(2,1)S(1)}, bf16[2,8,16,768]{3,2,1,0:T(8,128)(2,1)}, u32[]{:S(2)}) copy-start(bf16[2,8,16,768]{3,2,1,0:T(8,128)(2,1)} %refs_20_.1) | copy-start | bytes 1179652
  55.4 14.0 %slice-start = ((bf16[3,8,16,768]{3,2,1,0:T(8,128)(2,1)}), bf16[1,8,16,768]{3,2,1,0:T(8,128)(2,1)S(1)}, s32[]{:S(2)}) async-start(bf16[3,8,16,768]{3,2,1,0:T(8,128)(2,1)} %refs_4_.5), calls=%async_computation.4 | async-start | bytes 393216 | tf_op jit(solution)/shard_map/slice | solution.py:1512
  59.3 34.9 %collective-permute-start = (bf16[512,1536]{1,0:T(8,128)(2,1)}, bf16[512,1536]{1,0:T(8,128)(2,1)}, u32[]{:S(2)}, u32[]{:S(2)}) collective-permute-start(bf16[512,1536]{1,0:T(8,128)(2,1)} %first_norm.1.act_ref.refs_0_), channel_id=1, source_target_pairs={{0,1},{1,0},{2,3},{3,2},{4,5},{5,4},{6,7},{7,6},{8,9},{9,8},{10,11... | collective-permute-start | bytes 4718600 | tf_op jit(solution)/shard_map/ppermute | solution.py:1484
  128.6 27.6 %collective-permute-start.1 = (bf16[512,768]{1,0:T(8,128)(2,1)}, bf16[512,768]{1,0:T(8,128)(2,1)S(1)}, u32[]{:S(2)}, u32[]{:S(2)}) collective-permute-start(bf16[512,768]{1,0:T(8,128)(2,1)} %get-tuple-element.77), channel_id=1, source_target_pairs={{0,1},{1,0},{2,3},{3,2},{4,5},{5,4},{6,7},{7,6},{8,9},{9,8},{10,11... | collective-permute-start | bytes 2359304 | tf_op jit(solution)/shard_map/ppermute | solution.py:1484
  133.6 22.7 %collective-permute-start.3 = (bf16[16,9216]{1,0:T(8,128)(2,1)S(1)}, bf16[16,9216]{1,0:T(8,128)(2,1)S(1)}, u32[]{:S(2)}, u32[]{:S(2)}) collective-permute-start(bf16[16,9216]{1,0:T(8,128)(2,1)S(1)} %bitcast_dynamic-update-slice_fusion), channel_id=1, source_target_pairs={{0,1},{1,0},{2,3},{3,2},{4,5},{5,4},{6,7},{7,6},{8,9},{9,8},{10,11... | collective-permute-start | bytes 884744 | tf_op jit(solution)/shard_map/ppermute | solution.py:1484
  139.3 16.9 %collective-permute-start.4 = (bf16[2,64,768]{2,1,0:T(8,128)(2,1)}, bf16[2,64,768]{2,1,0:T(8,128)(2,1)S(1)}, u32[]{:S(2)}, u32[]{:S(2)}) collective-permute-start(bf16[2,64,768]{2,1,0:T(8,128)(2,1)} %text_heads.1.text_own_ref.refs_23_), channel_id=1, source_target_pairs={{0,1},{1,0},{2,3},{3,2},{4,5},{5,4},{6,7},{7,6},{8,9},{9,8},{10,11... | collective-permute-start | bytes 589832 | tf_op jit(solution)/shard_map/ppermute | solution.py:1484
  265.1 41.2 %copy-start.21 = (f32[16,1536]{1,0:T(8,128)S(1)}, f32[16,1536]{1,0:T(8,128)}, u32[]{:S(2)}) copy-start(f32[16,1536]{1,0:T(8,128)} %get-tuple-element.105) | copy-start | bytes 294916
  265.1 41.2 %copy-start.20 = (f32[16,1536]{1,0:T(8,128)S(1)}, f32[16,1536]{1,0:T(8,128)}, u32[]{:S(2)}) copy-start(f32[16,1536]{1,0:T(8,128)} %get-tuple-element.106) | copy-start | bytes 294916
  304.5 8.9 %copy-start.8 = (f32[2,64,768]{2,1,0:T(8,128)S(1)}, f32[2,64,768]{2,1,0:T(8,128)}, u32[]{:S(2)}) copy-start(f32[2,64,768]{2,1,0:T(8,128)} %get-tuple-element.98) | copy-start | bytes 1179652
  305.6 7.8 %collective-permute-start.8 = (bf16[2,64,768]{2,1,0:T(8,128)(2,1)S(1)}, bf16[2,64,768]{2,1,0:T(8,128)(2,1)S(1)}, u32[]{:S(2)}, u32[]{:S(2)}) collective-permute-start(bf16[2,64,768]{2,1,0:T(8,128)(2,1)S(1)} %convert_element_type.70), channel_id=1, source_target_pairs={{0,1},{1,0},{2,3},{3,2},{4,5},{5,4},{6,7},{7,6},{8,9},{9,8},{10,11... | collective-permute-start | bytes 589832 | tf_op jit(solution)/shard_map/ppermute | solution.py:1484
  309.6 20.7 %collective-permute-start.6 = (bf16[512,768]{1,0:T(8,128)(2,1)}, bf16[512,768]{1,0:T(8,128)(2,1)S(1)}, u32[]{:S(2)}, u32[]{:S(2)}) collective-permute-start(bf16[512,768]{1,0:T(8,128)(2,1)} %get-tuple-element.92), channel_id=1, source_target_pairs={{0,1},{1,0},{2,3},{3,2},{4,5},{5,4},{6,7},{7,6},{8,9},{9,8},{10,11... | collective-permute-start | bytes 2359304 | tf_op jit(solution)/shard_map/ppermute | solution.py:1484
  322.2 85.7 %collective-permute-start.11 = (bf16[16,13824]{1,0:T(8,128)(2,1)S(1)}, bf16[16,13824]{1,0:T(8,128)(2,1)S(1)}, u32[]{:S(2)}, u32[]{:S(2)}) collective-permute-start(bf16[16,13824]{1,0:T(8,128)(2,1)S(1)} %constant_dynamic-update-slice_fusion.21), channel_id=1, source_target_pairs={{0,1},{1,0},{2,3},{3,2},{4,5},{5,4},{6,7},{7,6},{8,9},{9,8},{10,11... | collective-permute-start | bytes 1327112 | tf_op jit(solution)/shard_map/ppermute | solution.py:1484
  386.1 14.5 %copy-start.10 = (f32[3,16,1536]{2,1,0:T(8,128)S(1)}, f32[3,16,1536]{2,1,0:T(8,128)}, u32[]{:S(2)}) copy-start(f32[3,16,1536]{2,1,0:T(8,128)} %get-tuple-element.101) | copy-start | bytes 884740
  401.8 5.2 collective-permute-start.10
  407.9 116.6 %all-gather.9.cloned.1.call-start = ((), (), s32[]{:S(2)}) async-start(), calls=%async_computation.1 | async-start | bytes 8425472 | tf_op jit(solution)/shard_map/all_gather | solution.py:1594
  408.8 32.6 %collective-permute-start.7 = (bf16[512,1536]{1,0:T(8,128)(2,1)}, bf16[512,1536]{1,0:T(8,128)(2,1)S(1)}, u32[]{:S(2)}, u32[]{:S(2)}) collective-permute-start(bf16[512,1536]{1,0:T(8,128)(2,1)} %get-tuple-element.96), channel_id=1, source_target_pairs={{0,1},{1,0},{2,3},{3,2},{4,5},{5,4},{6,7},{7,6},{8,9},{9,8},{10,11... | collective-permute-start | bytes 4718600 | tf_op jit(solution)/shard_map/ppermute | solution.py:1484
  410.4 30.4 %collective-permute-start.9 = (bf16[64,768]{1,0:T(8,128)(2,1)S(1)}, bf16[64,768]{1,0:T(8,128)(2,1)S(1)}, u32[]{:S(2)}, u32[]{:S(2)}) collective-permute-start(bf16[64,768]{1,0:T(8,128)(2,1)S(1)} %select_convert_fusion), channel_id=1, source_target_pairs={{0,1},{1,0},{2,3},{3,2},{4,5},{5,4},{6,7},{7,6},{8,9},{9,8},{10,11... | collective-permute-start | bytes 294920 | tf_op jit(solution)/shard_map/ppermute | solution.py:1484
  (20 other events, 72.6 us)
Sparse Core Ops, SparseCore 0:
  23.5 68.0 all-gather.10
  93.8 97.4 all-gather.12
  408.0 43.0 all-gather.6
  453.6 70.8 all-gather.8

commit v2 on v1

--- a/solution.py
+++ b/solution.py
@@ -62,7 +62,7 @@
     return (grad_rows, grad_down, grad_up)
 
 
-def causal_keep(first_row, block_rows, key_count):
+def causal_frames(first_row, block_rows, key_count):
     query_at = first_row + jnp.arange(block_rows, dtype=jnp.int32)[:, None]
     key_at = jnp.arange(key_count, dtype=jnp.int32)[None, :]
     return key_at <= query_at
@@ -88,7 +88,7 @@
             * score_scale
         )
         if causal:
-            scores = jnp.where(causal_keep(first_row, block_rows, key_end), scores, -1e30)
+            scores = jnp.where(causal_frames(first_row, block_rows, key_end), scores, -1e30)
         largest = jnp.max(scores, axis=-1, keepdims=True)
         exponent = jnp.exp(scores - largest)
         summed = jnp.sum(exponent, axis=-1, keepdims=True)
@@ -124,7 +124,7 @@
             * score_scale
         )
         if causal:
-            scores = jnp.where(causal_keep(first_row, block_rows, key_end), scores, -1e30)
+            scores = jnp.where(causal_frames(first_row, block_rows, key_end), scores, -1e30)
         probs = jnp.exp(scores - log_totals[:, :, first_row : first_row + block_rows])
         grad_values = grad_values.at[:, :key_end].add(
             jnp.einsum(
@@ -450,6 +450,7 @@
 WIDE = jnp.float32
 VMEM_BYTES = 58 * 1024 * 1024
 RANK_UNIT = 16
+COST_SCALE = 1
 
 
 def mm(left, right, left_dim=1, right_dim=0):
@@ -464,6 +465,10 @@
 
 def mm_tn(left, right):
     return mm(left, right, 0, 0)
+
+
+def low_rank(factor, rows):
+    return mm_nt(factor, rows).astype(LOW)
 
 
 def norm_rows(rows, gain):
@@ -506,7 +511,7 @@
     return pl.BlockSpec(shape, lambda *_: place, pipeline_mode=pl.Buffered(1))
 
 
-def call(body, grid, in_specs, out_specs, out_shape, scratch, flops, moved, name, args):
+def call(body, grid, in_specs, out_specs, out_shape, scratch, flops, moved, name, args, vmem=VMEM_BYTES):
     return pl.pallas_call(
         body,
         grid_spec=pltpu.PrefetchScalarGridSpec(
@@ -518,15 +523,84 @@
         ),
         out_shape=out_shape,
         compiler_params=pltpu.CompilerParams(
-            dimension_semantics=("arbitrary",) * len(grid), vmem_limit_bytes=VMEM_BYTES
+            dimension_semantics=("arbitrary",) * len(grid), vmem_limit_bytes=vmem
         ),
-        cost_estimate=pl.CostEstimate(flops=flops, bytes_accessed=moved, transcendentals=0),
+        cost_estimate=pl.CostEstimate(
+            flops=flops // COST_SCALE, bytes_accessed=moved // COST_SCALE, transcendentals=0
+        ),
         name=name,
     )(*args)
 
 
 def shaped(shape, dtype):
     return jax.ShapeDtypeStruct(shape, dtype)
+
+
+IN_PLACE = pl.BlockSpec(memory_space=pl.ANY)
+
+
+def factors_body(_, *refs):
+    out_ref = refs[-1]
+    first = 0
+    for ref in refs[:-1]:
+        size = ref.shape[-1]
+        out_ref[:, first : first + size] = ref[...]
+        first += size
+
+
+def picked_factors(meta, sources):
+    specs = []
+    total = 0
+    for table, entry, slot in sources:
+        if entry is None:
+            spec = pl.BlockSpec((None,) + table.shape[1:], lambda t, m, slot=slot: (m[slot], 0, 0))
+        else:
+            spec = pl.BlockSpec(
+                (None, None) + table.shape[2:], lambda t, m, entry=entry, slot=slot: (entry, m[slot], 0, 0)
+            )
+        specs.append(spec)
+        total += table.shape[-1]
+    shape = (RANK_UNIT, total)
+    return call(
+        factors_body, (1,), specs, whole(shape), shaped(shape, LOW), [], 0, 4 * RANK_UNIT * total,
+        "picked_factors", (meta,) + tuple(table for table, _, _ in sources),
+    )
+
+
+def share_body(_, parts, down_ref, up_ref, *refs):
+    out_ref = refs[-1]
+    step = pl.program_id(0)
+
+    @pl.when(step < parts)
+    def _():
+        out_ref[0] = down_ref[...]
+
+    @pl.when(step >= parts)
+    def _():
+        out_ref[0] = up_ref[...]
+
+
+def feed_share(meta, down_weight, up_weight, depth, after):
+    hidden, width = down_weight.shape
+    parts = hidden // width
+    return call(
+        lambda m, *refs: share_body(m, parts, *refs),
+        (2 * parts,),
+        [
+            pl.BlockSpec(
+                (depth, width), lambda t, m: (m[11] * parts + jnp.minimum(t, parts - 1), 0)
+            ),
+            pl.BlockSpec((depth, width), lambda t, m: (m[11], jnp.maximum(t - parts, 0))),
+        ]
+        + [IN_PLACE] * len(after),
+        pl.BlockSpec((1, depth, width), lambda t, m: (t, 0, 0)),
+        shaped((2 * parts, depth, width), LOW),
+        [],
+        0,
+        8 * parts * depth * width,
+        "feed_share",
+        (meta, down_weight, up_weight, *after),
+    )
 
 
 def first_norm_body(_, x_ref, gain_ref, out_ref):
@@ -552,13 +626,14 @@
     )
 
 
-def project_body(_, act_ref, weight_ref, down_ref, up_ref, out_ref):
+def project_body(_, act_ref, weight_ref, down_ref, up_ref, *refs):
+    out_ref = refs[-1]
     act = act_ref[...]
-    rank = mm_nt(act, down_ref[0, 0]).astype(LOW)
-    out_ref[0] = (mm(act, weight_ref[0]) + mm(rank, up_ref[0, 0])).astype(LOW)
-
-
-def project_heads(meta, act, weights, down, up, slots, skip, name):
+    rank = low_rank(down_ref[0, 0], act)
+    out_ref[0] = (mm(act, weight_ref[0]) + mm_tn(rank, up_ref[0, 0])).astype(LOW)
+
+
+def project_heads(meta, act, weights, down, up, slots, skip, name, after=()):
     rows, width = act.shape
     count, _, local = weights.shape
     first_slot = slots
@@ -570,29 +645,23 @@
             pl.BlockSpec((1, width, local), lambda j, m: (j, 0, 0)),
             pl.BlockSpec((1, 1, RANK_UNIT, width), lambda j, m: (j + skip, m[first_slot + j], 0, 0)),
             pl.BlockSpec((1, 1, RANK_UNIT, local), lambda j, m: (j + skip, m[first_slot + j], 0, 0)),
-        ],
+        ]
+        + [IN_PLACE] * len(after),
         pl.BlockSpec((1, rows, local), lambda j, m: (j, 0, 0)),
         shaped((count, rows, local), LOW),
         [],
         2 * rows * width * local * count,
         2 * (weights.size + act.size + count * rows * local),
         name,
-        (meta, act, weights, down, up),
-    )
-
-
-def project_back_body(
-    _, last, act_ref, grad_ref, weight_ref, down_ref, up_ref, out_ref, ga_ref, gb_ref, total_ref
-):
+        (meta, act, weights, down, up, *after),
+    )
+
+
+def project_back_body(_, last, grad_ref, weight_ref, down_ref, up_ref, after_ref, out_ref, total_ref):
     step = pl.program_id(0)
-    act = act_ref[...]
     grad = grad_ref[0]
-    down = down_ref[0, 0]
-    rank = mm_nt(act, down).astype(LOW)
-    grad_rank = mm_nt(grad, up_ref[0, 0]).astype(LOW)
-    ga_ref[0] = mm_tn(grad_rank, act)
-    gb_ref[0] = mm_tn(rank, grad)
-    part = mm_nt(grad, weight_ref[0]) + mm(grad_rank, down)
+    grad_rank = low_rank(up_ref[0, 0], grad)
+    part = mm_nt(grad, weight_ref[0]) + mm_tn(grad_rank, down_ref[0, 0])
 
     @pl.when(step == 0)
     def _():
@@ -607,39 +676,259 @@
         out_ref[...] = total_ref[...].astype(out_ref.dtype)
 
 
-def project_back_heads(meta, act, grads, weights, down, up, slots, skip, kind, name):
-    rows, width = act.shape
-    count, _, local = weights.shape
-    first_slot = slots
+def project_back_heads(meta, grads, weights, down, up, slots, skip, kind, name, after):
+    count, width, local = weights.shape
+    rows = grads.shape[1]
     return call(
         lambda m, *refs: project_back_body(m, count - 1, *refs),
         (count,),
         [
-            whole((rows, width)),
             pl.BlockSpec((1, rows, local), lambda j, m: (j, 0, 0)),
             pl.BlockSpec((1, width, local), lambda j, m: (j, 0, 0)),
-            pl.BlockSpec((1, 1, RANK_UNIT, width), lambda j, m: (j + skip, m[first_slot + j], 0, 0)),
-            pl.BlockSpec((1, 1, RANK_UNIT, local), lambda j, m: (j + skip, m[first_slot + j], 0, 0)),
+            pl.BlockSpec((1, 1, RANK_UNIT, width), lambda j, m: (j + skip, m[slots + j], 0, 0)),
+            pl.BlockSpec((1, 1, RANK_UNIT, local), lambda j, m: (j + skip, m[slots + j], 0, 0)),
+            IN_PLACE,
         ],
-        (
-            whole((rows, width)),
-            pl.BlockSpec((1, RANK_UNIT, width), lambda j, m: (j, 0, 0)),
-            pl.BlockSpec((1, RANK_UNIT, local), lambda j, m: (j, 0, 0)),
-        ),
-        (
-            shaped((rows, width), kind),
-            shaped((count, RANK_UNIT, width), WIDE),
-            shaped((count, RANK_UNIT, local), WIDE),
-        ),
+        whole((rows, width)),
+        shaped((rows, width), kind),
         [pltpu.VMEM((rows, width), WIDE)],
         2 * rows * width * local * count,
-        2 * (weights.size + act.size + count * rows * local) + 4 * rows * width,
+        2 * (weights.size + count * rows * local) + 4 * rows * width,
         name,
-        (meta, act, grads, weights, down, up),
-    )
-
-
-ROW_BLOCK = 256
+        (meta, grads, weights, down, up, after),
+    )
+
+
+def rank_grads_body(meta, count, parts, *refs):
+    acts = refs[:parts]
+    grads = refs[parts : 2 * parts]
+    downs = refs[2 * parts : 2 * parts + count]
+    ups = refs[2 * parts + count : 2 * parts + 2 * count]
+    mine_ref, theirs_ref, ga = refs[2 * parts + 2 * count :]
+    half = ga.shape[1] // 2
+    local = ups[0].shape[3]
+    down = jnp.concatenate([ref[0, 0] for ref in downs], axis=0)
+    for part in range(parts):
+        act = acts[part][...]
+        rank = low_rank(down, act)
+        grad_rank = jnp.concatenate(
+            [low_rank(ups[j][0, 0], grads[part][j]) for j in range(count)], axis=0
+        )
+        if part == 0:
+            ga[...] = mm(grad_rank, act)
+        else:
+            ga[...] += mm(grad_rank, act)
+        for j in range(count):
+            gb = mm(rank[RANK_UNIT * j : RANK_UNIT * (j + 1)], grads[part][j])
+            span = slice(count * half + j * local, count * half + (j + 1) * local)
+            if part == 0:
+                mine_ref[:, span] = gb
+            else:
+                mine_ref[:, span] += gb
+    side = meta[10]
+    for j in range(count):
+        rows = slice(RANK_UNIT * j, RANK_UNIT * (j + 1))
+        span = slice(j * half, (j + 1) * half)
+        mine_ref[:, span] = ga[rows, pl.ds(pl.multiple_of(side * half, 128), half)]
+        theirs = ga[rows, pl.ds(pl.multiple_of((1 - side) * half, 128), half)]
+        theirs_ref[:, span] = theirs.astype(LOW)
+
+
+def rank_grads(meta, acts, grads, down, up, slots, skip, name):
+    rows, width = acts[0].shape
+    count, _, local = grads[0].shape
+    parts = len(acts)
+
+    def table(size, j):
+        return pl.BlockSpec(
+            (1, 1, RANK_UNIT, size),
+            lambda t, m: (j + skip, m[slots + j], 0, 0),
+            pipeline_mode=pl.Buffered(1),
+        )
+
+    shared = count * width // 2
+    total = shared + count * local
+    return call(
+        lambda m, *refs: rank_grads_body(m, count, parts, *refs),
+        (1,),
+        [whole((rows, width))] * parts
+        + [whole((count, rows, local))] * parts
+        + [table(width, j) for j in range(count)]
+        + [table(local, j) for j in range(count)],
+        (whole((RANK_UNIT, total)), whole((RANK_UNIT, shared))),
+        (shaped((RANK_UNIT, total), WIDE), shaped((RANK_UNIT, shared), LOW)),
+        [pltpu.VMEM((RANK_UNIT * count, width), WIDE)],
+        8 * parts * rows * (width + local) * RANK_UNIT * count,
+        2 * parts * rows * (width + count * local),
+        name,
+        (meta, *acts, *grads, *([down] * count), *([up] * count)),
+    )
+
+
+def split_columns(meta, mine_ref, theirs_ref, first, array):
+    half = array.shape[-1] // 2
+    span = slice(first, first + half)
+    side = meta[10]
+    mine_ref[:, span] = array[:, pl.ds(pl.multiple_of(side * half, 128), half)]
+    theirs = array[:, pl.ds(pl.multiple_of((1 - side) * half, 128), half)]
+    theirs_ref[:, span] = theirs.astype(LOW)
+
+
+def own_columns(mine_ref, theirs_ref, first, array):
+    half = array.shape[-1] // 2
+    span = slice(first, first + half)
+    mine_ref[:, span] = array[:, :half]
+    theirs_ref[:, span] = array[:, half:].astype(LOW)
+
+
+def join(mine, received):
+    both = jnp.concatenate(received, axis=1).astype(WIDE)
+    width = both.shape[1]
+    return (mine + jnp.pad(both, ((0, 0), (0, mine.shape[1] - width)))).astype(LOW)
+
+
+def clip_names(label_ref):
+    clips, rank, width = label_ref.shape
+    return label_ref[...].reshape(clips * rank, width).astype(WIDE).T
+
+
+def slot_take(names, slots, rank):
+    source = lax.broadcasted_iota(jnp.int32, names.shape, 1)
+    target = (source & (rank - 1)) + rank * names.astype(jnp.int32)
+    place = lax.broadcasted_iota(jnp.int32, (slots * rank, names.shape[1]), 0)
+    return jnp.where(place == target, 1.0, 0.0).astype(LOW)
+
+
+def slot_sum_body(_, plan, slots, everyone_ref, label_ref, *refs):
+    names = refs[-1]
+    out_refs = refs[-1 - len({which for _, which, _ in plan}) : -1]
+    step = pl.program_id(0)
+    clips, rank, unit = everyone_ref.shape
+
+    @pl.when(step == 0)
+    def _():
+        names[...] = clip_names(label_ref)
+
+    column = jnp.int32(0)
+    chosen_out = jnp.int32(0)
+    for number, (place, which, _) in enumerate(plan):
+        column = jnp.where(step == number, place, column)
+        chosen_out = jnp.where(step == number, which, chosen_out)
+    take = slot_take(names[pl.ds(column, 1)], slots, rank)
+    total = mm(take, everyone_ref[...].reshape(clips * rank, unit))
+    for which, ref in enumerate(out_refs):
+
+        @pl.when(chosen_out == which)
+        def _():
+            ref[...] = total.reshape(ref.shape)
+
+
+def late_sum_body(_, plan, slots, carried, everyone_ref, label_ref, *refs):
+    count = len({which for _, which, _ in plan})
+    earlier = refs[: len(carried)]
+    out_refs = refs[-5 - count : -5]
+    names, arrived, totals, in_sems, out_sems = refs[-5:]
+    clips, rank, unit = arrived.shape[1:]
+    incoming = [
+        pltpu.make_async_copy(
+            everyone_ref.at[:, :, pl.ds(unit * number, unit)], arrived.at[number], in_sems.at[number]
+        )
+        for number in range(len(plan))
+    ]
+    for copy in incoming:
+        copy.start()
+    names[...] = clip_names(label_ref)
+    outgoing = []
+    for number, (which, ref) in enumerate(zip(carried, earlier)):
+        copy = pltpu.make_async_copy(ref.at[0], out_refs[which].at[0], out_sems.at[len(plan) + number])
+        copy.start()
+        outgoing.append(copy)
+    for number, (column, which, place) in enumerate(plan):
+        incoming[number].wait()
+        take = slot_take(names[column : column + 1], slots, rank)
+        total = mm(take, arrived[number].reshape(clips * rank, unit))
+        totals[number] = total.reshape(slots, rank, unit)
+        copy = pltpu.make_async_copy(totals.at[number], out_refs[which].at[place], out_sems.at[number])
+        copy.start()
+        outgoing.append(copy)
+    for copy in outgoing:
+        copy.wait()
+
+
+def late_sums(meta, everyone, plan, outs, slots, unit, carried, name, after):
+    clips, rank, total = everyone.shape
+    label_width = 2 * HEAD_DIM
+    units = len(plan)
+    return call(
+        lambda m, *refs: late_sum_body(m, plan, slots, tuple(carried), *refs),
+        (1,),
+        [IN_PLACE, whole((clips, rank, label_width), (0, 0, total // label_width - 1))]
+        + [whole(array.shape) for array in carried.values()]
+        + [IN_PLACE] * len(after),
+        (IN_PLACE,) * len(outs),
+        tuple(shaped((stack, slots, rank, width), WIDE) for stack, width in outs),
+        [
+            pltpu.VMEM((label_width, clips * rank), WIDE),
+            pltpu.VMEM((units, clips, rank, unit), LOW),
+            pltpu.VMEM((units, slots, rank, unit), WIDE),
+            pltpu.SemaphoreType.DMA((units,)),
+            pltpu.SemaphoreType.DMA((units + len(carried),)),
+        ],
+        0,
+        2 * everyone.size + 4 * slots * rank * total,
+        name,
+        (meta, everyone, everyone, *carried.values(), *after),
+    )
+
+
+def slot_sums(meta, everyone, plan, outs, slots, unit, name, after):
+    clips, rank, total = everyone.shape
+    steps = len(plan)
+
+    def place_of(which):
+        def place(t, m):
+            places = [(step, place) for step, (_, target, place) in enumerate(plan) if target == which]
+            value = jnp.int32(places[0][1])
+            for step, place in places:
+                value = jnp.where(t >= step, place, value)
+            return value
+
+        return place
+
+    out_specs = []
+    out_shapes = []
+    for which, (stack, width) in enumerate(outs):
+        place = place_of(which)
+        if stack is None:
+            out_specs.append(
+                pl.BlockSpec((slots, rank, unit), lambda t, m, place=place: (0, 0, place(t, m)))
+            )
+            out_shapes.append(shaped((slots, rank, width), WIDE))
+        else:
+            out_specs.append(
+                pl.BlockSpec((1, slots, rank, unit), lambda t, m, place=place: (place(t, m), 0, 0, 0))
+            )
+            out_shapes.append(shaped((stack, slots, rank, width), WIDE))
+    label_width = 2 * HEAD_DIM
+    return call(
+        lambda m, *refs: slot_sum_body(m, plan, slots, *refs),
+        (steps,),
+        [
+            pl.BlockSpec((clips, rank, unit), lambda t, m: (0, 0, t)),
+            whole((clips, rank, label_width), (0, 0, total // label_width - 1)),
+        ]
+        + [IN_PLACE] * len(after),
+        tuple(out_specs),
+        tuple(out_shapes),
+        [pltpu.VMEM((label_width, clips * rank), WIDE)],
+        0,
+        2 * everyone.size + 4 * slots * rank * total,
+        name,
+        (meta, everyone, everyone, *after),
+    )
+
+
+ROW_BLOCK = 512
 
 
 def order_frames(is_first, own, other, low_part, high_part):
@@ -654,48 +943,83 @@
         high_part[...] = own[...]
 
 
-def self_forward_body(meta, own_ref, other_ref, out_own_ref, out_other_ref, held, result):
+def causal_spans(first):
+    return [(first, first + ROW_BLOCK)] + [(key, key + ROW_BLOCK) for key in range(0, first, ROW_BLOCK)]
+
+
+def causal_keep(rows):
+    key_at = lax.broadcasted_iota(jnp.int32, (rows, rows), 0)
+    return key_at <= lax.broadcasted_iota(jnp.int32, (rows, rows), 1)
+
+
+def turned(rows):
+    return rows.astype(WIDE).T.astype(LOW)
+
+
+def self_forward_body(
+    meta,
+    own_ref,
+    other_ref,
+    out_own_ref,
+    out_other_ref,
+    log_own_ref,
+    log_other_ref,
+    held,
+    value_turned,
+    result,
+    logs,
+):
     half = own_ref.shape[1]
     is_first = meta[10] == 0
     order_frames(is_first, own_ref, other_ref, held.at[:, :half], held.at[:, half:])
-    left = lane_halves()
     masks = half_masks()
-    scale = HEAD_DIM**-0.5
-    query_at = lax.broadcasted_iota(jnp.int32, (ROW_BLOCK, ROW_BLOCK), 0)
-    key_at = lax.broadcasted_iota(jnp.int32, (ROW_BLOCK, ROW_BLOCK), 1)
-    keep = key_at <= query_at
+    keep = causal_keep(ROW_BLOCK)
     for first in range(0, 2 * half, ROW_BLOCK):
-        end = first + ROW_BLOCK
-        query = held[0, first:end] * jnp.asarray(scale, LOW)
-        keys = held[1, :end]
-        values = held[2, :end]
-        parts = []
+        span = slice(first, first + ROW_BLOCK)
+        values = turned(held[2, span])
+        for which in (0, 1):
+            value_turned[which, :HEAD_DIM, span] = values[HEAD_DIM * which : HEAD_DIM * (which + 1)]
+            value_turned[which, HEAD_DIM:, span] = jnp.ones((RANK_UNIT, ROW_BLOCK), LOW)
+    for first in range(0, 2 * half, ROW_BLOCK):
+        span = slice(first, first + ROW_BLOCK)
+        query = held[0, span] * jnp.asarray(HEAD_DIM**-0.5, LOW)
+        mixes = []
+        totals = []
         for which in (0, 1):
             one_query = query * masks[which]
-            near = jnp.where(keep, mm_nt(one_query, keys[first:]), -1e30)
-            largest = jnp.max(near, axis=-1, keepdims=True)
-            spread = values * masks[which] + masks[1 - which]
-            if first > 0:
-                far = mm_nt(one_query, keys[:first])
-                largest = jnp.maximum(largest, jnp.max(far, axis=-1, keepdims=True))
-                mixed = mm(jnp.exp(far - largest).astype(LOW), spread[:first])
-                mixed = mixed + mm(jnp.exp(near - largest).astype(LOW), spread[first:])
-            else:
-                mixed = mm(jnp.exp(near - largest).astype(LOW), spread)
-            parts.append(mixed)
-        mixed = jnp.where(left, parts[0], parts[1])
-        summed = pltpu.roll(jnp.where(left, parts[1], parts[0]), HEAD_DIM, 1)
-        result[first:end] = (mixed / summed).astype(LOW)
+            largest = None
+            scores = []
+            for begin, end in causal_spans(first):
+                score = mm_nt(held[1, begin:end], one_query)
+                if begin == first:
+                    score = jnp.where(keep, score, -1e30)
+                top = jnp.max(score, axis=0, keepdims=True)
+                largest = top if largest is None else jnp.maximum(largest, top)
+                scores.append(score)
+            mixed = None
+            for (begin, end), score in zip(causal_spans(first), scores):
+                weights = jnp.exp(score - largest).astype(LOW)
+                part = mm(value_turned[which, :, begin:end], weights)
+                mixed = part if mixed is None else mixed + part
+            summed = mixed[HEAD_DIM : HEAD_DIM + 1]
+            mixes.append(mixed[:HEAD_DIM] * (1.0 / summed))
+            totals.append(jnp.broadcast_to(jnp.log(summed) + largest, (HEAD_DIM, ROW_BLOCK)))
+        result[span] = jnp.concatenate(mixes, axis=0).T.astype(LOW)
+        logs[span] = jnp.concatenate(totals, axis=0).T
 
     @pl.when(is_first)
     def _():
         out_own_ref[...] = result[:half]
         out_other_ref[...] = result[half:]
+        log_own_ref[...] = logs[:half]
+        log_other_ref[...] = logs[half:]
 
     @pl.when(jnp.logical_not(is_first))
     def _():
         out_own_ref[...] = result[half:]
         out_other_ref[...] = result[:half]
+        log_own_ref[...] = logs[half:]
+        log_other_ref[...] = logs[:half]
 
 
 def self_forward(meta, own, other):
@@ -703,13 +1027,20 @@
     pair = 2 * HEAD_DIM
     three = pl.BlockSpec((3, half, pair), lambda p, m: (0, 0, p))
     one = pl.BlockSpec((half, pair), lambda p, m: (0, p))
+    rows = shaped((half, local), LOW)
+    logs = shaped((half, local), WIDE)
     return call(
         self_forward_body,
         (local // pair,),
         [three, three],
-        (one, one),
-        (shaped((half, local), LOW), shaped((half, local), LOW)),
-        [pltpu.VMEM((3, 2 * half, pair), LOW), pltpu.VMEM((2 * half, pair), LOW)],
+        (one, one, one, one),
+        (rows, rows, logs, logs),
+        [
+            pltpu.VMEM((3, 2 * half, pair), LOW),
+            pltpu.VMEM((2, HEAD_DIM + RANK_UNIT, 2 * half), LOW),
+            pltpu.VMEM((2 * half, pair), LOW),
+            pltpu.VMEM((2 * half, pair), WIDE),
+        ],
         20 * half * half * local,
         16 * half * local,
         "self_forward",
@@ -717,16 +1048,37 @@
     )
 
 
+def three_parts(column):
+    high = column.astype(LOW)
+    rest = column - high.astype(WIDE)
+    middle = rest.astype(LOW)
+    return high, middle, (rest - middle.astype(WIDE)).astype(LOW)
+
+
 def self_back_body(
     meta,
     own_ref,
     other_ref,
+    z_own_ref,
+    z_other_ref,
+    log_own_ref,
+    log_other_ref,
     grad_own_ref,
     grad_other_ref,
+    _early,
     out_own_ref,
     out_other_ref,
     held,
+    mixed,
+    logs,
     grads,
+    key_turned,
+    query_turned,
+    grad_turned,
+    query_wide,
+    key_wide,
+    grad_wide,
+    value_wide,
     key_total,
     value_total,
     result,
@@ -735,53 +1087,60 @@
     is_first = meta[10] == 0
     order_frames(is_first, own_ref, other_ref, held.at[:, :half], held.at[:, half:])
     order_frames(is_first, grad_own_ref, grad_other_ref, grads.at[:half], grads.at[half:])
+    order_frames(is_first, z_own_ref, z_other_ref, mixed.at[:half], mixed.at[half:])
+    order_frames(is_first, log_own_ref, log_other_ref, logs.at[:half], logs.at[half:])
     masks = half_masks()
     scale = HEAD_DIM**-0.5
-    query_at = lax.broadcasted_iota(jnp.int32, (ROW_BLOCK, ROW_BLOCK), 1)
-    key_at = lax.broadcasted_iota(jnp.int32, (ROW_BLOCK, ROW_BLOCK), 0)
-    keep = key_at <= query_at
+    lane = lax.broadcasted_iota(jnp.int32, (1, 2 * HEAD_DIM), 1)
+    keep = causal_keep(ROW_BLOCK)
+    for first in range(0, 2 * half, ROW_BLOCK):
+        span = slice(first, first + ROW_BLOCK)
+        grad = grads[span]
+        product = grad.astype(WIDE) * mixed[span].astype(WIDE)
+        query = held[0, span] * jnp.asarray(scale, LOW)
+        key_turned[:, span] = turned(held[1, span])
+        query_turned[:, span] = turned(query)
+        grad_turned[:, span] = turned(grad)
+        for which in (0, 1):
+            spare = HEAD_DIM * (1 - which)
+            marks = [jnp.where(lane == spare + i, 1.0, 0.0).astype(LOW) for i in range(3)]
+            marked = marks[0] + marks[1] + marks[2]
+            others = 1 - marked
+            inner = jnp.sum(product * masks[which].astype(WIDE), axis=-1, keepdims=True)
+            log_column = logs[span][:, HEAD_DIM * which : HEAD_DIM * which + 1]
+            query_rows = query * masks[which]
+            for part, mark in zip(three_parts(log_column), marks):
+                query_rows = query_rows - part * mark
+            query_wide[which, span] = query_rows
+            grad_rows = grad * masks[which]
+            for part, mark in zip(three_parts(inner), marks):
+                grad_rows = grad_rows - part * mark
+            grad_wide[which, span] = grad_rows
+            key_wide[which, span] = held[1, span] * others + marked
+            value_wide[which, span] = held[2, span] * others + marked
     key_total[...] = jnp.zeros_like(key_total)
     value_total[...] = jnp.zeros_like(value_total)
     for first in range(0, 2 * half, ROW_BLOCK):
-        end = first + ROW_BLOCK
-        query = held[0, first:end] * jnp.asarray(scale, LOW)
-        grad = grads[first:end]
-        spans = [(first, end)] + ([(0, first)] if first > 0 else [])
-        query_grad = None
-        for which in (0, 1):
-            mask = masks[which]
-            one_query = query * mask
-            one_grad = grad * mask
-            scores = []
-            for low_key, high_key in spans:
-                score = mm_nt(held[1, low_key:high_key], one_query)
-                if low_key == first:
+        span = slice(first, first + ROW_BLOCK)
+        query_grads = [None, None]
+        for begin, end in causal_spans(first):
+            for which in (0, 1):
+                head = slice(HEAD_DIM * which, HEAD_DIM * (which + 1))
+                score = mm_nt(key_wide[which, begin:end], query_wide[which, span])
+                if begin == first:
                     score = jnp.where(keep, score, -1e30)
-                scores.append(score)
-            largest = jnp.max(scores[0], axis=0, keepdims=True)
-            for score in scores[1:]:
-                largest = jnp.maximum(largest, jnp.max(score, axis=0, keepdims=True))
-            probs = [jnp.exp(score - largest) for score in scores]
-            summed = jnp.sum(probs[0], axis=0, keepdims=True)
-            for prob in probs[1:]:
-                summed = summed + jnp.sum(prob, axis=0, keepdims=True)
-            inverse = 1.0 / summed
-            probs = [prob * inverse for prob in probs]
-            prob_grads = [
-                mm_nt(held[2, low_key:high_key], one_grad) for low_key, high_key in spans
-            ]
-            inner = jnp.sum(probs[0] * prob_grads[0], axis=0, keepdims=True)
-            for prob, prob_grad in zip(probs[1:], prob_grads[1:]):
-                inner = inner + jnp.sum(prob * prob_grad, axis=0, keepdims=True)
-            for (low_key, high_key), prob, prob_grad in zip(spans, probs, prob_grads):
-                score_grad = (prob * (prob_grad - inner)).astype(LOW)
-                value_total[low_key:high_key] += mm(prob.astype(LOW), one_grad)
-                key_total[low_key:high_key] += mm(score_grad, one_query)
-                part = mm_tn(score_grad, held[1, low_key:high_key] * mask)
-                query_grad = part if query_grad is None else query_grad + part
-        result[0, first:end] = (query_grad * scale).astype(LOW)
-    result[1] = key_total[...].astype(LOW)
-    result[2] = value_total[...].astype(LOW)
+                prob = jnp.exp(score)
+                prob_grad = mm_nt(value_wide[which, begin:end], grad_wide[which, span])
+                score_grad = (prob * prob_grad).astype(LOW)
+                value_total[head, begin:end] += mm_nt(grad_turned[head, span], prob.astype(LOW))
+                key_total[head, begin:end] += mm_nt(query_turned[head, span], score_grad)
+                part = mm(key_turned[head, begin:end], score_grad)
+                query_grads[which] = part if query_grads[which] is None else query_grads[which] + part
+        result[0, span] = (jnp.concatenate(query_grads, axis=0).T * scale).astype(LOW)
+    for first in range(0, 2 * half, ROW_BLOCK):
+        span = slice(first, first + ROW_BLOCK)
+        result[1, span] = key_total[:, span].T.astype(LOW)
+        result[2, span] = value_total[:, span].T.astype(LOW)
 
     @pl.when(is_first)
     def _():
@@ -794,41 +1153,70 @@
         out_other_ref[...] = result[:, :half]
 
 
-def self_back(meta, own, other, grad_own, grad_other):
+def self_back(meta, own, other, z_own, z_other, log_own, log_other, grad_own, grad_other, after):
     _, half, local = own.shape
     pair = 2 * HEAD_DIM
+    full = 2 * half
     three = pl.BlockSpec((3, half, pair), lambda p, m: (0, 0, p))
     one = pl.BlockSpec((half, pair), lambda p, m: (0, p))
     return call(
         self_back_body,
         (local // pair,),
-        [three, three, one, one],
+        [three, three] + [one] * 6 + [IN_PLACE] * len(after),
         (three, three),
         (shaped(own.shape, LOW), shaped(own.shape, LOW)),
         [
-            pltpu.VMEM((3, 2 * half, pair), LOW),
-            pltpu.VMEM((2 * half, pair), LOW),
-            pltpu.VMEM((2 * half, pair), WIDE),
-            pltpu.VMEM((2 * half, pair), WIDE),
-            pltpu.VMEM((3, 2 * half, pair), LOW),
-        ],
-        50 * half * half * local,
+            pltpu.VMEM((3, full, pair), LOW),
+            pltpu.VMEM((full, pair), LOW),
+            pltpu.VMEM((full, pair), WIDE),
+            pltpu.VMEM((full, pair), LOW),
+        ]
+        + [pltpu.VMEM((pair, full), LOW)] * 3
+        + [pltpu.VMEM((2, full, pair), LOW)] * 4
+        + [pltpu.VMEM((pair, full), WIDE)] * 2
+        + [pltpu.VMEM((3, full, pair), LOW)],
+        500 * half * half * local,
         30 * half * local,
         "self_back",
-        (meta, own, other, grad_own, grad_other),
+        (meta, own, other, z_own, z_other, log_own, log_other, grad_own, grad_other, *after),
     )
 
 
 def halves_of(ref, local):
-    step = ref.shape[2] // 2
+    step = ref.shape[1] // 2
     return (
-        ref[:, 0, :step, :].reshape(local, ref.shape[3]),
-        ref[:, 0, step:, :].reshape(local, ref.shape[3]),
+        ref[:, :step, :].reshape(local, ref.shape[2]),
+        ref[:, step:, :].reshape(local, ref.shape[2]),
     )
 
 
 def full_of(ref):
-    return ref[:, 0].reshape(ref.shape[0] * ref.shape[2], ref.shape[3])
+    return ref[...].reshape(ref.shape[0] * ref.shape[1], ref.shape[2])
+
+
+def fetch_weights(step, order, sources, gathered, held, sems):
+    copies = {}
+    for which in order:
+        copies[which] = (
+            pltpu.make_async_copy(sources[which], held[2 * which], sems.at[2 * which]),
+            pltpu.make_async_copy(gathered.at[:, which], held[2 * which + 1], sems.at[2 * which + 1]),
+        )
+
+    @pl.when(step == 0)
+    def _():
+        for which in order:
+            for copy in copies[which]:
+                copy.start()
+
+    def ready(which):
+        @pl.when(step == 0)
+        def _():
+            for copy in copies[which]:
+                copy.wait()
+
+        return held[2 * which], held[2 * which + 1]
+
+    return ready
 
 
 def pair_tiles(keys, values, pair, masks):
@@ -840,29 +1228,25 @@
     return key_tile, value_tile
 
 
-def both_halves(left, values, reduce, empty):
-    first = reduce(jnp.where(left, values, empty), axis=-1, keepdims=True)
-    second = reduce(jnp.where(left, empty, values), axis=-1, keepdims=True)
-    return jnp.where(left, first, second)
-
-
-def text_weights(left, query, key_tile):
-    scores = mm_nt(query, key_tile)
-    return jnp.exp(scores - both_halves(left, scores, jnp.max, -1e30))
-
-
-def mix_text(query, keys, values, left, masks):
+def by_head(values, reduce):
+    keys, rows = values.shape
+    reduced = reduce(values.reshape(2, keys // 2, rows), axis=1, keepdims=True)
+    return jnp.broadcast_to(reduced, (2, keys // 2, rows)).reshape(keys, rows)
+
+
+def text_weights(key_tile, query):
+    scores = mm_nt(key_tile, query)
+    weights = jnp.exp(scores - by_head(scores, jnp.max))
+    return weights * (1.0 / by_head(weights, jnp.sum))
+
+
+def mix_text(query, keys, values, masks):
     mixed = []
-    ones = jnp.concatenate(
-        [jnp.broadcast_to(masks[0], (HEAD_DIM, 2 * HEAD_DIM)), jnp.broadcast_to(masks[1], (HEAD_DIM, 2 * HEAD_DIM))],
-        axis=0,
-    )
     for pair in range(query.shape[1] // (2 * HEAD_DIM)):
         key_tile, value_tile = pair_tiles(keys, values, pair, masks)
         one_query = query[:, 2 * HEAD_DIM * pair : 2 * HEAD_DIM * (pair + 1)]
-        weights = text_weights(left, one_query * jnp.asarray(HEAD_DIM**-0.5, LOW), key_tile)
-        weights = weights.astype(LOW)
-        mixed.append((mm(weights, value_tile) / mm(weights, ones)).astype(LOW))
+        weights = text_weights(key_tile, one_query * jnp.asarray(HEAD_DIM**-0.5, LOW))
+        mixed.append(mm_tn(weights.astype(LOW), value_tile).astype(LOW))
     return jnp.concatenate(mixed, axis=1)
 
 
@@ -871,12 +1255,10 @@
     x_ref,
     z_own_ref,
     z_other_ref,
-    out_own_ref,
-    out_other_ref,
-    query_own_ref,
-    query_other_ref,
-    cross_own_ref,
-    cross_other_ref,
+    out_weight_ref,
+    query_weight_ref,
+    cross_weight_ref,
+    gathered_ref,
     down3_ref,
     down3_other_ref,
     up3_ref,
@@ -897,44 +1279,52 @@
     query_out_other_ref,
     z2_own_ref,
     z2_other_ref,
+    *scratch,
 ):
     local = z_own_ref.shape[1]
-    left = lane_halves()
     masks = half_masks()
-
-    def out_product(own, other, weight_own, weight_other_ref, down, down_other, up):
-        rank = (mm_nt(own, down) + mm_nt(other, down_other)).astype(LOW)
+    ready = fetch_weights(
+        pl.program_id(0),
+        (0, 1, 2),
+        (out_weight_ref, query_weight_ref, cross_weight_ref),
+        gathered_ref,
+        scratch[:6],
+        scratch[6],
+    )
+
+    def out_product(own, other, which, down, down_other, up):
+        rank = (mm_nt(down, own) + mm_nt(down_other, other)).astype(LOW)
+        weight_own, weight_other_ref = ready(which)
         first, second = halves_of(weight_other_ref, local)
-        product = mm(own, weight_own[...]) + mm(rank, up)
+        product = mm(own, weight_own[...]) + mm_tn(rank, up)
         return product + jnp.concatenate([mm(other, first), mm(other, second)], axis=1)
 
     stream = x_ref[...].astype(WIDE) + out_product(
         z_own_ref[...],
         z_other_ref[...],
-        out_own_ref,
-        out_other_ref,
+        0,
         down3_ref[0, 0],
         down3_other_ref[...],
         up3_ref[0, 0],
     )
     stream_one_ref[...] = stream
     rows_two = norm_rows(stream, gain_two_ref[...])[0].astype(LOW)
-    rank = mm_nt(rows_two, down4_ref[0, 0]).astype(LOW)
-    query_own = (mm(rows_two, query_own_ref[...]) + mm(rank, up4_ref[0, 0])).astype(LOW)
+    rank = low_rank(down4_ref[0, 0], rows_two)
+    query_own_ref, query_other_ref = ready(1)
+    query_own = (mm(rows_two, query_own_ref[...]) + mm_tn(rank, up4_ref[0, 0])).astype(LOW)
     query_other = (
-        mm(rows_two, full_of(query_other_ref)) + mm(rank, up4_other_ref[...])
+        mm(rows_two, full_of(query_other_ref)) + mm_tn(rank, up4_other_ref[...])
     ).astype(LOW)
     query_out_own_ref[...] = query_own
     query_out_other_ref[...] = query_other
-    z2_own = mix_text(query_own, text_own_ref[0], text_own_ref[1], left, masks)
-    z2_other = mix_text(query_other, text_other_ref[0], text_other_ref[1], left, masks)
+    z2_own = mix_text(query_own, text_own_ref[0], text_own_ref[1], masks)
+    z2_other = mix_text(query_other, text_other_ref[0], text_other_ref[1], masks)
     z2_own_ref[...] = z2_own
     z2_other_ref[...] = z2_other
     stream = stream + out_product(
         z2_own,
         z2_other,
-        cross_own_ref,
-        cross_other_ref,
+        2,
         down7_ref[0, 0],
         down7_other_ref[...],
         up7_ref[0, 0],
@@ -951,18 +1341,13 @@
 
 
 def middle_specs(weights, gathered, tables, packed):
-    out_weight, query_weight, cross_weight = weights
     attention_down, attention_up, cross_down, cross_up = tables
-    shards, _, depth, local = gathered.shape
-    one = (shards, 1, depth, local)
-    rank = (RANK_UNIT, local)
+    rank = (RANK_UNIT, gathered.shape[3])
     specs = [
-        whole(out_weight.shape),
-        whole(one, (0, 0, 0, 0)),
-        whole(query_weight.shape),
-        whole(one, (0, 1, 0, 0)),
-        whole(cross_weight.shape),
-        whole(one, (0, 2, 0, 0)),
+        IN_PLACE,
+        IN_PLACE,
+        IN_PLACE,
+        IN_PLACE,
         chosen(attention_down, 0, 3),
         whole(rank, (0, 0)),
         chosen(attention_up, 0, 3),
@@ -973,12 +1358,7 @@
         whole(rank, (0, 1)),
         chosen(attention_up, 1, 7),
     ]
-    args = (
-        out_weight,
-        gathered,
-        query_weight,
-        gathered,
-        cross_weight,
+    args = weights + (
         gathered,
         attention_down,
         packed,
@@ -991,6 +1371,14 @@
         attention_up,
     )
     return specs, args
+
+
+def middle_scratch(weights, gathered):
+    shards, _, depth, local = gathered.shape
+    held = []
+    for weight in weights:
+        held += [pltpu.VMEM(weight.shape, LOW), pltpu.VMEM((shards, depth, local), LOW)]
+    return held + [pltpu.SemaphoreType.DMA((2 * len(weights),))]
 
 
 def middle_forward(meta, x, z_own, z_other, weights, gathered, tables, packed, text_own, text_other, gains):
@@ -1016,7 +1404,7 @@
             shaped((frames, local), LOW),
             shaped((frames, local), LOW),
         ),
-        [],
+        middle_scratch(weights, gathered),
         6 * frames * width * width,
         6 * width * width + 20 * frames * width,
         "middle_forward",
@@ -1025,7 +1413,7 @@
 
 
 def middle_back_body(
-    _,
+    meta,
     last,
     grad_ref,
     stream_one_ref,
@@ -1035,12 +1423,10 @@
     query_in_other_ref,
     z2_own_ref,
     z2_other_ref,
-    out_own_ref,
-    out_other_ref,
-    query_own_ref,
-    query_other_ref,
-    cross_own_ref,
-    cross_other_ref,
+    out_weight_ref,
+    query_weight_ref,
+    cross_weight_ref,
+    gathered_ref,
     down3_ref,
     down3_other_ref,
     up3_ref,
@@ -1058,16 +1444,27 @@
     dz_other_ref,
     text_grad_own_ref,
     text_grad_other_ref,
+    mine_ref,
+    theirs_ref,
+    key_total,
+    value_total,
     ga3_ref,
     gb3_ref,
     ga4_ref,
     gb4_ref,
     ga7_ref,
     gb7_ref,
-    key_total,
-    value_total,
+    *scratch,
 ):
     step = pl.program_id(0)
+    ready = fetch_weights(
+        step,
+        (2, 1, 0),
+        (out_weight_ref, query_weight_ref, cross_weight_ref),
+        gathered_ref,
+        scratch[:6],
+        scratch[6],
+    )
     local = z_own_ref.shape[1]
     pairs = local // (2 * HEAD_DIM)
     left = lane_halves()
@@ -1081,19 +1478,20 @@
         for ref in (ga3_ref, gb3_ref, ga4_ref, gb4_ref, ga7_ref, gb7_ref):
             ref[...] = jnp.zeros_like(ref)
 
-    def out_back(grad, own, other, weight_own, weight_other_ref, down, down_other, up, ga_ref, gb_ref):
-        rank = (mm_nt(own, down) + mm_nt(other, down_other)).astype(LOW)
-        grad_rank = mm_nt(grad, up).astype(LOW)
-        ga_ref[:, :local] += mm_tn(grad_rank, own)
-        ga_ref[:, local:] += mm_tn(grad_rank, other)
-        gb_ref[...] += mm_tn(rank, grad)
+    def out_back(grad, own, other, which, down, down_other, up, ga_ref, gb_ref):
+        rank = (mm_nt(down, own) + mm_nt(down_other, other)).astype(LOW)
+        grad_rank = low_rank(up, grad)
+        ga_ref[:, :local] += mm(grad_rank, own)
+        ga_ref[:, local:] += mm(grad_rank, other)
+        gb_ref[...] += mm(rank, grad)
+        weight_own, weight_other_ref = ready(which)
         first, second = halves_of(weight_other_ref, local)
         middle = grad.shape[1] // 2
-        grad_own = mm_nt(grad, weight_own[...]) + mm(grad_rank, down)
+        grad_own = mm_nt(grad, weight_own[...]) + mm_tn(grad_rank, down)
         grad_other = (
             mm_nt(grad[:, :middle], first)
             + mm_nt(grad[:, middle:], second)
-            + mm(grad_rank, down_other)
+            + mm_tn(grad_rank, down_other)
         )
         return grad_own.astype(LOW), grad_other.astype(LOW)
 
@@ -1102,18 +1500,12 @@
         grad.astype(LOW),
         z2_own_ref[...],
         z2_other_ref[...],
-        cross_own_ref,
-        cross_other_ref,
+        2,
         down7_ref[0, 0],
         down7_other_ref[...],
         up7_ref[0, 0],
         ga7_ref,
         gb7_ref,
-    )
-
-    ones = jnp.concatenate(
-        [jnp.broadcast_to(masks[0], (HEAD_DIM, 2 * HEAD_DIM)), jnp.broadcast_to(masks[1], (HEAD_DIM, 2 * HEAD_DIM))],
-        axis=0,
     )
 
     def text_back(query, dz2, keys, values, part):
@@ -1123,16 +1515,13 @@
             key_tile, value_tile = pair_tiles(keys, values, pair, masks)
             one_query = query[:, span] * scale
             one_grad = dz2[:, span]
-            weights = text_weights(left, one_query, key_tile)
-            probs = weights / mm(weights.astype(LOW), ones)
-            prob_grads = mm_nt(one_grad, value_tile)
-            inner = both_halves(left, probs * prob_grads, jnp.sum, 0.0)
+            probs = text_weights(key_tile, one_query)
+            prob_grads = mm_nt(value_tile, one_grad)
+            inner = by_head(probs * prob_grads, jnp.sum)
             score_grads = (probs * (prob_grads - inner)).astype(LOW)
-            query_grads.append(
-                (mm(score_grads, key_tile) * HEAD_DIM**-0.5).astype(LOW)
-            )
-            key_total[part, pair] += mm_tn(score_grads, one_query)
-            value_total[part, pair] += mm_tn(probs.astype(LOW), one_grad)
+            query_grads.append((mm_tn(score_grads, key_tile) * HEAD_DIM**-0.5).astype(LOW))
+            key_total[part, pair] += mm(score_grads, one_query)
+            value_total[part, pair] += mm(probs.astype(LOW), one_grad)
         return jnp.concatenate(query_grads, axis=1)
 
     dq_own = text_back(query_in_own_ref[...], dz2_own, text_own_ref[0], text_own_ref[1], 0)
@@ -1140,15 +1529,16 @@
 
     rows_two, normed, inverse = norm_rows(stream_one_ref[...], gain_two_ref[...])
     rows_two = rows_two.astype(LOW)
-    rank = mm_nt(rows_two, down4_ref[0, 0]).astype(LOW)
-    grad_rank = (mm_nt(dq_own, up4_ref[0, 0]) + mm_nt(dq_other, up4_other_ref[...])).astype(LOW)
-    ga4_ref[...] += mm_tn(grad_rank, rows_two)
-    gb4_ref[:, :local] += mm_tn(rank, dq_own)
-    gb4_ref[:, local:] += mm_tn(rank, dq_other)
+    rank = low_rank(down4_ref[0, 0], rows_two)
+    grad_rank = (mm_nt(up4_ref[0, 0], dq_own) + mm_nt(up4_other_ref[...], dq_other)).astype(LOW)
+    ga4_ref[...] += mm(grad_rank, rows_two)
+    gb4_ref[:, :local] += mm(rank, dq_own)
+    gb4_ref[:, local:] += mm(rank, dq_other)
+    query_own_ref, query_other_ref = ready(1)
     grad_rows = (
         mm_nt(dq_own, query_own_ref[...])
         + mm_nt(dq_other, full_of(query_other_ref))
-        + mm(grad_rank, down4_ref[0, 0])
+        + mm_tn(grad_rank, down4_ref[0, 0])
     )
     grad = grad + norm_back(grad_rows, gain_two_ref[...], normed, inverse)
     grad_one_ref[...] = grad
@@ -1156,8 +1546,7 @@
         grad.astype(LOW),
         z_own_ref[...],
         z_other_ref[...],
-        out_own_ref,
-        out_other_ref,
+        0,
         down3_ref[0, 0],
         down3_other_ref[...],
         up3_ref[0, 0],
@@ -1169,12 +1558,18 @@
 
     @pl.when(step == last)
     def _():
+        split_columns(meta, mine_ref, theirs_ref, 0, ga4_ref)
+        own_columns(mine_ref, theirs_ref, local, gb4_ref)
+        own_columns(mine_ref, theirs_ref, 2 * local, ga3_ref)
+        own_columns(mine_ref, theirs_ref, 3 * local, ga7_ref)
+        split_columns(meta, mine_ref, theirs_ref, 4 * local, gb3_ref)
+        split_columns(meta, mine_ref, theirs_ref, 5 * local, gb7_ref)
         for total, slot in ((key_total, 0), (value_total, 1)):
             for part, ref in ((0, text_grad_own_ref), (1, text_grad_other_ref)):
                 for pair in range(pairs):
                     span = slice(2 * HEAD_DIM * pair, 2 * HEAD_DIM * (pair + 1))
                     tile = total[part, pair]
-                    ref[slot, :, span] = jnp.where(left, tile[:HEAD_DIM], tile[HEAD_DIM:])
+                    ref[slot, :, span] = jnp.where(left, tile[:HEAD_DIM], tile[HEAD_DIM:]).astype(ref.dtype)
 
 
 def middle_back(
@@ -1189,24 +1584,28 @@
     narrow = pl.BlockSpec((block, local), lambda t, m: (t, 0))
     specs, args = middle_specs(weights, gathered, tables, packed)
     rank = (RANK_UNIT, width)
+    packs = (RANK_UNIT, 6 * local)
     steps = frames // block
     return call(
         lambda m, *refs: middle_back_body(m, steps - 1, *refs),
         (steps,),
         [wide, wide] + [narrow] * 6 + specs + [whole(text_own.shape), whole(text_other.shape), whole((1, width))],
-        (wide, narrow, narrow, whole(text_own.shape), whole(text_own.shape)) + (whole(rank),) * 6,
+        (wide, narrow, narrow, whole(text_own.shape), whole(text_own.shape), whole(packs), whole(packs)),
         (
             shaped((frames, width), WIDE),
             shaped((frames, local), LOW),
             shaped((frames, local), LOW),
             shaped(text_own.shape, WIDE),
-            shaped(text_own.shape, WIDE),
-        )
-        + (shaped(rank, WIDE),) * 6,
+            shaped(text_own.shape, LOW),
+            shaped(packs, WIDE),
+            shaped(packs, LOW),
+        ),
         [
             pltpu.VMEM((2, pairs, 2 * HEAD_DIM, 2 * HEAD_DIM), WIDE),
             pltpu.VMEM((2, pairs, 2 * HEAD_DIM, 2 * HEAD_DIM), WIDE),
-        ],
+        ]
+        + [pltpu.VMEM(rank, WIDE)] * 6
+        + middle_scratch(weights, gathered),
         6 * frames * width * width,
         6 * width * width + 24 * frames * width,
         "middle_back",
@@ -1228,21 +1627,21 @@
         span = slice(first, first + block)
         rows = rows_ref[span]
         cot = cot_ref[span]
-        pre = mm(rows, up_weight) + mm(rank8[span], up_rank)
-        grad_hidden = mm_nt(cot, down_weight) + mm(grad_rank9[span], down_rank)
+        pre = mm(rows, up_weight) + mm_tn(rank8[:, span], up_rank)
+        grad_hidden = mm_nt(cot, down_weight) + mm_tn(grad_rank9[:, span], down_rank)
         hidden, slope = gelu_parts(pre)
         hidden = hidden.astype(LOW)
         grad_pre = (grad_hidden * slope).astype(LOW)
         branch[span] += mm(hidden, down_weight)
-        rank9[span] += mm_nt(hidden, down_rank)
+        rank9[:, span] += mm_nt(down_rank, hidden)
         grad_rows[span] += mm_nt(grad_pre, up_weight)
-        grad_rank8[span] += mm_nt(grad_pre, up_rank)
-        one = mm_tn(grad_rank9[span], hidden)
-        two = mm_tn(rank8[span], grad_pre)
+        grad_rank8[:, span] += mm_nt(up_rank, grad_pre)
+        one = mm(grad_rank9[:, span], hidden)
+        two = mm(rank8[:, span], grad_pre)
         ga9 = one if ga9 is None else ga9 + one
         gb8 = two if gb8 is None else gb8 + two
-    ga9_ref[...] = ga9
-    gb8_ref[...] = gb8
+    ga9_ref[...] = ga9.astype(ga9_ref.dtype)
+    gb8_ref[...] = gb8.astype(gb8_ref.dtype)
 
 
 def feed_own_body(
@@ -1253,8 +1652,8 @@
 ):
     @pl.when(pl.program_id(0) == 0)
     def _():
-        rank8[...] = mm_nt(rows_ref[...], down8_ref[0]).astype(LOW)
-        grad_rank9[...] = mm_nt(cot_ref[...], up9_ref[0]).astype(LOW)
+        rank8[...] = low_rank(down8_ref[0], rows_ref[...])
+        grad_rank9[...] = low_rank(up9_ref[0], cot_ref[...])
         for ref in (branch_ref, grad_rows_ref, rank9_ref, grad_rank8_ref):
             ref[...] = jnp.zeros_like(ref)
 
@@ -1274,7 +1673,7 @@
     grads = pl.BlockSpec((RANK_UNIT, tile), lambda t, m: (0, t))
     picked = pl.BlockSpec((1, RANK_UNIT, width), lambda t, m: (m[8], 0, 0))
     picked_out = pl.BlockSpec((1, RANK_UNIT, width), lambda t, m: (m[9], 0, 0))
-    rank = (frames, RANK_UNIT)
+    rank = (RANK_UNIT, frames)
     return call(
         feed_own_body,
         (hidden // tile,),
@@ -1306,20 +1705,28 @@
 
 
 def feed_other_body(
-    _, last, rows_ref, cot_ref, up_weight_ref, down_weight_ref, up_rank_ref, down_rank_ref,
+    meta, last, rows_ref, cot_ref, up_weight_ref, down_weight_ref, up_rank_ref, down_rank_ref,
     down8_ref, up9_ref, branch_in_ref, grad_rows_in_ref, rank9_in_ref, grad_rank8_in_ref,
     stream_ref, gain_ref,
-    out_ref, grad_ref, ga9_ref, gb8_ref, ga8_ref, gb9_ref,
-    branch, grad_rows, rank9, grad_rank8, rank8, grad_rank9,
+    out_ref, grad_ref, ga9_ref, gb8_ref, mine_ref, theirs_ref,
+    branch, grad_rows, rank9, grad_rank8, rank8, grad_rank9, ga8_ref, gb9_ref, branch_in, grad_rows_in, stream_in, sems,
 ):
     step = pl.program_id(0)
+    copies = [
+        pltpu.make_async_copy(source, target, sems.at[i])
+        for i, (source, target) in enumerate(
+            ((branch_in_ref, branch_in), (grad_rows_in_ref, grad_rows_in), (stream_ref, stream_in))
+        )
+    ]
 
     @pl.when(step == 0)
     def _():
-        rank8[...] = mm_nt(rows_ref[...], down8_ref[0]).astype(LOW)
-        grad_rank9[...] = mm_nt(cot_ref[...], up9_ref[0]).astype(LOW)
-        branch[...] = branch_in_ref[...]
-        grad_rows[...] = grad_rows_in_ref[...]
+        for copy in copies:
+            copy.start()
+        rank8[...] = low_rank(down8_ref[0], rows_ref[...])
+        grad_rank9[...] = low_rank(up9_ref[0], cot_ref[...])
+        branch[...] = jnp.zeros_like(branch)
+        grad_rows[...] = jnp.zeros_like(grad_rows)
         rank9[...] = rank9_in_ref[...]
         grad_rank8[...] = grad_rank8_in_ref[...]
 
@@ -1333,19 +1740,23 @@
 
     @pl.when(step == last)
     def _():
+        for copy in copies:
+            copy.wait()
         frames = rows_ref.shape[0]
         block = min(128, frames)
         last8 = grad_rank8[...].astype(LOW)
         last9 = rank9[...].astype(LOW)
-        ga8_ref[...] = mm_tn(last8, rows_ref[...])
-        gb9_ref[...] = mm_tn(last9, cot_ref[...])
+        ga8_ref[...] = mm(last8, rows_ref[...])
+        gb9_ref[...] = mm(last9, cot_ref[...])
+        split_columns(meta, mine_ref, theirs_ref, 0, ga8_ref)
+        split_columns(meta, mine_ref, theirs_ref, ga8_ref.shape[1] // 2, gb9_ref)
         for first in range(0, frames, block):
             span = slice(first, first + block)
-            stream = stream_ref[span]
-            out = stream + branch[span] + mm(last9[span], up9_ref[0])
+            stream = stream_in[span]
+            out = stream + (branch[span] + branch_in[span]) + mm_tn(last9[:, span], up9_ref[0])
             out_ref[span] = out.astype(LOW)
             _, normed, inverse = norm_rows(stream, gain_ref[...])
-            grad = grad_rows[span] + mm(last8[span], down8_ref[0])
+            grad = grad_rows[span] + grad_rows_in[span] + mm_tn(last8[:, span], down8_ref[0])
             grad_ref[span] = cot_ref[span].astype(WIDE) + norm_back(
                 grad, gain_ref[...], normed, inverse
             )
@@ -1363,9 +1774,10 @@
     grads = pl.BlockSpec((RANK_UNIT, tile), lambda t, m: (0, t))
     picked = pl.BlockSpec((1, RANK_UNIT, width), lambda t, m: (m[8], 0, 0))
     picked_out = pl.BlockSpec((1, RANK_UNIT, width), lambda t, m: (m[9], 0, 0))
-    rank = (frames, RANK_UNIT)
+    rank = (RANK_UNIT, frames)
     steps = hidden // tile
     full = whole((frames, width))
+    wide = pltpu.VMEM((frames, width), WIDE)
     return call(
         lambda m, *refs: feed_other_body(m, steps - 1, *refs),
         (steps,),
@@ -1381,29 +1793,35 @@
             pl.BlockSpec((RANK_UNIT, tile), lambda t, m: (0, (first_pack + hidden) // tile + t)),
             picked,
             picked_out,
-            full,
-            full,
+            IN_PLACE,
+            IN_PLACE,
             whole(rank),
             whole(rank),
-            full,
+            IN_PLACE,
             whole((1, width)),
         ],
         (full, full, grads, grads, whole((RANK_UNIT, width)), whole((RANK_UNIT, width))),
         (
             shaped((frames, width), LOW),
             shaped((frames, width), WIDE),
-            shaped((RANK_UNIT, hidden), WIDE),
-            shaped((RANK_UNIT, hidden), WIDE),
+            shaped((RANK_UNIT, hidden), LOW),
+            shaped((RANK_UNIT, hidden), LOW),
             shaped((RANK_UNIT, width), WIDE),
-            shaped((RANK_UNIT, width), WIDE),
+            shaped((RANK_UNIT, width), LOW),
         ),
         [
-            pltpu.VMEM((frames, width), WIDE),
-            pltpu.VMEM((frames, width), WIDE),
+            wide,
+            wide,
             pltpu.VMEM(rank, WIDE),
             pltpu.VMEM(rank, WIDE),
             pltpu.VMEM(rank, LOW),
             pltpu.VMEM(rank, LOW),
+            pltpu.VMEM((RANK_UNIT, width), WIDE),
+            pltpu.VMEM((RANK_UNIT, width), WIDE),
+            wide,
+            wide,
+            wide,
+            pltpu.SemaphoreType.DMA((3,)),
         ],
         8 * frames * width * hidden,
         4 * width * hidden + 24 * frames * width,
@@ -1414,27 +1832,28 @@
     )
 
 
-def last_norm_body(_, x_ref, own_ref, other_ref, grad_ref, gain_ref, out_ref):
+def last_norm_body(_, x_ref, own_ref, other_ref, grad_ref, gain_ref, after_ref, out_ref):
     _, normed, inverse = norm_rows(x_ref[...].astype(WIDE), gain_ref[...])
     total = own_ref[...] + other_ref[...].astype(WIDE)
     out_ref[...] = grad_ref[...] + norm_back(total, gain_ref[...], normed, inverse)
 
 
-def last_norm(meta, x, own, other, grad, gain):
+def last_norm(meta, x, own, other, grad, gain, after):
     frames, width = x.shape
     block = min(256, frames)
     rows = pl.BlockSpec((block, width), lambda t, _: (t, 0))
     return call(
         last_norm_body,
         (frames // block,),
-        [rows, rows, rows, rows, whole((1, width))],
+        [rows, rows, rows, rows, whole((1, width)), IN_PLACE],
         rows,
         shaped(x.shape, WIDE),
         [],
         20 * x.size,
         16 * x.size,
         "last_norm",
-        (meta, x, own, other, grad, gain),
+        (meta, x, own, other, grad, gain, after),
+        vmem=VMEM_BYTES // 2,
     )
 
 
@@ -1475,7 +1894,7 @@
     place = lax.axis_index("dp")
     side = lax.axis_index("tensor")
     picks = clip_adapter_index[0]
-    meta = jnp.concatenate([picks, side[None].astype(jnp.int32)])
+    meta = jnp.concatenate([picks, jnp.stack([side, place]).astype(jnp.int32)])
     gain_one, gain_two, gain_three = (
         vec.reshape(1, width) for vec in (self_norm_gain, cross_norm_gain, feed_norm_gain)
     )
@@ -1500,42 +1919,37 @@
 
     rows_one = first_norm(meta, x, gain_one)
     rows_one_other = swap(rows_one)
-
-    def pick(table, slot):
-        return lax.dynamic_index_in_dim(table, picks[slot], axis=0, keepdims=False)
-
-    packed = swap(
-        jnp.concatenate(
-            [
-                pick(attention_first_factors[0], 3),
-                pick(attention_first_factors[1], 7),
-                pick(cross_second_factors[0], 4),
-                jnp.zeros((RANK_UNIT, local), LOW),
-                pick(input_second_factors, 8),
-                pick(output_first_factors, 9),
-            ],
-            axis=1,
-        )
-    )
+    factors = picked_factors(
+        meta,
+        [
+            (attention_first_factors, 0, 3),
+            (attention_first_factors, 1, 7),
+            (cross_second_factors, 0, 4),
+            (cross_second_factors, 0, 4),
+            (input_second_factors, None, 8),
+            (output_first_factors, None, 9),
+        ],
+    )
+    packed = swap(factors)
     first_pack = 4 * local
 
-    parts = hidden // width
-    down_share = share(down_weight, parts * depth).reshape(parts, depth, width)
-    up_share = side_by_side(share(up_weight, depth), parts)
-    share_two = swap(jnp.concatenate([down_share, up_share], axis=0))
-    gathered_two = lax.all_gather(share_two, "dp", axis=0)
-
+    heads_own = project_heads(
+        meta, rows_one, self_query_key_value_weight, self_first_factors, self_second_factors, 0, 0, "own_heads"
+    )
     text_own = project_heads(
         meta, text, cross_key_value_weight, cross_first_factors, cross_second_factors, 5, 1, "text_heads"
     )
     text_other = swap(text_own)
-    heads_own = project_heads(
-        meta, rows_one, self_query_key_value_weight, self_first_factors, self_second_factors, 0, 0, "own_heads"
+    share_two = feed_share(
+        meta, down_weight, up_weight, depth, (heads_own, text_own, rows_one_other, factors)
     )
     heads_other = project_heads(
-        meta, rows_one_other, self_query_key_value_weight, self_first_factors, self_second_factors, 0, 0, "other_heads"
-    )
-    z_own_frames, z_other_frames = self_forward(meta, heads_own, heads_other)
+        meta, rows_one_other, self_query_key_value_weight, self_first_factors, self_second_factors,
+        0, 0, "other_heads", (share_two,),
+    )
+    z_own_frames, z_other_frames, log_own, log_other = self_forward(meta, heads_own, heads_other)
+    share_two, z_other_frames = lax.optimization_barrier((swap(share_two), z_other_frames))
+    gathered_two = lax.all_gather(share_two, "dp", axis=0)
     z_other_heads = swap(z_other_frames)
     weights = (self_output_weight, cross_query_weight, cross_output_weight)
     tables = (attention_first_factors, attention_second_factors, cross_first_factors, cross_second_factors)
@@ -1548,108 +1962,109 @@
         meta, rows_three, cot, up_weight, down_weight, input_first_factors, input_second_factors,
         output_first_factors, output_second_factors, tile,
     )
-    output, grad_two, ga9_other, gb8_other, ga8, gb9 = feed_other(
+    output, grad_two, ga9_other, gb8_other, feed_mine, feed_theirs = feed_other(
         meta, rows_three, cot, gathered_two, packed, first_pack, input_first_factors,
         output_second_factors, (branch, grad_rows, rank9, grad_rank8), stream_two, gain_three, tile,
     )
 
+    gb8_received = swap(gb8_other)
+    ga9_received = swap(ga9_other)
+    feed_received = swap(feed_theirs)
+
     (
-        grad_one, dz_own_heads, dz_other_heads, text_grad_own, text_grad_other,
-        ga3, gb3, ga4, gb4, ga7, gb7,
+        grad_one, dz_own_heads, dz_other_heads, text_grad_own, text_grad_other, mine, theirs,
     ) = middle_back(
         meta, grad_two, stream_one, z_own_frames, z_other_heads, q_own, q_other, z2_own, z2_other,
         weights, gathered_one, tables, packed, text_own, text_other, gain_two,
     )
+    gb8_received, ga9_received, feed_received, dz_other_heads, theirs, text_grad_other = lax.optimization_barrier(
+        (gb8_received, ga9_received, feed_received, dz_other_heads, theirs, text_grad_other)
+    )
     dz_other_frames = swap(dz_other_heads)
-    text_heads_grad = (text_grad_own + swap(text_grad_other.astype(LOW)).astype(WIDE)).astype(LOW)
-    text_rows, ga56, gb56 = project_back_heads(
-        meta, text, text_heads_grad, cross_key_value_weight, cross_first_factors, cross_second_factors,
-        5, 1, WIDE, "text_back",
-    )
-    grads_own, grads_other = self_back(meta, heads_own, heads_other, dz_own_heads, dz_other_frames)
-    partial_other, ga012_other, gb012_other = project_back_heads(
-        meta, rows_one_other, grads_other, self_query_key_value_weight, self_first_factors,
-        self_second_factors, 0, 0, LOW, "other_back",
-    )
+
+    unit = local
+    hidden_units = hidden // unit
+    labels = jnp.zeros((RANK_UNIT, 2 * HEAD_DIM), LOW).at[:, : picks.shape[0]].set(picks.astype(LOW)[None])
+    early = jnp.concatenate(
+        [
+            join(mine, [swap(theirs)]),
+            join(feed_mine, [feed_received]),
+            join(jnp.concatenate([gb8_own, ga9_own], axis=1), [gb8_received, ga9_received]),
+            labels,
+        ],
+        axis=1,
+    )
+    early_all = lax.all_gather(early, "dp", axis=0)
+    grads_own, grads_other = self_back(
+        meta, heads_own, heads_other, z_own_frames, z_other_frames, log_own, log_other,
+        dz_own_heads, dz_other_frames, (early,),
+    )
+    text_grad_other, grads_own = lax.optimization_barrier((swap(text_grad_other), grads_own))
+    text_heads_grad = (text_grad_own + text_grad_other.astype(WIDE)).astype(LOW)
+    text_mine_rank, text_theirs_rank = rank_grads(
+        meta, [text], [text_heads_grad], cross_first_factors, cross_second_factors, 5, 1, "text_ranks"
+    )
+    text_theirs_rank = swap(text_theirs_rank)
+    mine, theirs = rank_grads(
+        meta, [rows_one, rows_one_other], [grads_own, grads_other], self_first_factors,
+        self_second_factors, 0, 0, "self_ranks",
+    )
+    partial_other = project_back_heads(
+        meta, grads_other, self_query_key_value_weight, self_first_factors, self_second_factors,
+        0, 0, LOW, "other_back", theirs,
+    )
+    labels = lax.dynamic_index_in_dim(early_all[:, :, -2 * HEAD_DIM :], place, axis=0, keepdims=False)
+    late = jnp.concatenate(
+        [join(mine, [swap(theirs)]), join(text_mine_rank, [text_theirs_rank]), labels], axis=1
+    )
+    late_all = lax.all_gather(late, "dp", axis=0)
     received = swap(partial_other)
-    partial_own, ga012_own, gb012_own = project_back_heads(
-        meta, rows_one, grads_own, self_query_key_value_weight, self_first_factors,
-        self_second_factors, 0, 0, WIDE, "own_back",
-    )
-    input_grad = last_norm(meta, x, partial_own, received, grad_one, gain_one)
-
-    def my_half(array):
-        return lax.dynamic_slice_in_dim(array, side * (array.shape[1] // 2), array.shape[1] // 2, axis=1)
-
-    def other_half(array):
-        return lax.dynamic_slice_in_dim(
-            array, (1 - side) * (array.shape[1] // 2), array.shape[1] // 2, axis=1
-        )
-
-    def over_clips(mine, theirs, ready, columns):
-        received_part = swap(jnp.concatenate(theirs, axis=1).astype(LOW)).astype(WIDE)
-        both = jnp.concatenate(mine, axis=1) + received_part
-        labels = jnp.zeros((RANK_UNIT, 2 * HEAD_DIM), WIDE).at[0, : picks.shape[0]].set(picks.astype(WIDE))
-        payload = jnp.concatenate([both] + ready + [labels], axis=1).astype(LOW)
-        everyone = lax.all_gather(payload, "dp", axis=0)
-        names = everyone[:, 0, -2 * HEAD_DIM :][:, : picks.shape[0]].astype(jnp.int32)
-        results = []
-        first = 0
-        for column, size in columns:
-            choose = (names[:, column, None] == jnp.arange(slots, dtype=jnp.int32)[None]).astype(LOW)
-            results.append(
-                jnp.einsum(
-                    "cn,cpq->npq", choose, everyone[:, :, first : first + size],
-                    preferred_element_type=WIDE,
-                )
-            )
-            first += size
-        return results
-
-    def text_half(which):
-        return text_rows[:, : width // 2] if which == 0 else text_rows[:, width // 2 :]
-
-    text_mine = jnp.where(side == 0, text_half(0), text_half(1))
-    text_theirs = jnp.where(side == 0, text_half(1), text_half(0))
-    text_grad = text_mine + swap(text_theirs.astype(LOW)).astype(WIDE)
-
-    half_width = width // 2
-    early = over_clips(
-        [my_half(ga8), my_half(gb9), my_half(gb3), my_half(gb7), my_half(ga4), my_half(ga56[0]), my_half(ga56[1])]
-        + [ga9_own, gb8_own, ga3[:, :local], ga7[:, :local], gb4[:, :local]],
-        [other_half(ga8), other_half(gb9), other_half(gb3), other_half(gb7), other_half(ga4), other_half(ga56[0]), other_half(ga56[1])]
-        + [ga9_other, gb8_other, ga3[:, local:], ga7[:, local:], gb4[:, local:]],
-        [gb56[0], gb56[1]],
-        [
-            (8, half_width), (9, half_width), (3, half_width), (7, half_width), (4, half_width),
-            (5, half_width), (6, half_width), (9, hidden), (8, hidden), (3, local), (7, local), (4, local),
-            (5, local), (6, local),
-        ],
-    )
-    ga8_sum, gb9_sum, gb3_sum, gb7_sum, ga4_sum, ga5_sum, ga6_sum = early[:7]
-    ga9_sum, gb8_sum, ga3_sum, ga7_sum, gb4_sum, gb5_sum, gb6_sum = early[7:]
-    ga012 = ga012_own + ga012_other
-    gb012 = gb012_own + gb012_other
-    late = over_clips(
-        [my_half(ga012[j]) for j in range(3)],
-        [other_half(ga012[j]) for j in range(3)],
-        [gb012[j] for j in range(3)],
-        [(j, half_width) for j in range(3)] + [(j, local) for j in range(3)],
+    text_rows = project_back_heads(
+        meta, text_heads_grad, cross_key_value_weight, cross_first_factors, cross_second_factors,
+        5, 1, WIDE, "text_back", partial_other,
+    )
+    text_halves = (text_rows[:, : width // 2], text_rows[:, width // 2 :])
+    text_mine = jnp.where(side == 0, text_halves[0], text_halves[1])
+    text_theirs = jnp.where(side == 0, text_halves[1], text_halves[0])
+    text_received = swap(text_theirs.astype(LOW))
+    partial_own = project_back_heads(
+        meta, grads_own, self_query_key_value_weight, self_first_factors, self_second_factors,
+        0, 0, WIDE, "own_back", late,
+    )
+    sums = slot_sums(
+        meta,
+        early_all,
+        [(4, 0, 0), (4, 1, 0), (3, 2, 0), (7, 2, 1), (3, 3, 0), (7, 3, 1), (8, 4, 0), (9, 5, 0)]
+        + [(8, 6, i) for i in range(hidden_units)]
+        + [(9, 7, i) for i in range(hidden_units)],
+        [(1, unit), (1, unit), (2, unit), (2, unit), (None, unit), (None, unit), (None, hidden), (None, hidden)],
+        slots, unit, "early_slots", (partial_own,),
+    )
+    sum_cross_a, sum_cross_b, sum_out_a, sum_out_b, sum_up_a, sum_down_b, sum_up_b, sum_down_a = sums
+    received, text_received, sum_cross_a = lax.optimization_barrier((received, text_received, sum_cross_a))
+    text_grad = text_mine + text_received.astype(WIDE)
+    input_grad = last_norm(meta, x, partial_own, received, grad_one, gain_one, sum_cross_a)
+    sum_self_a, sum_self_b, sum_cross_a, sum_cross_b = late_sums(
+        meta, late_all,
+        [(0, 0, 0), (1, 0, 1), (2, 0, 2), (0, 1, 0), (1, 1, 1), (2, 1, 2)]
+        + [(5, 2, 1), (6, 2, 2), (5, 3, 1), (6, 3, 2)],
+        [(3, unit), (3, unit), (3, unit), (3, unit)], slots, unit,
+        {2: sum_cross_a, 3: sum_cross_b}, "late_slots", (input_grad,),
     )
     return (
         output[None],
         input_grad[None],
         text_grad[None],
-        jnp.stack(late[:3]),
-        jnp.stack(late[3:]),
-        jnp.stack([ga4_sum, ga5_sum, ga6_sum]),
-        jnp.stack([gb4_sum, gb5_sum, gb6_sum]),
-        jnp.stack([ga3_sum, ga7_sum]),
-        jnp.stack([gb3_sum, gb7_sum]),
-        ga8_sum,
-        gb8_sum,
-        ga9_sum,
-        gb9_sum,
+        sum_self_a,
+        sum_self_b,
+        sum_cross_a,
+        sum_cross_b,
+        sum_out_a,
+        sum_out_b,
+        sum_up_a,
+        sum_up_b,
+        sum_down_a,
+        sum_down_b,
     )
 
 

time: 562 us -> 427 us (0.76)
  waiting for transfers between devices: 171 us -> 78.3 us
  local copies, waits for them, and re-layouts: 42.5 us -> 12.4 us
  between operations: 24.4 us -> 14.6 us
  matrix products: 7.61 us -> 0 us
    all_gather x2, waiting for transfers between devices: 67.7 us -> 0.02 us  [the longest x1 0.02 us: on_pair(): early_all = lax.all_gather(early, 'dp', axis=0)]
    ppermute x12 -> x16, waiting for transfers between devices: 104 us -> 71.5 us  [swap(): return lax.ppermute(array, 'tensor', [(0, 1), (1, 0)])]
    unnamed x94 -> x52, local copies, waits for them, and re-layouts: 25 us -> 7.74 us
    slice x14 -> x1, local copies, waits for them, and re-layouts: 10.4 us -> 0.85 us  [on_pair(): early_all[:, :, -2 * HEAD_DIM:]]
    dot_general x20 -> x0, matrix products: 7.61 us -> none  [over_clips(): jnp.einsum('cn,cpq->npq', choose, everyone[:, :, first:first + size], pre...]
    all_gather x1, waiting for transfers between devices: 0.02 us -> 6.72 us  [on_pair(): gathered_two = lax.all_gather(share_two, 'dp', axis=0)]
    ppermute x12 -> x16, starting transfers between devices: 15.8 us -> 19.5 us  [swap(): return lax.ppermute(array, 'tensor', [(0, 1), (1, 0)])]
    pallas_call x14 -> x20, Pallas kernels: 286 us -> 288 us  [call(): pl.pallas_call(body, grid_spec=pltpu.PrefetchScalarGridSpec(num_scalar_pr...]
  transfers between devices with their start and end apart: 16 -> 20, of which waited for: 10 -> 8; matrix products, arithmetic and copies ran while one was open for 4% -> 2% of each run, Pallas kernels for 37% -> 58%
where the time goes in v2:
time: 427 us; the launch traced here: 421 us
  Pallas kernels  288 us (67%)
  waiting for transfers between devices  78.3 us (18%)
  starting transfers between devices  20 us (5%)
  between operations  14.6 us (3%)
  local copies, waits for them, and re-layouts  12.4 us (3%)
  other arithmetic  7.99 us (2%)
    pallas_call x20, Pallas kernels, call(): pl.pallas_call(body, grid_spec=pltpu.PrefetchScalarGridSpec(num_scalar_pr...  288 us
    ppermute x16, waiting for transfers between devices, swap(): return lax.ppermute(array, 'tensor', [(0, 1), (1, 0)])  71.5 us
    ppermute x16, starting transfers between devices, swap(): return lax.ppermute(array, 'tensor', [(0, 1), (1, 0)])  19.5 us
  transfers between devices with their start and end apart: 20, of which 8 were waited for; matrix products, arithmetic and copies ran while one was open for 2% of the time, Pallas kernels for 58%

profile of v2, /device:TPU:0, one launch (start us, length us, event | category | flops | bytes accessed | tf_op | source)
XLA Modules:
  0.0 421.0 jit_solution(17358649964810330831)
XLA Ops:
  12.4 10.2 %collective-permute-done.3 = bf16[3,96,768]{2,1,0:T(8,128)(2,1)S(1)} collective-permute-done((bf16[3,96,768]{2,1,0:T(8,128)(2,1)S(1)}, bf16[3,96,768]{2,1,0:T(8,128)(2,1)S(1)}, u32[]{:S(2)}, u32[]{:S(2)}) %collective-permute-start.3) | collective-permute-done | bytes 442400 | tf_op jit(solution)/shard_map/ppermute | solution.py:1903
  24.6 3.7 first_norm.1.act_ref.refs_0_
  32.5 4.9 %text_heads.1.refs_3_.text_own_ref.refs_21_ = bf16[2,64,768]{2,1,0:T(8,128)(2,1)} custom-call(s32[12]{0:T(128)} %pad_add_fusion._.m.meta, bf16[64,1536]{1,0:T(8,128)(2,1)} %bitcast.35, bf16[2,1536,768]{2,1,0:T(8,128)(2,1)} %refs_1_.9, bf16[3,8,16,1536]{3,2,1,0:T(8,128)(2,1)} %refs_2_.9, bf16[3,8,16,768]{3,2,1,0:T(8,128)(2,1)} %refs_3_.9), custom_call_target="tpu_custom_call" | custom-call | flops 301989888 | bytes 5111808 | tf_op jit(solution)/shard_map/text_heads/pallas_call | solution.py:515
  37.4 10.5 %own_heads.1.refs_2_.own_ref = bf16[3,512,768]{2,1,0:T(8,128)(2,1)} custom-call(s32[12]{0:T(128)} %pad_add_fusion._.m.meta, bf16[512,1536]{1,0:T(8,128)(2,1)} %first_norm.1.act_ref.refs_0_, bf16[3,1536,768]{2,1,0:T(8,128)(2,1)} %refs_1_.8, bf16[3,8,16,1536]{3,2,1,0:T(8,128)(2,1)} %refs_2_.8, bf16[3,8,16,768]{3,2,1,0:T(8,128)(2,1)} %refs_3_.8), custom_call_target="tpu_custom_call" | custom-call | flops 3623878656 | bytes 11010048 | tf_op jit(solution)/shard_map/own_heads/pallas_call | solution.py:515
  47.9 16.3 %collective-permute-done.refs_4_.act_ref.refs_1_ = bf16[512,1536]{1,0:T(8,128)(2,1)S(1)} collective-permute-done((bf16[512,1536]{1,0:T(8,128)(2,1)}, bf16[512,1536]{1,0:T(8,128)(2,1)S(1)}, u32[]{:S(2)}, u32[]{:S(2)}) %collective-permute-start) | collective-permute-done | bytes 1572896 | tf_op jit(solution)/shard_map/ppermute | solution.py:1903
  65.3 4.3 %feed_share.1.refs_0_ = bf16[4,96,1536]{2,1,0:T(8,128)(2,1)} custom-call(s32[12]{0:T(128)} %pad_add_fusion._.m.meta, bf16[3072,1536]{1,0:T(8,128)(2,1)} %down_weight_ref.1, bf16[1536,3072]{1,0:T(8,128)(2,1)} %up_weight_ref.1, bf16[3,512,768]{2,1,0:T(8,128)(2,1)} %own_heads.1.refs_2_.own_ref, bf16[2,64,768]{2,1,0:T(8,128)(2,1)} %text_heads.1.refs_3_.text_own_ref.refs_21_, ...), custom_call_target="tpu_custom_call" | custom-call | bytes 2359296 | tf_op jit(solution)/shard_map/feed_share/pallas_call | solution.py:515
  71.0 10.5 %other_heads.1.other_ref = bf16[3,512,768]{2,1,0:T(8,128)(2,1)} custom-call(s32[12]{0:T(128)} %pad_add_fusion._.m.meta, bf16[512,1536]{1,0:T(8,128)(2,1)} %copy-done.6, bf16[3,1536,768]{2,1,0:T(8,128)(2,1)} %refs_1_.8, bf16[3,8,16,1536]{3,2,1,0:T(8,128)(2,1)} %refs_2_.8, bf16[3,8,16,768]{3,2,1,0:T(8,128)(2,1)} %refs_3_.8, bf16[4,96,1536]{2,1,0:T(8,128)(2,1)} %feed_share.1.refs_0_), custom_call_target="tpu_custom_call" | custom-call | flops 3623878656 | bytes 11010048 | tf_op jit(solution)/shard_map/other_heads/pallas_call | solution.py:515
  81.5 18.5 %self_forward.1 = (bf16[512,768]{1,0:T(8,128)(2,1)}, bf16[512,768]{1,0:T(8,128)(2,1)}, f32[512,768]{1,0:T(8,128)}, f32[512,768]{1,0:T(8,128)}) custom-call(s32[12]{0:T(128)} %pad_add_fusion._.m.meta, bf16[3,512,768]{2,1,0:T(8,128)(2,1)} %own_heads.1.refs_2_.own_ref, bf16[3,512,768]{2,1,0:T(8,128)(2,1)} %other_heads.1.other_ref), custom_call_target="tpu_custom_call" | custom-call | flops 4026531840 | bytes 6291456 | tf_op jit(solution)/shard_map/self_forward/pallas_call | solution.py:515
  106.8 19.5 %collective-permute-done.5.text_other_ref.refs_22_ = bf16[2,64,768]{2,1,0:T(8,128)(2,1)S(1)} collective-permute-done((bf16[2,64,768]{2,1,0:T(8,128)(2,1)S(1)}, bf16[2,64,768]{2,1,0:T(8,128)(2,1)S(1)}, u32[]{:S(2)}, u32[]{:S(2)}) %collective-permute-start.5) | collective-permute-done | bytes 196640 | tf_op jit(solution)/shard_map/ppermute | solution.py:1903
  130.5 28.7 %middle_forward.1 = (f32[512,1536]{1,0:T(8,128)}, f32[512,1536]{1,0:T(8,128)}, bf16[512,1536]{1,0:T(8,128)(2,1)}, bf16[512,768]{1,0:T(8,128)(2,1)}, bf16[512,768...) custom-call(s32[12]{0:T(128)} %pad_add_fusion._.m.meta, bf16[512,1536]{1,0:T(8,128)(2,1)} %bitcast.25, ...), custom_call_target="tpu_custom_call" | custom-call | flops 7247757312 | bytes 29884416 | tf_op jit(solution)/shard_map/middle_forward/pallas_call | solution.py:515
  159.2 34.7 %feed_own.1 = (f32[512,1536]{1,0:T(8,128)}, f32[512,1536]{1,0:T(8,128)}, f32[16,512]{1,0:T(8,128)}, f32[16,512]{1,0:T(8,128)}, f32[16,3072]{1,0:T(8,128)}, /*index=5*/f32[16,3072]{1,0:T(8,128)}) custom-call(s32[12]{0:T(128)} %pad_add_fusion._.m.meta, bf16[512,1536]{1,0:T(8,128)(2,1)} %get-tuple-element.89.rows_ref.refs_0_, bf16[512,1536]{1,0:T(8,128)(2,1)} %bitcast.44, ...), custom_call_target="tpu_custom_call" | custom-call | flops 19327352832 | bytes 28311552 | tf_op jit(solution)/shard_map/feed_own/pallas_call | solution.py:515
  193.9 6.7 %all-gather.11.cloned.1.call-done = bf16[64,96,1536]{2,1,0:T(8,128)(2,1)} async-done(((bf16[4,96,1536]{2,1,0:T(8,128)(2,1)}), bf16[64,96,1536]{2,1,0:T(8,128)(2,1)}) %all-gather.11.cloned.1.call-update) | async-done | bytes 18874384 | tf_op jit(solution)/shard_map/all_gather | solution.py:1952
  200.7 37.2 %feed_other.1 = (bf16[512,1536]{1,0:T(8,128)(2,1)}, f32[512,1536]{1,0:T(8,128)}, bf16[16,3072]{1,0:T(8,128)(2,1)}, bf16[16,3072]{1,0:T(8,128)(2,1)}, f32[16,1536]{1,0:T(8,128)}, /*index=5*/bf16[16,1536]{1,0:T(8,128)(2,1)}) custom-call(s32[12]{0:T(128)} %pad_add_fusion._.m.meta, bf16[512,1536]{1,0:T(8,128)(2,1)} %get-tuple-element.89.rows_ref.refs_0_, ...), custom_call_target="tpu_custom_call" | custom-call | flops 19327352832 | bytes 37748736 | tf_op jit(solution)/shard_map/feed_other/pallas_call | solution.py:515
  241.5 31.3 %middle_back.1 = (f32[512,1536]{1,0:T(8,128)}, bf16[512,768]{1,0:T(8,128)(2,1)}, bf16[512,768]{1,0:T(8,128)(2,1)}, f32[2,64,768]{2,1,0:T(8,128)}, bf16[2,64,768]...) custom-call(s32[12]{0:T(128)} %pad_add_fusion._.m.meta, f32[512,1536]{1,0:T(8,128)} %get-tuple-element.100.refs_0_, ...), custom_call_target="tpu_custom_call" | custom-call | flops 7247757312 | bytes 33030144 | tf_op jit(solution)/shard_map/middle_back/pallas_call | solution.py:515
  275.0 4.9 %collective-permute-done.11 = bf16[16,4608]{1,0:T(8,128)(2,1)S(1)} collective-permute-done((bf16[16,4608]{1,0:T(8,128)(2,1)}, bf16[16,4608]{1,0:T(8,128)(2,1)S(1)}, u32[]{:S(2)}, u32[]{:S(2)}) %collective-permute-start.11) | collective-permute-done | bytes 147488 | tf_op jit(solution)/shard_map/ppermute | solution.py:1903
  282.4 14.3 %collective-permute-done.10.grad_other_ref = bf16[512,768]{1,0:T(8,128)(2,1)S(1)} collective-permute-done((bf16[512,768]{1,0:T(8,128)(2,1)}, bf16[512,768]{1,0:T(8,128)(2,1)S(1)}, u32[]{:S(2)}, u32[]{:S(2)}) %collective-permute-start.10) | collective-permute-done | bytes 786464 | tf_op jit(solution)/shard_map/ppermute | solution.py:1903
  297.7 35.0 %self_back.1 = (bf16[3,512,768]{2,1,0:T(8,128)(2,1)}, bf16[3,512,768]{2,1,0:T(8,128)(2,1)}) custom-call(s32[12]{0:T(128)} %pad_add_fusion._.m.meta, bf16[3,512,768]{2,1,0:T(8,128)(2,1)} %own_heads.1.refs_2_.own_ref, bf16[3,512,768]{2,1,0:T(8,128)(2,1)} %other_heads.1.other_ref, bf16[512,768]{1,0:T(8,128)(2,1)} %get-tuple-element.86.z_own_ref.refs_2_, ...), custom_call_target="tpu_custom_call" | custom-call | flops 100663296000 | bytes 11796480 | tf_op jit(solution)/shard_map/self_back/pallas_call | solution.py:515
  336.7 8.5 %self_ranks.1 = (f32[16,4608]{1,0:T(8,128)}, bf16[16,2304]{1,0:T(8,128)(2,1)}) custom-call(s32[12]{0:T(128)} %pad_add_fusion._.m.meta, bf16[512,1536]{1,0:T(8,128)(2,1)} %first_norm.1.act_ref.refs_0_, bf16[512,1536]{1,0:T(8,128)(2,1)} %copy-done.6, bf16[3,512,768]{2,1,0:T(8,128)(2,1)} %get-tuple-element.123.refs_2_.refs_0_, ...), custom_call_target="tpu_custom_call" | custom-call | flops 905969664 | bytes 7864320 | tf_op jit(solution)/shard_map/self_ranks/pallas_call | solution.py:515
  352.4 11.1 %other_back.1.refs_4_ = bf16[512,1536]{1,0:T(8,128)(2,1)} custom-call(s32[12]{0:T(128)} %pad_add_fusion._.m.meta, bf16[3,512,768]{2,1,0:T(8,128)(2,1)} %get-tuple-element.124.refs_3_.refs_0_, bf16[3,1536,768]{2,1,0:T(8,128)(2,1)} %refs_1_.8, bf16[3,8,16,1536]{3,2,1,0:T(8,128)(2,1)} %refs_2_.8, bf16[3,8,16,768]{3,2,1,0:T(8,128)(2,1)} %refs_3_.8, ...), custom_call_target="tpu_custom_call" | custom-call | flops 3623878656 | bytes 12582912 | tf_op jit(solution)/shard_map/other_back/pallas_call | solution.py:515
  364.9 5.5 %text_back.1 = f32[64,1536]{1,0:T(8,128)} custom-call(s32[12]{0:T(128)} %pad_add_fusion._.m.meta, bf16[2,64,768]{2,1,0:T(8,128)(2,1)} %add_convert_fusion.refs_1_.refs_0_, bf16[2,1536,768]{2,1,0:T(8,128)(2,1)} %refs_1_.9, bf16[3,8,16,1536]{3,2,1,0:T(8,128)(2,1)} %refs_2_.9, bf16[3,8,16,768]{3,2,1,0:T(8,128)(2,1)} %refs_3_.9, bf16[512,1536]{1,0:T(8,128)(2,1)} %other_back.1.refs_4_), custom_call_target="tpu_custom_call" | custom-call | flops 301989888 | bytes 5308416 | tf_op jit(solution)/shard_map/text_back/pallas_call | solution.py:515
  372.1 11.6 %own_back.1.refs_2_.own_ref = f32[512,1536]{1,0:T(8,128)} custom-call(s32[12]{0:T(128)} %pad_add_fusion._.m.meta, bf16[3,512,768]{2,1,0:T(8,128)(2,1)} %get-tuple-element.123.refs_2_.refs_0_, bf16[3,1536,768]{2,1,0:T(8,128)(2,1)} %refs_1_.8, bf16[3,8,16,1536]{3,2,1,0:T(8,128)(2,1)} %refs_2_.8, bf16[3,8,16,768]{3,2,1,0:T(8,128)(2,1)} %refs_3_.8, ...), custom_call_target="tpu_custom_call" | custom-call | flops 3623878656 | bytes 12582912 | tf_op jit(solution)/shard_map/own_back/pallas_call | solution.py:515
  383.7 14.9 %early_slots.1 = (f32[1,8,16,768]{3,2,1,0:T(8,128)}, f32[1,8,16,768]{3,2,1,0:T(8,128)}, f32[2,8,16,768]{3,2,1,0:T(8,128)}, f32[2,8,16,768]{3,2,1,0:T(8,128)}, f3...) custom-call(s32[12]{0:T(128)} %pad_add_fusion._.m.meta, ...), custom_call_target="tpu_custom_call" | custom-call | bytes 12713984 | tf_op jit(solution)/shard_map/early_slots/pallas_call | solution.py:515
  401.7 5.3 %last_norm.1.refs_4_ = f32[512,1536]{1,0:T(8,128)} custom-call(s32[12]{0:T(128)S(1)} %copy-done.4, bf16[512,1536]{1,0:T(8,128)(2,1)S(1)} %bitcast.26, f32[512,1536]{1,0:T(8,128)S(1)} %copy-done, bf16[512,1536]{1,0:T(8,128)(2,1)} %collective-permute-done.14.other_ref, f32[512,1536]{1,0:T(8,128)S(1)} %copy-done.2, f32[1,1536]{1,0:T(1,128)S(1)} %copy-done.5, ...), custom_call_target="tpu_custom_call" | custom-call | flops 15728640 | bytes 12582912 | tf_op jit(solution)/shard_map/last_norm/pallas_call | solution.py:515
  407.7 6.3 %late_slots.1 = (f32[3,8,16,768]{3,2,1,0:T(8,128)}, f32[3,8,16,768]{3,2,1,0:T(8,128)}, f32[3,8,16,768]{3,2,1,0:T(8,128)}, f32[3,8,16,768]{3,2,1,0:T(8,128)}) custom-call(s32[12]{0:T(128)} %pad_add_fusion._.m.meta, bf16[16,16,7808]{2,1,0:T(8,128)(2,1)} %bitcast.30, bf16[16,16,7808]{2,1,0:T(8,128)(2,1)} %bitcast.31, ...), custom_call_target="tpu_custom_call" | custom-call | bytes 7995392 | tf_op jit(solution)/shard_map/late_slots/pallas_call | solution.py:515
  (118 shorter events, 51.9 us)
Async XLA Ops:
  7.2 122.4 %all-gather.9.cloned.1.call-start = ((), (), s32[]{:S(2)}) async-start(), calls=%async_computation | async-start | bytes 7520256 | tf_op jit(solution)/shard_map/all_gather | solution.py:1918
  9.4 13.2 %collective-permute-start.3 = (bf16[3,96,768]{2,1,0:T(8,128)(2,1)S(1)}, bf16[3,96,768]{2,1,0:T(8,128)(2,1)S(1)}, u32[]{:S(2)}, u32[]{:S(2)}) collective-permute-start(bf16[3,96,768]{2,1,0:T(8,128)(2,1)S(1)} %pad_maximum_fusion), channel_id=1, source_target_pairs={{0,1},{1,0},{2,3},{3,2},{4,5},{5,4},{6,7},{7,6},{8,9},{9,8},{10,11... | collective-permute-start | bytes 1327112 | tf_op jit(solution)/shard_map/ppermute | solution.py:1903
  23.4 177.3 %all-gather.11.cloned.1.call-start = ((), (), s32[]{:S(2)}) async-start(), calls=%async_computation.1 | async-start | bytes 20054016 | tf_op jit(solution)/shard_map/all_gather | solution.py:1952
  28.4 35.8 %collective-permute-start = (bf16[512,1536]{1,0:T(8,128)(2,1)}, bf16[512,1536]{1,0:T(8,128)(2,1)S(1)}, u32[]{:S(2)}, u32[]{:S(2)}) collective-permute-start(bf16[512,1536]{1,0:T(8,128)(2,1)} %first_norm.1.act_ref.refs_0_), channel_id=1, source_target_pairs={{0,1},{1,0},{2,3},{3,2},{4,5},{5,4},{6,7},{7,6},{8,9},{9,8},{10,11... | collective-permute-start | bytes 4718600 | tf_op jit(solution)/shard_map/ppermute | solution.py:1903
  69.6 30.4 %collective-permute-start.1 = (bf16[4,96,1536]{2,1,0:T(8,128)(2,1)}, bf16[4,96,1536]{2,1,0:T(8,128)(2,1)S(1)}, u32[]{:S(2)}, u32[]{:S(2)}) collective-permute-start(bf16[4,96,1536]{2,1,0:T(8,128)(2,1)} %feed_share.1.refs_0_), channel_id=1, source_target_pairs={{0,1},{1,0},{2,3},{3,2},{4,5},{5,4},{6,7},{7,6},{8,9},{9,8},{10,11... | collective-permute-start | bytes 3538952 | tf_op jit(solution)/shard_map/ppermute | solution.py:1903
  101.0 249.8 %all-gather.13.cloned.1.call-start = ((), (), s32[]{:S(2)}) async-start(), calls=%async_computation.2 | async-start | bytes 6754304 | tf_op jit(solution)/shard_map/all_gather | solution.py:1997
  101.4 28.1 %collective-permute-start.2 = (bf16[512,768]{1,0:T(8,128)(2,1)}, bf16[512,768]{1,0:T(8,128)(2,1)S(1)}, u32[]{:S(2)}, u32[]{:S(2)}) collective-permute-start(bf16[512,768]{1,0:T(8,128)(2,1)} %get-tuple-element.88.z_other_ref), channel_id=1, source_target_pairs={{0,1},{1,0},{2,3},{3,2},{4,5},{5,4},{6,7},{7,6},{8,9},{9,8},{10,11... | collective-permute-start | bytes 2359304 | tf_op jit(solution)/shard_map/ppermute | solution.py:1903
  102.3 24.1 %collective-permute-start.5 = (bf16[2,64,768]{2,1,0:T(8,128)(2,1)S(1)}, bf16[2,64,768]{2,1,0:T(8,128)(2,1)S(1)}, u32[]{:S(2)}, u32[]{:S(2)}) collective-permute-start(bf16[2,64,768]{2,1,0:T(8,128)(2,1)S(1)} %copy-done.9), channel_id=1, source_target_pairs={{0,1},{1,0},{2,3},{3,2},{4,5},{5,4},{6,7},{7,6},{8,9},{9,8},{10,11... | collective-permute-start | bytes 589832 | tf_op jit(solution)/shard_map/ppermute | solution.py:1903
  103.5 26.0 %collective-permute-start.4 = (bf16[16,9216]{1,0:T(8,128)(2,1)S(1)}, bf16[16,9216]{1,0:T(8,128)(2,1)S(1)}, u32[]{:S(2)}, u32[]{:S(2)}) collective-permute-start(bf16[16,9216]{1,0:T(8,128)(2,1)S(1)} %copy-done.11), channel_id=1, source_target_pairs={{0,1},{1,0},{2,3},{3,2},{4,5},{5,4},{6,7},{7,6},{8,9},{9,8},{10,11... | collective-permute-start | bytes 884744 | tf_op jit(solution)/shard_map/ppermute | solution.py:1903
  237.9 34.9 %collective-permute-start.6 = (bf16[16,3072]{1,0:T(8,128)(2,1)}, bf16[16,3072]{1,0:T(8,128)(2,1)S(1)}, u32[]{:S(2)}, u32[]{:S(2)}) collective-permute-start(bf16[16,3072]{1,0:T(8,128)(2,1)} %get-tuple-element.97), channel_id=1, source_target_pairs={{0,1},{1,0},{2,3},{3,2},{4,5},{5,4},{6,7},{7,6},{8,9},{9,8},{10,11... | collective-permute-start | bytes 294920 | tf_op jit(solution)/shard_map/ppermute | solution.py:1903
  239.4 33.4 %collective-permute-start.7 = (bf16[16,3072]{1,0:T(8,128)(2,1)}, bf16[16,3072]{1,0:T(8,128)(2,1)S(1)}, u32[]{:S(2)}, u32[]{:S(2)}) collective-permute-start(bf16[16,3072]{1,0:T(8,128)(2,1)} %get-tuple-element.98), channel_id=1, source_target_pairs={{0,1},{1,0},{2,3},{3,2},{4,5},{5,4},{6,7},{7,6},{8,9},{9,8},{10,11... | collective-permute-start | bytes 294920 | tf_op jit(solution)/shard_map/ppermute | solution.py:1903
  240.0 32.8 %collective-permute-start.8 = (bf16[16,1536]{1,0:T(8,128)(2,1)}, bf16[16,1536]{1,0:T(8,128)(2,1)S(1)}, u32[]{:S(2)}, u32[]{:S(2)}) collective-permute-start(bf16[16,1536]{1,0:T(8,128)(2,1)} %get-tuple-element.99), channel_id=1, source_target_pairs={{0,1},{1,0},{2,3},{3,2},{4,5},{5,4},{6,7},{7,6},{8,9},{9,8},{10,11... | collective-permute-start | bytes 147464 | tf_op jit(solution)/shard_map/ppermute | solution.py:1903
  241.5 33.5 %copy-start.16 = (f32[16,3072]{1,0:T(8,128)S(1)}, f32[16,3072]{1,0:T(8,128)}, u32[]{:S(2)}) copy-start(f32[16,3072]{1,0:T(8,128)} %get-tuple-element.119) | copy-start | bytes 589828
  241.5 33.5 %copy-start.17 = (f32[16,3072]{1,0:T(8,128)S(1)}, f32[16,3072]{1,0:T(8,128)}, u32[]{:S(2)}) copy-start(f32[16,3072]{1,0:T(8,128)} %get-tuple-element.118) | copy-start | bytes 589828
  241.5 33.5 %copy-start.19 = (f32[16,1536]{1,0:T(8,128)S(1)}, f32[16,1536]{1,0:T(8,128)}, u32[]{:S(2)}) copy-start(f32[16,1536]{1,0:T(8,128)} %get-tuple-element.116) | copy-start | bytes 294916
  272.9 7.1 %collective-permute-start.11 = (bf16[16,4608]{1,0:T(8,128)(2,1)}, bf16[16,4608]{1,0:T(8,128)(2,1)S(1)}, u32[]{:S(2)}, u32[]{:S(2)}) collective-permute-start(bf16[16,4608]{1,0:T(8,128)(2,1)} %get-tuple-element.115), channel_id=1, source_target_pairs={{0,1},{1,0},{2,3},{3,2},{4,5},{5,4},{6,7},{7,6},{8,9},{9,8},{10,11... | collective-permute-start | bytes 442376 | tf_op jit(solution)/shard_map/ppermute | solution.py:1903
  273.5 23.3 %collective-permute-start.10 = (bf16[512,768]{1,0:T(8,128)(2,1)}, bf16[512,768]{1,0:T(8,128)(2,1)S(1)}, u32[]{:S(2)}, u32[]{:S(2)}) collective-permute-start(bf16[512,768]{1,0:T(8,128)(2,1)} %get-tuple-element.113), channel_id=1, source_target_pairs={{0,1},{1,0},{2,3},{3,2},{4,5},{5,4},{6,7},{7,6},{8,9},{9,8},{10,11... | collective-permute-start | bytes 2359304 | tf_op jit(solution)/shard_map/ppermute | solution.py:1903
  281.8 125.9 %all-gather.15.cloned.1.call-start = ((), (), s32[]{:S(2)}) async-start(), calls=%async_computation.3 | async-start | bytes 4247552 | tf_op jit(solution)/shard_map/all_gather | solution.py:2020
  281.8 50.8 %collective-permute-start.9 = (bf16[2,64,768]{2,1,0:T(8,128)(2,1)S(1)}, bf16[2,64,768]{2,1,0:T(8,128)(2,1)S(1)}, u32[]{:S(2)}, u32[]{:S(2)}) collective-permute-start(bf16[2,64,768]{2,1,0:T(8,128)(2,1)S(1)} %copy-done.25), channel_id=1, source_target_pairs={{0,1},{1,0},{2,3},{3,2},{4,5},{5,4},{6,7},{7,6},{8,9},{9,8},{10,11... | collective-permute-start | bytes 589832 | tf_op jit(solution)/shard_map/ppermute | solution.py:1903
  297.7 35.0 %copy-start.14 = (f32[2,64,768]{2,1,0:T(8,128)S(1)}, f32[2,64,768]{2,1,0:T(8,128)}, u32[]{:S(2)}) copy-start(f32[2,64,768]{2,1,0:T(8,128)} %get-tuple-element.127) | copy-start | bytes 1179652
  336.1 10.5 %collective-permute-start.13 = (bf16[16,1536]{1,0:T(8,128)(2,1)}, bf16[16,1536]{1,0:T(8,128)(2,1)S(1)}, u32[]{:S(2)}, u32[]{:S(2)}) collective-permute-start(bf16[16,1536]{1,0:T(8,128)(2,1)} %get-tuple-element.130), channel_id=1, source_target_pairs={{0,1},{1,0},{2,3},{3,2},{4,5},{5,4},{6,7},{7,6},{8,9},{9,8},{10,11... | collective-permute-start | bytes 147464 | tf_op jit(solution)/shard_map/ppermute | solution.py:1903
  345.2 4.6 %collective-permute-start.12 = (bf16[16,2304]{1,0:T(8,128)(2,1)}, bf16[16,2304]{1,0:T(8,128)(2,1)S(1)}, u32[]{:S(2)}, u32[]{:S(2)}) collective-permute-start(bf16[16,2304]{1,0:T(8,128)(2,1)} %get-tuple-element.126.refs_4_), channel_id=1, source_target_pairs={{0,1},{1,0},{2,3},{3,2},{4,5},{5,4},{6,7},{7,6},{8,9},{9,8},{10,11... | collective-permute-start | bytes 221192 | tf_op jit(solution)/shard_map/ppermute | solution.py:1903
  363.5 35.2 %collective-permute-start.14 = (bf16[512,1536]{1,0:T(8,128)(2,1)}, bf16[512,1536]{1,0:T(8,128)(2,1)}, u32[]{:S(2)}, u32[]{:S(2)}) collective-permute-start(bf16[512,1536]{1,0:T(8,128)(2,1)} %other_back.1.refs_4_), channel_id=1, source_target_pairs={{0,1},{1,0},{2,3},{3,2},{4,5},{5,4},{6,7},{7,6},{8,9},{9,8},{10,11... | collective-permute-start | bytes 4718600 | tf_op jit(solution)/shard_map/ppermute | solution.py:1903
  371.4 27.2 %collective-permute-start.15 = (bf16[64,768]{1,0:T(8,128)(2,1)S(1)}, bf16[64,768]{1,0:T(8,128)(2,1)S(1)}, u32[]{:S(2)}, u32[]{:S(2)}) collective-permute-start(bf16[64,768]{1,0:T(8,128)(2,1)S(1)} %select_convert_fusion), channel_id=1, source_target_pairs={{0,1},{1,0},{2,3},{3,2},{4,5},{5,4},{6,7},{7,6},{8,9},{9,8},{10,11... | collective-permute-start | bytes 294920 | tf_op jit(solution)/shard_map/ppermute | solution.py:1903
  (22 other events, 220.7 us)
Sparse Core Ops, SparseCore 0:
  23.5 68.2 all-gather.8
  101.2 99.4 all-gather.10
  281.9 61.2 all-gather.12
  352.5 49.0 all-gather.14

commit v3 on v2

--- a/solution.py
+++ b/solution.py
@@ -511,7 +511,7 @@
     return pl.BlockSpec(shape, lambda *_: place, pipeline_mode=pl.Buffered(1))
 
 
-def call(body, grid, in_specs, out_specs, out_shape, scratch, flops, moved, name, args, vmem=VMEM_BYTES):
+def call(body, grid, in_specs, out_specs, out_shape, scratch, flops, moved, name, args):
     return pl.pallas_call(
         body,
         grid_spec=pltpu.PrefetchScalarGridSpec(
@@ -523,7 +523,7 @@
         ),
         out_shape=out_shape,
         compiler_params=pltpu.CompilerParams(
-            dimension_semantics=("arbitrary",) * len(grid), vmem_limit_bytes=vmem
+            dimension_semantics=("arbitrary",) * len(grid), vmem_limit_bytes=VMEM_BYTES
         ),
         cost_estimate=pl.CostEstimate(
             flops=flops // COST_SCALE, bytes_accessed=moved // COST_SCALE, transcendentals=0
@@ -700,15 +700,28 @@
 
 
 def rank_grads_body(meta, count, parts, *refs):
-    acts = refs[:parts]
-    grads = refs[parts : 2 * parts]
+    acts = []
+    grads = []
+    act_scratch, grad_scratch, sems = refs[-3:]
+    copies = []
+    for part in range(parts):
+        pairs = ((refs[part], act_scratch.at[part]), (refs[parts + part], grad_scratch.at[part]))
+        copies.append(
+            [pltpu.make_async_copy(*pair, sems.at[2 * part + number]) for number, pair in enumerate(pairs)]
+        )
+        for copy in copies[-1]:
+            copy.start()
+        acts.append(act_scratch.at[part])
+        grads.append(grad_scratch.at[part])
     downs = refs[2 * parts : 2 * parts + count]
     ups = refs[2 * parts + count : 2 * parts + 2 * count]
-    mine_ref, theirs_ref, ga = refs[2 * parts + 2 * count :]
+    mine_ref, theirs_ref, ga = refs[-6:-3]
     half = ga.shape[1] // 2
     local = ups[0].shape[3]
     down = jnp.concatenate([ref[0, 0] for ref in downs], axis=0)
     for part in range(parts):
+        for copy in copies[part]:
+            copy.wait()
         act = acts[part][...]
         rank = low_rank(down, act)
         grad_rank = jnp.concatenate(
@@ -751,13 +764,17 @@
     return call(
         lambda m, *refs: rank_grads_body(m, count, parts, *refs),
         (1,),
-        [whole((rows, width))] * parts
-        + [whole((count, rows, local))] * parts
+        [IN_PLACE] * (2 * parts)
         + [table(width, j) for j in range(count)]
         + [table(local, j) for j in range(count)],
         (whole((RANK_UNIT, total)), whole((RANK_UNIT, shared))),
         (shaped((RANK_UNIT, total), WIDE), shaped((RANK_UNIT, shared), LOW)),
-        [pltpu.VMEM((RANK_UNIT * count, width), WIDE)],
+        [
+            pltpu.VMEM((RANK_UNIT * count, width), WIDE),
+            pltpu.VMEM((parts, rows, width), LOW),
+            pltpu.VMEM((parts, count, rows, local), LOW),
+            pltpu.SemaphoreType.DMA((2 * parts,)),
+        ],
         8 * parts * rows * (width + local) * RANK_UNIT * count,
         2 * parts * rows * (width + count * local),
         name,
@@ -799,31 +816,7 @@
     return jnp.where(place == target, 1.0, 0.0).astype(LOW)
 
 
-def slot_sum_body(_, plan, slots, everyone_ref, label_ref, *refs):
-    names = refs[-1]
-    out_refs = refs[-1 - len({which for _, which, _ in plan}) : -1]
-    step = pl.program_id(0)
-    clips, rank, unit = everyone_ref.shape
-
-    @pl.when(step == 0)
-    def _():
-        names[...] = clip_names(label_ref)
-
-    column = jnp.int32(0)
-    chosen_out = jnp.int32(0)
-    for number, (place, which, _) in enumerate(plan):
-        column = jnp.where(step == number, place, column)
-        chosen_out = jnp.where(step == number, which, chosen_out)
-    take = slot_take(names[pl.ds(column, 1)], slots, rank)
-    total = mm(take, everyone_ref[...].reshape(clips * rank, unit))
-    for which, ref in enumerate(out_refs):
-
-        @pl.when(chosen_out == which)
-        def _():
-            ref[...] = total.reshape(ref.shape)
-
-
-def late_sum_body(_, plan, slots, carried, everyone_ref, label_ref, *refs):
+def slot_sum_body(_, plan, slots, carried, everyone_ref, label_ref, *refs):
     count = len({which for _, which, _ in plan})
     earlier = refs[: len(carried)]
     out_refs = refs[-5 - count : -5]
@@ -848,25 +841,30 @@
         take = slot_take(names[column : column + 1], slots, rank)
         total = mm(take, arrived[number].reshape(clips * rank, unit))
         totals[number] = total.reshape(slots, rank, unit)
-        copy = pltpu.make_async_copy(totals.at[number], out_refs[which].at[place], out_sems.at[number])
+        out_ref = out_refs[which]
+        target = out_ref.at[place] if len(out_ref.shape) == 4 else out_ref.at[:, :, pl.ds(unit * place, unit)]
+        copy = pltpu.make_async_copy(totals.at[number], target, out_sems.at[number])
         copy.start()
         outgoing.append(copy)
     for copy in outgoing:
         copy.wait()
 
 
-def late_sums(meta, everyone, plan, outs, slots, unit, carried, name, after):
+def slot_sums(meta, everyone, plan, outs, slots, unit, carried, name, after):
     clips, rank, total = everyone.shape
     label_width = 2 * HEAD_DIM
     units = len(plan)
     return call(
-        lambda m, *refs: late_sum_body(m, plan, slots, tuple(carried), *refs),
+        lambda m, *refs: slot_sum_body(m, plan, slots, tuple(carried), *refs),
         (1,),
         [IN_PLACE, whole((clips, rank, label_width), (0, 0, total // label_width - 1))]
         + [whole(array.shape) for array in carried.values()]
         + [IN_PLACE] * len(after),
         (IN_PLACE,) * len(outs),
-        tuple(shaped((stack, slots, rank, width), WIDE) for stack, width in outs),
+        tuple(
+            shaped((slots, rank, width) if stack is None else (stack, slots, rank, width), WIDE)
+            for stack, width in outs
+        ),
         [
             pltpu.VMEM((label_width, clips * rank), WIDE),
             pltpu.VMEM((units, clips, rank, unit), LOW),
@@ -881,72 +879,6 @@
     )
 
 
-def slot_sums(meta, everyone, plan, outs, slots, unit, name, after):
-    clips, rank, total = everyone.shape
-    steps = len(plan)
-
-    def place_of(which):
-        def place(t, m):
-            places = [(step, place) for step, (_, target, place) in enumerate(plan) if target == which]
-            value = jnp.int32(places[0][1])
-            for step, place in places:
-                value = jnp.where(t >= step, place, value)
-            return value
-
-        return place
-
-    out_specs = []
-    out_shapes = []
-    for which, (stack, width) in enumerate(outs):
-        place = place_of(which)
-        if stack is None:
-            out_specs.append(
-                pl.BlockSpec((slots, rank, unit), lambda t, m, place=place: (0, 0, place(t, m)))
-            )
-            out_shapes.append(shaped((slots, rank, width), WIDE))
-        else:
-            out_specs.append(
-                pl.BlockSpec((1, slots, rank, unit), lambda t, m, place=place: (place(t, m), 0, 0, 0))
-            )
-            out_shapes.append(shaped((stack, slots, rank, width), WIDE))
-    label_width = 2 * HEAD_DIM
-    return call(
-        lambda m, *refs: slot_sum_body(m, plan, slots, *refs),
-        (steps,),
-        [
-            pl.BlockSpec((clips, rank, unit), lambda t, m: (0, 0, t)),
-            whole((clips, rank, label_width), (0, 0, total // label_width - 1)),
-        ]
-        + [IN_PLACE] * len(after),
-        tuple(out_specs),
-        tuple(out_shapes),
-        [pltpu.VMEM((label_width, clips * rank), WIDE)],
-        0,
-        2 * everyone.size + 4 * slots * rank * total,
-        name,
-        (meta, everyone, everyone, *after),
-    )
-
-
-ROW_BLOCK = 512
-
-
-def order_frames(is_first, own, other, low_part, high_part):
-    @pl.when(is_first)
-    def _():
-        low_part[...] = own[...]
-        high_part[...] = other[...]
-
-    @pl.when(jnp.logical_not(is_first))
-    def _():
-        low_part[...] = other[...]
-        high_part[...] = own[...]
-
-
-def causal_spans(first):
-    return [(first, first + ROW_BLOCK)] + [(key, key + ROW_BLOCK) for key in range(0, first, ROW_BLOCK)]
-
-
 def causal_keep(rows):
     key_at = lax.broadcasted_iota(jnp.int32, (rows, rows), 0)
     return key_at <= lax.broadcasted_iota(jnp.int32, (rows, rows), 1)
@@ -956,73 +888,100 @@
     return rows.astype(WIDE).T.astype(LOW)
 
 
+def forward_block(query, keys, value_turned, diagonal, earlier=None):
+    score = mm_nt(keys, query)
+    if diagonal:
+        score = jnp.where(causal_keep(score.shape[0]), score, -1e30)
+    largest = jnp.max(score, axis=0, keepdims=True)
+    if earlier is not None:
+        largest = jnp.maximum(largest, earlier[0])
+    mixed = mm(value_turned, jnp.exp(score - largest).astype(LOW))
+    if earlier is not None:
+        mixed = mixed + earlier[1] * jnp.exp(earlier[0] - largest)
+    return largest, mixed
+
+
+def values_of(rows_ref):
+    values = turned(rows_ref[2])
+    ones = jnp.ones((RANK_UNIT, values.shape[1]), LOW)
+    return [
+        jnp.concatenate([values[HEAD_DIM * which : HEAD_DIM * (which + 1)], ones], axis=0)
+        for which in (0, 1)
+    ]
+
+
+def forward_finish(blocks, out_ref, log_ref):
+    mixes = []
+    totals = []
+    for largest, mixed in blocks:
+        summed = mixed[HEAD_DIM : HEAD_DIM + 1]
+        mixes.append(mixed[:HEAD_DIM] * (1.0 / summed))
+        totals.append(jnp.broadcast_to(jnp.log(summed) + largest, (HEAD_DIM, summed.shape[1])))
+    out_ref[...] = jnp.concatenate(mixes, axis=0).T.astype(LOW)
+    log_ref[...] = jnp.concatenate(totals, axis=0).T
+
+
+MIXED_ROWS = HEAD_DIM + RANK_UNIT
+PART_ROWS = MIXED_ROWS + 8
+
+
+def self_forward_own_body(_, own_ref, part_ref):
+    masks = half_masks()
+    query = own_ref[0] * jnp.asarray(HEAD_DIM**-0.5, LOW)
+    values = values_of(own_ref)
+    for which in (0, 1):
+        largest, mixed = forward_block(query * masks[which], own_ref[1], values[which], True)
+        part_ref[0, which, :MIXED_ROWS] = mixed
+        part_ref[0, which, MIXED_ROWS:] = jnp.broadcast_to(largest, (8, largest.shape[1]))
+
+
+def self_forward_own(meta, own, after):
+    _, half, local = own.shape
+    pair = 2 * HEAD_DIM
+    shape = (local // pair, 2, PART_ROWS, half)
+    return call(
+        lambda m, own_ref, after_ref, part_ref: self_forward_own_body(m, own_ref, part_ref),
+        (local // pair,),
+        [pl.BlockSpec((3, half, pair), lambda p, m: (0, 0, p)), IN_PLACE],
+        pl.BlockSpec((1,) + shape[1:], lambda p, m: (p, 0, 0, 0)),
+        shaped(shape, WIDE),
+        [],
+        4 * half * half * local,
+        10 * half * local,
+        "self_forward_own",
+        (meta, own, after),
+    )
+
+
 def self_forward_body(
-    meta,
-    own_ref,
-    other_ref,
-    out_own_ref,
-    out_other_ref,
-    log_own_ref,
-    log_other_ref,
-    held,
-    value_turned,
-    result,
-    logs,
+    meta, part_ref, own_ref, other_ref, out_own_ref, out_other_ref, log_own_ref, log_other_ref, keys, values, queries
 ):
-    half = own_ref.shape[1]
-    is_first = meta[10] == 0
-    order_frames(is_first, own_ref, other_ref, held.at[:, :half], held.at[:, half:])
+    side = meta[10]
     masks = half_masks()
-    keep = causal_keep(ROW_BLOCK)
-    for first in range(0, 2 * half, ROW_BLOCK):
-        span = slice(first, first + ROW_BLOCK)
-        values = turned(held[2, span])
-        for which in (0, 1):
-            value_turned[which, :HEAD_DIM, span] = values[HEAD_DIM * which : HEAD_DIM * (which + 1)]
-            value_turned[which, HEAD_DIM:, span] = jnp.ones((RANK_UNIT, ROW_BLOCK), LOW)
-    for first in range(0, 2 * half, ROW_BLOCK):
-        span = slice(first, first + ROW_BLOCK)
-        query = held[0, span] * jnp.asarray(HEAD_DIM**-0.5, LOW)
-        mixes = []
-        totals = []
-        for which in (0, 1):
-            one_query = query * masks[which]
-            largest = None
-            scores = []
-            for begin, end in causal_spans(first):
-                score = mm_nt(held[1, begin:end], one_query)
-                if begin == first:
-                    score = jnp.where(keep, score, -1e30)
-                top = jnp.max(score, axis=0, keepdims=True)
-                largest = top if largest is None else jnp.maximum(largest, top)
-                scores.append(score)
-            mixed = None
-            for (begin, end), score in zip(causal_spans(first), scores):
-                weights = jnp.exp(score - largest).astype(LOW)
-                part = mm(value_turned[which, :, begin:end], weights)
-                mixed = part if mixed is None else mixed + part
-            summed = mixed[HEAD_DIM : HEAD_DIM + 1]
-            mixes.append(mixed[:HEAD_DIM] * (1.0 / summed))
-            totals.append(jnp.broadcast_to(jnp.log(summed) + largest, (HEAD_DIM, ROW_BLOCK)))
-        result[span] = jnp.concatenate(mixes, axis=0).T.astype(LOW)
-        logs[span] = jnp.concatenate(totals, axis=0).T
-
-    @pl.when(is_first)
-    def _():
-        out_own_ref[...] = result[:half]
-        out_other_ref[...] = result[half:]
-        log_own_ref[...] = logs[:half]
-        log_other_ref[...] = logs[half:]
-
-    @pl.when(jnp.logical_not(is_first))
-    def _():
-        out_own_ref[...] = result[half:]
-        out_other_ref[...] = result[:half]
-        log_own_ref[...] = logs[half:]
-        log_other_ref[...] = logs[:half]
-
-
-def self_forward(meta, own, other):
+    for slot, ref in ((0, own_ref), (1, other_ref)):
+        keys[slot] = ref[1]
+        queries[slot] = ref[0] * jnp.asarray(HEAD_DIM**-0.5, LOW)
+        for which, value in enumerate(values_of(ref)):
+            values[slot, which] = value
+    blocks = []
+    for which in (0, 1):
+        own = (part_ref[0, which, MIXED_ROWS : MIXED_ROWS + 1], part_ref[0, which, :MIXED_ROWS])
+        other = forward_block(queries[1] * masks[which], keys[1], values[1, which], True)
+        earlier = (jnp.where(side == 0, other[0], own[0]), jnp.where(side == 0, other[1], own[1]))
+        later = forward_block(
+            queries[1 - side] * masks[which], keys[side], values[side, which], False, earlier
+        )
+        blocks.append(
+            (
+                (jnp.where(side == 0, own[0], later[0]), jnp.where(side == 0, own[1], later[1])),
+                (jnp.where(side == 0, later[0], other[0]), jnp.where(side == 0, later[1], other[1])),
+            )
+        )
+    forward_finish([blocks[0][0], blocks[1][0]], out_own_ref, log_own_ref)
+    forward_finish([blocks[0][1], blocks[1][1]], out_other_ref, log_other_ref)
+
+
+def self_forward(meta, part, own, other):
     _, half, local = own.shape
     pair = 2 * HEAD_DIM
     three = pl.BlockSpec((3, half, pair), lambda p, m: (0, 0, p))
@@ -1032,19 +991,18 @@
     return call(
         self_forward_body,
         (local // pair,),
-        [three, three],
+        [pl.BlockSpec((1,) + part.shape[1:], lambda p, m: (p, 0, 0, 0)), three, three],
         (one, one, one, one),
         (rows, rows, logs, logs),
         [
-            pltpu.VMEM((3, 2 * half, pair), LOW),
-            pltpu.VMEM((2, HEAD_DIM + RANK_UNIT, 2 * half), LOW),
-            pltpu.VMEM((2 * half, pair), LOW),
-            pltpu.VMEM((2 * half, pair), WIDE),
+            pltpu.VMEM((2, half, pair), LOW),
+            pltpu.VMEM((2, 2, MIXED_ROWS, half), LOW),
+            pltpu.VMEM((2, half, pair), LOW),
         ],
-        20 * half * half * local,
-        16 * half * local,
+        12 * half * half * local,
+        20 * half * local,
         "self_forward",
-        (meta, own, other),
+        (meta, part, own, other),
     )
 
 
@@ -1055,8 +1013,93 @@
     return high, middle, (rest - middle.astype(WIDE)).astype(LOW)
 
 
+def back_scratch(slots, half):
+    pair = 2 * HEAD_DIM
+    return [pltpu.VMEM((slots, pair, half), LOW)] * 3 + [pltpu.VMEM((slots, 2, half, pair), LOW)] * 4
+
+
+def back_prepare_keys(slot, rows_ref, scratch):
+    key_turned, _, _, _, key_wide, _, value_wide = scratch
+    lane = lax.broadcasted_iota(jnp.int32, (1, 2 * HEAD_DIM), 1)
+    key_turned[slot] = turned(rows_ref[1])
+    for which in (0, 1):
+        spare = HEAD_DIM * (1 - which)
+        marked = jnp.where((lane >= spare) & (lane < spare + 3), 1.0, 0.0).astype(LOW)
+        key_wide[slot, which] = rows_ref[1] * (1 - marked) + marked
+        value_wide[slot, which] = rows_ref[2] * (1 - marked) + marked
+
+
+def back_prepare_queries(slot, rows_ref, mixed_ref, logs_ref, grad_ref, scratch):
+    _, query_turned, grad_turned, query_wide, _, grad_wide, _ = scratch
+    masks = half_masks()
+    lane = lax.broadcasted_iota(jnp.int32, (1, 2 * HEAD_DIM), 1)
+    grad = grad_ref[...]
+    product = grad.astype(WIDE) * mixed_ref[...].astype(WIDE)
+    query = rows_ref[0] * jnp.asarray(HEAD_DIM**-0.5, LOW)
+    logs = logs_ref[...]
+    query_turned[slot] = turned(query)
+    grad_turned[slot] = turned(grad)
+    for which in (0, 1):
+        spare = HEAD_DIM * (1 - which)
+        marks = [jnp.where(lane == spare + i, 1.0, 0.0).astype(LOW) for i in range(3)]
+        inner = jnp.sum(product * masks[which].astype(WIDE), axis=-1, keepdims=True)
+        query_rows = query * masks[which]
+        for part, mark in zip(three_parts(logs[:, HEAD_DIM * which : HEAD_DIM * which + 1]), marks):
+            query_rows = query_rows - part * mark
+        query_wide[slot, which] = query_rows
+        grad_rows = grad * masks[which]
+        for part, mark in zip(three_parts(inner), marks):
+            grad_rows = grad_rows - part * mark
+        grad_wide[slot, which] = grad_rows
+
+
+def back_block(query_slot, key_slot, diagonal, scratch, totals):
+    key_turned, query_turned, grad_turned, query_wide, key_wide, grad_wide, value_wide = scratch
+    half = key_turned.shape[2]
+    for which in (0, 1):
+        head = slice(HEAD_DIM * which, HEAD_DIM * (which + 1))
+        score = mm_nt(key_wide[key_slot, which], query_wide[query_slot, which])
+        if diagonal:
+            score = jnp.where(causal_keep(half), score, -1e30)
+        prob = jnp.exp(score)
+        prob_grad = mm_nt(value_wide[key_slot, which], grad_wide[query_slot, which])
+        score_grad = (prob * prob_grad).astype(LOW)
+        totals[2, key_slot, head] += mm_nt(grad_turned[query_slot, head], prob.astype(LOW))
+        totals[1, key_slot, head] += mm_nt(query_turned[query_slot, head], score_grad)
+        totals[0, query_slot, head] += mm(key_turned[key_slot, head], score_grad)
+
+
+def self_back_own_body(_, own_ref, z_ref, log_ref, grad_ref, out_ref, *scratch):
+    totals = scratch[-1]
+    totals[...] = jnp.zeros_like(totals)
+    back_prepare_keys(0, own_ref, scratch[:-1])
+    back_prepare_queries(0, own_ref, z_ref, log_ref, grad_ref, scratch[:-1])
+    back_block(0, 0, True, scratch[:-1], totals)
+    out_ref[...] = totals[:, 0]
+
+
+def self_back_own(meta, own, z_own, log_own, grad_own):
+    _, half, local = own.shape
+    pair = 2 * HEAD_DIM
+    three = pl.BlockSpec((3, half, pair), lambda p, m: (0, 0, p))
+    one = pl.BlockSpec((half, pair), lambda p, m: (0, p))
+    return call(
+        self_back_own_body,
+        (local // pair,),
+        [three, one, one, one],
+        pl.BlockSpec((3, pair, half), lambda p, m: (0, p, 0)),
+        shaped((3, local, half), WIDE),
+        back_scratch(1, half) + [pltpu.VMEM((3, 1, pair, half), WIDE)],
+        100 * half * half * local,
+        24 * half * local,
+        "self_back_own",
+        (meta, own, z_own, log_own, grad_own),
+    )
+
+
 def self_back_body(
     meta,
+    part_ref,
     own_ref,
     other_ref,
     z_own_ref,
@@ -1068,117 +1111,50 @@
     _early,
     out_own_ref,
     out_other_ref,
-    held,
-    mixed,
-    logs,
-    grads,
-    key_turned,
-    query_turned,
-    grad_turned,
-    query_wide,
-    key_wide,
-    grad_wide,
-    value_wide,
-    key_total,
-    value_total,
-    result,
+    *scratch,
 ):
-    half = own_ref.shape[1]
-    is_first = meta[10] == 0
-    order_frames(is_first, own_ref, other_ref, held.at[:, :half], held.at[:, half:])
-    order_frames(is_first, grad_own_ref, grad_other_ref, grads.at[:half], grads.at[half:])
-    order_frames(is_first, z_own_ref, z_other_ref, mixed.at[:half], mixed.at[half:])
-    order_frames(is_first, log_own_ref, log_other_ref, logs.at[:half], logs.at[half:])
-    masks = half_masks()
-    scale = HEAD_DIM**-0.5
-    lane = lax.broadcasted_iota(jnp.int32, (1, 2 * HEAD_DIM), 1)
-    keep = causal_keep(ROW_BLOCK)
-    for first in range(0, 2 * half, ROW_BLOCK):
-        span = slice(first, first + ROW_BLOCK)
-        grad = grads[span]
-        product = grad.astype(WIDE) * mixed[span].astype(WIDE)
-        query = held[0, span] * jnp.asarray(scale, LOW)
-        key_turned[:, span] = turned(held[1, span])
-        query_turned[:, span] = turned(query)
-        grad_turned[:, span] = turned(grad)
-        for which in (0, 1):
-            spare = HEAD_DIM * (1 - which)
-            marks = [jnp.where(lane == spare + i, 1.0, 0.0).astype(LOW) for i in range(3)]
-            marked = marks[0] + marks[1] + marks[2]
-            others = 1 - marked
-            inner = jnp.sum(product * masks[which].astype(WIDE), axis=-1, keepdims=True)
-            log_column = logs[span][:, HEAD_DIM * which : HEAD_DIM * which + 1]
-            query_rows = query * masks[which]
-            for part, mark in zip(three_parts(log_column), marks):
-                query_rows = query_rows - part * mark
-            query_wide[which, span] = query_rows
-            grad_rows = grad * masks[which]
-            for part, mark in zip(three_parts(inner), marks):
-                grad_rows = grad_rows - part * mark
-            grad_wide[which, span] = grad_rows
-            key_wide[which, span] = held[1, span] * others + marked
-            value_wide[which, span] = held[2, span] * others + marked
-    key_total[...] = jnp.zeros_like(key_total)
-    value_total[...] = jnp.zeros_like(value_total)
-    for first in range(0, 2 * half, ROW_BLOCK):
-        span = slice(first, first + ROW_BLOCK)
-        query_grads = [None, None]
-        for begin, end in causal_spans(first):
-            for which in (0, 1):
-                head = slice(HEAD_DIM * which, HEAD_DIM * (which + 1))
-                score = mm_nt(key_wide[which, begin:end], query_wide[which, span])
-                if begin == first:
-                    score = jnp.where(keep, score, -1e30)
-                prob = jnp.exp(score)
-                prob_grad = mm_nt(value_wide[which, begin:end], grad_wide[which, span])
-                score_grad = (prob * prob_grad).astype(LOW)
-                value_total[head, begin:end] += mm_nt(grad_turned[head, span], prob.astype(LOW))
-                key_total[head, begin:end] += mm_nt(query_turned[head, span], score_grad)
-                part = mm(key_turned[head, begin:end], score_grad)
-                query_grads[which] = part if query_grads[which] is None else query_grads[which] + part
-        result[0, span] = (jnp.concatenate(query_grads, axis=0).T * scale).astype(LOW)
-    for first in range(0, 2 * half, ROW_BLOCK):
-        span = slice(first, first + ROW_BLOCK)
-        result[1, span] = key_total[:, span].T.astype(LOW)
-        result[2, span] = value_total[:, span].T.astype(LOW)
-
-    @pl.when(is_first)
+    totals = scratch[-1]
+    scratch = scratch[:-1]
+    side = meta[10]
+    totals[:, 0] = part_ref[...]
+    totals[:, 1] = jnp.zeros_like(totals[:, 1])
+
+    @pl.when(side == 0)
     def _():
-        out_own_ref[...] = result[:, :half]
-        out_other_ref[...] = result[:, half:]
-
-    @pl.when(jnp.logical_not(is_first))
+        back_prepare_keys(0, own_ref, scratch)
+
+    @pl.when(side != 0)
     def _():
-        out_own_ref[...] = result[:, half:]
-        out_other_ref[...] = result[:, :half]
-
-
-def self_back(meta, own, other, z_own, z_other, log_own, log_other, grad_own, grad_other, after):
+        back_prepare_queries(0, own_ref, z_own_ref, log_own_ref, grad_own_ref, scratch)
+
+    back_prepare_keys(1, other_ref, scratch)
+    back_prepare_queries(1, other_ref, z_other_ref, log_other_ref, grad_other_ref, scratch)
+    back_block(1, 1, True, scratch, totals)
+    back_block(1 - side, side, False, scratch, totals)
+    for slot, ref in ((0, out_own_ref), (1, out_other_ref)):
+        ref[0] = (totals[0, slot].T * HEAD_DIM**-0.5).astype(LOW)
+        ref[1] = totals[1, slot].T.astype(LOW)
+        ref[2] = totals[2, slot].T.astype(LOW)
+
+
+def self_back(meta, part, own, other, z_own, z_other, log_own, log_other, grad_own, grad_other, after):
     _, half, local = own.shape
     pair = 2 * HEAD_DIM
-    full = 2 * half
     three = pl.BlockSpec((3, half, pair), lambda p, m: (0, 0, p))
     one = pl.BlockSpec((half, pair), lambda p, m: (0, p))
     return call(
         self_back_body,
         (local // pair,),
-        [three, three] + [one] * 6 + [IN_PLACE] * len(after),
+        [pl.BlockSpec((3, pair, half), lambda p, m: (0, p, 0)), three, three]
+        + [one] * 6
+        + [IN_PLACE] * len(after),
         (three, three),
         (shaped(own.shape, LOW), shaped(own.shape, LOW)),
-        [
-            pltpu.VMEM((3, full, pair), LOW),
-            pltpu.VMEM((full, pair), LOW),
-            pltpu.VMEM((full, pair), WIDE),
-            pltpu.VMEM((full, pair), LOW),
-        ]
-        + [pltpu.VMEM((pair, full), LOW)] * 3
-        + [pltpu.VMEM((2, full, pair), LOW)] * 4
-        + [pltpu.VMEM((pair, full), WIDE)] * 2
-        + [pltpu.VMEM((3, full, pair), LOW)],
-        500 * half * half * local,
-        30 * half * local,
+        back_scratch(2, half) + [pltpu.VMEM((3, 2, pair, half), WIDE)],
+        200 * half * half * local,
+        40 * half * local,
         "self_back",
-        (meta, own, other, z_own, z_other, log_own, log_other, grad_own, grad_other, *after),
+        (meta, part, own, other, z_own, z_other, log_own, log_other, grad_own, grad_other, *after),
     )
 
 
@@ -1194,7 +1170,7 @@
     return ref[...].reshape(ref.shape[0] * ref.shape[1], ref.shape[2])
 
 
-def fetch_weights(step, order, sources, gathered, held, sems):
+def fetch_weights(step, order, sources, gathered, held, sems, between=()):
     copies = {}
     for which in order:
         copies[which] = (
@@ -1204,8 +1180,10 @@
 
     @pl.when(step == 0)
     def _():
-        for which in order:
+        for place, which in enumerate(order):
             for copy in copies[which]:
+                copy.start()
+            for copy in between[place] if between else ():
                 copy.start()
 
     def ready(which):
@@ -1219,19 +1197,28 @@
     return ready
 
 
-def pair_tiles(keys, values, pair, masks):
-    span = slice(2 * HEAD_DIM * pair, 2 * HEAD_DIM * (pair + 1))
-    key_part = keys[:, span]
-    value_part = values[:, span]
-    key_tile = jnp.concatenate([key_part * masks[0], key_part * masks[1]], axis=0)
-    value_tile = jnp.concatenate([value_part * masks[0], value_part * masks[1]], axis=0)
-    return key_tile, value_tile
+TILE_HEADS = 4
+
+
+def tile_span(tile):
+    return slice(TILE_HEADS * HEAD_DIM * tile, TILE_HEADS * HEAD_DIM * (tile + 1))
+
+
+def tile_masks():
+    lane = lax.broadcasted_iota(jnp.int32, (1, TILE_HEADS * HEAD_DIM), 1)
+    return [jnp.where(lane // HEAD_DIM == head, 1.0, 0.0).astype(LOW) for head in range(TILE_HEADS)]
+
+
+def text_tile(rows, tile, masks):
+    part = rows[:, tile_span(tile)]
+    return jnp.concatenate([part * mask for mask in masks], axis=0)
 
 
 def by_head(values, reduce):
     keys, rows = values.shape
-    reduced = reduce(values.reshape(2, keys // 2, rows), axis=1, keepdims=True)
-    return jnp.broadcast_to(reduced, (2, keys // 2, rows)).reshape(keys, rows)
+    apart = values.reshape(TILE_HEADS, keys // TILE_HEADS, rows)
+    reduced = reduce(apart, axis=1, keepdims=True)
+    return jnp.broadcast_to(reduced, apart.shape).reshape(keys, rows)
 
 
 def text_weights(key_tile, query):
@@ -1240,13 +1227,13 @@
     return weights * (1.0 / by_head(weights, jnp.sum))
 
 
-def mix_text(query, keys, values, masks):
+def mix_text(query, keys, values):
+    masks = tile_masks()
     mixed = []
-    for pair in range(query.shape[1] // (2 * HEAD_DIM)):
-        key_tile, value_tile = pair_tiles(keys, values, pair, masks)
-        one_query = query[:, 2 * HEAD_DIM * pair : 2 * HEAD_DIM * (pair + 1)]
-        weights = text_weights(key_tile, one_query * jnp.asarray(HEAD_DIM**-0.5, LOW))
-        mixed.append(mm_tn(weights.astype(LOW), value_tile).astype(LOW))
+    for tile in range(query.shape[1] // (TILE_HEADS * HEAD_DIM)):
+        one_query = query[:, tile_span(tile)] * jnp.asarray(HEAD_DIM**-0.5, LOW)
+        weights = text_weights(text_tile(keys, tile, masks), one_query)
+        mixed.append(mm_tn(weights.astype(LOW), text_tile(values, tile, masks)).astype(LOW))
     return jnp.concatenate(mixed, axis=1)
 
 
@@ -1282,7 +1269,6 @@
     *scratch,
 ):
     local = z_own_ref.shape[1]
-    masks = half_masks()
     ready = fetch_weights(
         pl.program_id(0),
         (0, 1, 2),
@@ -1317,8 +1303,8 @@
     ).astype(LOW)
     query_out_own_ref[...] = query_own
     query_out_other_ref[...] = query_other
-    z2_own = mix_text(query_own, text_own_ref[0], text_own_ref[1], masks)
-    z2_other = mix_text(query_other, text_other_ref[0], text_other_ref[1], masks)
+    z2_own = mix_text(query_own, text_own_ref[0], text_own_ref[1])
+    z2_other = mix_text(query_other, text_other_ref[0], text_other_ref[1])
     z2_own_ref[...] = z2_own
     z2_other_ref[...] = z2_other
     stream = stream + out_product(
@@ -1384,7 +1370,7 @@
 def middle_forward(meta, x, z_own, z_other, weights, gathered, tables, packed, text_own, text_other, gains):
     frames, width = x.shape
     local = z_own.shape[1]
-    block = min(256, frames)
+    block = min(512, frames)
     wide = pl.BlockSpec((block, width), lambda t, m: (t, 0))
     narrow = pl.BlockSpec((block, local), lambda t, m: (t, 0))
     specs, args = middle_specs(weights, gathered, tables, packed)
@@ -1439,6 +1425,13 @@
     text_own_ref,
     text_other_ref,
     gain_two_ref,
+    text_ref,
+    down5_ref,
+    down6_ref,
+    up5_ref,
+    up6_ref,
+    up5_other_ref,
+    up6_other_ref,
     grad_one_ref,
     dz_own_ref,
     dz_other_ref,
@@ -1446,6 +1439,8 @@
     text_grad_other_ref,
     mine_ref,
     theirs_ref,
+    text_mine_ref,
+    text_theirs_ref,
     key_total,
     value_total,
     ga3_ref,
@@ -1457,6 +1452,16 @@
     *scratch,
 ):
     step = pl.program_id(0)
+    late = scratch[7:12]
+    late_sems = scratch[13]
+    late_copies = [
+        pltpu.make_async_copy(source, target, late_sems.at[number])
+        for number, (source, target) in enumerate(
+            zip((query_in_own_ref, query_in_other_ref, stream_one_ref, z_own_ref, z_other_ref), late)
+        )
+    ]
+    query_in_own_ref, query_in_other_ref, stream_one_ref, z_own_ref, z_other_ref = late
+    grad_one_copy = pltpu.make_async_copy(scratch[12], grad_one_ref, late_sems.at[5])
     ready = fetch_weights(
         step,
         (2, 1, 0),
@@ -1464,11 +1469,11 @@
         gathered_ref,
         scratch[:6],
         scratch[6],
+        (late_copies[:2], late_copies[2:], ()),
     )
     local = z_own_ref.shape[1]
-    pairs = local // (2 * HEAD_DIM)
-    left = lane_halves()
-    masks = half_masks()
+    tiles = local // (TILE_HEADS * HEAD_DIM)
+    masks = tile_masks()
     scale = jnp.asarray(HEAD_DIM**-0.5, LOW)
 
     @pl.when(step == 0)
@@ -1510,23 +1515,27 @@
 
     def text_back(query, dz2, keys, values, part):
         query_grads = []
-        for pair in range(pairs):
-            span = slice(2 * HEAD_DIM * pair, 2 * HEAD_DIM * (pair + 1))
-            key_tile, value_tile = pair_tiles(keys, values, pair, masks)
-            one_query = query[:, span] * scale
-            one_grad = dz2[:, span]
+        for tile in range(tiles):
+            key_tile = text_tile(keys, tile, masks)
+            value_tile = text_tile(values, tile, masks)
+            one_query = query[:, tile_span(tile)] * scale
+            one_grad = dz2[:, tile_span(tile)]
             probs = text_weights(key_tile, one_query)
             prob_grads = mm_nt(value_tile, one_grad)
             inner = by_head(probs * prob_grads, jnp.sum)
             score_grads = (probs * (prob_grads - inner)).astype(LOW)
             query_grads.append((mm_tn(score_grads, key_tile) * HEAD_DIM**-0.5).astype(LOW))
-            key_total[part, pair] += mm(score_grads, one_query)
-            value_total[part, pair] += mm(probs.astype(LOW), one_grad)
+            key_total[part, tile] += mm(score_grads, one_query)
+            value_total[part, tile] += mm(probs.astype(LOW), one_grad)
         return jnp.concatenate(query_grads, axis=1)
 
+    for copy in late_copies[:2]:
+        copy.wait()
     dq_own = text_back(query_in_own_ref[...], dz2_own, text_own_ref[0], text_own_ref[1], 0)
     dq_other = text_back(query_in_other_ref[...], dz2_other, text_other_ref[0], text_other_ref[1], 1)
 
+    for copy in late_copies[2:]:
+        copy.wait()
     rows_two, normed, inverse = norm_rows(stream_one_ref[...], gain_two_ref[...])
     rows_two = rows_two.astype(LOW)
     rank = low_rank(down4_ref[0, 0], rows_two)
@@ -1541,7 +1550,8 @@
         + mm_tn(grad_rank, down4_ref[0, 0])
     )
     grad = grad + norm_back(grad_rows, gain_two_ref[...], normed, inverse)
-    grad_one_ref[...] = grad
+    scratch[12][...] = grad
+    grad_one_copy.start()
     dz_own, dz_other = out_back(
         grad.astype(LOW),
         z_own_ref[...],
@@ -1555,6 +1565,7 @@
     )
     dz_own_ref[...] = dz_own
     dz_other_ref[...] = dz_other
+    grad_one_copy.wait()
 
     @pl.when(step == last)
     def _():
@@ -1566,31 +1577,52 @@
         split_columns(meta, mine_ref, theirs_ref, 5 * local, gb7_ref)
         for total, slot in ((key_total, 0), (value_total, 1)):
             for part, ref in ((0, text_grad_own_ref), (1, text_grad_other_ref)):
-                for pair in range(pairs):
-                    span = slice(2 * HEAD_DIM * pair, 2 * HEAD_DIM * (pair + 1))
-                    tile = total[part, pair]
-                    ref[slot, :, span] = jnp.where(left, tile[:HEAD_DIM], tile[HEAD_DIM:]).astype(ref.dtype)
+                for tile in range(tiles):
+                    stacked = total[part, tile]
+                    rows = 0.0
+                    for head, mask in enumerate(masks):
+                        rows = rows + stacked[HEAD_DIM * head : HEAD_DIM * (head + 1)] * mask.astype(WIDE)
+                    ref[slot, :, tile_span(tile)] = rows.astype(ref.dtype)
+        text = text_ref[...]
+        factors = ((down5_ref, up5_ref, up5_other_ref), (down6_ref, up6_ref, up6_other_ref))
+        for slot, (down_ref, up_ref, up_other_ref) in enumerate(factors):
+            grad_own = text_grad_own_ref[slot].astype(LOW)
+            grad_other = text_grad_other_ref[slot]
+            rank = low_rank(down_ref[0, 0], text)
+            grad_rank = mm_nt(up_ref[0, 0], grad_own) + mm_nt(up_other_ref[...], grad_other)
+            ga4_ref[...] = mm(grad_rank.astype(LOW), text)
+            split_columns(meta, text_mine_ref, text_theirs_ref, slot * local, ga4_ref)
+            span = slice((2 + slot) * local, (3 + slot) * local)
+            text_mine_ref[:, span] = mm(rank, grad_own)
+            text_theirs_ref[:, span] = mm(rank, grad_other).astype(LOW)
 
 
 def middle_back(
     meta, grad, stream_one, z_own, z_other, q_own, q_other, z2_own, z2_other,
-    weights, gathered, tables, packed, text_own, text_other, gain,
+    weights, gathered, tables, packed, text_own, text_other, gain, text,
 ):
     frames, width = grad.shape
     local = z_own.shape[1]
-    pairs = local // (2 * HEAD_DIM)
-    block = min(256, frames)
-    wide = pl.BlockSpec((block, width), lambda t, m: (t, 0))
-    narrow = pl.BlockSpec((block, local), lambda t, m: (t, 0))
+    tiles = local // (TILE_HEADS * HEAD_DIM)
+    wide = whole((frames, width))
+    narrow = whole((frames, local))
     specs, args = middle_specs(weights, gathered, tables, packed)
     rank = (RANK_UNIT, width)
     packs = (RANK_UNIT, 6 * local)
-    steps = frames // block
+    text_packs = (RANK_UNIT, 4 * local)
+    _, _, cross_down, cross_up = tables
     return call(
-        lambda m, *refs: middle_back_body(m, steps - 1, *refs),
-        (steps,),
-        [wide, wide] + [narrow] * 6 + specs + [whole(text_own.shape), whole(text_other.shape), whole((1, width))],
-        (wide, narrow, narrow, whole(text_own.shape), whole(text_own.shape), whole(packs), whole(packs)),
+        lambda m, *refs: middle_back_body(m, 0, *refs),
+        (1,),
+        [wide, IN_PLACE]
+        + [IN_PLACE] * 4
+        + [narrow] * 2
+        + specs
+        + [whole(text_own.shape), whole(text_other.shape), whole((1, width)), whole(text.shape)]
+        + [chosen(cross_down, 1, 5), chosen(cross_down, 2, 6), chosen(cross_up, 1, 5), chosen(cross_up, 2, 6)]
+        + [whole((RANK_UNIT, local), (0, 3)), whole((RANK_UNIT, local), (0, 4))],
+        (IN_PLACE, narrow, narrow, whole(text_own.shape), whole(text_own.shape))
+        + (whole(packs), whole(packs), whole(text_packs), whole(text_packs)),
         (
             shaped((frames, width), WIDE),
             shaped((frames, local), LOW),
@@ -1599,19 +1631,26 @@
             shaped(text_own.shape, LOW),
             shaped(packs, WIDE),
             shaped(packs, LOW),
+            shaped(text_packs, WIDE),
+            shaped(text_packs, LOW),
         ),
         [
-            pltpu.VMEM((2, pairs, 2 * HEAD_DIM, 2 * HEAD_DIM), WIDE),
-            pltpu.VMEM((2, pairs, 2 * HEAD_DIM, 2 * HEAD_DIM), WIDE),
+            pltpu.VMEM((2, tiles, TILE_HEADS * HEAD_DIM, TILE_HEADS * HEAD_DIM), WIDE),
+            pltpu.VMEM((2, tiles, TILE_HEADS * HEAD_DIM, TILE_HEADS * HEAD_DIM), WIDE),
         ]
         + [pltpu.VMEM(rank, WIDE)] * 6
-        + middle_scratch(weights, gathered),
+        + middle_scratch(weights, gathered)
+        + [pltpu.VMEM((frames, local), LOW)] * 2
+        + [pltpu.VMEM((frames, width), WIDE)]
+        + [pltpu.VMEM((frames, local), LOW)] * 2
+        + [pltpu.VMEM((frames, width), WIDE), pltpu.SemaphoreType.DMA((6,))],
         6 * frames * width * width,
         6 * width * width + 24 * frames * width,
         "middle_back",
         (meta, grad, stream_one, z_own, z_other, q_own, q_other, z2_own, z2_other)
         + args
-        + (text_own, text_other, gain),
+        + (text_own, text_other, gain, text)
+        + (cross_down, cross_down, cross_up, cross_up, packed, packed),
     )
 
 
@@ -1621,27 +1660,27 @@
 ):
     frames = rows_ref.shape[0]
     block = min(256, frames)
-    ga9 = None
-    gb8 = None
+    low_pre = mm_tn(rank8[...], up_rank)
+    low_grad = mm_tn(grad_rank9[...], down_rank)
+    hidden_blocks = []
+    grad_blocks = []
     for first in range(0, frames, block):
         span = slice(first, first + block)
-        rows = rows_ref[span]
-        cot = cot_ref[span]
-        pre = mm(rows, up_weight) + mm_tn(rank8[:, span], up_rank)
-        grad_hidden = mm_nt(cot, down_weight) + mm_tn(grad_rank9[:, span], down_rank)
+        pre = mm(rows_ref[span], up_weight) + low_pre[span]
+        grad_hidden = mm_nt(cot_ref[span], down_weight) + low_grad[span]
         hidden, slope = gelu_parts(pre)
         hidden = hidden.astype(LOW)
         grad_pre = (grad_hidden * slope).astype(LOW)
         branch[span] += mm(hidden, down_weight)
-        rank9[:, span] += mm_nt(down_rank, hidden)
         grad_rows[span] += mm_nt(grad_pre, up_weight)
-        grad_rank8[:, span] += mm_nt(up_rank, grad_pre)
-        one = mm(grad_rank9[:, span], hidden)
-        two = mm(rank8[:, span], grad_pre)
-        ga9 = one if ga9 is None else ga9 + one
-        gb8 = two if gb8 is None else gb8 + two
-    ga9_ref[...] = ga9.astype(ga9_ref.dtype)
-    gb8_ref[...] = gb8.astype(gb8_ref.dtype)
+        hidden_blocks.append(hidden)
+        grad_blocks.append(grad_pre)
+    hidden = jnp.concatenate(hidden_blocks, axis=0)
+    grad_pre = jnp.concatenate(grad_blocks, axis=0)
+    rank9[...] += mm_nt(down_rank, hidden)
+    grad_rank8[...] += mm_nt(up_rank, grad_pre)
+    ga9_ref[...] = mm(grad_rank9[...], hidden).astype(ga9_ref.dtype)
+    gb8_ref[...] = mm(rank8[...], grad_pre).astype(gb8_ref.dtype)
 
 
 def feed_own_body(
@@ -1853,7 +1892,6 @@
         16 * x.size,
         "last_norm",
         (meta, x, own, other, grad, gain, after),
-        vmem=VMEM_BYTES // 2,
     )
 
 
@@ -1915,9 +1953,9 @@
     query_share = share(cross_query_weight, depth)
     cross_share = side_by_side(share(cross_output_weight, step), 2).reshape(depth, local)
     share_one = swap(jnp.stack([out_share, query_share, cross_share]))
+    rows_one = first_norm(meta, x, gain_one)
+    share_one, rows_one = lax.optimization_barrier((share_one, rows_one))
     gathered_one = lax.all_gather(share_one, "dp", axis=0)
-
-    rows_one = first_norm(meta, x, gain_one)
     rows_one_other = swap(rows_one)
     factors = picked_factors(
         meta,
@@ -1925,29 +1963,31 @@
             (attention_first_factors, 0, 3),
             (attention_first_factors, 1, 7),
             (cross_second_factors, 0, 4),
-            (cross_second_factors, 0, 4),
+            (cross_second_factors, 1, 5),
+            (cross_second_factors, 2, 6),
             (input_second_factors, None, 8),
             (output_first_factors, None, 9),
         ],
     )
     packed = swap(factors)
-    first_pack = 4 * local
+    first_pack = 5 * local
 
     heads_own = project_heads(
         meta, rows_one, self_query_key_value_weight, self_first_factors, self_second_factors, 0, 0, "own_heads"
     )
+    part_own = self_forward_own(meta, heads_own, factors)
     text_own = project_heads(
         meta, text, cross_key_value_weight, cross_first_factors, cross_second_factors, 5, 1, "text_heads"
     )
     text_other = swap(text_own)
     share_two = feed_share(
-        meta, down_weight, up_weight, depth, (heads_own, text_own, rows_one_other, factors)
+        meta, down_weight, up_weight, depth, (part_own, text_own, rows_one_other)
     )
     heads_other = project_heads(
         meta, rows_one_other, self_query_key_value_weight, self_first_factors, self_second_factors,
         0, 0, "other_heads", (share_two,),
     )
-    z_own_frames, z_other_frames, log_own, log_other = self_forward(meta, heads_own, heads_other)
+    z_own_frames, z_other_frames, log_own, log_other = self_forward(meta, part_own, heads_own, heads_other)
     share_two, z_other_frames = lax.optimization_barrier((swap(share_two), z_other_frames))
     gathered_two = lax.all_gather(share_two, "dp", axis=0)
     z_other_heads = swap(z_other_frames)
@@ -1972,22 +2012,25 @@
     feed_received = swap(feed_theirs)
 
     (
-        grad_one, dz_own_heads, dz_other_heads, text_grad_own, text_grad_other, mine, theirs,
+        grad_one, dz_own_heads, dz_other_heads, text_grad_own, text_grad_other, middle_mine, middle_theirs,
+        text_mine_rank, text_theirs_rank,
     ) = middle_back(
         meta, grad_two, stream_one, z_own_frames, z_other_heads, q_own, q_other, z2_own, z2_other,
-        weights, gathered_one, tables, packed, text_own, text_other, gain_two,
-    )
-    gb8_received, ga9_received, feed_received, dz_other_heads, theirs, text_grad_other = lax.optimization_barrier(
-        (gb8_received, ga9_received, feed_received, dz_other_heads, theirs, text_grad_other)
-    )
-    dz_other_frames = swap(dz_other_heads)
+        weights, gathered_one, tables, packed, text_own, text_other, gain_two, text,
+    )
+    gb8_received, ga9_received, feed_received, dz_other_heads = lax.optimization_barrier(
+        (gb8_received, ga9_received, feed_received, dz_other_heads)
+    )
+    dz_other_frames, text_theirs_rank, text_grad_other = lax.optimization_barrier(
+        (swap(dz_other_heads), text_theirs_rank, text_grad_other)
+    )
 
     unit = local
     hidden_units = hidden // unit
     labels = jnp.zeros((RANK_UNIT, 2 * HEAD_DIM), LOW).at[:, : picks.shape[0]].set(picks.astype(LOW)[None])
     early = jnp.concatenate(
         [
-            join(mine, [swap(theirs)]),
+            join(middle_mine, [swap(middle_theirs)]),
             join(feed_mine, [feed_received]),
             join(jnp.concatenate([gb8_own, ga9_own], axis=1), [gb8_received, ga9_received]),
             labels,
@@ -1995,16 +2038,15 @@
         axis=1,
     )
     early_all = lax.all_gather(early, "dp", axis=0)
+    grads_part = self_back_own(meta, heads_own, z_own_frames, log_own, dz_own_heads)
     grads_own, grads_other = self_back(
-        meta, heads_own, heads_other, z_own_frames, z_other_frames, log_own, log_other,
+        meta, grads_part, heads_own, heads_other, z_own_frames, z_other_frames, log_own, log_other,
         dz_own_heads, dz_other_frames, (early,),
     )
-    text_grad_other, grads_own = lax.optimization_barrier((swap(text_grad_other), grads_own))
+    text_grad_other, text_received_rank, grads_own = lax.optimization_barrier(
+        (swap(text_grad_other), swap(text_theirs_rank), grads_own)
+    )
     text_heads_grad = (text_grad_own + text_grad_other.astype(WIDE)).astype(LOW)
-    text_mine_rank, text_theirs_rank = rank_grads(
-        meta, [text], [text_heads_grad], cross_first_factors, cross_second_factors, 5, 1, "text_ranks"
-    )
-    text_theirs_rank = swap(text_theirs_rank)
     mine, theirs = rank_grads(
         meta, [rows_one, rows_one_other], [grads_own, grads_other], self_first_factors,
         self_second_factors, 0, 0, "self_ranks",
@@ -2013,12 +2055,12 @@
         meta, grads_other, self_query_key_value_weight, self_first_factors, self_second_factors,
         0, 0, LOW, "other_back", theirs,
     )
+    received = swap(partial_other)
     labels = lax.dynamic_index_in_dim(early_all[:, :, -2 * HEAD_DIM :], place, axis=0, keepdims=False)
     late = jnp.concatenate(
-        [join(mine, [swap(theirs)]), join(text_mine_rank, [text_theirs_rank]), labels], axis=1
+        [join(mine, [swap(theirs)]), join(text_mine_rank, [text_received_rank]), labels], axis=1
     )
     late_all = lax.all_gather(late, "dp", axis=0)
-    received = swap(partial_other)
     text_rows = project_back_heads(
         meta, text_heads_grad, cross_key_value_weight, cross_first_factors, cross_second_factors,
         5, 1, WIDE, "text_back", partial_other,
@@ -2031,25 +2073,25 @@
         meta, grads_own, self_query_key_value_weight, self_first_factors, self_second_factors,
         0, 0, WIDE, "own_back", late,
     )
-    sums = slot_sums(
+    sum_query_a, sum_query_b, sum_out_a, sum_out_b, sum_up_a, sum_down_b, sum_up_b, sum_down_a = slot_sums(
         meta,
         early_all,
         [(4, 0, 0), (4, 1, 0), (3, 2, 0), (7, 2, 1), (3, 3, 0), (7, 3, 1), (8, 4, 0), (9, 5, 0)]
         + [(8, 6, i) for i in range(hidden_units)]
         + [(9, 7, i) for i in range(hidden_units)],
         [(1, unit), (1, unit), (2, unit), (2, unit), (None, unit), (None, unit), (None, hidden), (None, hidden)],
-        slots, unit, "early_slots", (partial_own,),
-    )
-    sum_cross_a, sum_cross_b, sum_out_a, sum_out_b, sum_up_a, sum_down_b, sum_up_b, sum_down_a = sums
-    received, text_received, sum_cross_a = lax.optimization_barrier((received, text_received, sum_cross_a))
+        slots, unit, {}, "early_slots", (partial_own,),
+    )
+    received, text_received, sum_up_a = lax.optimization_barrier((received, text_received, sum_up_a))
     text_grad = text_mine + text_received.astype(WIDE)
-    input_grad = last_norm(meta, x, partial_own, received, grad_one, gain_one, sum_cross_a)
-    sum_self_a, sum_self_b, sum_cross_a, sum_cross_b = late_sums(
-        meta, late_all,
+    input_grad = last_norm(meta, x, partial_own, received, grad_one, gain_one, sum_up_a)
+    sum_self_a, sum_self_b, sum_cross_a, sum_cross_b = slot_sums(
+        meta,
+        late_all,
         [(0, 0, 0), (1, 0, 1), (2, 0, 2), (0, 1, 0), (1, 1, 1), (2, 1, 2)]
         + [(5, 2, 1), (6, 2, 2), (5, 3, 1), (6, 3, 2)],
-        [(3, unit), (3, unit), (3, unit), (3, unit)], slots, unit,
-        {2: sum_cross_a, 3: sum_cross_b}, "late_slots", (input_grad,),
+        [(3, unit), (3, unit), (3, unit), (3, unit)],
+        slots, unit, {2: sum_query_a, 3: sum_query_b}, "late_slots", (input_grad,),
     )
     return (
         output[None],

time: 427 us -> 407 us (0.953)
  Pallas kernels: 288 us -> 276 us
  waiting for transfers between devices: 78.3 us -> 70.8 us
    ppermute x16, waiting for transfers between devices: 71.5 us -> 56.7 us  [swap(): return lax.ppermute(array, 'tensor', [(0, 1), (1, 0)])]
    pallas_call x20 -> x21, Pallas kernels: 288 us -> 276 us  [call(): pl.pallas_call(body, grid_spec=pltpu.PrefetchScalarGridSpec(num_scalar_pr...]
    all_gather x1, waiting for transfers between devices: 6.72 us -> 13.9 us  [on_pair(): gathered_two = lax.all_gather(share_two, 'dp', axis=0)]
  transfers between devices with their start and end apart: 20 -> 20, of which waited for: 8 -> 9; matrix products, arithmetic and copies ran while one was open for 2% -> 2% of each run, Pallas kernels for 58% -> 58%
where the time goes in v3:
time: 407 us; the launch traced here: 401 us
  Pallas kernels  276 us (68%)
  waiting for transfers between devices  70.8 us (17%)
  starting transfers between devices  21.6 us (5%)
  between operations  14.5 us (4%)
  local copies, waits for them, and re-layouts  9.77 us (2%)
  other arithmetic  8.18 us (2%)
    pallas_call x21, Pallas kernels, call(): pl.pallas_call(body, grid_spec=pltpu.PrefetchScalarGridSpec(num_scalar_pr...  276 us
    ppermute x16, waiting for transfers between devices, swap(): return lax.ppermute(array, 'tensor', [(0, 1), (1, 0)])  56.7 us
    ppermute x16, starting transfers between devices, swap(): return lax.ppermute(array, 'tensor', [(0, 1), (1, 0)])  21.5 us
    all_gather x1, waiting for transfers between devices, on_pair(): gathered_two = lax.all_gather(share_two, 'dp', axis=0)  13.9 us
  transfers between devices with their start and end apart: 20, of which 9 were waited for; matrix products, arithmetic and copies ran while one was open for 2% of the time, Pallas kernels for 58%

profile of v3, /device:TPU:0, one launch (start us, length us, event | category | flops | bytes accessed | tf_op | source)
XLA Modules:
  0.0 400.9 jit_solution(2111975435737403053)
XLA Ops:
  17.3 5.3 %collective-permute-done = bf16[3,96,768]{2,1,0:T(8,128)(2,1)S(1)} collective-permute-done((bf16[3,96,768]{2,1,0:T(8,128)(2,1)S(1)}, bf16[3,96,768]{2,1,0:T(8,128)(2,1)S(1)}, u32[]{:S(2)}, u32[]{:S(2)}) %collective-permute-start) | collective-permute-done | bytes 442400 | tf_op jit(solution)/shard_map/ppermute | solution.py:1941
  27.7 4.8 %text_heads.1.refs_3_.text_own_ref.refs_21_ = bf16[2,64,768]{2,1,0:T(8,128)(2,1)} custom-call(s32[12]{0:T(128)} %pad_add_fusion._.m.meta, bf16[64,1536]{1,0:T(8,128)(2,1)} %bitcast.35, bf16[2,1536,768]{2,1,0:T(8,128)(2,1)} %refs_1_.9, bf16[3,8,16,1536]{3,2,1,0:T(8,128)(2,1)} %refs_2_.7, bf16[3,8,16,768]{3,2,1,0:T(8,128)(2,1)} %refs_3_.7), custom_call_target="tpu_custom_call" | custom-call | flops 301989888 | bytes 5111808 | tf_op jit(solution)/shard_map/text_heads/pallas_call | solution.py:515
  32.4 10.6 %own_heads.1.own_ref = bf16[3,512,768]{2,1,0:T(8,128)(2,1)} custom-call(s32[12]{0:T(128)} %pad_add_fusion._.m.meta, bf16[512,1536]{1,0:T(8,128)(2,1)} %first_norm.1.act_ref.refs_0_, bf16[3,1536,768]{2,1,0:T(8,128)(2,1)} %refs_1_.8, bf16[3,8,16,1536]{3,2,1,0:T(8,128)(2,1)} %refs_2_.6, bf16[3,8,16,768]{3,2,1,0:T(8,128)(2,1)} %refs_3_.6), custom_call_target="tpu_custom_call" | custom-call | flops 3623878656 | bytes 11010048 | tf_op jit(solution)/shard_map/own_heads/pallas_call | solution.py:515
  43.0 8.5 %self_forward_own.1.refs_2_.part_ref = f32[6,2,88,512]{3,2,1,0:T(8,128)} custom-call(s32[12]{0:T(128)} %pad_add_fusion._.m.meta, bf16[3,512,768]{2,1,0:T(8,128)(2,1)} %own_heads.1.own_ref, bf16[16,9984]{1,0:T(8,128)(2,1)} %picked_factors.1.after_ref), custom_call_target="tpu_custom_call" | custom-call | flops 805306368 | bytes 3932160 | tf_op jit(solution)/shard_map/self_forward_own/pallas_call | solution.py:515
  51.5 7.7 %collective-permute-done.1.refs_4_.act_ref.refs_1_ = bf16[512,1536]{1,0:T(8,128)(2,1)S(1)} collective-permute-done((bf16[512,1536]{1,0:T(8,128)(2,1)}, bf16[512,1536]{1,0:T(8,128)(2,1)S(1)}, u32[]{:S(2)}, u32[]{:S(2)}) %collective-permute-start.1) | collective-permute-done | bytes 1572896 | tf_op jit(solution)/shard_map/ppermute | solution.py:1941
  66.1 10.5 %other_heads.1.other_ref = bf16[3,512,768]{2,1,0:T(8,128)(2,1)} custom-call(s32[12]{0:T(128)} %pad_add_fusion._.m.meta, bf16[512,1536]{1,0:T(8,128)(2,1)} %copy-done, bf16[3,1536,768]{2,1,0:T(8,128)(2,1)} %refs_1_.8, bf16[3,8,16,1536]{3,2,1,0:T(8,128)(2,1)} %refs_2_.6, bf16[3,8,16,768]{3,2,1,0:T(8,128)(2,1)} %refs_3_.6, bf16[4,96,1536]{2,1,0:T(8,128)(2,1)} %feed_share.1.refs_0_), custom_call_target="tpu_custom_call" | custom-call | flops 3623878656 | bytes 11010048 | tf_op jit(solution)/shard_map/other_heads/pallas_call | solution.py:515
  76.6 15.9 %self_forward.1 = (bf16[512,768]{1,0:T(8,128)(2,1)}, bf16[512,768]{1,0:T(8,128)(2,1)}, f32[512,768]{1,0:T(8,128)}, f32[512,768]{1,0:T(8,128)}) custom-call(s32[12]{0:T(128)} %pad_add_fusion._.m.meta, f32[6,2,88,512]{3,2,1,0:T(8,128)} %self_forward_own.1.refs_2_.part_ref, bf16[3,512,768]{2,1,0:T(8,128)(2,1)} %own_heads.1.own_ref, ...), custom_call_target="tpu_custom_call" | custom-call | flops 2415919104 | bytes 7864320 | tf_op jit(solution)/shard_map/self_forward/pallas_call | solution.py:515
  98.8 19.7 %collective-permute-done.5.text_other_ref.refs_22_ = bf16[2,64,768]{2,1,0:T(8,128)(2,1)S(1)} collective-permute-done((bf16[2,64,768]{2,1,0:T(8,128)(2,1)S(1)}, bf16[2,64,768]{2,1,0:T(8,128)(2,1)S(1)}, u32[]{:S(2)}, u32[]{:S(2)}) %collective-permute-start.5) | collective-permute-done | bytes 196640 | tf_op jit(solution)/shard_map/ppermute | solution.py:1941
  122.9 23.6 %middle_forward.1 = (f32[512,1536]{1,0:T(8,128)}, f32[512,1536]{1,0:T(8,128)}, bf16[512,1536]{1,0:T(8,128)(2,1)}, bf16[512,768]{1,0:T(8,128)(2,1)}, bf16[512,768...) custom-call(s32[12]{0:T(128)} %pad_add_fusion._.m.meta, bf16[512,1536]{1,0:T(8,128)(2,1)} %bitcast.33, ...), custom_call_target="tpu_custom_call" | custom-call | flops 7247757312 | bytes 29884416 | tf_op jit(solution)/shard_map/middle_forward/pallas_call | solution.py:515
  146.5 32.5 %feed_own.1 = (f32[512,1536]{1,0:T(8,128)}, f32[512,1536]{1,0:T(8,128)}, f32[16,512]{1,0:T(8,128)}, f32[16,512]{1,0:T(8,128)}, f32[16,3072]{1,0:T(8,128)}, /*index=5*/f32[16,3072]{1,0:T(8,128)}) custom-call(s32[12]{0:T(128)} %pad_add_fusion._.m.meta, bf16[512,1536]{1,0:T(8,128)(2,1)} %get-tuple-element.95.rows_ref.refs_0_, bf16[512,1536]{1,0:T(8,128)(2,1)} %bitcast.44, ...), custom_call_target="tpu_custom_call" | custom-call | flops 19327352832 | bytes 28311552 | tf_op jit(solution)/shard_map/feed_own/pallas_call | solution.py:515
  179.0 13.9 %all-gather.11.cloned.1.call-done = bf16[64,96,1536]{2,1,0:T(8,128)(2,1)} async-done(((bf16[4,96,1536]{2,1,0:T(8,128)(2,1)}), bf16[64,96,1536]{2,1,0:T(8,128)(2,1)}) %all-gather.11.cloned.1.call-update) | async-done | bytes 18874384 | tf_op jit(solution)/shard_map/all_gather | solution.py:1992
  192.9 35.8 %feed_other.1 = (bf16[512,1536]{1,0:T(8,128)(2,1)}, f32[512,1536]{1,0:T(8,128)}, bf16[16,3072]{1,0:T(8,128)(2,1)}, bf16[16,3072]{1,0:T(8,128)(2,1)}, f32[16,1536]{1,0:T(8,128)}, /*index=5*/bf16[16,1536]{1,0:T(8,128)(2,1)}) custom-call(s32[12]{0:T(128)} %pad_add_fusion._.m.meta, bf16[512,1536]{1,0:T(8,128)(2,1)} %get-tuple-element.95.rows_ref.refs_0_, ...), custom_call_target="tpu_custom_call" | custom-call | flops 19327352832 | bytes 37748736 | tf_op jit(solution)/shard_map/feed_other/pallas_call | solution.py:515
  232.3 26.1 %middle_back.1 = (f32[512,1536]{1,0:T(8,128)}, bf16[512,768]{1,0:T(8,128)(2,1)}, bf16[512,768]{1,0:T(8,128)(2,1)}, f32[2,64,768]{2,1,0:T(8,128)}, bf16[2,64,768]...) custom-call(s32[12]{0:T(128)} %pad_add_fusion._.m.meta, ...), custom_call_target="tpu_custom_call" | custom-call | flops 7247757312 | bytes 33030144 | tf_op jit(solution)/shard_map/middle_back/pallas_call | solution.py:515
  259.1 4.7 %collective-permute-done.12 = bf16[16,4608]{1,0:T(8,128)(2,1)S(1)} collective-permute-done((bf16[16,4608]{1,0:T(8,128)(2,1)}, bf16[16,4608]{1,0:T(8,128)(2,1)S(1)}, u32[]{:S(2)}, u32[]{:S(2)}) %collective-permute-start.12) | collective-permute-done | bytes 147488 | tf_op jit(solution)/shard_map/ppermute | solution.py:1941
  266.3 13.7 %self_back_own.1.part_ref = f32[3,768,512]{2,1,0:T(8,128)} custom-call(s32[12]{0:T(128)} %pad_add_fusion._.m.meta, bf16[3,512,768]{2,1,0:T(8,128)(2,1)} %own_heads.1.own_ref, bf16[512,768]{1,0:T(8,128)(2,1)} %get-tuple-element.91.z_own_ref.refs_2_.z_ref, f32[512,768]{1,0:T(8,128)} %get-tuple-element.118.log_ref.log_own_ref, ...), custom_call_target="tpu_custom_call" | custom-call | flops 20132659200 | bytes 9437184 | tf_op jit(solution)/shard_map/self_back_own/pallas_call | solution.py:515
  285.5 26.4 %self_back.1 = (bf16[3,512,768]{2,1,0:T(8,128)(2,1)}, bf16[3,512,768]{2,1,0:T(8,128)(2,1)}) custom-call(s32[12]{0:T(128)} %pad_add_fusion._.m.meta, f32[3,768,512]{2,1,0:T(8,128)} %self_back_own.1.part_ref, bf16[3,512,768]{2,1,0:T(8,128)(2,1)} %own_heads.1.own_ref, bf16[3,512,768]{2,1,0:T(8,128)(2,1)} %other_heads.1.other_ref, ...), custom_call_target="tpu_custom_call" | custom-call | flops 40265318400 | bytes 15728640 | tf_op jit(solution)/shard_map/self_back/pallas_call | solution.py:515
  312.0 8.4 %self_ranks.1 = (f32[16,4608]{1,0:T(8,128)}, bf16[16,2304]{1,0:T(8,128)(2,1)}) custom-call(s32[12]{0:T(128)} %pad_add_fusion._.m.meta, bf16[512,1536]{1,0:T(8,128)(2,1)} %first_norm.1.act_ref.refs_0_, bf16[512,1536]{1,0:T(8,128)(2,1)} %copy-done, bf16[3,512,768]{2,1,0:T(8,128)(2,1)} %get-tuple-element.131.refs_2_.refs_0_, ...), custom_call_target="tpu_custom_call" | custom-call | flops 905969664 | bytes 7864320 | tf_op jit(solution)/shard_map/self_ranks/pallas_call | solution.py:515
  329.3 11.2 %other_back.1.refs_4_ = bf16[512,1536]{1,0:T(8,128)(2,1)} custom-call(s32[12]{0:T(128)} %pad_add_fusion._.m.meta, bf16[3,512,768]{2,1,0:T(8,128)(2,1)} %get-tuple-element.132.refs_3_.refs_0_, bf16[3,1536,768]{2,1,0:T(8,128)(2,1)} %refs_1_.8, bf16[3,8,16,1536]{3,2,1,0:T(8,128)(2,1)} %refs_2_.6, bf16[3,8,16,768]{3,2,1,0:T(8,128)(2,1)} %refs_3_.6, ...), custom_call_target="tpu_custom_call" | custom-call | flops 3623878656 | bytes 12582912 | tf_op jit(solution)/shard_map/other_back/pallas_call | solution.py:515
  343.3 5.5 %text_back.1 = f32[64,1536]{1,0:T(8,128)} custom-call(s32[12]{0:T(128)} %pad_add_fusion._.m.meta, bf16[2,64,768]{2,1,0:T(8,128)(2,1)} %add_convert_fusion.refs_0_, bf16[2,1536,768]{2,1,0:T(8,128)(2,1)} %refs_1_.9, bf16[3,8,16,1536]{3,2,1,0:T(8,128)(2,1)} %refs_2_.7, bf16[3,8,16,768]{3,2,1,0:T(8,128)(2,1)} %refs_3_.7, bf16[512,1536]{1,0:T(8,128)(2,1)} %other_back.1.refs_4_), custom_call_target="tpu_custom_call" | custom-call | flops 301989888 | bytes 5308416 | tf_op jit(solution)/shard_map/text_back/pallas_call | solution.py:515
  349.9 11.9 %own_back.1.refs_2_.own_ref = f32[512,1536]{1,0:T(8,128)} custom-call(s32[12]{0:T(128)} %pad_add_fusion._.m.meta, bf16[3,512,768]{2,1,0:T(8,128)(2,1)} %get-tuple-element.131.refs_2_.refs_0_, bf16[3,1536,768]{2,1,0:T(8,128)(2,1)} %refs_1_.8, bf16[3,8,16,1536]{3,2,1,0:T(8,128)(2,1)} %refs_2_.6, bf16[3,8,16,768]{3,2,1,0:T(8,128)(2,1)} %refs_3_.6, ...), custom_call_target="tpu_custom_call" | custom-call | flops 3623878656 | bytes 12582912 | tf_op jit(solution)/shard_map/own_back/pallas_call | solution.py:515
  361.7 7.2 %early_slots.1 = (f32[1,8,16,768]{3,2,1,0:T(8,128)}, f32[1,8,16,768]{3,2,1,0:T(8,128)}, f32[2,8,16,768]{3,2,1,0:T(8,128)}, f32[2,8,16,768]{3,2,1,0:T(8,128)}, f3...) custom-call(s32[12]{0:T(128)} %pad_add_fusion._.m.meta, ...), custom_call_target="tpu_custom_call" | custom-call | bytes 12713984 | tf_op jit(solution)/shard_map/early_slots/pallas_call | solution.py:515
  368.9 9.8 %collective-permute-done.15 = bf16[64,768]{1,0:T(8,128)(2,1)S(1)} collective-permute-done((bf16[64,768]{1,0:T(8,128)(2,1)S(1)}, bf16[64,768]{1,0:T(8,128)(2,1)S(1)}, u32[]{:S(2)}, u32[]{:S(2)}) %collective-permute-start.15) | collective-permute-done | bytes 98336 | tf_op jit(solution)/shard_map/ppermute | solution.py:1941
  379.9 6.9 %last_norm.1.refs_4_ = f32[512,1536]{1,0:T(8,128)} custom-call(s32[12]{0:T(128)} %pad_add_fusion._.m.meta, bf16[512,1536]{1,0:T(8,128)(2,1)} %bitcast.34, f32[512,1536]{1,0:T(8,128)} %own_back.1.refs_2_.own_ref, bf16[512,1536]{1,0:T(8,128)(2,1)} %copy-done.4, f32[512,1536]{1,0:T(8,128)} %get-tuple-element.141.grad_ref, f32[1,1536]{1,0:T(1,128)} %reshape.72.gain_ref, ...), custom_call_target="tpu_custom_call" | custom-call | flops 15728640 | bytes 12582912 | tf_op jit(solution)/shard_map/last_norm/pallas_call | solution.py:515
  387.6 6.3 %late_slots.1 = (f32[3,8,16,768]{3,2,1,0:T(8,128)}, f32[3,8,16,768]{3,2,1,0:T(8,128)}, f32[3,8,16,768]{3,2,1,0:T(8,128)}, f32[3,8,16,768]{3,2,1,0:T(8,128)}) custom-call(s32[12]{0:T(128)} %pad_add_fusion._.m.meta, bf16[16,16,7808]{2,1,0:T(8,128)(2,1)} %bitcast.27, bf16[16,16,7808]{2,1,0:T(8,128)(2,1)} %bitcast.28, ...), custom_call_target="tpu_custom_call" | custom-call | bytes 7995392 | tf_op jit(solution)/shard_map/late_slots/pallas_call | solution.py:515
  (113 shorter events, 59.5 us)
Async XLA Ops:
  7.2 114.8 %all-gather.9.cloned.1.call-start = ((), (), s32[]{:S(2)}) async-start(), calls=%async_computation | async-start | bytes 7520256 | tf_op jit(solution)/shard_map/all_gather | solution.py:1958
  9.4 13.2 %collective-permute-start = (bf16[3,96,768]{2,1,0:T(8,128)(2,1)S(1)}, bf16[3,96,768]{2,1,0:T(8,128)(2,1)S(1)}, u32[]{:S(2)}, u32[]{:S(2)}) collective-permute-start(bf16[3,96,768]{2,1,0:T(8,128)(2,1)S(1)} %pad_maximum_fusion), channel_id=1, source_target_pairs={{0,1},{1,0},{2,3},{3,2},{4,5},{5,4},{6,7},{7,6},{8,9},{9,8},{10,11... | collective-permute-start | bytes 1327112 | tf_op jit(solution)/shard_map/ppermute | solution.py:1941
  23.4 169.5 %all-gather.11.cloned.1.call-start = ((), (), s32[]{:S(2)}) async-start(), calls=%async_computation.1 | async-start | bytes 20054016 | tf_op jit(solution)/shard_map/all_gather | solution.py:1992
  23.4 35.9 %collective-permute-start.1 = (bf16[512,1536]{1,0:T(8,128)(2,1)}, bf16[512,1536]{1,0:T(8,128)(2,1)S(1)}, u32[]{:S(2)}, u32[]{:S(2)}) collective-permute-start(bf16[512,1536]{1,0:T(8,128)(2,1)} %first_norm.1.act_ref.refs_0_), channel_id=1, source_target_pairs={{0,1},{1,0},{2,3},{3,2},{4,5},{5,4},{6,7},{7,6},{8,9},{9,8},{10,11... | collective-permute-start | bytes 4718600 | tf_op jit(solution)/shard_map/ppermute | solution.py:1941
  64.7 27.8 %collective-permute-start.2 = (bf16[4,96,1536]{2,1,0:T(8,128)(2,1)}, bf16[4,96,1536]{2,1,0:T(8,128)(2,1)S(1)}, u32[]{:S(2)}, u32[]{:S(2)}) collective-permute-start(bf16[4,96,1536]{2,1,0:T(8,128)(2,1)} %feed_share.1.refs_0_), channel_id=1, source_target_pairs={{0,1},{1,0},{2,3},{3,2},{4,5},{5,4},{6,7},{7,6},{8,9},{9,8},{10,11... | collective-permute-start | bytes 3538952 | tf_op jit(solution)/shard_map/ppermute | solution.py:1941
  76.6 21.6 %copy-start.17 = (f32[1536]{0:T(1024)S(1)}, f32[1536]{0:T(1024)}, u32[]{:S(2)}) copy-start(f32[1536]{0:T(1024)} %param.32) | copy-start | bytes 18436
  93.6 234.2 %all-gather.13.cloned.1.call-start = ((), (), s32[]{:S(2)}) async-start(), calls=%async_computation.2 | async-start | bytes 6754304 | tf_op jit(solution)/shard_map/all_gather | solution.py:2040
  93.6 28.4 %collective-permute-start.3 = (bf16[512,768]{1,0:T(8,128)(2,1)}, bf16[512,768]{1,0:T(8,128)(2,1)S(1)}, u32[]{:S(2)}, u32[]{:S(2)}) collective-permute-start(bf16[512,768]{1,0:T(8,128)(2,1)} %get-tuple-element.93.z_other_ref), channel_id=1, source_target_pairs={{0,1},{1,0},{2,3},{3,2},{4,5},{5,4},{6,7},{7,6},{8,9},{9,8},{10,11... | collective-permute-start | bytes 2359304 | tf_op jit(solution)/shard_map/ppermute | solution.py:1941
  94.1 24.4 %collective-permute-start.5 = (bf16[2,64,768]{2,1,0:T(8,128)(2,1)S(1)}, bf16[2,64,768]{2,1,0:T(8,128)(2,1)S(1)}, u32[]{:S(2)}, u32[]{:S(2)}) collective-permute-start(bf16[2,64,768]{2,1,0:T(8,128)(2,1)S(1)} %copy-done.3), channel_id=1, source_target_pairs={{0,1},{1,0},{2,3},{3,2},{4,5},{5,4},{6,7},{7,6},{8,9},{9,8},{10,11... | collective-permute-start | bytes 589832 | tf_op jit(solution)/shard_map/ppermute | solution.py:1941
  95.7 26.2 %collective-permute-start.4 = (bf16[16,9984]{1,0:T(8,128)(2,1)S(1)}, bf16[16,9984]{1,0:T(8,128)(2,1)S(1)}, u32[]{:S(2)}, u32[]{:S(2)}) collective-permute-start(bf16[16,9984]{1,0:T(8,128)(2,1)S(1)} %copy-done.5), channel_id=1, source_target_pairs={{0,1},{1,0},{2,3},{3,2},{4,5},{5,4},{6,7},{7,6},{8,9},{9,8},{10,11... | collective-permute-start | bytes 958472 | tf_op jit(solution)/shard_map/ppermute | solution.py:1941
  228.7 30.3 %collective-permute-start.6 = (bf16[16,3072]{1,0:T(8,128)(2,1)}, bf16[16,3072]{1,0:T(8,128)(2,1)S(1)}, u32[]{:S(2)}, u32[]{:S(2)}) collective-permute-start(bf16[16,3072]{1,0:T(8,128)(2,1)} %get-tuple-element.103), channel_id=1, source_target_pairs={{0,1},{1,0},{2,3},{3,2},{4,5},{5,4},{6,7},{7,6},{8,9},{9,8},{10,11... | collective-permute-start | bytes 294920 | tf_op jit(solution)/shard_map/ppermute | solution.py:1941
  230.3 28.7 %collective-permute-start.7 = (bf16[16,3072]{1,0:T(8,128)(2,1)}, bf16[16,3072]{1,0:T(8,128)(2,1)S(1)}, u32[]{:S(2)}, u32[]{:S(2)}) collective-permute-start(bf16[16,3072]{1,0:T(8,128)(2,1)} %get-tuple-element.104), channel_id=1, source_target_pairs={{0,1},{1,0},{2,3},{3,2},{4,5},{5,4},{6,7},{7,6},{8,9},{9,8},{10,11... | collective-permute-start | bytes 294920 | tf_op jit(solution)/shard_map/ppermute | solution.py:1941
  230.8 28.2 %collective-permute-start.8 = (bf16[16,1536]{1,0:T(8,128)(2,1)}, bf16[16,1536]{1,0:T(8,128)(2,1)S(1)}, u32[]{:S(2)}, u32[]{:S(2)}) collective-permute-start(bf16[16,1536]{1,0:T(8,128)(2,1)} %get-tuple-element.105), channel_id=1, source_target_pairs={{0,1},{1,0},{2,3},{3,2},{4,5},{5,4},{6,7},{7,6},{8,9},{9,8},{10,11... | collective-permute-start | bytes 147464 | tf_op jit(solution)/shard_map/ppermute | solution.py:1941
  232.3 26.7 %copy-start.12 = (f32[16,3072]{1,0:T(8,128)S(1)}, f32[16,3072]{1,0:T(8,128)}, u32[]{:S(2)}) copy-start(f32[16,3072]{1,0:T(8,128)} %get-tuple-element.127) | copy-start | bytes 589828
  232.3 26.7 %copy-start.13 = (f32[16,3072]{1,0:T(8,128)S(1)}, f32[16,3072]{1,0:T(8,128)}, u32[]{:S(2)}) copy-start(f32[16,3072]{1,0:T(8,128)} %get-tuple-element.126) | copy-start | bytes 589828
  232.3 26.8 %copy-start.14 = (f32[16,1536]{1,0:T(8,128)S(1)}, f32[16,1536]{1,0:T(8,128)}, u32[]{:S(2)}) copy-start(f32[16,1536]{1,0:T(8,128)} %get-tuple-element.124) | copy-start | bytes 294916
  258.4 5.5 %collective-permute-start.12 = (bf16[16,4608]{1,0:T(8,128)(2,1)}, bf16[16,4608]{1,0:T(8,128)(2,1)S(1)}, u32[]{:S(2)}, u32[]{:S(2)}) collective-permute-start(bf16[16,4608]{1,0:T(8,128)(2,1)} %get-tuple-element.123), channel_id=1, source_target_pairs={{0,1},{1,0},{2,3},{3,2},{4,5},{5,4},{6,7},{7,6},{8,9},{9,8},{10,11... | collective-permute-start | bytes 442376 | tf_op jit(solution)/shard_map/ppermute | solution.py:1941
  265.7 121.9 %all-gather.15.cloned.1.call-start = ((), (), s32[]{:S(2)}) async-start(), calls=%async_computation.3 | async-start | bytes 4247552 | tf_op jit(solution)/shard_map/all_gather | solution.py:2063
  265.7 17.8 %collective-permute-start.9 = (bf16[512,768]{1,0:T(8,128)(2,1)S(1)}, bf16[512,768]{1,0:T(8,128)(2,1)S(1)}, u32[]{:S(2)}, u32[]{:S(2)}) collective-permute-start(bf16[512,768]{1,0:T(8,128)(2,1)S(1)} %copy-done.19), channel_id=1, source_target_pairs={{0,1},{1,0},{2,3},{3,2},{4,5},{5,4},{6,7},{7,6},{8,9},{9,8},{10,11... | collective-permute-start | bytes 2359304 | tf_op jit(solution)/shard_map/ppermute | solution.py:1941
  283.5 28.5 %collective-permute-start.10 = (bf16[2,64,768]{2,1,0:T(8,128)(2,1)S(1)}, bf16[2,64,768]{2,1,0:T(8,128)(2,1)S(1)}, u32[]{:S(2)}, u32[]{:S(2)}) collective-permute-start(bf16[2,64,768]{2,1,0:T(8,128)(2,1)S(1)} %copy-done.21), channel_id=1, source_target_pairs={{0,1},{1,0},{2,3},{3,2},{4,5},{5,4},{6,7},{7,6},{8,9},{9,8},{10,11... | collective-permute-start | bytes 589832 | tf_op jit(solution)/shard_map/ppermute | solution.py:1941
  284.0 28.0 %collective-permute-start.11 = (bf16[16,3072]{1,0:T(8,128)(2,1)S(1)}, bf16[16,3072]{1,0:T(8,128)(2,1)S(1)}, u32[]{:S(2)}, u32[]{:S(2)}) collective-permute-start(bf16[16,3072]{1,0:T(8,128)(2,1)S(1)} %copy-done.22), channel_id=1, source_target_pairs={{0,1},{1,0},{2,3},{3,2},{4,5},{5,4},{6,7},{7,6},{8,9},{9,8},{10,11... | collective-permute-start | bytes 294920 | tf_op jit(solution)/shard_map/ppermute | solution.py:1941
  320.4 6.3 %collective-permute-start.13 = (bf16[16,2304]{1,0:T(8,128)(2,1)}, bf16[16,2304]{1,0:T(8,128)(2,1)S(1)}, u32[]{:S(2)}, u32[]{:S(2)}) collective-permute-start(bf16[16,2304]{1,0:T(8,128)(2,1)} %get-tuple-element.134.refs_4_), channel_id=1, source_target_pairs={{0,1},{1,0},{2,3},{3,2},{4,5},{5,4},{6,7},{7,6},{8,9},{9,8},{10,11... | collective-permute-start | bytes 221192 | tf_op jit(solution)/shard_map/ppermute | solution.py:1941
  340.5 38.2 %collective-permute-start.14 = (bf16[512,1536]{1,0:T(8,128)(2,1)}, bf16[512,1536]{1,0:T(8,128)(2,1)S(1)}, u32[]{:S(2)}, u32[]{:S(2)}) collective-permute-start(bf16[512,1536]{1,0:T(8,128)(2,1)} %other_back.1.refs_4_), channel_id=1, source_target_pairs={{0,1},{1,0},{2,3},{3,2},{4,5},{5,4},{6,7},{7,6},{8,9},{9,8},{10,11... | collective-permute-start | bytes 4718600 | tf_op jit(solution)/shard_map/ppermute | solution.py:1941
  349.8 28.9 %collective-permute-start.15 = (bf16[64,768]{1,0:T(8,128)(2,1)S(1)}, bf16[64,768]{1,0:T(8,128)(2,1)S(1)}, u32[]{:S(2)}, u32[]{:S(2)}) collective-permute-start(bf16[64,768]{1,0:T(8,128)(2,1)S(1)} %select_convert_fusion), channel_id=1, source_target_pairs={{0,1},{1,0},{2,3},{3,2},{4,5},{5,4},{6,7},{7,6},{8,9},{9,8},{10,11... | collective-permute-start | bytes 294920 | tf_op jit(solution)/shard_map/ppermute | solution.py:1941
  (19 other events, 154.5 us)
Sparse Core Ops, SparseCore 0:
  23.5 68.1 all-gather.8
  93.8 99.0 all-gather.10
  265.8 61.2 all-gather.12
  329.7 49.6 all-gather.14

commit v4 on v3

--- a/solution.py
+++ b/solution.py
@@ -627,9 +627,10 @@
 
 
 def project_body(_, act_ref, weight_ref, down_ref, up_ref, *refs):
-    out_ref = refs[-1]
+    out_ref, rank_ref = refs[-2:]
     act = act_ref[...]
     rank = low_rank(down_ref[0, 0], act)
+    rank_ref[0] = rank
     out_ref[0] = (mm(act, weight_ref[0]) + mm_tn(rank, up_ref[0, 0])).astype(LOW)
 
 
@@ -647,8 +648,11 @@
             pl.BlockSpec((1, 1, RANK_UNIT, local), lambda j, m: (j + skip, m[first_slot + j], 0, 0)),
         ]
         + [IN_PLACE] * len(after),
-        pl.BlockSpec((1, rows, local), lambda j, m: (j, 0, 0)),
-        shaped((count, rows, local), LOW),
+        (
+            pl.BlockSpec((1, rows, local), lambda j, m: (j, 0, 0)),
+            pl.BlockSpec((1, RANK_UNIT, rows), lambda j, m: (j, 0, 0)),
+        ),
+        (shaped((count, rows, local), LOW), shaped((count, RANK_UNIT, rows), LOW)),
         [],
         2 * rows * width * local * count,
         2 * (weights.size + act.size + count * rows * local),
@@ -676,14 +680,15 @@
         out_ref[...] = total_ref[...].astype(out_ref.dtype)
 
 
-def project_back_heads(meta, grads, weights, down, up, slots, skip, kind, name, after):
+def project_back_heads(meta, grads, weights, down, up, slots, skip, kind, name, after, part=(0, 1)):
     count, width, local = weights.shape
-    rows = grads.shape[1]
+    which, parts = part
+    rows = grads.shape[1] // parts
     return call(
         lambda m, *refs: project_back_body(m, count - 1, *refs),
         (count,),
         [
-            pl.BlockSpec((1, rows, local), lambda j, m: (j, 0, 0)),
+            pl.BlockSpec((1, rows, local), lambda j, m: (j, which, 0)),
             pl.BlockSpec((1, width, local), lambda j, m: (j, 0, 0)),
             pl.BlockSpec((1, 1, RANK_UNIT, width), lambda j, m: (j + skip, m[slots + j], 0, 0)),
             pl.BlockSpec((1, 1, RANK_UNIT, local), lambda j, m: (j + skip, m[slots + j], 0, 0)),
@@ -699,45 +704,29 @@
     )
 
 
-def rank_grads_body(meta, count, parts, *refs):
-    acts = []
-    grads = []
-    act_scratch, grad_scratch, sems = refs[-3:]
+def first_grads_body(meta, count, parts, *refs):
+    ups = refs[2 * parts : 2 * parts + count]
+    mine_ref, theirs_ref, ga, act_scratch, grad_scratch, sems = refs[-6:]
+    half = ga.shape[1] // 2
     copies = []
     for part in range(parts):
-        pairs = ((refs[part], act_scratch.at[part]), (refs[parts + part], grad_scratch.at[part]))
+        pairs = ((refs[parts + part], grad_scratch.at[part]), (refs[part], act_scratch.at[part]))
         copies.append(
             [pltpu.make_async_copy(*pair, sems.at[2 * part + number]) for number, pair in enumerate(pairs)]
         )
         for copy in copies[-1]:
             copy.start()
-        acts.append(act_scratch.at[part])
-        grads.append(grad_scratch.at[part])
-    downs = refs[2 * parts : 2 * parts + count]
-    ups = refs[2 * parts + count : 2 * parts + 2 * count]
-    mine_ref, theirs_ref, ga = refs[-6:-3]
-    half = ga.shape[1] // 2
-    local = ups[0].shape[3]
-    down = jnp.concatenate([ref[0, 0] for ref in downs], axis=0)
     for part in range(parts):
-        for copy in copies[part]:
-            copy.wait()
-        act = acts[part][...]
-        rank = low_rank(down, act)
+        copies[part][0].wait()
         grad_rank = jnp.concatenate(
-            [low_rank(ups[j][0, 0], grads[part][j]) for j in range(count)], axis=0
+            [low_rank(ups[j][0, 0], grad_scratch[part, j]) for j in range(count)], axis=0
         )
+        copies[part][1].wait()
+        product = mm(grad_rank, act_scratch[part])
         if part == 0:
-            ga[...] = mm(grad_rank, act)
+            ga[...] = product
         else:
-            ga[...] += mm(grad_rank, act)
-        for j in range(count):
-            gb = mm(rank[RANK_UNIT * j : RANK_UNIT * (j + 1)], grads[part][j])
-            span = slice(count * half + j * local, count * half + (j + 1) * local)
-            if part == 0:
-                mine_ref[:, span] = gb
-            else:
-                mine_ref[:, span] += gb
+            ga[...] += product
     side = meta[10]
     for j in range(count):
         rows = slice(RANK_UNIT * j, RANK_UNIT * (j + 1))
@@ -747,48 +736,80 @@
         theirs_ref[:, span] = theirs.astype(LOW)
 
 
-def rank_grads(meta, acts, grads, down, up, slots, skip, name):
+def first_grads(meta, acts, grads, up, slots, name):
     rows, width = acts[0].shape
     count, _, local = grads[0].shape
     parts = len(acts)
 
-    def table(size, j):
+    def table(j):
         return pl.BlockSpec(
-            (1, 1, RANK_UNIT, size),
-            lambda t, m: (j + skip, m[slots + j], 0, 0),
-            pipeline_mode=pl.Buffered(1),
+            (1, 1, RANK_UNIT, local), lambda t, m: (j, m[slots + j], 0, 0), pipeline_mode=pl.Buffered(1)
         )
 
-    shared = count * width // 2
-    total = shared + count * local
+    shape = (RANK_UNIT, count * width // 2)
     return call(
-        lambda m, *refs: rank_grads_body(m, count, parts, *refs),
+        lambda m, *refs: first_grads_body(m, count, parts, *refs),
         (1,),
-        [IN_PLACE] * (2 * parts)
-        + [table(width, j) for j in range(count)]
-        + [table(local, j) for j in range(count)],
-        (whole((RANK_UNIT, total)), whole((RANK_UNIT, shared))),
-        (shaped((RANK_UNIT, total), WIDE), shaped((RANK_UNIT, shared), LOW)),
+        [IN_PLACE] * (2 * parts) + [table(j) for j in range(count)],
+        (whole(shape), whole(shape)),
+        (shaped(shape, WIDE), shaped(shape, LOW)),
         [
             pltpu.VMEM((RANK_UNIT * count, width), WIDE),
             pltpu.VMEM((parts, rows, width), LOW),
             pltpu.VMEM((parts, count, rows, local), LOW),
             pltpu.SemaphoreType.DMA((2 * parts,)),
         ],
-        8 * parts * rows * (width + local) * RANK_UNIT * count,
+        4 * parts * rows * (width + local) * RANK_UNIT * count,
         2 * parts * rows * (width + count * local),
         name,
-        (meta, *acts, *grads, *([down] * count), *([up] * count)),
-    )
-
-
-def split_columns(meta, mine_ref, theirs_ref, first, array):
+        (meta, *acts, *grads, *([up] * count)),
+    )
+
+
+def second_grads_body(_, parts, *refs):
+    out_ref, grad_scratch, sems = refs[-3:]
+    count, _, local = refs[parts].shape
+    copies = [
+        pltpu.make_async_copy(refs[parts + part].at[j], grad_scratch.at[part, j], sems.at[part * count + j])
+        for part in range(parts)
+        for j in range(count)
+    ]
+    for j in range(count):
+        for part in range(parts):
+            copies[part * count + j].start()
+    for j in range(count):
+        total = None
+        for part in range(parts):
+            copies[part * count + j].wait()
+            product = mm(refs[part][j], grad_scratch[part, j])
+            total = product if total is None else total + product
+        out_ref[:, j * local : (j + 1) * local] = total.astype(LOW)
+
+
+def second_grads(meta, ranks, grads, name, after):
+    count, rows, local = grads[0].shape
+    parts = len(ranks)
+    shape = (RANK_UNIT, count * local)
+    return call(
+        lambda m, *refs: second_grads_body(m, parts, *refs),
+        (1,),
+        [whole(ranks[0].shape)] * parts + [IN_PLACE] * (parts + 1),
+        whole(shape),
+        shaped(shape, LOW),
+        [pltpu.VMEM((parts, count, rows, local), LOW), pltpu.SemaphoreType.DMA((parts * count,))],
+        2 * parts * rows * local * RANK_UNIT * count,
+        2 * parts * rows * count * local,
+        name,
+        (meta, *ranks, *grads, after),
+    )
+
+
+def split_columns(meta, mine_ref, theirs_ref, first, array, skip=0):
     half = array.shape[-1] // 2
-    span = slice(first, first + half)
     side = meta[10]
-    mine_ref[:, span] = array[:, pl.ds(pl.multiple_of(side * half, 128), half)]
+    mine_ref[:, first : first + half] = array[:, pl.ds(pl.multiple_of(side * half, 128), half)]
     theirs = array[:, pl.ds(pl.multiple_of((1 - side) * half, 128), half)]
-    theirs_ref[:, span] = theirs.astype(LOW)
+    theirs_ref[:, skip + first : skip + first + half] = theirs.astype(LOW)
 
 
 def own_columns(mine_ref, theirs_ref, first, array):
@@ -816,20 +837,19 @@
     return jnp.where(place == target, 1.0, 0.0).astype(LOW)
 
 
-def slot_sum_body(_, plan, slots, carried, everyone_ref, label_ref, *refs):
-    count = len({which for _, which, _ in plan})
-    earlier = refs[: len(carried)]
-    out_refs = refs[-5 - count : -5]
-    names, arrived, totals, in_sems, out_sems = refs[-5:]
-    clips, rank, unit = arrived.shape[1:]
-    incoming = [
+def slot_copies(unit, count, everyone_ref, arrived, in_sems):
+    return [
         pltpu.make_async_copy(
             everyone_ref.at[:, :, pl.ds(unit * number, unit)], arrived.at[number], in_sems.at[number]
         )
-        for number in range(len(plan))
+        for number in range(count)
     ]
-    for copy in incoming:
-        copy.start()
+
+
+def slot_work(plan, slots, carried, everyone_ref, label_ref, earlier, out_refs, scratch):
+    names, arrived, totals, in_sems, out_sems = scratch
+    clips, rank, unit = arrived.shape[1:]
+    incoming = slot_copies(unit, len(plan), everyone_ref, arrived, in_sems)
     names[...] = clip_names(label_ref)
     outgoing = []
     for number, (which, ref) in enumerate(zip(carried, earlier)):
@@ -850,30 +870,53 @@
         copy.wait()
 
 
-def slot_sums(meta, everyone, plan, outs, slots, unit, carried, name, after):
+def slot_scratch(everyone, plan, slots, unit, carried):
+    clips, rank, _ = everyone.shape
+    units = len(plan)
+    return [
+        pltpu.VMEM((2 * HEAD_DIM, clips * rank), WIDE),
+        pltpu.VMEM((units, clips, rank, unit), LOW),
+        pltpu.VMEM((units, slots, rank, unit), WIDE),
+        pltpu.SemaphoreType.DMA((units,)),
+        pltpu.SemaphoreType.DMA((units + len(carried),)),
+    ]
+
+
+def slot_specs(everyone, carried):
     clips, rank, total = everyone.shape
     label_width = 2 * HEAD_DIM
-    units = len(plan)
+    return [IN_PLACE, whole((clips, rank, label_width), (0, 0, total // label_width - 1))] + [
+        whole(array.shape) for array in carried.values()
+    ]
+
+
+def slot_shapes(everyone, outs, slots):
+    rank = everyone.shape[1]
+    return tuple(
+        shaped((slots, rank, width) if stack is None else (stack, slots, rank, width), WIDE)
+        for stack, width in outs
+    )
+
+
+def slot_sum_body(_, plan, slots, carried, outs, everyone_ref, label_ref, *refs):
+    scratch = refs[-5:]
+    for copy in slot_copies(scratch[1].shape[3], len(plan), everyone_ref, scratch[1], scratch[3]):
+        copy.start()
+    slot_work(
+        plan, slots, carried, everyone_ref, label_ref, refs[: len(carried)], refs[-5 - outs : -5], scratch
+    )
+
+
+def slot_sums(meta, everyone, plan, outs, slots, unit, carried, name, after):
     return call(
-        lambda m, *refs: slot_sum_body(m, plan, slots, tuple(carried), *refs),
+        lambda m, *refs: slot_sum_body(m, plan, slots, tuple(carried), len(outs), *refs),
         (1,),
-        [IN_PLACE, whole((clips, rank, label_width), (0, 0, total // label_width - 1))]
-        + [whole(array.shape) for array in carried.values()]
-        + [IN_PLACE] * len(after),
+        slot_specs(everyone, carried) + [IN_PLACE] * len(after),
         (IN_PLACE,) * len(outs),
-        tuple(
-            shaped((slots, rank, width) if stack is None else (stack, slots, rank, width), WIDE)
-            for stack, width in outs
-        ),
-        [
-            pltpu.VMEM((label_width, clips * rank), WIDE),
-            pltpu.VMEM((units, clips, rank, unit), LOW),
-            pltpu.VMEM((units, slots, rank, unit), WIDE),
-            pltpu.SemaphoreType.DMA((units,)),
-            pltpu.SemaphoreType.DMA((units + len(carried),)),
-        ],
+        slot_shapes(everyone, outs, slots),
+        slot_scratch(everyone, plan, slots, unit, carried),
         0,
-        2 * everyone.size + 4 * slots * rank * total,
+        2 * everyone.size,
         name,
         (meta, everyone, everyone, *carried.values(), *after),
     )
@@ -1029,11 +1072,11 @@
         value_wide[slot, which] = rows_ref[2] * (1 - marked) + marked
 
 
-def back_prepare_queries(slot, rows_ref, mixed_ref, logs_ref, grad_ref, scratch):
+def back_prepare_queries(slot, rows_ref, mixed_ref, logs_ref, grad_refs, scratch):
     _, query_turned, grad_turned, query_wide, _, grad_wide, _ = scratch
     masks = half_masks()
     lane = lax.broadcasted_iota(jnp.int32, (1, 2 * HEAD_DIM), 1)
-    grad = grad_ref[...]
+    grad = jnp.concatenate([ref[...] for ref in grad_refs], axis=0)
     product = grad.astype(WIDE) * mixed_ref[...].astype(WIDE)
     query = rows_ref[0] * jnp.asarray(HEAD_DIM**-0.5, LOW)
     logs = logs_ref[...]
@@ -1073,7 +1116,7 @@
     totals = scratch[-1]
     totals[...] = jnp.zeros_like(totals)
     back_prepare_keys(0, own_ref, scratch[:-1])
-    back_prepare_queries(0, own_ref, z_ref, log_ref, grad_ref, scratch[:-1])
+    back_prepare_queries(0, own_ref, z_ref, log_ref, (grad_ref,), scratch[:-1])
     back_block(0, 0, True, scratch[:-1], totals)
     out_ref[...] = totals[:, 0]
 
@@ -1107,7 +1150,8 @@
     log_own_ref,
     log_other_ref,
     grad_own_ref,
-    grad_other_ref,
+    grad_first_ref,
+    grad_second_ref,
     _early,
     out_own_ref,
     out_other_ref,
@@ -1125,10 +1169,10 @@
 
     @pl.when(side != 0)
     def _():
-        back_prepare_queries(0, own_ref, z_own_ref, log_own_ref, grad_own_ref, scratch)
+        back_prepare_queries(0, own_ref, z_own_ref, log_own_ref, (grad_own_ref,), scratch)
 
     back_prepare_keys(1, other_ref, scratch)
-    back_prepare_queries(1, other_ref, z_other_ref, log_other_ref, grad_other_ref, scratch)
+    back_prepare_queries(1, other_ref, z_other_ref, log_other_ref, (grad_first_ref, grad_second_ref), scratch)
     back_block(1, 1, True, scratch, totals)
     back_block(1 - side, side, False, scratch, totals)
     for slot, ref in ((0, out_own_ref), (1, out_other_ref)):
@@ -1137,7 +1181,7 @@
         ref[2] = totals[2, slot].T.astype(LOW)
 
 
-def self_back(meta, part, own, other, z_own, z_other, log_own, log_other, grad_own, grad_other, after):
+def self_back(meta, part, own, other, z_own, z_other, log_own, log_other, grad_own, grads_other, after):
     _, half, local = own.shape
     pair = 2 * HEAD_DIM
     three = pl.BlockSpec((3, half, pair), lambda p, m: (0, 0, p))
@@ -1146,7 +1190,8 @@
         self_back_body,
         (local // pair,),
         [pl.BlockSpec((3, pair, half), lambda p, m: (0, p, 0)), three, three]
-        + [one] * 6
+        + [one] * 5
+        + [pl.BlockSpec((half // 2, pair), lambda p, m: (0, p))] * 2
         + [IN_PLACE] * len(after),
         (three, three),
         (shaped(own.shape, LOW), shaped(own.shape, LOW)),
@@ -1154,7 +1199,7 @@
         200 * half * half * local,
         40 * half * local,
         "self_back",
-        (meta, part, own, other, z_own, z_other, log_own, log_other, grad_own, grad_other, *after),
+        (meta, part, own, other, z_own, z_other, log_own, log_other, grad_own, *grads_other, *after),
     )
 
 
@@ -1434,9 +1479,9 @@
     up6_other_ref,
     grad_one_ref,
     dz_own_ref,
-    dz_other_ref,
+    dz_first_ref,
+    dz_second_ref,
     text_grad_own_ref,
-    text_grad_other_ref,
     mine_ref,
     theirs_ref,
     text_mine_ref,
@@ -1564,7 +1609,9 @@
         gb3_ref,
     )
     dz_own_ref[...] = dz_own
-    dz_other_ref[...] = dz_other
+    half = dz_first_ref.shape[0]
+    dz_first_ref[...] = dz_other[:half]
+    dz_second_ref[...] = dz_other[half:]
     grad_one_copy.wait()
 
     @pl.when(step == last)
@@ -1575,26 +1622,31 @@
         own_columns(mine_ref, theirs_ref, 3 * local, ga7_ref)
         split_columns(meta, mine_ref, theirs_ref, 4 * local, gb3_ref)
         split_columns(meta, mine_ref, theirs_ref, 5 * local, gb7_ref)
-        for total, slot in ((key_total, 0), (value_total, 1)):
-            for part, ref in ((0, text_grad_own_ref), (1, text_grad_other_ref)):
+        texts = text_ref.shape[0]
+        for slot, total in enumerate((key_total, value_total)):
+            for part in (0, 1):
                 for tile in range(tiles):
                     stacked = total[part, tile]
                     rows = 0.0
                     for head, mask in enumerate(masks):
                         rows = rows + stacked[HEAD_DIM * head : HEAD_DIM * (head + 1)] * mask.astype(WIDE)
-                    ref[slot, :, tile_span(tile)] = rows.astype(ref.dtype)
+                    if part == 0:
+                        text_grad_own_ref[slot, :, tile_span(tile)] = rows
+                    else:
+                        text_theirs_ref[texts * slot : texts * (slot + 1), tile_span(tile)] = rows.astype(LOW)
         text = text_ref[...]
         factors = ((down5_ref, up5_ref, up5_other_ref), (down6_ref, up6_ref, up6_other_ref))
         for slot, (down_ref, up_ref, up_other_ref) in enumerate(factors):
             grad_own = text_grad_own_ref[slot].astype(LOW)
-            grad_other = text_grad_other_ref[slot]
+            grad_other = text_theirs_ref[texts * slot : texts * (slot + 1)]
             rank = low_rank(down_ref[0, 0], text)
             grad_rank = mm_nt(up_ref[0, 0], grad_own) + mm_nt(up_other_ref[...], grad_other)
             ga4_ref[...] = mm(grad_rank.astype(LOW), text)
-            split_columns(meta, text_mine_ref, text_theirs_ref, slot * local, ga4_ref)
-            span = slice((2 + slot) * local, (3 + slot) * local)
-            text_mine_ref[:, span] = mm(rank, grad_own)
-            text_theirs_ref[:, span] = mm(rank, grad_other).astype(LOW)
+            first = slice(2 * texts + RANK_UNIT * slot, 2 * texts + RANK_UNIT * (slot + 1))
+            second = slice(2 * texts + RANK_UNIT * (2 + slot), 2 * texts + RANK_UNIT * (3 + slot))
+            split_columns(meta, text_mine_ref.at[:, pl.ds(slot * local, local)], text_theirs_ref.at[first], 0, ga4_ref)
+            text_mine_ref[:, (2 + slot) * local : (3 + slot) * local] = mm(rank, grad_own)
+            text_theirs_ref[second] = mm(rank, grad_other).astype(LOW)
 
 
 def middle_back(
@@ -1610,6 +1662,7 @@
     rank = (RANK_UNIT, width)
     packs = (RANK_UNIT, 6 * local)
     text_packs = (RANK_UNIT, 4 * local)
+    text_rows = (2 * text.shape[0] + 4 * RANK_UNIT, local)
     _, _, cross_down, cross_up = tables
     return call(
         lambda m, *refs: middle_back_body(m, 0, *refs),
@@ -1621,18 +1674,18 @@
         + [whole(text_own.shape), whole(text_other.shape), whole((1, width)), whole(text.shape)]
         + [chosen(cross_down, 1, 5), chosen(cross_down, 2, 6), chosen(cross_up, 1, 5), chosen(cross_up, 2, 6)]
         + [whole((RANK_UNIT, local), (0, 3)), whole((RANK_UNIT, local), (0, 4))],
-        (IN_PLACE, narrow, narrow, whole(text_own.shape), whole(text_own.shape))
-        + (whole(packs), whole(packs), whole(text_packs), whole(text_packs)),
+        (IN_PLACE, narrow, whole((frames // 2, local)), whole((frames // 2, local)), whole(text_own.shape))
+        + (whole(packs), whole(packs), whole(text_packs), whole(text_rows)),
         (
             shaped((frames, width), WIDE),
             shaped((frames, local), LOW),
-            shaped((frames, local), LOW),
+            shaped((frames // 2, local), LOW),
+            shaped((frames // 2, local), LOW),
             shaped(text_own.shape, WIDE),
-            shaped(text_own.shape, LOW),
             shaped(packs, WIDE),
             shaped(packs, LOW),
             shaped(text_packs, WIDE),
-            shaped(text_packs, LOW),
+            shaped(text_rows, LOW),
         ),
         [
             pltpu.VMEM((2, tiles, TILE_HEADS * HEAD_DIM, TILE_HEADS * HEAD_DIM), WIDE),
@@ -1686,8 +1739,7 @@
 def feed_own_body(
     _, rows_ref, cot_ref, up_weight_ref, down_weight_ref, up_rank_ref, down_rank_ref,
     down8_ref, up9_ref,
-    branch_ref, grad_rows_ref, rank9_ref, grad_rank8_ref, ga9_ref, gb8_ref,
-    rank8, grad_rank9,
+    branch_ref, grad_rows_ref, rank9_ref, grad_rank8_ref, rank8, grad_rank9, ga9_ref, gb8_ref,
 ):
     @pl.when(pl.program_id(0) == 0)
     def _():
@@ -1726,16 +1778,18 @@
             picked,
             picked_out,
         ],
-        (whole((frames, width)), whole((frames, width)), whole(rank), whole(rank), grads, grads),
+        (whole((frames, width)), whole((frames, width))) + (whole(rank),) * 4 + (grads, grads),
         (
             shaped((frames, width), WIDE),
             shaped((frames, width), WIDE),
             shaped(rank, WIDE),
             shaped(rank, WIDE),
+            shaped(rank, LOW),
+            shaped(rank, LOW),
             shaped((RANK_UNIT, hidden), WIDE),
             shaped((RANK_UNIT, hidden), WIDE),
         ),
-        [pltpu.VMEM(rank, LOW), pltpu.VMEM(rank, LOW)],
+        [],
         8 * frames * width * hidden,
         4 * width * hidden + 12 * frames * width,
         "feed_own",
@@ -1745,10 +1799,10 @@
 
 def feed_other_body(
     meta, last, rows_ref, cot_ref, up_weight_ref, down_weight_ref, up_rank_ref, down_rank_ref,
-    down8_ref, up9_ref, branch_in_ref, grad_rows_in_ref, rank9_in_ref, grad_rank8_in_ref,
+    down8_ref, up9_ref, branch_in_ref, grad_rows_in_ref, rank9_in_ref, grad_rank8_in_ref, rank8, grad_rank9,
     stream_ref, gain_ref,
-    out_ref, grad_ref, ga9_ref, gb8_ref, mine_ref, theirs_ref,
-    branch, grad_rows, rank9, grad_rank8, rank8, grad_rank9, ga8_ref, gb9_ref, branch_in, grad_rows_in, stream_in, sems,
+    out_ref, grad_ref, mine_ref, theirs_ref,
+    branch, grad_rows, rank9, grad_rank8, ga8_ref, gb9_ref, branch_in, grad_rows_in, stream_in, sems,
 ):
     step = pl.program_id(0)
     copies = [
@@ -1762,14 +1816,16 @@
     def _():
         for copy in copies:
             copy.start()
-        rank8[...] = low_rank(down8_ref[0], rows_ref[...])
-        grad_rank9[...] = low_rank(up9_ref[0], cot_ref[...])
         branch[...] = jnp.zeros_like(branch)
         grad_rows[...] = jnp.zeros_like(grad_rows)
         rank9[...] = rank9_in_ref[...]
         grad_rank8[...] = grad_rank8_in_ref[...]
 
     shards, _, depth, tile = up_weight_ref.shape
+    hidden = (last + 1) * tile
+    first = pl.multiple_of(step * tile, 128)
+    gb8_ref = theirs_ref.at[:, pl.ds(first, tile)]
+    ga9_ref = theirs_ref.at[:, pl.ds(pl.multiple_of(hidden + first, 128), tile)]
     up_weight = up_weight_ref[...].reshape(shards * depth, tile)
     down_weight = down_weight_ref[...].reshape(tile, down_weight_ref.shape[3])
     feed_tile(
@@ -1787,8 +1843,9 @@
         last9 = rank9[...].astype(LOW)
         ga8_ref[...] = mm(last8, rows_ref[...])
         gb9_ref[...] = mm(last9, cot_ref[...])
-        split_columns(meta, mine_ref, theirs_ref, 0, ga8_ref)
-        split_columns(meta, mine_ref, theirs_ref, ga8_ref.shape[1] // 2, gb9_ref)
+        half = ga8_ref.shape[1] // 2
+        split_columns(meta, mine_ref, theirs_ref, 0, ga8_ref, 2 * hidden)
+        split_columns(meta, mine_ref, theirs_ref, half, gb9_ref, 2 * hidden)
         for first in range(0, frames, block):
             span = slice(first, first + block)
             stream = stream_in[span]
@@ -1810,7 +1867,6 @@
     per_half = width // tile
     own_shards = tile // (quarters // 2 * depth)
     down_first = quarters // 2
-    grads = pl.BlockSpec((RANK_UNIT, tile), lambda t, m: (0, t))
     picked = pl.BlockSpec((1, RANK_UNIT, width), lambda t, m: (m[8], 0, 0))
     picked_out = pl.BlockSpec((1, RANK_UNIT, width), lambda t, m: (m[9], 0, 0))
     rank = (RANK_UNIT, frames)
@@ -1836,25 +1892,23 @@
             IN_PLACE,
             whole(rank),
             whole(rank),
+            whole(rank),
+            whole(rank),
             IN_PLACE,
             whole((1, width)),
         ],
-        (full, full, grads, grads, whole((RANK_UNIT, width)), whole((RANK_UNIT, width))),
+        (full, full, whole((RANK_UNIT, width)), whole((RANK_UNIT, 2 * hidden + width))),
         (
             shaped((frames, width), LOW),
             shaped((frames, width), WIDE),
-            shaped((RANK_UNIT, hidden), LOW),
-            shaped((RANK_UNIT, hidden), LOW),
             shaped((RANK_UNIT, width), WIDE),
-            shaped((RANK_UNIT, width), LOW),
+            shaped((RANK_UNIT, 2 * hidden + width), LOW),
         ),
         [
             wide,
             wide,
             pltpu.VMEM(rank, WIDE),
             pltpu.VMEM(rank, WIDE),
-            pltpu.VMEM(rank, LOW),
-            pltpu.VMEM(rank, LOW),
             pltpu.VMEM((RANK_UNIT, width), WIDE),
             pltpu.VMEM((RANK_UNIT, width), WIDE),
             wide,
@@ -1871,27 +1925,50 @@
     )
 
 
-def last_norm_body(_, x_ref, own_ref, other_ref, grad_ref, gain_ref, after_ref, out_ref):
+def last_norm_body(_, half, slot_part, x_ref, own_ref, first_ref, second_ref, grad_ref, gain_ref, *refs):
+    plan, slots, carried, outs = slot_part
+    step = pl.program_id(0)
+    everyone_ref, label_ref = refs[:2]
+    earlier = refs[2 : 2 + len(carried)]
+    out_ref = refs[-6 - outs]
+    scratch = refs[-5:]
+
+    @pl.when(step == 0)
+    def _():
+        for copy in slot_copies(scratch[1].shape[3], len(plan), everyone_ref, scratch[1], scratch[3]):
+            copy.start()
+
     _, normed, inverse = norm_rows(x_ref[...].astype(WIDE), gain_ref[...])
-    total = own_ref[...] + other_ref[...].astype(WIDE)
+    other = jnp.where(step < half, first_ref[...].astype(WIDE), second_ref[...].astype(WIDE))
+    total = own_ref[...] + other
     out_ref[...] = grad_ref[...] + norm_back(total, gain_ref[...], normed, inverse)
 
-
-def last_norm(meta, x, own, other, grad, gain, after):
+    @pl.when(step == 2 * half - 1)
+    def _():
+        slot_work(plan, slots, carried, everyone_ref, label_ref, earlier, refs[-5 - outs : -5], scratch)
+
+
+def last_norm(meta, x, own, received, grad, gain, everyone, plan, outs, slots, unit, carried, after):
     frames, width = x.shape
-    block = min(256, frames)
+    block = min(256, frames // 2)
+    half = frames // 2 // block
     rows = pl.BlockSpec((block, width), lambda t, _: (t, 0))
+    first = pl.BlockSpec((block, width), lambda t, _: (jnp.minimum(t, half - 1), 0))
+    second = pl.BlockSpec((block, width), lambda t, _: (jnp.maximum(t - half, 0), 0))
+    slot_part = (plan, slots, tuple(carried), len(outs))
     return call(
-        last_norm_body,
-        (frames // block,),
-        [rows, rows, rows, rows, whole((1, width)), IN_PLACE],
-        rows,
-        shaped(x.shape, WIDE),
-        [],
+        lambda m, *refs: last_norm_body(m, half, slot_part, *refs),
+        (2 * half,),
+        [rows, rows, first, second, rows, whole((1, width))]
+        + slot_specs(everyone, carried)
+        + [IN_PLACE] * len(after),
+        (rows,) + (IN_PLACE,) * len(outs),
+        (shaped(x.shape, WIDE),) + slot_shapes(everyone, outs, slots),
+        slot_scratch(everyone, plan, slots, unit, carried),
         20 * x.size,
         16 * x.size,
         "last_norm",
-        (meta, x, own, other, grad, gain, after),
+        (meta, x, own, *received, grad, gain, everyone, everyone, *carried.values(), *after),
     )
 
 
@@ -1952,7 +2029,7 @@
     out_share = side_by_side(share(self_output_weight, step), 2).reshape(depth, local)
     query_share = share(cross_query_weight, depth)
     cross_share = side_by_side(share(cross_output_weight, step), 2).reshape(depth, local)
-    share_one = swap(jnp.stack([out_share, query_share, cross_share]))
+    share_one = jnp.stack([swap(out_share), swap(query_share), swap(cross_share)])
     rows_one = first_norm(meta, x, gain_one)
     share_one, rows_one = lax.optimization_barrier((share_one, rows_one))
     gathered_one = lax.all_gather(share_one, "dp", axis=0)
@@ -1972,18 +2049,18 @@
     packed = swap(factors)
     first_pack = 5 * local
 
-    heads_own = project_heads(
+    heads_own, ranks_own = project_heads(
         meta, rows_one, self_query_key_value_weight, self_first_factors, self_second_factors, 0, 0, "own_heads"
     )
     part_own = self_forward_own(meta, heads_own, factors)
-    text_own = project_heads(
+    text_own, _ = project_heads(
         meta, text, cross_key_value_weight, cross_first_factors, cross_second_factors, 5, 1, "text_heads"
     )
     text_other = swap(text_own)
     share_two = feed_share(
         meta, down_weight, up_weight, depth, (part_own, text_own, rows_one_other)
     )
-    heads_other = project_heads(
+    heads_other, ranks_other = project_heads(
         meta, rows_one_other, self_query_key_value_weight, self_first_factors, self_second_factors,
         0, 0, "other_heads", (share_two,),
     )
@@ -1998,31 +2075,29 @@
         text_own, text_other, (gain_two, gain_three),
     )
     tile = local
-    branch, grad_rows, rank9, grad_rank8, ga9_own, gb8_own = feed_own(
+    *carried, ga9_own, gb8_own = feed_own(
         meta, rows_three, cot, up_weight, down_weight, input_first_factors, input_second_factors,
         output_first_factors, output_second_factors, tile,
     )
-    output, grad_two, ga9_other, gb8_other, feed_mine, feed_theirs = feed_other(
+    output, grad_two, feed_mine, feed_theirs = feed_other(
         meta, rows_three, cot, gathered_two, packed, first_pack, input_first_factors,
-        output_second_factors, (branch, grad_rows, rank9, grad_rank8), stream_two, gain_three, tile,
-    )
-
-    gb8_received = swap(gb8_other)
-    ga9_received = swap(ga9_other)
+        output_second_factors, carried, stream_two, gain_three, tile,
+    )
+
     feed_received = swap(feed_theirs)
 
     (
-        grad_one, dz_own_heads, dz_other_heads, text_grad_own, text_grad_other, middle_mine, middle_theirs,
-        text_mine_rank, text_theirs_rank,
+        grad_one, dz_own_heads, *dz_other_heads, text_grad_own, middle_mine, middle_theirs,
+        text_mine_rank, text_theirs,
     ) = middle_back(
         meta, grad_two, stream_one, z_own_frames, z_other_heads, q_own, q_other, z2_own, z2_other,
         weights, gathered_one, tables, packed, text_own, text_other, gain_two, text,
     )
-    gb8_received, ga9_received, feed_received, dz_other_heads = lax.optimization_barrier(
-        (gb8_received, ga9_received, feed_received, dz_other_heads)
-    )
-    dz_other_frames, text_theirs_rank, text_grad_other = lax.optimization_barrier(
-        (swap(dz_other_heads), text_theirs_rank, text_grad_other)
+    feed_received, middle_theirs, *dz_other_heads = lax.optimization_barrier(
+        (feed_received, middle_theirs, *dz_other_heads)
+    )
+    *dz_other_frames, text_theirs = lax.optimization_barrier(
+        (*[swap(half) for half in dz_other_heads], text_theirs)
     )
 
     unit = local
@@ -2031,8 +2106,8 @@
     early = jnp.concatenate(
         [
             join(middle_mine, [swap(middle_theirs)]),
-            join(feed_mine, [feed_received]),
-            join(jnp.concatenate([gb8_own, ga9_own], axis=1), [gb8_received, ga9_received]),
+            join(feed_mine, [feed_received[:, 2 * hidden :]]),
+            join(jnp.concatenate([gb8_own, ga9_own], axis=1), [feed_received[:, : 2 * hidden]]),
             labels,
         ],
         axis=1,
@@ -2043,27 +2118,34 @@
         meta, grads_part, heads_own, heads_other, z_own_frames, z_other_frames, log_own, log_other,
         dz_own_heads, dz_other_frames, (early,),
     )
-    text_grad_other, text_received_rank, grads_own = lax.optimization_barrier(
-        (swap(text_grad_other), swap(text_theirs_rank), grads_own)
-    )
+    text_received, grads_own = lax.optimization_barrier((swap(text_theirs), grads_own))
+    texts = text.shape[0]
+    text_grad_other = text_received[: 2 * texts].reshape(text_grad_own.shape)
+    text_received_rank = side_by_side(
+        text_received[2 * texts :].reshape(4, RANK_UNIT, local).transpose(1, 0, 2).reshape(RANK_UNIT, -1), 1
+    )[0]
     text_heads_grad = (text_grad_own + text_grad_other.astype(WIDE)).astype(LOW)
-    mine, theirs = rank_grads(
-        meta, [rows_one, rows_one_other], [grads_own, grads_other], self_first_factors,
-        self_second_factors, 0, 0, "self_ranks",
-    )
-    partial_other = project_back_heads(
-        meta, grads_other, self_query_key_value_weight, self_first_factors, self_second_factors,
-        0, 0, LOW, "other_back", theirs,
-    )
-    received = swap(partial_other)
+    mine, theirs = first_grads(
+        meta, [rows_one, rows_one_other], [grads_own, grads_other], self_second_factors, 0, "self_first"
+    )
+    seconds = second_grads(meta, [ranks_own, ranks_other], [grads_own, grads_other], "self_second", theirs)
+    theirs, seconds = lax.optimization_barrier((swap(theirs), seconds))
+    partial_other = [
+        project_back_heads(
+            meta, grads_other, self_query_key_value_weight, self_first_factors, self_second_factors,
+            0, 0, LOW, "other_back", seconds, (part, 2),
+        )
+        for part in range(2)
+    ]
+    received = [swap(part) for part in partial_other]
     labels = lax.dynamic_index_in_dim(early_all[:, :, -2 * HEAD_DIM :], place, axis=0, keepdims=False)
     late = jnp.concatenate(
-        [join(mine, [swap(theirs)]), join(text_mine_rank, [text_received_rank]), labels], axis=1
+        [join(mine, [theirs]), seconds, join(text_mine_rank, [text_received_rank]), labels], axis=1
     )
     late_all = lax.all_gather(late, "dp", axis=0)
     text_rows = project_back_heads(
         meta, text_heads_grad, cross_key_value_weight, cross_first_factors, cross_second_factors,
-        5, 1, WIDE, "text_back", partial_other,
+        5, 1, WIDE, "text_back", partial_other[1],
     )
     text_halves = (text_rows[:, : width // 2], text_rows[:, width // 2 :])
     text_mine = jnp.where(side == 0, text_halves[0], text_halves[1])
@@ -2082,16 +2164,15 @@
         [(1, unit), (1, unit), (2, unit), (2, unit), (None, unit), (None, unit), (None, hidden), (None, hidden)],
         slots, unit, {}, "early_slots", (partial_own,),
     )
-    received, text_received, sum_up_a = lax.optimization_barrier((received, text_received, sum_up_a))
+    *received, text_received, sum_up_a = lax.optimization_barrier((*received, text_received, sum_up_a))
     text_grad = text_mine + text_received.astype(WIDE)
-    input_grad = last_norm(meta, x, partial_own, received, grad_one, gain_one, sum_up_a)
-    sum_self_a, sum_self_b, sum_cross_a, sum_cross_b = slot_sums(
-        meta,
+    input_grad, sum_self_a, sum_self_b, sum_cross_a, sum_cross_b = last_norm(
+        meta, x, partial_own, received, grad_one, gain_one,
         late_all,
         [(0, 0, 0), (1, 0, 1), (2, 0, 2), (0, 1, 0), (1, 1, 1), (2, 1, 2)]
         + [(5, 2, 1), (6, 2, 2), (5, 3, 1), (6, 3, 2)],
         [(3, unit), (3, unit), (3, unit), (3, unit)],
-        slots, unit, {2: sum_query_a, 3: sum_query_b}, "late_slots", (input_grad,),
+        slots, unit, {2: sum_query_a, 3: sum_query_b}, (sum_up_a,),
     )
     return (
         output[None],

time: 407 us -> 400 us (0.983)
  waiting for transfers between devices: 70.8 us -> 54.9 us
  Pallas kernels: 276 us -> 281 us
    ppermute x16 -> x17, waiting for transfers between devices: 56.7 us -> 40.5 us  [swap(): return lax.ppermute(array, 'tensor', [(0, 1), (1, 0)])]
    pallas_call x21 -> x22, Pallas kernels: 276 us -> 281 us  [call(): pl.pallas_call(body, grid_spec=pltpu.PrefetchScalarGridSpec(num_scalar_pr...]
    ppermute x16 -> x17, starting transfers between devices: 21.5 us -> 23.4 us  [swap(): return lax.ppermute(array, 'tensor', [(0, 1), (1, 0)])]
  transfers between devices with their start and end apart: 20 -> 21, of which waited for: 9 -> 9; matrix products, arithmetic and copies ran while one was open for 2% -> 2% of each run, Pallas kernels for 58% -> 60%
where the time goes in v4:
time: 400 us; the launch traced here: 393 us
  Pallas kernels  281 us (70%)
  waiting for transfers between devices  54.9 us (14%)
  starting transfers between devices  23.6 us (6%)
  between operations  14.6 us (4%)
  other arithmetic  9.65 us (2%)
  local copies, waits for them, and re-layouts  8.87 us (2%)
    pallas_call x22, Pallas kernels, call(): pl.pallas_call(body, grid_spec=pltpu.PrefetchScalarGridSpec(num_scalar_pr...  281 us
    ppermute x17, waiting for transfers between devices, swap(): return lax.ppermute(array, 'tensor', [(0, 1), (1, 0)])  40.5 us
    ppermute x17, starting transfers between devices, swap(): return lax.ppermute(array, 'tensor', [(0, 1), (1, 0)])  23.4 us
    all_gather x1, waiting for transfers between devices, on_pair(): gathered_two = lax.all_gather(share_two, 'dp', axis=0)  13.3 us
  transfers between devices with their start and end apart: 21, of which 9 were waited for; matrix products, arithmetic and copies ran while one was open for 2% of the time, Pallas kernels for 60%

profile of v4, /device:TPU:0, one launch (start us, length us, event | category | flops | bytes accessed | tf_op | source)
XLA Modules:
  0.0 393.0 jit_solution(3920461361844026035)
XLA Ops:
  26.6 4.8 %text_heads.1 = (bf16[2,64,768]{2,1,0:T(8,128)(2,1)}, bf16[2,16,64]{2,1,0:T(8,128)(2,1)}) custom-call(s32[12]{0:T(128)} %pad_add_fusion._.m.meta, bf16[64,1536]{1,0:T(8,128)(2,1)} %bitcast.42, bf16[2,1536,768]{2,1,0:T(8,128)(2,1)} %refs_1_.11, bf16[3,8,16,1536]{3,2,1,0:T(8,128)(2,1)} %refs_2_.9, bf16[3,8,16,768]{3,2,1,0:T(8,128)(2,1)} %refs_3_.9), custom_call_target="tpu_custom_call" | custom-call | flops 301989888 | bytes 5111808 | tf_op jit(solution)/shard_map/text_heads/pallas_call | solution.py:515
  31.4 10.6 %own_heads.1 = (bf16[3,512,768]{2,1,0:T(8,128)(2,1)}, bf16[3,16,512]{2,1,0:T(8,128)(2,1)}) custom-call(s32[12]{0:T(128)} %pad_add_fusion._.m.meta, bf16[512,1536]{1,0:T(8,128)(2,1)} %first_norm.1.act_ref.refs_0_, bf16[3,1536,768]{2,1,0:T(8,128)(2,1)} %refs_1_.10, bf16[3,8,16,1536]{3,2,1,0:T(8,128)(2,1)} %refs_2_.8, bf16[3,8,16,768]{3,2,1,0:T(8,128)(2,1)} %refs_3_.8), custom_call_target="tpu_custom_call" | custom-call | flops 3623878656 | bytes 11010048 | tf_op jit(solution)/shard_map/own_heads/pallas_call | solution.py:515
  42.0 8.5 %self_forward_own.1.refs_2_.part_ref = f32[6,2,88,512]{3,2,1,0:T(8,128)} custom-call(s32[12]{0:T(128)} %pad_add_fusion._.m.meta, bf16[3,512,768]{2,1,0:T(8,128)(2,1)} %get-tuple-element.99.own_ref, bf16[16,9984]{1,0:T(8,128)(2,1)} %picked_factors.1.after_ref), custom_call_target="tpu_custom_call" | custom-call | flops 805306368 | bytes 3932160 | tf_op jit(solution)/shard_map/self_forward_own/pallas_call | solution.py:515
  50.5 7.7 %collective-permute-done.3.refs_4_.act_ref.refs_1_ = bf16[512,1536]{1,0:T(8,128)(2,1)S(1)} collective-permute-done((bf16[512,1536]{1,0:T(8,128)(2,1)}, bf16[512,1536]{1,0:T(8,128)(2,1)S(1)}, u32[]{:S(2)}, u32[]{:S(2)}) %collective-permute-start.3) | collective-permute-done | bytes 1572896 | tf_op jit(solution)/shard_map/ppermute | solution.py:2018
  65.1 10.5 %other_heads.1 = (bf16[3,512,768]{2,1,0:T(8,128)(2,1)}, bf16[3,16,512]{2,1,0:T(8,128)(2,1)}) custom-call(s32[12]{0:T(128)} %pad_add_fusion._.m.meta, bf16[512,1536]{1,0:T(8,128)(2,1)} %copy-done.1, bf16[3,1536,768]{2,1,0:T(8,128)(2,1)} %refs_1_.10, bf16[3,8,16,1536]{3,2,1,0:T(8,128)(2,1)} %refs_2_.8, bf16[3,8,16,768]{3,2,1,0:T(8,128)(2,1)} %refs_3_.8, ...), custom_call_target="tpu_custom_call" | custom-call | flops 3623878656 | bytes 11010048 | tf_op jit(solution)/shard_map/other_heads/pallas_call | solution.py:515
  75.6 15.9 %self_forward.1 = (bf16[512,768]{1,0:T(8,128)(2,1)}, bf16[512,768]{1,0:T(8,128)(2,1)}, f32[512,768]{1,0:T(8,128)}, f32[512,768]{1,0:T(8,128)}) custom-call(s32[12]{0:T(128)} %pad_add_fusion._.m.meta, f32[6,2,88,512]{3,2,1,0:T(8,128)} %self_forward_own.1.refs_2_.part_ref, bf16[3,512,768]{2,1,0:T(8,128)(2,1)} %get-tuple-element.99.own_ref, ...), custom_call_target="tpu_custom_call" | custom-call | flops 2415919104 | bytes 7864320 | tf_op jit(solution)/shard_map/self_forward/pallas_call | solution.py:515
  97.8 19.7 %collective-permute-done.7.text_other_ref.refs_22_ = bf16[2,64,768]{2,1,0:T(8,128)(2,1)S(1)} collective-permute-done((bf16[2,64,768]{2,1,0:T(8,128)(2,1)S(1)}, bf16[2,64,768]{2,1,0:T(8,128)(2,1)S(1)}, u32[]{:S(2)}, u32[]{:S(2)}) %collective-permute-start.7) | collective-permute-done | bytes 196640 | tf_op jit(solution)/shard_map/ppermute | solution.py:2018
  121.9 23.5 %middle_forward.1 = (f32[512,1536]{1,0:T(8,128)}, f32[512,1536]{1,0:T(8,128)}, bf16[512,1536]{1,0:T(8,128)(2,1)}, bf16[512,768]{1,0:T(8,128)(2,1)}, bf16[512,768...) custom-call(s32[12]{0:T(128)} %pad_add_fusion._.m.meta, bf16[512,1536]{1,0:T(8,128)(2,1)} %bitcast.40, ...), custom_call_target="tpu_custom_call" | custom-call | flops 7247757312 | bytes 29884416 | tf_op jit(solution)/shard_map/middle_forward/pallas_call | solution.py:515
  145.5 33.1 %feed_own.1 = (f32[512,1536]{1,0:T(8,128)}, f32[512,1536]{1,0:T(8,128)}, f32[16,512]{1,0:T(8,128)}, f32[16,512]{1,0:T(8,128)}, bf16[16,512]{1,0:T(8,128)(2,1)}, ...) custom-call(s32[12]{0:T(128)} %pad_add_fusion._.m.meta, ...), custom_call_target="tpu_custom_call" | custom-call | flops 19327352832 | bytes 28311552 | tf_op jit(solution)/shard_map/feed_own/pallas_call | solution.py:515
  178.6 13.3 %all-gather.11.cloned.1.call-done = bf16[64,96,1536]{2,1,0:T(8,128)(2,1)} async-done(((bf16[4,96,1536]{2,1,0:T(8,128)(2,1)}), bf16[64,96,1536]{2,1,0:T(8,128)(2,1)}) %all-gather.11.cloned.1.call-update) | async-done | bytes 18874384 | tf_op jit(solution)/shard_map/all_gather | solution.py:2069
  191.9 35.0 %feed_other.1 = (bf16[512,1536]{1,0:T(8,128)(2,1)}, f32[512,1536]{1,0:T(8,128)}, f32[16,1536]{1,0:T(8,128)}, bf16[16,7680]{1,0:T(8,128)(2,1)}) custom-call(s32[12]{0:T(128)} %pad_add_fusion._.m.meta, bf16[512,1536]{1,0:T(8,128)(2,1)} %get-tuple-element.106.rows_ref.refs_0_, bf16[512,1536]{1,0:T(8,128)(2,1)} %bitcast.60, bf16[16,4,96,1536]{3,2,1,0:T(8,128)(2,1)} %bitcast.56, ...), custom_call_target="tpu_custom_call" | custom-call | flops 19327352832 | bytes 37748736 | tf_op jit(solution)/shard_map/feed_other/pallas_call | solution.py:515
  228.5 26.2 %middle_back.1 = (f32[512,1536]{1,0:T(8,128)}, bf16[512,768]{1,0:T(8,128)(2,1)}, bf16[256,768]{1,0:T(8,128)(2,1)}, bf16[256,768]{1,0:T(8,128)(2,1)}, f32[2,64,76...) custom-call(s32[12]{0:T(128)} %pad_add_fusion._.m.meta, ...), custom_call_target="tpu_custom_call" | custom-call | flops 7247757312 | bytes 33030144 | tf_op jit(solution)/shard_map/middle_back/pallas_call | solution.py:515
  255.4 5.3 %collective-permute-done.12 = bf16[16,4608]{1,0:T(8,128)(2,1)S(1)} collective-permute-done((bf16[16,4608]{1,0:T(8,128)(2,1)}, bf16[16,4608]{1,0:T(8,128)(2,1)S(1)}, u32[]{:S(2)}, u32[]{:S(2)}) %collective-permute-start.12) | collective-permute-done | bytes 147488 | tf_op jit(solution)/shard_map/ppermute | solution.py:2018
  264.7 13.7 %self_back_own.1.part_ref = f32[3,768,512]{2,1,0:T(8,128)} custom-call(s32[12]{0:T(128)} %pad_add_fusion._.m.meta, bf16[3,512,768]{2,1,0:T(8,128)(2,1)} %get-tuple-element.99.own_ref, bf16[512,768]{1,0:T(8,128)(2,1)} %get-tuple-element.102.z_own_ref.refs_2_.z_ref, f32[512,768]{1,0:T(8,128)} %get-tuple-element.130.log_ref.log_own_ref, ...), custom_call_target="tpu_custom_call" | custom-call | flops 20132659200 | bytes 9437184 | tf_op jit(solution)/shard_map/self_back_own/pallas_call | solution.py:515
  282.0 25.8 %self_back.1 = (bf16[3,512,768]{2,1,0:T(8,128)(2,1)}, bf16[3,512,768]{2,1,0:T(8,128)(2,1)}) custom-call(s32[12]{0:T(128)} %pad_add_fusion._.m.meta, f32[3,768,512]{2,1,0:T(8,128)} %self_back_own.1.part_ref, bf16[3,512,768]{2,1,0:T(8,128)(2,1)} %get-tuple-element.99.own_ref, bf16[3,512,768]{2,1,0:T(8,128)(2,1)} %get-tuple-element.101.other_ref, ...), custom_call_target="tpu_custom_call" | custom-call | flops 40265318400 | bytes 15728640 | tf_op jit(solution)/shard_map/self_back/pallas_call | solution.py:515
  307.9 6.5 %self_first.1 = (f32[16,2304]{1,0:T(8,128)}, bf16[16,2304]{1,0:T(8,128)(2,1)}) custom-call(s32[12]{0:T(128)} %pad_add_fusion._.m.meta, bf16[512,1536]{1,0:T(8,128)(2,1)} %first_norm.1.act_ref.refs_0_, bf16[512,1536]{1,0:T(8,128)(2,1)} %copy-done.1, bf16[3,512,768]{2,1,0:T(8,128)(2,1)} %get-tuple-element.142.refs_2_.refs_0_, ...), custom_call_target="tpu_custom_call" | custom-call | flops 452984832 | bytes 7864320 | tf_op jit(solution)/shard_map/self_first/pallas_call | solution.py:515
  314.3 4.6 %collective-permute-start.13 = (bf16[16,2304]{1,0:T(8,128)(2,1)}, bf16[16,2304]{1,0:T(8,128)(2,1)S(1)}, u32[]{:S(2)}, u32[]{:S(2)}) collective-permute-start(bf16[16,2304]{1,0:T(8,128)(2,1)} %get-tuple-element.145.refs_4_), channel_id=1, source_target_pairs={{0,1},{1,0},{2,3},{3,2},{4,5},{5,4},{6,7},{7,6},{8,9},{9,8},{10,11... | collective-permute-start | bytes 221192 | tf_op jit(solution)/shard_map/ppermute | solution.py:2018
  319.1 5.1 %self_second.1.refs_4_ = bf16[16,2304]{1,0:T(8,128)(2,1)} custom-call(s32[12]{0:T(128)} %pad_add_fusion._.m.meta, bf16[3,16,512]{2,1,0:T(8,128)(2,1)} %get-tuple-element.146.refs_0_, bf16[3,16,512]{2,1,0:T(8,128)(2,1)} %get-tuple-element.147.refs_1_, bf16[3,512,768]{2,1,0:T(8,128)(2,1)} %get-tuple-element.142.refs_2_.refs_0_, ...), custom_call_target="tpu_custom_call" | custom-call | flops 75497472 | bytes 4718592 | tf_op jit(solution)/shard_map/self_second/pallas_call | solution.py:515
  326.8 8.2 %other_back.3.refs_4_ = bf16[256,1536]{1,0:T(8,128)(2,1)} custom-call(s32[12]{0:T(128)} %pad_add_fusion._.m.meta, bf16[3,512,768]{2,1,0:T(8,128)(2,1)} %get-tuple-element.143.refs_3_.refs_0_, bf16[3,1536,768]{2,1,0:T(8,128)(2,1)} %refs_1_.10, bf16[3,8,16,1536]{3,2,1,0:T(8,128)(2,1)} %refs_2_.8, bf16[3,8,16,768]{3,2,1,0:T(8,128)(2,1)} %refs_3_.8, ...), custom_call_target="tpu_custom_call" | custom-call | flops 1811939328 | bytes 9830400 | tf_op jit(solution)/shard_map/other_back/pallas_call | solution.py:515
  336.0 8.2 %other_back.2 = bf16[256,1536]{1,0:T(8,128)(2,1)} custom-call(s32[12]{0:T(128)} %pad_add_fusion._.m.meta, bf16[3,512,768]{2,1,0:T(8,128)(2,1)} %get-tuple-element.143.refs_3_.refs_0_, bf16[3,1536,768]{2,1,0:T(8,128)(2,1)} %refs_1_.10, bf16[3,8,16,1536]{3,2,1,0:T(8,128)(2,1)} %refs_2_.8, bf16[3,8,16,768]{3,2,1,0:T(8,128)(2,1)} %refs_3_.8, ...), custom_call_target="tpu_custom_call" | custom-call | flops 1811939328 | bytes 9830400 | tf_op jit(solution)/shard_map/other_back/pallas_call | solution.py:515
  345.9 5.5 %text_back.1 = f32[64,1536]{1,0:T(8,128)} custom-call(s32[12]{0:T(128)} %pad_add_fusion._.m.meta, bf16[2,64,768]{2,1,0:T(8,128)(2,1)} %fusion.1.refs_0_, bf16[2,1536,768]{2,1,0:T(8,128)(2,1)} %refs_1_.11, bf16[3,8,16,1536]{3,2,1,0:T(8,128)(2,1)} %refs_2_.9, bf16[3,8,16,768]{3,2,1,0:T(8,128)(2,1)} %refs_3_.9, bf16[256,1536]{1,0:T(8,128)(2,1)} %other_back.3.refs_4_), custom_call_target="tpu_custom_call" | custom-call | flops 301989888 | bytes 5308416 | tf_op jit(solution)/shard_map/text_back/pallas_call | solution.py:515
  353.5 11.9 %own_back.1.refs_2_.refs_1_ = f32[512,1536]{1,0:T(8,128)} custom-call(s32[12]{0:T(128)} %pad_add_fusion._.m.meta, bf16[3,512,768]{2,1,0:T(8,128)(2,1)} %get-tuple-element.142.refs_2_.refs_0_, bf16[3,1536,768]{2,1,0:T(8,128)(2,1)} %refs_1_.10, bf16[3,8,16,1536]{3,2,1,0:T(8,128)(2,1)} %refs_2_.8, bf16[3,8,16,768]{3,2,1,0:T(8,128)(2,1)} %refs_3_.8, ...), custom_call_target="tpu_custom_call" | custom-call | flops 3623878656 | bytes 12582912 | tf_op jit(solution)/shard_map/own_back/pallas_call | solution.py:515
  365.4 7.3 %early_slots.1 = (f32[1,8,16,768]{3,2,1,0:T(8,128)}, f32[1,8,16,768]{3,2,1,0:T(8,128)}, f32[2,8,16,768]{3,2,1,0:T(8,128)}, f32[2,8,16,768]{3,2,1,0:T(8,128)}, f3...) custom-call(s32[12]{0:T(128)} %pad_add_fusion._.m.meta, ...), custom_call_target="tpu_custom_call" | custom-call | bytes 6356992 | tf_op jit(solution)/shard_map/early_slots/pallas_call | solution.py:515
  375.2 10.8 %last_norm.1 = (f32[512,1536]{1,0:T(8,128)}, f32[3,8,16,768]{3,2,1,0:T(8,128)}, f32[3,8,16,768]{3,2,1,0:T(8,128)}, f32[3,8,16,768]{3,2,1,0:T(8,128)}, f32[3,8,16,768]{3,2,1,0:T(8,128)}) custom-call(s32[12]{0:T(128)} %pad_add_fusion._.m.meta, bf16[512,1536]{1,0:T(8,128)(2,1)} %bitcast.41, f32[512,1536]{1,0:T(8,128)} %own_back.1.refs_2_.refs_1_, ...), custom_call_target="tpu_custom_call" | custom-call | flops 15728640 | bytes 12582912 | tf_op jit(solution)/shard_map/last_norm/pallas_call | solution.py:515
  (125 shorter events, 56.7 us)
Async XLA Ops:
  7.2 113.8 %all-gather.9.cloned.1.call-start = ((), (), s32[]{:S(2)}) async-start(), calls=%async_computation | async-start | bytes 7520256 | tf_op jit(solution)/shard_map/all_gather | solution.py:2035
  8.3 12.5 %collective-permute-start.2 = (bf16[96,768]{1,0:T(8,128)(2,1)S(1)}, bf16[96,768]{1,0:T(8,128)(2,1)S(1)}, u32[]{:S(2)}, u32[]{:S(2)}) collective-permute-start(bf16[96,768]{1,0:T(8,128)(2,1)S(1)} %bitcast.53), channel_id=1, source_target_pairs={{0,1},{1,0},{2,3},{3,2},{4,5},{5,4},{6,7},{7,6},{8,9},{9,8},{10,11... | collective-permute-start | bytes 442376 | tf_op jit(solution)/shard_map/ppermute | solution.py:2018
  11.4 9.4 %collective-permute-start = (bf16[96,768]{1,0:T(8,128)(2,1)S(1)}, bf16[96,768]{1,0:T(8,128)(2,1)S(1)}, u32[]{:S(2)}, u32[]{:S(2)}) collective-permute-start(bf16[96,768]{1,0:T(8,128)(2,1)S(1)} %bitcast.54), channel_id=1, source_target_pairs={{0,1},{1,0},{2,3},{3,2},{4,5},{5,4},{6,7},{7,6},{8,9},{9,8},{10,11... | collective-permute-start | bytes 442376 | tf_op jit(solution)/shard_map/ppermute | solution.py:2018
  12.4 9.1 %collective-permute-start.1 = (bf16[96,768]{1,0:T(8,128)(2,1)S(1)}, bf16[96,768]{1,0:T(8,128)(2,1)S(1)}, u32[]{:S(2)}, u32[]{:S(2)}) collective-permute-start(bf16[96,768]{1,0:T(8,128)(2,1)S(1)} %constant_dynamic-slice_fusion.1), channel_id=1, source_target_pairs={{0,1},{1,0},{2,3},{3,2},{4,5},{5,4},{6,7},{7,6},{8,9},{9,8},{10,11... | collective-permute-start | bytes 442376 | tf_op jit(solution)/shard_map/ppermute | solution.py:2018
  22.3 169.5 %all-gather.11.cloned.1.call-start = ((), (), s32[]{:S(2)}) async-start(), calls=%async_computation.1 | async-start | bytes 20054016 | tf_op jit(solution)/shard_map/all_gather | solution.py:2069
  22.4 35.9 %collective-permute-start.3 = (bf16[512,1536]{1,0:T(8,128)(2,1)}, bf16[512,1536]{1,0:T(8,128)(2,1)S(1)}, u32[]{:S(2)}, u32[]{:S(2)}) collective-permute-start(bf16[512,1536]{1,0:T(8,128)(2,1)} %first_norm.1.act_ref.refs_0_), channel_id=1, source_target_pairs={{0,1},{1,0},{2,3},{3,2},{4,5},{5,4},{6,7},{7,6},{8,9},{9,8},{10,11... | collective-permute-start | bytes 4718600 | tf_op jit(solution)/shard_map/ppermute | solution.py:2018
  63.7 27.8 %collective-permute-start.4 = (bf16[4,96,1536]{2,1,0:T(8,128)(2,1)}, bf16[4,96,1536]{2,1,0:T(8,128)(2,1)S(1)}, u32[]{:S(2)}, u32[]{:S(2)}) collective-permute-start(bf16[4,96,1536]{2,1,0:T(8,128)(2,1)} %feed_share.1.refs_0_), channel_id=1, source_target_pairs={{0,1},{1,0},{2,3},{3,2},{4,5},{5,4},{6,7},{7,6},{8,9},{9,8},{10,11... | collective-permute-start | bytes 3538952 | tf_op jit(solution)/shard_map/ppermute | solution.py:2018
  92.6 231.8 %all-gather.13.cloned.1.call-start = ((), (), s32[]{:S(2)}) async-start(), calls=%async_computation.2 | async-start | bytes 6754304 | tf_op jit(solution)/shard_map/all_gather | solution.py:2115
  92.6 28.3 %collective-permute-start.5 = (bf16[512,768]{1,0:T(8,128)(2,1)}, bf16[512,768]{1,0:T(8,128)(2,1)S(1)}, u32[]{:S(2)}, u32[]{:S(2)}) collective-permute-start(bf16[512,768]{1,0:T(8,128)(2,1)} %get-tuple-element.104.z_other_ref), channel_id=1, source_target_pairs={{0,1},{1,0},{2,3},{3,2},{4,5},{5,4},{6,7},{7,6},{8,9},{9,8},{10,11... | collective-permute-start | bytes 2359304 | tf_op jit(solution)/shard_map/ppermute | solution.py:2018
  93.1 24.4 %collective-permute-start.7 = (bf16[2,64,768]{2,1,0:T(8,128)(2,1)S(1)}, bf16[2,64,768]{2,1,0:T(8,128)(2,1)S(1)}, u32[]{:S(2)}, u32[]{:S(2)}) collective-permute-start(bf16[2,64,768]{2,1,0:T(8,128)(2,1)S(1)} %copy-done.9), channel_id=1, source_target_pairs={{0,1},{1,0},{2,3},{3,2},{4,5},{5,4},{6,7},{7,6},{8,9},{9,8},{10,11... | collective-permute-start | bytes 589832 | tf_op jit(solution)/shard_map/ppermute | solution.py:2018
  94.7 26.2 %collective-permute-start.6 = (bf16[16,9984]{1,0:T(8,128)(2,1)S(1)}, bf16[16,9984]{1,0:T(8,128)(2,1)S(1)}, u32[]{:S(2)}, u32[]{:S(2)}) collective-permute-start(bf16[16,9984]{1,0:T(8,128)(2,1)S(1)} %copy-done.3), channel_id=1, source_target_pairs={{0,1},{1,0},{2,3},{3,2},{4,5},{5,4},{6,7},{7,6},{8,9},{9,8},{10,11... | collective-permute-start | bytes 958472 | tf_op jit(solution)/shard_map/ppermute | solution.py:2018
  226.9 27.8 %collective-permute-start.8 = (bf16[16,7680]{1,0:T(8,128)(2,1)}, bf16[16,7680]{1,0:T(8,128)(2,1)S(1)}, u32[]{:S(2)}, u32[]{:S(2)}) collective-permute-start(bf16[16,7680]{1,0:T(8,128)(2,1)} %get-tuple-element.116), channel_id=1, source_target_pairs={{0,1},{1,0},{2,3},{3,2},{4,5},{5,4},{6,7},{7,6},{8,9},{9,8},{10,11... | collective-permute-start | bytes 737288 | tf_op jit(solution)/shard_map/ppermute | solution.py:2018
  228.5 26.8 %copy-start.13 = (f32[16,3072]{1,0:T(8,128)S(1)}, f32[16,3072]{1,0:T(8,128)}, u32[]{:S(2)}) copy-start(f32[16,3072]{1,0:T(8,128)} %get-tuple-element.140) | copy-start | bytes 589828
  228.5 26.8 %copy-start.14 = (f32[16,3072]{1,0:T(8,128)S(1)}, f32[16,3072]{1,0:T(8,128)}, u32[]{:S(2)}) copy-start(f32[16,3072]{1,0:T(8,128)} %get-tuple-element.139) | copy-start | bytes 589828
  228.5 26.9 %copy-start.16 = (f32[16,1536]{1,0:T(8,128)S(1)}, f32[16,1536]{1,0:T(8,128)}, u32[]{:S(2)}) copy-start(f32[16,1536]{1,0:T(8,128)} %get-tuple-element.137) | copy-start | bytes 294916
  254.7 6.0 %collective-permute-start.12 = (bf16[16,4608]{1,0:T(8,128)(2,1)}, bf16[16,4608]{1,0:T(8,128)(2,1)S(1)}, u32[]{:S(2)}, u32[]{:S(2)}) collective-permute-start(bf16[16,4608]{1,0:T(8,128)(2,1)} %get-tuple-element.136), channel_id=1, source_target_pairs={{0,1},{1,0},{2,3},{3,2},{4,5},{5,4},{6,7},{7,6},{8,9},{9,8},{10,11... | collective-permute-start | bytes 442376 | tf_op jit(solution)/shard_map/ppermute | solution.py:2018
  262.6 112.6 %all-gather.15.cloned.1.call-start = ((), (), s32[]{:S(2)}) async-start(), calls=%async_computation.3 | async-start | bytes 4247552 | tf_op jit(solution)/shard_map/all_gather | solution.py:2145
  262.6 15.8 %collective-permute-start.10 = (bf16[256,768]{1,0:T(8,128)(2,1)S(1)}, bf16[256,768]{1,0:T(8,128)(2,1)S(1)}, u32[]{:S(2)}, u32[]{:S(2)}) collective-permute-start(bf16[256,768]{1,0:T(8,128)(2,1)S(1)} %copy-done.21), channel_id=1, source_target_pairs={{0,1},{1,0},{2,3},{3,2},{4,5},{5,4},{6,7},{7,6},{8,9},{9,8},{10,11... | collective-permute-start | bytes 1179656 | tf_op jit(solution)/shard_map/ppermute | solution.py:2018
  263.2 18.0 %collective-permute-start.9 = (bf16[256,768]{1,0:T(8,128)(2,1)S(1)}, bf16[256,768]{1,0:T(8,128)(2,1)S(1)}, u32[]{:S(2)}, u32[]{:S(2)}) collective-permute-start(bf16[256,768]{1,0:T(8,128)(2,1)S(1)} %copy-done.20), channel_id=1, source_target_pairs={{0,1},{1,0},{2,3},{3,2},{4,5},{5,4},{6,7},{7,6},{8,9},{9,8},{10,11... | collective-permute-start | bytes 1179656 | tf_op jit(solution)/shard_map/ppermute | solution.py:2018
  281.3 26.6 %collective-permute-start.11 = (bf16[192,768]{1,0:T(8,128)(2,1)S(1)}, bf16[192,768]{1,0:T(8,128)(2,1)S(1)}, u32[]{:S(2)}, u32[]{:S(2)}) collective-permute-start(bf16[192,768]{1,0:T(8,128)(2,1)S(1)} %copy-done.24), channel_id=1, source_target_pairs={{0,1},{1,0},{2,3},{3,2},{4,5},{5,4},{6,7},{7,6},{8,9},{9,8},{10,11... | collective-permute-start | bytes 884744 | tf_op jit(solution)/shard_map/ppermute | solution.py:2018
  314.3 9.9 %collective-permute-start.13 = (bf16[16,2304]{1,0:T(8,128)(2,1)}, bf16[16,2304]{1,0:T(8,128)(2,1)S(1)}, u32[]{:S(2)}, u32[]{:S(2)}) collective-permute-start(bf16[16,2304]{1,0:T(8,128)(2,1)} %get-tuple-element.145.refs_4_), channel_id=1, source_target_pairs={{0,1},{1,0},{2,3},{3,2},{4,5},{5,4},{6,7},{7,6},{8,9},{9,8},{10,11... | collective-permute-start | bytes 221192 | tf_op jit(solution)/shard_map/ppermute | solution.py:2018
  335.0 38.5 %collective-permute-start.15 = (bf16[256,1536]{1,0:T(8,128)(2,1)}, bf16[256,1536]{1,0:T(8,128)(2,1)S(1)}, u32[]{:S(2)}, u32[]{:S(2)}) collective-permute-start(bf16[256,1536]{1,0:T(8,128)(2,1)} %other_back.3.refs_4_), channel_id=1, source_target_pairs={{0,1},{1,0},{2,3},{3,2},{4,5},{5,4},{6,7},{7,6},{8,9},{9,8},{10,11... | collective-permute-start | bytes 2359304 | tf_op jit(solution)/shard_map/ppermute | solution.py:2018
  344.2 29.3 %collective-permute-start.14 = (bf16[256,1536]{1,0:T(8,128)(2,1)}, bf16[256,1536]{1,0:T(8,128)(2,1)S(1)}, u32[]{:S(2)}, u32[]{:S(2)}) collective-permute-start(bf16[256,1536]{1,0:T(8,128)(2,1)} %other_back.2), channel_id=1, source_target_pairs={{0,1},{1,0},{2,3},{3,2},{4,5},{5,4},{6,7},{7,6},{8,9},{9,8},{10,11... | collective-permute-start | bytes 2359304 | tf_op jit(solution)/shard_map/ppermute | solution.py:2018
  352.4 21.1 %collective-permute-start.16 = (bf16[64,768]{1,0:T(8,128)(2,1)S(1)}, bf16[64,768]{1,0:T(8,128)(2,1)S(1)}, u32[]{:S(2)}, u32[]{:S(2)}) collective-permute-start(bf16[64,768]{1,0:T(8,128)(2,1)S(1)} %select_convert_fusion), channel_id=1, source_target_pairs={{0,1},{1,0},{2,3},{3,2},{4,5},{5,4},{6,7},{7,6},{8,9},{9,8},{10,11... | collective-permute-start | bytes 294920 | tf_op jit(solution)/shard_map/ppermute | solution.py:2018
  (23 other events, 211.2 us)
Sparse Core Ops, SparseCore 0:
  22.5 68.1 all-gather.8
  92.8 99.0 all-gather.10
  262.7 61.2 all-gather.12
  326.9 48.2 all-gather.14

commit v5 on v4

--- a/solution.py
+++ b/solution.py
@@ -1056,11 +1056,6 @@
     return high, middle, (rest - middle.astype(WIDE)).astype(LOW)
 
 
-def back_scratch(slots, half):
-    pair = 2 * HEAD_DIM
-    return [pltpu.VMEM((slots, pair, half), LOW)] * 3 + [pltpu.VMEM((slots, 2, half, pair), LOW)] * 4
-
-
 def back_prepare_keys(slot, rows_ref, scratch):
     key_turned, _, _, _, key_wide, _, value_wide = scratch
     lane = lax.broadcasted_iota(jnp.int32, (1, 2 * HEAD_DIM), 1)
@@ -1096,29 +1091,38 @@
         grad_wide[slot, which] = grad_rows
 
 
-def back_block(query_slot, key_slot, diagonal, scratch, totals):
-    key_turned, query_turned, grad_turned, query_wide, key_wide, grad_wide, value_wide = scratch
+def back_block(queries, query_slot, keys, key_slot, diagonal, totals):
+    _, query_turned, grad_turned, query_wide, _, grad_wide, _ = queries
+    key_turned, _, _, _, key_wide, _, value_wide = keys
     half = key_turned.shape[2]
     for which in (0, 1):
         head = slice(HEAD_DIM * which, HEAD_DIM * (which + 1))
-        score = mm_nt(key_wide[key_slot, which], query_wide[query_slot, which])
+        score = mm_nt(key_wide[0, which], query_wide[0, which])
         if diagonal:
             score = jnp.where(causal_keep(half), score, -1e30)
         prob = jnp.exp(score)
-        prob_grad = mm_nt(value_wide[key_slot, which], grad_wide[query_slot, which])
+        prob_grad = mm_nt(value_wide[0, which], grad_wide[0, which])
         score_grad = (prob * prob_grad).astype(LOW)
-        totals[2, key_slot, head] += mm_nt(grad_turned[query_slot, head], prob.astype(LOW))
-        totals[1, key_slot, head] += mm_nt(query_turned[query_slot, head], score_grad)
-        totals[0, query_slot, head] += mm(key_turned[key_slot, head], score_grad)
-
-
-def self_back_own_body(_, own_ref, z_ref, log_ref, grad_ref, out_ref, *scratch):
-    totals = scratch[-1]
+        totals[2, key_slot, head] += mm_nt(grad_turned[0, head], prob.astype(LOW))
+        totals[1, key_slot, head] += mm_nt(query_turned[0, head], score_grad)
+        totals[0, query_slot, head] += mm(key_turned[0, head], score_grad)
+
+
+def self_back_own_body(_, own_ref, z_ref, log_ref, grad_ref, out_ref, *refs):
+    prepared = refs[:-1]
+    totals = refs[-1]
     totals[...] = jnp.zeros_like(totals)
-    back_prepare_keys(0, own_ref, scratch[:-1])
-    back_prepare_queries(0, own_ref, z_ref, log_ref, (grad_ref,), scratch[:-1])
-    back_block(0, 0, True, scratch[:-1], totals)
+    back_prepare_keys(0, own_ref, prepared)
+    back_prepare_queries(0, own_ref, z_ref, log_ref, (grad_ref,), prepared)
+    back_block(prepared, 0, prepared, 0, True, totals)
     out_ref[...] = totals[:, 0]
+
+
+def prepared_specs(half):
+    pair = 2 * HEAD_DIM
+    return (pl.BlockSpec((1, pair, half), lambda p, m: (0, p, 0)),) * 3 + (
+        pl.BlockSpec((1, 2, half, pair), lambda p, m: (0, 0, 0, p)),
+    ) * 4
 
 
 def self_back_own(meta, own, z_own, log_own, grad_own):
@@ -1130,11 +1134,13 @@
         self_back_own_body,
         (local // pair,),
         [three, one, one, one],
-        pl.BlockSpec((3, pair, half), lambda p, m: (0, p, 0)),
-        shaped((3, local, half), WIDE),
-        back_scratch(1, half) + [pltpu.VMEM((3, 1, pair, half), WIDE)],
+        (pl.BlockSpec((3, pair, half), lambda p, m: (0, p, 0)),) + prepared_specs(half),
+        (shaped((3, local, half), WIDE),)
+        + (shaped((1, local, half), LOW),) * 3
+        + (shaped((1, 2, half, local), LOW),) * 4,
+        [pltpu.VMEM((3, 1, pair, half), WIDE)],
         100 * half * half * local,
-        24 * half * local,
+        50 * half * local,
         "self_back_own",
         (meta, own, z_own, log_own, grad_own),
     )
@@ -1143,63 +1149,53 @@
 def self_back_body(
     meta,
     part_ref,
-    own_ref,
-    other_ref,
-    z_own_ref,
-    z_other_ref,
-    log_own_ref,
-    log_other_ref,
-    grad_own_ref,
-    grad_first_ref,
-    grad_second_ref,
-    _early,
-    out_own_ref,
-    out_other_ref,
-    *scratch,
+    *refs,
 ):
-    totals = scratch[-1]
-    scratch = scratch[:-1]
+    own = refs[:7]
+    other_ref, z_ref, log_ref, grad_first_ref, grad_second_ref, _, out_own_ref, out_other_ref = refs[7:15]
+    other = refs[15:22]
+    totals = refs[22]
     side = meta[10]
     totals[:, 0] = part_ref[...]
     totals[:, 1] = jnp.zeros_like(totals[:, 1])
+    back_prepare_keys(0, other_ref, other)
+    back_prepare_queries(0, other_ref, z_ref, log_ref, (grad_first_ref, grad_second_ref), other)
+    back_block(other, 1, other, 1, True, totals)
 
     @pl.when(side == 0)
     def _():
-        back_prepare_keys(0, own_ref, scratch)
+        back_block(other, 1, own, 0, False, totals)
 
     @pl.when(side != 0)
     def _():
-        back_prepare_queries(0, own_ref, z_own_ref, log_own_ref, (grad_own_ref,), scratch)
-
-    back_prepare_keys(1, other_ref, scratch)
-    back_prepare_queries(1, other_ref, z_other_ref, log_other_ref, (grad_first_ref, grad_second_ref), scratch)
-    back_block(1, 1, True, scratch, totals)
-    back_block(1 - side, side, False, scratch, totals)
+        back_block(own, 0, other, 1, False, totals)
+
     for slot, ref in ((0, out_own_ref), (1, out_other_ref)):
         ref[0] = (totals[0, slot].T * HEAD_DIM**-0.5).astype(LOW)
         ref[1] = totals[1, slot].T.astype(LOW)
         ref[2] = totals[2, slot].T.astype(LOW)
 
 
-def self_back(meta, part, own, other, z_own, z_other, log_own, log_other, grad_own, grads_other, after):
-    _, half, local = own.shape
+def self_back(meta, part, prepared, other, z_other, log_other, grads_other, after):
+    _, half, local = other.shape
     pair = 2 * HEAD_DIM
     three = pl.BlockSpec((3, half, pair), lambda p, m: (0, 0, p))
     one = pl.BlockSpec((half, pair), lambda p, m: (0, p))
     return call(
         self_back_body,
         (local // pair,),
-        [pl.BlockSpec((3, pair, half), lambda p, m: (0, p, 0)), three, three]
-        + [one] * 5
+        [pl.BlockSpec((3, pair, half), lambda p, m: (0, p, 0)), *prepared_specs(half), three, one, one]
         + [pl.BlockSpec((half // 2, pair), lambda p, m: (0, p))] * 2
-        + [IN_PLACE] * len(after),
+        + [IN_PLACE],
         (three, three),
-        (shaped(own.shape, LOW), shaped(own.shape, LOW)),
-        back_scratch(2, half) + [pltpu.VMEM((3, 2, pair, half), WIDE)],
+        (shaped(other.shape, LOW), shaped(other.shape, LOW)),
+        [pltpu.VMEM((1, pair, half), LOW)] * 3
+        + [pltpu.VMEM((1, 2, half, pair), LOW)] * 4
+        + [pltpu.VMEM((3, 2, pair, half), WIDE)],
         200 * half * half * local,
-        40 * half * local,
+        60 * half * local,
         "self_back",
-        (meta, part, own, other, z_own, z_other, log_own, log_other, grad_own, *grads_other, *after),
+        (meta, part, *prepared, other, z_other, log_other, *grads_other, after),
     )
 
 
@@ -1311,6 +1307,9 @@
     query_out_other_ref,
     z2_own_ref,
     z2_other_ref,
+    rank3_ref,
+    rank4_ref,
+    rank7_ref,
     *scratch,
 ):
     local = z_own_ref.shape[1]
@@ -1323,8 +1322,9 @@
         scratch[6],
     )
 
-    def out_product(own, other, which, down, down_other, up):
+    def out_product(own, other, which, down, down_other, up, rank_ref):
         rank = (mm_nt(down, own) + mm_nt(down_other, other)).astype(LOW)
+        rank_ref[...] = rank
         weight_own, weight_other_ref = ready(which)
         first, second = halves_of(weight_other_ref, local)
         product = mm(own, weight_own[...]) + mm_tn(rank, up)
@@ -1337,10 +1337,12 @@
         down3_ref[0, 0],
         down3_other_ref[...],
         up3_ref[0, 0],
+        rank3_ref,
     )
     stream_one_ref[...] = stream
     rows_two = norm_rows(stream, gain_two_ref[...])[0].astype(LOW)
     rank = low_rank(down4_ref[0, 0], rows_two)
+    rank4_ref[...] = rank
     query_own_ref, query_other_ref = ready(1)
     query_own = (mm(rows_two, query_own_ref[...]) + mm_tn(rank, up4_ref[0, 0])).astype(LOW)
     query_other = (
@@ -1359,6 +1361,7 @@
         down7_ref[0, 0],
         down7_other_ref[...],
         up7_ref[0, 0],
+        rank7_ref,
     )
     stream_two_ref[...] = stream
     rows_three_ref[...] = norm_rows(stream, gain_three_ref[...])[0].astype(LOW)
@@ -1418,6 +1421,7 @@
     block = min(512, frames)
     wide = pl.BlockSpec((block, width), lambda t, m: (t, 0))
     narrow = pl.BlockSpec((block, local), lambda t, m: (t, 0))
+    ranks = pl.BlockSpec((RANK_UNIT, block), lambda t, m: (0, t))
     specs, args = middle_specs(weights, gathered, tables, packed)
     return call(
         middle_forward_body,
@@ -1425,7 +1429,7 @@
         [wide, narrow, narrow]
         + specs
         + [whole(text_own.shape), whole(text_other.shape), whole((1, width)), whole((1, width))],
-        (wide, wide, wide, narrow, narrow, narrow, narrow),
+        (wide, wide, wide, narrow, narrow, narrow, narrow) + (ranks,) * 3,
         (
             shaped((frames, width), WIDE),
             shaped((frames, width), WIDE),
@@ -1434,7 +1438,8 @@
             shaped((frames, local), LOW),
             shaped((frames, local), LOW),
             shaped((frames, local), LOW),
-        ),
+        )
+        + (shaped((RANK_UNIT, frames), LOW),) * 3,
         middle_scratch(weights, gathered),
         6 * frames * width * width,
         6 * width * width + 20 * frames * width,
@@ -1477,6 +1482,9 @@
     up6_ref,
     up5_other_ref,
     up6_other_ref,
+    rank3_ref,
+    rank4_ref,
+    rank7_ref,
     grad_one_ref,
     dz_own_ref,
     dz_first_ref,
@@ -1528,8 +1536,7 @@
         for ref in (ga3_ref, gb3_ref, ga4_ref, gb4_ref, ga7_ref, gb7_ref):
             ref[...] = jnp.zeros_like(ref)
 
-    def out_back(grad, own, other, which, down, down_other, up, ga_ref, gb_ref):
-        rank = (mm_nt(down, own) + mm_nt(down_other, other)).astype(LOW)
+    def out_back(grad, own, other, which, down, down_other, up, ga_ref, gb_ref, rank):
         grad_rank = low_rank(up, grad)
         ga_ref[:, :local] += mm(grad_rank, own)
         ga_ref[:, local:] += mm(grad_rank, other)
@@ -1556,6 +1563,7 @@
         up7_ref[0, 0],
         ga7_ref,
         gb7_ref,
+        rank7_ref[...],
     )
 
     def text_back(query, dz2, keys, values, part):
@@ -1583,7 +1591,7 @@
         copy.wait()
     rows_two, normed, inverse = norm_rows(stream_one_ref[...], gain_two_ref[...])
     rows_two = rows_two.astype(LOW)
-    rank = low_rank(down4_ref[0, 0], rows_two)
+    rank = rank4_ref[...]
     grad_rank = (mm_nt(up4_ref[0, 0], dq_own) + mm_nt(up4_other_ref[...], dq_other)).astype(LOW)
     ga4_ref[...] += mm(grad_rank, rows_two)
     gb4_ref[:, :local] += mm(rank, dq_own)
@@ -1607,6 +1615,7 @@
         up3_ref[0, 0],
         ga3_ref,
         gb3_ref,
+        rank3_ref[...],
     )
     dz_own_ref[...] = dz_own
     half = dz_first_ref.shape[0]
@@ -1651,7 +1660,7 @@
 
 def middle_back(
     meta, grad, stream_one, z_own, z_other, q_own, q_other, z2_own, z2_other,
-    weights, gathered, tables, packed, text_own, text_other, gain, text,
+    weights, gathered, tables, packed, text_own, text_other, gain, text, ranks,
 ):
     frames, width = grad.shape
     local = z_own.shape[1]
@@ -1673,7 +1682,8 @@
         + specs
         + [whole(text_own.shape), whole(text_other.shape), whole((1, width)), whole(text.shape)]
         + [chosen(cross_down, 1, 5), chosen(cross_down, 2, 6), chosen(cross_up, 1, 5), chosen(cross_up, 2, 6)]
-        + [whole((RANK_UNIT, local), (0, 3)), whole((RANK_UNIT, local), (0, 4))],
+        + [whole((RANK_UNIT, local), (0, 3)), whole((RANK_UNIT, local), (0, 4))]
+        + [whole((RANK_UNIT, frames))] * 3,
         (IN_PLACE, narrow, whole((frames // 2, local)), whole((frames // 2, local)), whole(text_own.shape))
         + (whole(packs), whole(packs), whole(text_packs), whole(text_rows)),
         (
@@ -1703,7 +1713,8 @@
         (meta, grad, stream_one, z_own, z_other, q_own, q_other, z2_own, z2_other)
         + args
         + (text_own, text_other, gain, text)
-        + (cross_down, cross_down, cross_up, cross_up, packed, packed),
+        + (cross_down, cross_down, cross_up, cross_up, packed, packed)
+        + tuple(ranks),
     )
 
 
@@ -2070,7 +2081,7 @@
     z_other_heads = swap(z_other_frames)
     weights = (self_output_weight, cross_query_weight, cross_output_weight)
     tables = (attention_first_factors, attention_second_factors, cross_first_factors, cross_second_factors)
-    stream_one, stream_two, rows_three, q_own, q_other, z2_own, z2_other = middle_forward(
+    stream_one, stream_two, rows_three, q_own, q_other, z2_own, z2_other, *middle_ranks = middle_forward(
         meta, x, z_own_frames, z_other_heads, weights, gathered_one, tables, packed,
         text_own, text_other, (gain_two, gain_three),
     )
@@ -2091,7 +2102,7 @@
         text_mine_rank, text_theirs,
     ) = middle_back(
         meta, grad_two, stream_one, z_own_frames, z_other_heads, q_own, q_other, z2_own, z2_other,
-        weights, gathered_one, tables, packed, text_own, text_other, gain_two, text,
+        weights, gathered_one, tables, packed, text_own, text_other, gain_two, text, middle_ranks,
     )
     feed_received, middle_theirs, *dz_other_heads = lax.optimization_barrier(
         (feed_received, middle_theirs, *dz_other_heads)
@@ -2113,10 +2124,9 @@
         axis=1,
     )
     early_all = lax.all_gather(early, "dp", axis=0)
-    grads_part = self_back_own(meta, heads_own, z_own_frames, log_own, dz_own_heads)
+    grads_part, *prepared = self_back_own(meta, heads_own, z_own_frames, log_own, dz_own_heads)
     grads_own, grads_other = self_back(
-        meta, grads_part, heads_own, heads_other, z_own_frames, z_other_frames, log_own, log_other,
-        dz_own_heads, dz_other_frames, (early,),
+        meta, grads_part, prepared, heads_other, z_other_frames, log_other, dz_other_frames, early
     )
     text_received, grads_own = lax.optimization_barrier((swap(text_theirs), grads_own))
     texts = text.shape[0]

time: 400 us -> 399 us (level)
    all_gather x1, waiting for transfers between devices: 0.02 us -> 4.18 us  [on_pair(): early_all = lax.all_gather(early, 'dp', axis=0)]
  transfers between devices with their start and end apart: 21 -> 21, of which waited for: 9 -> 10; matrix products, arithmetic and copies ran while one was open for 2% -> 2% of each run, Pallas kernels for 60% -> 60%
where the time goes in v5:
time: 399 us; the launch traced here: 392 us
  Pallas kernels  280 us (70%)
  waiting for transfers between devices  57.1 us (14%)
  starting transfers between devices  20.7 us (5%)
  between operations  14.6 us (4%)
  other arithmetic  9.72 us (2%)
  local copies, waits for them, and re-layouts  9.18 us (2%)
    pallas_call x22, Pallas kernels, call(): pl.pallas_call(body, grid_spec=pltpu.PrefetchScalarGridSpec(num_scalar_pr...  280 us
    ppermute x17, waiting for transfers between devices, swap(): return lax.ppermute(array, 'tensor', [(0, 1), (1, 0)])  39.4 us
    ppermute x17, starting transfers between devices, swap(): return lax.ppermute(array, 'tensor', [(0, 1), (1, 0)])  20.5 us
    all_gather x1, waiting for transfers between devices, on_pair(): gathered_two = lax.all_gather(share_two, 'dp', axis=0)  13.3 us
  transfers between devices with their start and end apart: 21, of which 10 were waited for; matrix products, arithmetic and copies ran while one was open for 2% of the time, Pallas kernels for 60%

profile of v5, /device:TPU:0, one launch (start us, length us, event | category | flops | bytes accessed | tf_op | source)
XLA Modules:
  0.0 391.7 jit_solution(9661127115327443778)
XLA Ops:
  26.6 4.8 %text_heads.1 = (bf16[2,64,768]{2,1,0:T(8,128)(2,1)}, bf16[2,16,64]{2,1,0:T(8,128)(2,1)}) custom-call(s32[12]{0:T(128)} %pad_add_fusion._.m.meta, bf16[64,1536]{1,0:T(8,128)(2,1)} %bitcast.42, bf16[2,1536,768]{2,1,0:T(8,128)(2,1)} %refs_1_.11, bf16[3,8,16,1536]{3,2,1,0:T(8,128)(2,1)} %refs_2_.9, bf16[3,8,16,768]{3,2,1,0:T(8,128)(2,1)} %refs_3_.9), custom_call_target="tpu_custom_call" | custom-call | flops 301989888 | bytes 5111808 | tf_op jit(solution)/shard_map/text_heads/pallas_call | solution.py:515
  31.4 10.6 %own_heads.1 = (bf16[3,512,768]{2,1,0:T(8,128)(2,1)}, bf16[3,16,512]{2,1,0:T(8,128)(2,1)}) custom-call(s32[12]{0:T(128)} %pad_add_fusion._.m.meta, bf16[512,1536]{1,0:T(8,128)(2,1)} %first_norm.1.act_ref.refs_0_, bf16[3,1536,768]{2,1,0:T(8,128)(2,1)} %refs_1_.10, bf16[3,8,16,1536]{3,2,1,0:T(8,128)(2,1)} %refs_2_.8, bf16[3,8,16,768]{3,2,1,0:T(8,128)(2,1)} %refs_3_.8), custom_call_target="tpu_custom_call" | custom-call | flops 3623878656 | bytes 11010048 | tf_op jit(solution)/shard_map/own_heads/pallas_call | solution.py:515
  42.1 8.5 %self_forward_own.1.refs_2_.part_ref = f32[6,2,88,512]{3,2,1,0:T(8,128)} custom-call(s32[12]{0:T(128)} %pad_add_fusion._.m.meta, bf16[3,512,768]{2,1,0:T(8,128)(2,1)} %get-tuple-element.110.own_ref, bf16[16,9984]{1,0:T(8,128)(2,1)} %picked_factors.1.after_ref), custom_call_target="tpu_custom_call" | custom-call | flops 805306368 | bytes 3932160 | tf_op jit(solution)/shard_map/self_forward_own/pallas_call | solution.py:515
  50.6 7.7 %collective-permute-done.3.refs_4_.act_ref.refs_1_ = bf16[512,1536]{1,0:T(8,128)(2,1)S(1)} collective-permute-done((bf16[512,1536]{1,0:T(8,128)(2,1)}, bf16[512,1536]{1,0:T(8,128)(2,1)S(1)}, u32[]{:S(2)}, u32[]{:S(2)}) %collective-permute-start.3) | collective-permute-done | bytes 1572896 | tf_op jit(solution)/shard_map/ppermute | solution.py:2029
  59.4 4.3 %feed_share.1.refs_0_ = bf16[4,96,1536]{2,1,0:T(8,128)(2,1)} custom-call(s32[12]{0:T(128)} %pad_add_fusion._.m.meta, bf16[3072,1536]{1,0:T(8,128)(2,1)} %down_weight_ref.1, bf16[1536,3072]{1,0:T(8,128)(2,1)} %up_weight_ref.1, f32[6,2,88,512]{3,2,1,0:T(8,128)} %self_forward_own.1.refs_2_.part_ref, ...), custom_call_target="tpu_custom_call" | custom-call | bytes 2359296 | tf_op jit(solution)/shard_map/feed_share/pallas_call | solution.py:515
  65.1 10.5 %other_heads.1 = (bf16[3,512,768]{2,1,0:T(8,128)(2,1)}, bf16[3,16,512]{2,1,0:T(8,128)(2,1)}) custom-call(s32[12]{0:T(128)} %pad_add_fusion._.m.meta, bf16[512,1536]{1,0:T(8,128)(2,1)} %copy-done.1, bf16[3,1536,768]{2,1,0:T(8,128)(2,1)} %refs_1_.10, bf16[3,8,16,1536]{3,2,1,0:T(8,128)(2,1)} %refs_2_.8, bf16[3,8,16,768]{3,2,1,0:T(8,128)(2,1)} %refs_3_.8, ...), custom_call_target="tpu_custom_call" | custom-call | flops 3623878656 | bytes 11010048 | tf_op jit(solution)/shard_map/other_heads/pallas_call | solution.py:515
  75.6 15.8 %self_forward.1 = (bf16[512,768]{1,0:T(8,128)(2,1)}, bf16[512,768]{1,0:T(8,128)(2,1)}, f32[512,768]{1,0:T(8,128)}, f32[512,768]{1,0:T(8,128)}) custom-call(s32[12]{0:T(128)} %pad_add_fusion._.m.meta, f32[6,2,88,512]{3,2,1,0:T(8,128)} %self_forward_own.1.refs_2_.part_ref, bf16[3,512,768]{2,1,0:T(8,128)(2,1)} %get-tuple-element.110.own_ref, ...), custom_call_target="tpu_custom_call" | custom-call | flops 2415919104 | bytes 7864320 | tf_op jit(solution)/shard_map/self_forward/pallas_call | solution.py:515
  97.7 19.7 %collective-permute-done.7.text_other_ref.refs_22_ = bf16[2,64,768]{2,1,0:T(8,128)(2,1)S(1)} collective-permute-done((bf16[2,64,768]{2,1,0:T(8,128)(2,1)S(1)}, bf16[2,64,768]{2,1,0:T(8,128)(2,1)S(1)}, u32[]{:S(2)}, u32[]{:S(2)}) %collective-permute-start.7) | collective-permute-done | bytes 196640 | tf_op jit(solution)/shard_map/ppermute | solution.py:2029
  121.8 23.6 %middle_forward.1 = (f32[512,1536]{1,0:T(8,128)}, f32[512,1536]{1,0:T(8,128)}, bf16[512,1536]{1,0:T(8,128)(2,1)}, bf16[512,768]{1,0:T(8,128)(2,1)}, bf16[512,768...) custom-call(s32[12]{0:T(128)} %pad_add_fusion._.m.meta, ...), custom_call_target="tpu_custom_call" | custom-call | flops 7247757312 | bytes 29884416 | tf_op jit(solution)/shard_map/middle_forward/pallas_call | solution.py:515
  145.4 33.1 %feed_own.1 = (f32[512,1536]{1,0:T(8,128)}, f32[512,1536]{1,0:T(8,128)}, f32[16,512]{1,0:T(8,128)}, f32[16,512]{1,0:T(8,128)}, bf16[16,512]{1,0:T(8,128)(2,1)}, ...) custom-call(s32[12]{0:T(128)} %pad_add_fusion._.m.meta, ...), custom_call_target="tpu_custom_call" | custom-call | flops 19327352832 | bytes 28311552 | tf_op jit(solution)/shard_map/feed_own/pallas_call | solution.py:515
  178.5 13.3 %all-gather.11.cloned.1.call-done = bf16[64,96,1536]{2,1,0:T(8,128)(2,1)} async-done(((bf16[4,96,1536]{2,1,0:T(8,128)(2,1)}), bf16[64,96,1536]{2,1,0:T(8,128)(2,1)}) %all-gather.11.cloned.1.call-update) | async-done | bytes 18874384 | tf_op jit(solution)/shard_map/all_gather | solution.py:2080
  191.8 35.1 %feed_other.1 = (bf16[512,1536]{1,0:T(8,128)(2,1)}, f32[512,1536]{1,0:T(8,128)}, f32[16,1536]{1,0:T(8,128)}, bf16[16,7680]{1,0:T(8,128)(2,1)}) custom-call(s32[12]{0:T(128)} %pad_add_fusion._.m.meta, bf16[512,1536]{1,0:T(8,128)(2,1)} %get-tuple-element.117.rows_ref.refs_0_, bf16[512,1536]{1,0:T(8,128)(2,1)} %bitcast.60, bf16[16,4,96,1536]{3,2,1,0:T(8,128)(2,1)} %bitcast.56, ...), custom_call_target="tpu_custom_call" | custom-call | flops 19327352832 | bytes 37748736 | tf_op jit(solution)/shard_map/feed_other/pallas_call | solution.py:515
  228.5 25.4 %middle_back.1 = (f32[512,1536]{1,0:T(8,128)}, bf16[512,768]{1,0:T(8,128)(2,1)}, bf16[256,768]{1,0:T(8,128)(2,1)}, bf16[256,768]{1,0:T(8,128)(2,1)}, f32[2,64,76...) custom-call(s32[12]{0:T(128)} %pad_add_fusion._.m.meta, ...), custom_call_target="tpu_custom_call" | custom-call | flops 7247757312 | bytes 33030144 | tf_op jit(solution)/shard_map/middle_back/pallas_call | solution.py:515
  254.6 5.3 %collective-permute-done.12 = bf16[16,4608]{1,0:T(8,128)(2,1)S(1)} collective-permute-done((bf16[16,4608]{1,0:T(8,128)(2,1)}, bf16[16,4608]{1,0:T(8,128)(2,1)S(1)}, u32[]{:S(2)}, u32[]{:S(2)}) %collective-permute-start.12) | collective-permute-done | bytes 147488 | tf_op jit(solution)/shard_map/ppermute | solution.py:2029
  263.9 14.7 %self_back_own.1 = (f32[3,768,512]{2,1,0:T(8,128)}, bf16[1,768,512]{2,1,0:T(8,128)(2,1)}, bf16[1,768,512]{2,1,0:T(8,128)(2,1)}, bf16[1,768,512]{2,1,0:T(8,128)(2...) custom-call(s32[12]{0:T(128)} %pad_add_fusion._.m.meta, ...), custom_call_target="tpu_custom_call" | custom-call | flops 20132659200 | bytes 19660800 | tf_op jit(solution)/shard_map/self_back_own/pallas_call | solution.py:515
  281.2 24.8 %self_back.1 = (bf16[3,512,768]{2,1,0:T(8,128)(2,1)}, bf16[3,512,768]{2,1,0:T(8,128)(2,1)}) custom-call(s32[12]{0:T(128)} %pad_add_fusion._.m.meta, f32[3,768,512]{2,1,0:T(8,128)} %get-tuple-element.146.part_ref, bf16[1,768,512]{2,1,0:T(8,128)(2,1)} %get-tuple-element.147.refs_0_, bf16[1,768,512]{2,1,0:T(8,128)(2,1)} %get-tuple-element.148.refs_1_, ...), custom_call_target="tpu_custom_call" | custom-call | flops 40265318400 | bytes 23592960 | tf_op jit(solution)/shard_map/self_back/pallas_call | solution.py:515
  306.0 6.3 %self_first.1 = (f32[16,2304]{1,0:T(8,128)}, bf16[16,2304]{1,0:T(8,128)(2,1)}) custom-call(s32[12]{0:T(128)} %pad_add_fusion._.m.meta, bf16[512,1536]{1,0:T(8,128)(2,1)} %first_norm.1.act_ref.refs_0_, bf16[512,1536]{1,0:T(8,128)(2,1)} %copy-done.1, bf16[3,512,768]{2,1,0:T(8,128)(2,1)} %get-tuple-element.164.refs_2_.refs_0_, ...), custom_call_target="tpu_custom_call" | custom-call | flops 452984832 | bytes 7864320 | tf_op jit(solution)/shard_map/self_first/pallas_call | solution.py:515
  313.8 5.0 %self_second.1.refs_4_ = bf16[16,2304]{1,0:T(8,128)(2,1)} custom-call(s32[12]{0:T(128)} %pad_add_fusion._.m.meta, bf16[3,16,512]{2,1,0:T(8,128)(2,1)} %get-tuple-element.168.refs_0_, bf16[3,16,512]{2,1,0:T(8,128)(2,1)} %get-tuple-element.169.refs_1_, bf16[3,512,768]{2,1,0:T(8,128)(2,1)} %get-tuple-element.164.refs_2_.refs_0_, ...), custom_call_target="tpu_custom_call" | custom-call | flops 75497472 | bytes 4718592 | tf_op jit(solution)/shard_map/self_second/pallas_call | solution.py:515
  325.6 8.2 %other_back.3.refs_4_ = bf16[256,1536]{1,0:T(8,128)(2,1)} custom-call(s32[12]{0:T(128)} %pad_add_fusion._.m.meta, bf16[3,512,768]{2,1,0:T(8,128)(2,1)} %get-tuple-element.165.refs_3_.refs_0_, bf16[3,1536,768]{2,1,0:T(8,128)(2,1)} %refs_1_.10, bf16[3,8,16,1536]{3,2,1,0:T(8,128)(2,1)} %refs_2_.8, bf16[3,8,16,768]{3,2,1,0:T(8,128)(2,1)} %refs_3_.8, ...), custom_call_target="tpu_custom_call" | custom-call | flops 1811939328 | bytes 9830400 | tf_op jit(solution)/shard_map/other_back/pallas_call | solution.py:515
  335.3 8.1 %other_back.2 = bf16[256,1536]{1,0:T(8,128)(2,1)} custom-call(s32[12]{0:T(128)} %pad_add_fusion._.m.meta, bf16[3,512,768]{2,1,0:T(8,128)(2,1)} %get-tuple-element.165.refs_3_.refs_0_, bf16[3,1536,768]{2,1,0:T(8,128)(2,1)} %refs_1_.10, bf16[3,8,16,1536]{3,2,1,0:T(8,128)(2,1)} %refs_2_.8, bf16[3,8,16,768]{3,2,1,0:T(8,128)(2,1)} %refs_3_.8, ...), custom_call_target="tpu_custom_call" | custom-call | flops 1811939328 | bytes 9830400 | tf_op jit(solution)/shard_map/other_back/pallas_call | solution.py:515
  344.6 5.5 %text_back.1 = f32[64,1536]{1,0:T(8,128)} custom-call(s32[12]{0:T(128)} %pad_add_fusion._.m.meta, bf16[2,64,768]{2,1,0:T(8,128)(2,1)} %fusion.1.refs_0_, bf16[2,1536,768]{2,1,0:T(8,128)(2,1)} %refs_1_.11, bf16[3,8,16,1536]{3,2,1,0:T(8,128)(2,1)} %refs_2_.9, bf16[3,8,16,768]{3,2,1,0:T(8,128)(2,1)} %refs_3_.9, bf16[256,1536]{1,0:T(8,128)(2,1)} %other_back.3.refs_4_), custom_call_target="tpu_custom_call" | custom-call | flops 301989888 | bytes 5308416 | tf_op jit(solution)/shard_map/text_back/pallas_call | solution.py:515
  352.7 11.9 %own_back.1.refs_2_.refs_1_ = f32[512,1536]{1,0:T(8,128)} custom-call(s32[12]{0:T(128)} %pad_add_fusion._.m.meta, bf16[3,512,768]{2,1,0:T(8,128)(2,1)} %get-tuple-element.164.refs_2_.refs_0_, bf16[3,1536,768]{2,1,0:T(8,128)(2,1)} %refs_1_.10, bf16[3,8,16,1536]{3,2,1,0:T(8,128)(2,1)} %refs_2_.8, bf16[3,8,16,768]{3,2,1,0:T(8,128)(2,1)} %refs_3_.8, ...), custom_call_target="tpu_custom_call" | custom-call | flops 3623878656 | bytes 12582912 | tf_op jit(solution)/shard_map/own_back/pallas_call | solution.py:515
  364.6 7.3 %early_slots.1 = (f32[1,8,16,768]{3,2,1,0:T(8,128)}, f32[1,8,16,768]{3,2,1,0:T(8,128)}, f32[2,8,16,768]{3,2,1,0:T(8,128)}, f32[2,8,16,768]{3,2,1,0:T(8,128)}, f3...) custom-call(s32[12]{0:T(128)} %pad_add_fusion._.m.meta, ...), custom_call_target="tpu_custom_call" | custom-call | bytes 6356992 | tf_op jit(solution)/shard_map/early_slots/pallas_call | solution.py:515
  373.8 10.8 %last_norm.1 = (f32[512,1536]{1,0:T(8,128)}, f32[3,8,16,768]{3,2,1,0:T(8,128)}, f32[3,8,16,768]{3,2,1,0:T(8,128)}, f32[3,8,16,768]{3,2,1,0:T(8,128)}, f32[3,8,16,768]{3,2,1,0:T(8,128)}) custom-call(s32[12]{0:T(128)} %pad_add_fusion._.m.meta, bf16[512,1536]{1,0:T(8,128)(2,1)} %bitcast.41, f32[512,1536]{1,0:T(8,128)} %own_back.1.refs_2_.refs_1_, ...), custom_call_target="tpu_custom_call" | custom-call | flops 15728640 | bytes 12582912 | tf_op jit(solution)/shard_map/last_norm/pallas_call | solution.py:515
  (125 shorter events, 56.8 us)
Async XLA Ops:
  7.2 113.7 %all-gather.9.cloned.1.call-start = ((), (), s32[]{:S(2)}) async-start(), calls=%async_computation | async-start | bytes 7520256 | tf_op jit(solution)/shard_map/all_gather | solution.py:2046
  8.3 12.4 %collective-permute-start.2 = (bf16[96,768]{1,0:T(8,128)(2,1)S(1)}, bf16[96,768]{1,0:T(8,128)(2,1)S(1)}, u32[]{:S(2)}, u32[]{:S(2)}) collective-permute-start(bf16[96,768]{1,0:T(8,128)(2,1)S(1)} %bitcast.53), channel_id=1, source_target_pairs={{0,1},{1,0},{2,3},{3,2},{4,5},{5,4},{6,7},{7,6},{8,9},{9,8},{10,11... | collective-permute-start | bytes 442376 | tf_op jit(solution)/shard_map/ppermute | solution.py:2029
  11.4 9.3 %collective-permute-start = (bf16[96,768]{1,0:T(8,128)(2,1)S(1)}, bf16[96,768]{1,0:T(8,128)(2,1)S(1)}, u32[]{:S(2)}, u32[]{:S(2)}) collective-permute-start(bf16[96,768]{1,0:T(8,128)(2,1)S(1)} %bitcast.54), channel_id=1, source_target_pairs={{0,1},{1,0},{2,3},{3,2},{4,5},{5,4},{6,7},{7,6},{8,9},{9,8},{10,11... | collective-permute-start | bytes 442376 | tf_op jit(solution)/shard_map/ppermute | solution.py:2029
  12.4 9.1 %collective-permute-start.1 = (bf16[96,768]{1,0:T(8,128)(2,1)S(1)}, bf16[96,768]{1,0:T(8,128)(2,1)S(1)}, u32[]{:S(2)}, u32[]{:S(2)}) collective-permute-start(bf16[96,768]{1,0:T(8,128)(2,1)S(1)} %constant_dynamic-slice_fusion.1), channel_id=1, source_target_pairs={{0,1},{1,0},{2,3},{3,2},{4,5},{5,4},{6,7},{7,6},{8,9},{9,8},{10,11... | collective-permute-start | bytes 442376 | tf_op jit(solution)/shard_map/ppermute | solution.py:2029
  22.3 169.5 %all-gather.11.cloned.1.call-start = ((), (), s32[]{:S(2)}) async-start(), calls=%async_computation.1 | async-start | bytes 20054016 | tf_op jit(solution)/shard_map/all_gather | solution.py:2080
  22.4 35.9 %collective-permute-start.3 = (bf16[512,1536]{1,0:T(8,128)(2,1)}, bf16[512,1536]{1,0:T(8,128)(2,1)S(1)}, u32[]{:S(2)}, u32[]{:S(2)}) collective-permute-start(bf16[512,1536]{1,0:T(8,128)(2,1)} %first_norm.1.act_ref.refs_0_), channel_id=1, source_target_pairs={{0,1},{1,0},{2,3},{3,2},{4,5},{5,4},{6,7},{7,6},{8,9},{9,8},{10,11... | collective-permute-start | bytes 4718600 | tf_op jit(solution)/shard_map/ppermute | solution.py:2029
  63.7 27.8 %collective-permute-start.4 = (bf16[4,96,1536]{2,1,0:T(8,128)(2,1)}, bf16[4,96,1536]{2,1,0:T(8,128)(2,1)S(1)}, u32[]{:S(2)}, u32[]{:S(2)}) collective-permute-start(bf16[4,96,1536]{2,1,0:T(8,128)(2,1)} %feed_share.1.refs_0_), channel_id=1, source_target_pairs={{0,1},{1,0},{2,3},{3,2},{4,5},{5,4},{6,7},{7,6},{8,9},{9,8},{10,11... | collective-permute-start | bytes 3538952 | tf_op jit(solution)/shard_map/ppermute | solution.py:2029
  92.5 230.6 %all-gather.13.cloned.1.call-start = ((), (), s32[]{:S(2)}) async-start(), calls=%async_computation.2 | async-start | bytes 6754304 | tf_op jit(solution)/shard_map/all_gather | solution.py:2126
  92.5 28.3 %collective-permute-start.5 = (bf16[512,768]{1,0:T(8,128)(2,1)}, bf16[512,768]{1,0:T(8,128)(2,1)S(1)}, u32[]{:S(2)}, u32[]{:S(2)}) collective-permute-start(bf16[512,768]{1,0:T(8,128)(2,1)} %get-tuple-element.115.refs_8_), channel_id=1, source_target_pairs={{0,1},{1,0},{2,3},{3,2},{4,5},{5,4},{6,7},{7,6},{8,9},{9,8},{10,11... | collective-permute-start | bytes 2359304 | tf_op jit(solution)/shard_map/ppermute | solution.py:2029
  93.0 24.4 %collective-permute-start.7 = (bf16[2,64,768]{2,1,0:T(8,128)(2,1)S(1)}, bf16[2,64,768]{2,1,0:T(8,128)(2,1)S(1)}, u32[]{:S(2)}, u32[]{:S(2)}) collective-permute-start(bf16[2,64,768]{2,1,0:T(8,128)(2,1)S(1)} %copy-done.9), channel_id=1, source_target_pairs={{0,1},{1,0},{2,3},{3,2},{4,5},{5,4},{6,7},{7,6},{8,9},{9,8},{10,11... | collective-permute-start | bytes 589832 | tf_op jit(solution)/shard_map/ppermute | solution.py:2029
  94.6 26.2 %collective-permute-start.6 = (bf16[16,9984]{1,0:T(8,128)(2,1)S(1)}, bf16[16,9984]{1,0:T(8,128)(2,1)S(1)}, u32[]{:S(2)}, u32[]{:S(2)}) collective-permute-start(bf16[16,9984]{1,0:T(8,128)(2,1)S(1)} %copy-done.3), channel_id=1, source_target_pairs={{0,1},{1,0},{2,3},{3,2},{4,5},{5,4},{6,7},{7,6},{8,9},{9,8},{10,11... | collective-permute-start | bytes 958472 | tf_op jit(solution)/shard_map/ppermute | solution.py:2029
  226.9 27.0 %collective-permute-start.8 = (bf16[16,7680]{1,0:T(8,128)(2,1)}, bf16[16,7680]{1,0:T(8,128)(2,1)S(1)}, u32[]{:S(2)}, u32[]{:S(2)}) collective-permute-start(bf16[16,7680]{1,0:T(8,128)(2,1)} %get-tuple-element.127), channel_id=1, source_target_pairs={{0,1},{1,0},{2,3},{3,2},{4,5},{5,4},{6,7},{7,6},{8,9},{9,8},{10,11... | collective-permute-start | bytes 737288 | tf_op jit(solution)/shard_map/ppermute | solution.py:2029
  228.5 26.1 %copy-start.13 = (f32[16,3072]{1,0:T(8,128)S(1)}, f32[16,3072]{1,0:T(8,128)}, u32[]{:S(2)}) copy-start(f32[16,3072]{1,0:T(8,128)} %get-tuple-element.162) | copy-start | bytes 589828
  228.5 26.1 %copy-start.14 = (f32[16,3072]{1,0:T(8,128)S(1)}, f32[16,3072]{1,0:T(8,128)}, u32[]{:S(2)}) copy-start(f32[16,3072]{1,0:T(8,128)} %get-tuple-element.161) | copy-start | bytes 589828
  228.5 26.1 %copy-start.16 = (f32[16,1536]{1,0:T(8,128)S(1)}, f32[16,1536]{1,0:T(8,128)}, u32[]{:S(2)}) copy-start(f32[16,1536]{1,0:T(8,128)} %get-tuple-element.159) | copy-start | bytes 294916
  253.9 6.0 %collective-permute-start.12 = (bf16[16,4608]{1,0:T(8,128)(2,1)}, bf16[16,4608]{1,0:T(8,128)(2,1)S(1)}, u32[]{:S(2)}, u32[]{:S(2)}) collective-permute-start(bf16[16,4608]{1,0:T(8,128)(2,1)} %get-tuple-element.158), channel_id=1, source_target_pairs={{0,1},{1,0},{2,3},{3,2},{4,5},{5,4},{6,7},{7,6},{8,9},{9,8},{10,11... | collective-permute-start | bytes 442376 | tf_op jit(solution)/shard_map/ppermute | solution.py:2029
  261.8 111.7 %all-gather.15.cloned.1.call-start = ((), (), s32[]{:S(2)}) async-start(), calls=%async_computation.3 | async-start | bytes 4247552 | tf_op jit(solution)/shard_map/all_gather | solution.py:2155
  261.9 16.8 %collective-permute-start.10 = (bf16[256,768]{1,0:T(8,128)(2,1)S(1)}, bf16[256,768]{1,0:T(8,128)(2,1)S(1)}, u32[]{:S(2)}, u32[]{:S(2)}) collective-permute-start(bf16[256,768]{1,0:T(8,128)(2,1)S(1)} %copy-done.21), channel_id=1, source_target_pairs={{0,1},{1,0},{2,3},{3,2},{4,5},{5,4},{6,7},{7,6},{8,9},{9,8},{10,11... | collective-permute-start | bytes 1179656 | tf_op jit(solution)/shard_map/ppermute | solution.py:2029
  262.5 18.0 %collective-permute-start.9 = (bf16[256,768]{1,0:T(8,128)(2,1)S(1)}, bf16[256,768]{1,0:T(8,128)(2,1)S(1)}, u32[]{:S(2)}, u32[]{:S(2)}) collective-permute-start(bf16[256,768]{1,0:T(8,128)(2,1)S(1)} %copy-done.20), channel_id=1, source_target_pairs={{0,1},{1,0},{2,3},{3,2},{4,5},{5,4},{6,7},{7,6},{8,9},{9,8},{10,11... | collective-permute-start | bytes 1179656 | tf_op jit(solution)/shard_map/ppermute | solution.py:2029
  280.5 25.5 %collective-permute-start.11 = (bf16[192,768]{1,0:T(8,128)(2,1)S(1)}, bf16[192,768]{1,0:T(8,128)(2,1)S(1)}, u32[]{:S(2)}, u32[]{:S(2)}) collective-permute-start(bf16[192,768]{1,0:T(8,128)(2,1)S(1)} %copy-done.24), channel_id=1, source_target_pairs={{0,1},{1,0},{2,3},{3,2},{4,5},{5,4},{6,7},{7,6},{8,9},{9,8},{10,11... | collective-permute-start | bytes 884744 | tf_op jit(solution)/shard_map/ppermute | solution.py:2029
  312.3 6.6 %collective-permute-start.13 = (bf16[16,2304]{1,0:T(8,128)(2,1)}, bf16[16,2304]{1,0:T(8,128)(2,1)S(1)}, u32[]{:S(2)}, u32[]{:S(2)}) collective-permute-start(bf16[16,2304]{1,0:T(8,128)(2,1)} %get-tuple-element.167.refs_4_), channel_id=1, source_target_pairs={{0,1},{1,0},{2,3},{3,2},{4,5},{5,4},{6,7},{7,6},{8,9},{9,8},{10,11... | collective-permute-start | bytes 221192 | tf_op jit(solution)/shard_map/ppermute | solution.py:2029
  333.7 38.9 %collective-permute-start.15 = (bf16[256,1536]{1,0:T(8,128)(2,1)}, bf16[256,1536]{1,0:T(8,128)(2,1)S(1)}, u32[]{:S(2)}, u32[]{:S(2)}) collective-permute-start(bf16[256,1536]{1,0:T(8,128)(2,1)} %other_back.3.refs_4_), channel_id=1, source_target_pairs={{0,1},{1,0},{2,3},{3,2},{4,5},{5,4},{6,7},{7,6},{8,9},{9,8},{10,11... | collective-permute-start | bytes 2359304 | tf_op jit(solution)/shard_map/ppermute | solution.py:2029
  343.4 29.2 %collective-permute-start.14 = (bf16[256,1536]{1,0:T(8,128)(2,1)}, bf16[256,1536]{1,0:T(8,128)(2,1)S(1)}, u32[]{:S(2)}, u32[]{:S(2)}) collective-permute-start(bf16[256,1536]{1,0:T(8,128)(2,1)} %other_back.2), channel_id=1, source_target_pairs={{0,1},{1,0},{2,3},{3,2},{4,5},{5,4},{6,7},{7,6},{8,9},{9,8},{10,11... | collective-permute-start | bytes 2359304 | tf_op jit(solution)/shard_map/ppermute | solution.py:2029
  351.3 21.3 %collective-permute-start.16 = (bf16[64,768]{1,0:T(8,128)(2,1)S(1)}, bf16[64,768]{1,0:T(8,128)(2,1)S(1)}, u32[]{:S(2)}, u32[]{:S(2)}) collective-permute-start(bf16[64,768]{1,0:T(8,128)(2,1)S(1)} %select_convert_fusion), channel_id=1, source_target_pairs={{0,1},{1,0},{2,3},{3,2},{4,5},{5,4},{6,7},{7,6},{8,9},{9,8},{10,11... | collective-permute-start | bytes 294920 | tf_op jit(solution)/shard_map/ppermute | solution.py:2029
  (23 other events, 205.7 us)
Sparse Core Ops, SparseCore 0:
  22.5 68.1 all-gather.8
  92.8 99.0 all-gather.10
  261.9 61.1 all-gather.12
  325.7 47.7 all-gather.14

commit v6 on v5

--- a/solution.py
+++ b/solution.py
@@ -882,8 +882,8 @@
     ]
 
 
-def slot_specs(everyone, carried):
-    clips, rank, total = everyone.shape
+def slot_specs(labelled, carried):
+    clips, rank, total = labelled.shape
     label_width = 2 * HEAD_DIM
     return [IN_PLACE, whole((clips, rank, label_width), (0, 0, total // label_width - 1))] + [
         whole(array.shape) for array in carried.values()
@@ -1814,6 +1814,7 @@
     stream_ref, gain_ref,
     out_ref, grad_ref, mine_ref, theirs_ref,
     branch, grad_rows, rank9, grad_rank8, ga8_ref, gb9_ref, branch_in, grad_rows_in, stream_in, sems,
+    out_held, grad_held, out_sems,
 ):
     step = pl.program_id(0)
     copies = [
@@ -1857,16 +1858,23 @@
         half = ga8_ref.shape[1] // 2
         split_columns(meta, mine_ref, theirs_ref, 0, ga8_ref, 2 * hidden)
         split_columns(meta, mine_ref, theirs_ref, half, gb9_ref, 2 * hidden)
+        flushes = []
         for first in range(0, frames, block):
             span = slice(first, first + block)
             stream = stream_in[span]
             out = stream + (branch[span] + branch_in[span]) + mm_tn(last9[:, span], up9_ref[0])
-            out_ref[span] = out.astype(LOW)
+            out_held[span] = out.astype(LOW)
+            flushes.append(pltpu.make_async_copy(out_held.at[span], out_ref.at[span], out_sems.at[len(flushes)]))
+            flushes[-1].start()
             _, normed, inverse = norm_rows(stream, gain_ref[...])
             grad = grad_rows[span] + grad_rows_in[span] + mm_tn(last8[:, span], down8_ref[0])
-            grad_ref[span] = cot_ref[span].astype(WIDE) + norm_back(
+            grad_held[span] = cot_ref[span].astype(WIDE) + norm_back(
                 grad, gain_ref[...], normed, inverse
             )
+            flushes.append(pltpu.make_async_copy(grad_held.at[span], grad_ref.at[span], out_sems.at[len(flushes)]))
+            flushes[-1].start()
+        for copy in flushes:
+            copy.wait()
 
 
 def feed_other(
@@ -1908,7 +1916,7 @@
             IN_PLACE,
             whole((1, width)),
         ],
-        (full, full, whole((RANK_UNIT, width)), whole((RANK_UNIT, 2 * hidden + width))),
+        (IN_PLACE, IN_PLACE, whole((RANK_UNIT, width)), whole((RANK_UNIT, 2 * hidden + width))),
         (
             shaped((frames, width), LOW),
             shaped((frames, width), WIDE),
@@ -1926,6 +1934,9 @@
             wide,
             wide,
             pltpu.SemaphoreType.DMA((3,)),
+            pltpu.VMEM((frames, width), LOW),
+            wide,
+            pltpu.SemaphoreType.DMA((2 * (frames // min(128, frames)),)),
         ],
         8 * frames * width * hidden,
         4 * width * hidden + 24 * frames * width,
@@ -1959,7 +1970,7 @@
         slot_work(plan, slots, carried, everyone_ref, label_ref, earlier, refs[-5 - outs : -5], scratch)
 
 
-def last_norm(meta, x, own, received, grad, gain, everyone, plan, outs, slots, unit, carried, after):
+def last_norm(meta, x, own, received, grad, gain, everyone, labelled, plan, outs, slots, unit, carried, after):
     frames, width = x.shape
     block = min(256, frames // 2)
     half = frames // 2 // block
@@ -1971,7 +1982,7 @@
         lambda m, *refs: last_norm_body(m, half, slot_part, *refs),
         (2 * half,),
         [rows, rows, first, second, rows, whole((1, width))]
-        + slot_specs(everyone, carried)
+        + slot_specs(labelled, carried)
         + [IN_PLACE] * len(after),
         (rows,) + (IN_PLACE,) * len(outs),
         (shaped(x.shape, WIDE),) + slot_shapes(everyone, outs, slots),
@@ -1979,7 +1990,7 @@
         20 * x.size,
         16 * x.size,
         "last_norm",
-        (meta, x, own, *received, grad, gain, everyone, everyone, *carried.values(), *after),
+        (meta, x, own, *received, grad, gain, everyone, labelled, *carried.values(), *after),
     )
 
 
@@ -2148,10 +2159,10 @@
         for part in range(2)
     ]
     received = [swap(part) for part in partial_other]
-    labels = lax.dynamic_index_in_dim(early_all[:, :, -2 * HEAD_DIM :], place, axis=0, keepdims=False)
     late = jnp.concatenate(
-        [join(mine, [theirs]), seconds, join(text_mine_rank, [text_received_rank]), labels], axis=1
-    )
+        [join(mine, [theirs]), seconds, join(text_mine_rank, [text_received_rank])], axis=1
+    )
+    late, early_all = lax.optimization_barrier((late, early_all))
     late_all = lax.all_gather(late, "dp", axis=0)
     text_rows = project_back_heads(
         meta, text_heads_grad, cross_key_value_weight, cross_first_factors, cross_second_factors,
@@ -2179,6 +2190,7 @@
     input_grad, sum_self_a, sum_self_b, sum_cross_a, sum_cross_b = last_norm(
         meta, x, partial_own, received, grad_one, gain_one,
         late_all,
+        early_all,
         [(0, 0, 0), (1, 0, 1), (2, 0, 2), (0, 1, 0), (1, 1, 1), (2, 1, 2)]
         + [(5, 2, 1), (6, 2, 2), (5, 3, 1), (6, 3, 2)],
         [(3, unit), (3, unit), (3, unit), (3, unit)],

time: 399 us -> 397 us (level)
  transfers between devices with their start and end apart: 21 -> 21, of which waited for: 10 -> 10; matrix products, arithmetic and copies ran while one was open for 2% -> 3% of each run, Pallas kernels for 60% -> 60%
where the time goes in v6:
time: 397 us; the launch traced here: 391 us
  Pallas kernels  280 us (71%)
  waiting for transfers between devices  57.7 us (15%)
  starting transfers between devices  20.8 us (5%)
  between operations  14.6 us (4%)
  other arithmetic  9.6 us (2%)
  local copies, waits for them, and re-layouts  8.03 us (2%)
    pallas_call x22, Pallas kernels, call(): pl.pallas_call(body, grid_spec=pltpu.PrefetchScalarGridSpec(num_scalar_pr...  280 us
    ppermute x17, waiting for transfers between devices, swap(): return lax.ppermute(array, 'tensor', [(0, 1), (1, 0)])  39.5 us
    ppermute x17, starting transfers between devices, swap(): return lax.ppermute(array, 'tensor', [(0, 1), (1, 0)])  20.6 us
    all_gather x1, waiting for transfers between devices, on_pair(): gathered_two = lax.all_gather(share_two, 'dp', axis=0)  13.3 us
  transfers between devices with their start and end apart: 21, of which 10 were waited for; matrix products, arithmetic and copies ran while one was open for 3% of the time, Pallas kernels for 60%

profile of v6, /device:TPU:0, one launch (start us, length us, event | category | flops | bytes accessed | tf_op | source)
XLA Modules:
  0.0 390.6 jit_solution(3204048461710818400)
XLA Ops:
  26.6 4.8 %text_heads.1 = (bf16[2,64,768]{2,1,0:T(8,128)(2,1)}, bf16[2,16,64]{2,1,0:T(8,128)(2,1)}) custom-call(s32[12]{0:T(128)} %pad_add_fusion._.m.meta, bf16[64,1536]{1,0:T(8,128)(2,1)} %bitcast.39, bf16[2,1536,768]{2,1,0:T(8,128)(2,1)} %refs_1_.11, bf16[3,8,16,1536]{3,2,1,0:T(8,128)(2,1)} %refs_2_.9, bf16[3,8,16,768]{3,2,1,0:T(8,128)(2,1)} %refs_3_.9), custom_call_target="tpu_custom_call" | custom-call | flops 301989888 | bytes 5111808 | tf_op jit(solution)/shard_map/text_heads/pallas_call | solution.py:515
  31.4 10.6 %own_heads.1 = (bf16[3,512,768]{2,1,0:T(8,128)(2,1)}, bf16[3,16,512]{2,1,0:T(8,128)(2,1)}) custom-call(s32[12]{0:T(128)} %pad_add_fusion._.m.meta, bf16[512,1536]{1,0:T(8,128)(2,1)} %first_norm.1.act_ref.refs_0_, bf16[3,1536,768]{2,1,0:T(8,128)(2,1)} %refs_1_.10, bf16[3,8,16,1536]{3,2,1,0:T(8,128)(2,1)} %refs_2_.8, bf16[3,8,16,768]{3,2,1,0:T(8,128)(2,1)} %refs_3_.8), custom_call_target="tpu_custom_call" | custom-call | flops 3623878656 | bytes 11010048 | tf_op jit(solution)/shard_map/own_heads/pallas_call | solution.py:515
  42.1 8.5 %self_forward_own.1.refs_2_.part_ref = f32[6,2,88,512]{3,2,1,0:T(8,128)} custom-call(s32[12]{0:T(128)} %pad_add_fusion._.m.meta, bf16[3,512,768]{2,1,0:T(8,128)(2,1)} %get-tuple-element.112.own_ref, bf16[16,9984]{1,0:T(8,128)(2,1)} %picked_factors.1.after_ref), custom_call_target="tpu_custom_call" | custom-call | flops 805306368 | bytes 3932160 | tf_op jit(solution)/shard_map/self_forward_own/pallas_call | solution.py:515
  50.6 7.7 %collective-permute-done.3.refs_4_.act_ref.refs_1_ = bf16[512,1536]{1,0:T(8,128)(2,1)S(1)} collective-permute-done((bf16[512,1536]{1,0:T(8,128)(2,1)}, bf16[512,1536]{1,0:T(8,128)(2,1)S(1)}, u32[]{:S(2)}, u32[]{:S(2)}) %collective-permute-start.3) | collective-permute-done | bytes 1572896 | tf_op jit(solution)/shard_map/ppermute | solution.py:2040
  59.4 4.3 %feed_share.1.refs_0_ = bf16[4,96,1536]{2,1,0:T(8,128)(2,1)} custom-call(s32[12]{0:T(128)} %pad_add_fusion._.m.meta, bf16[3072,1536]{1,0:T(8,128)(2,1)} %down_weight_ref.1, bf16[1536,3072]{1,0:T(8,128)(2,1)} %up_weight_ref.1, f32[6,2,88,512]{3,2,1,0:T(8,128)} %self_forward_own.1.refs_2_.part_ref, ...), custom_call_target="tpu_custom_call" | custom-call | bytes 2359296 | tf_op jit(solution)/shard_map/feed_share/pallas_call | solution.py:515
  65.1 10.5 %other_heads.1 = (bf16[3,512,768]{2,1,0:T(8,128)(2,1)}, bf16[3,16,512]{2,1,0:T(8,128)(2,1)}) custom-call(s32[12]{0:T(128)} %pad_add_fusion._.m.meta, bf16[512,1536]{1,0:T(8,128)(2,1)} %copy-done.1, bf16[3,1536,768]{2,1,0:T(8,128)(2,1)} %refs_1_.10, bf16[3,8,16,1536]{3,2,1,0:T(8,128)(2,1)} %refs_2_.8, bf16[3,8,16,768]{3,2,1,0:T(8,128)(2,1)} %refs_3_.8, ...), custom_call_target="tpu_custom_call" | custom-call | flops 3623878656 | bytes 11010048 | tf_op jit(solution)/shard_map/other_heads/pallas_call | solution.py:515
  75.6 15.8 %self_forward.1 = (bf16[512,768]{1,0:T(8,128)(2,1)}, bf16[512,768]{1,0:T(8,128)(2,1)}, f32[512,768]{1,0:T(8,128)}, f32[512,768]{1,0:T(8,128)}) custom-call(s32[12]{0:T(128)} %pad_add_fusion._.m.meta, f32[6,2,88,512]{3,2,1,0:T(8,128)} %self_forward_own.1.refs_2_.part_ref, bf16[3,512,768]{2,1,0:T(8,128)(2,1)} %get-tuple-element.112.own_ref, ...), custom_call_target="tpu_custom_call" | custom-call | flops 2415919104 | bytes 7864320 | tf_op jit(solution)/shard_map/self_forward/pallas_call | solution.py:515
  97.7 19.7 %collective-permute-done.7.text_other_ref.refs_22_ = bf16[2,64,768]{2,1,0:T(8,128)(2,1)S(1)} collective-permute-done((bf16[2,64,768]{2,1,0:T(8,128)(2,1)S(1)}, bf16[2,64,768]{2,1,0:T(8,128)(2,1)S(1)}, u32[]{:S(2)}, u32[]{:S(2)}) %collective-permute-start.7) | collective-permute-done | bytes 196640 | tf_op jit(solution)/shard_map/ppermute | solution.py:2040
  121.8 23.6 %middle_forward.1 = (f32[512,1536]{1,0:T(8,128)}, f32[512,1536]{1,0:T(8,128)}, bf16[512,1536]{1,0:T(8,128)(2,1)}, bf16[512,768]{1,0:T(8,128)(2,1)}, bf16[512,768...) custom-call(s32[12]{0:T(128)} %pad_add_fusion._.m.meta, ...), custom_call_target="tpu_custom_call" | custom-call | flops 7247757312 | bytes 29884416 | tf_op jit(solution)/shard_map/middle_forward/pallas_call | solution.py:515
  145.4 33.1 %feed_own.1 = (f32[512,1536]{1,0:T(8,128)}, f32[512,1536]{1,0:T(8,128)}, f32[16,512]{1,0:T(8,128)}, f32[16,512]{1,0:T(8,128)}, bf16[16,512]{1,0:T(8,128)(2,1)}, ...) custom-call(s32[12]{0:T(128)} %pad_add_fusion._.m.meta, ...), custom_call_target="tpu_custom_call" | custom-call | flops 19327352832 | bytes 28311552 | tf_op jit(solution)/shard_map/feed_own/pallas_call | solution.py:515
  178.5 13.3 %all-gather.11.cloned.1.call-done = bf16[64,96,1536]{2,1,0:T(8,128)(2,1)} async-done(((bf16[4,96,1536]{2,1,0:T(8,128)(2,1)}), bf16[64,96,1536]{2,1,0:T(8,128)(2,1)}) %all-gather.11.cloned.1.call-update) | async-done | bytes 18874384 | tf_op jit(solution)/shard_map/all_gather | solution.py:2091
  191.8 34.5 %feed_other.1 = (bf16[512,1536]{1,0:T(8,128)(2,1)}, f32[512,1536]{1,0:T(8,128)}, f32[16,1536]{1,0:T(8,128)}, bf16[16,7680]{1,0:T(8,128)(2,1)}) custom-call(s32[12]{0:T(128)} %pad_add_fusion._.m.meta, bf16[512,1536]{1,0:T(8,128)(2,1)} %get-tuple-element.119.rows_ref.refs_0_, bf16[512,1536]{1,0:T(8,128)(2,1)} %bitcast.57, bf16[16,4,96,1536]{3,2,1,0:T(8,128)(2,1)} %bitcast.53, ...), custom_call_target="tpu_custom_call" | custom-call | flops 19327352832 | bytes 37748736 | tf_op jit(solution)/shard_map/feed_other/pallas_call | solution.py:515
  227.9 25.4 %middle_back.1 = (f32[512,1536]{1,0:T(8,128)}, bf16[512,768]{1,0:T(8,128)(2,1)}, bf16[256,768]{1,0:T(8,128)(2,1)}, bf16[256,768]{1,0:T(8,128)(2,1)}, f32[2,64,76...) custom-call(s32[12]{0:T(128)} %pad_add_fusion._.m.meta, ...), custom_call_target="tpu_custom_call" | custom-call | flops 7247757312 | bytes 33030144 | tf_op jit(solution)/shard_map/middle_back/pallas_call | solution.py:515
  254.1 5.3 %collective-permute-done.12 = bf16[16,4608]{1,0:T(8,128)(2,1)S(1)} collective-permute-done((bf16[16,4608]{1,0:T(8,128)(2,1)}, bf16[16,4608]{1,0:T(8,128)(2,1)S(1)}, u32[]{:S(2)}, u32[]{:S(2)}) %collective-permute-start.12) | collective-permute-done | bytes 147488 | tf_op jit(solution)/shard_map/ppermute | solution.py:2040
  263.4 14.7 %self_back_own.1 = (f32[3,768,512]{2,1,0:T(8,128)}, bf16[1,768,512]{2,1,0:T(8,128)(2,1)}, bf16[1,768,512]{2,1,0:T(8,128)(2,1)}, bf16[1,768,512]{2,1,0:T(8,128)(2...) custom-call(s32[12]{0:T(128)} %pad_add_fusion._.m.meta, ...), custom_call_target="tpu_custom_call" | custom-call | flops 20132659200 | bytes 19660800 | tf_op jit(solution)/shard_map/self_back_own/pallas_call | solution.py:515
  280.7 24.8 %self_back.1 = (bf16[3,512,768]{2,1,0:T(8,128)(2,1)}, bf16[3,512,768]{2,1,0:T(8,128)(2,1)}) custom-call(s32[12]{0:T(128)} %pad_add_fusion._.m.meta, f32[3,768,512]{2,1,0:T(8,128)} %get-tuple-element.148.part_ref, bf16[1,768,512]{2,1,0:T(8,128)(2,1)} %get-tuple-element.149.refs_0_, bf16[1,768,512]{2,1,0:T(8,128)(2,1)} %get-tuple-element.150.refs_1_, ...), custom_call_target="tpu_custom_call" | custom-call | flops 40265318400 | bytes 23592960 | tf_op jit(solution)/shard_map/self_back/pallas_call | solution.py:515
  305.5 6.3 %self_first.1 = (f32[16,2304]{1,0:T(8,128)}, bf16[16,2304]{1,0:T(8,128)(2,1)}) custom-call(s32[12]{0:T(128)} %pad_add_fusion._.m.meta, bf16[512,1536]{1,0:T(8,128)(2,1)} %first_norm.1.act_ref.refs_0_, bf16[512,1536]{1,0:T(8,128)(2,1)} %copy-done.1, bf16[3,512,768]{2,1,0:T(8,128)(2,1)} %get-tuple-element.166.refs_2_.refs_0_, ...), custom_call_target="tpu_custom_call" | custom-call | flops 452984832 | bytes 7864320 | tf_op jit(solution)/shard_map/self_first/pallas_call | solution.py:515
  313.3 5.1 %self_second.1.refs_4_ = bf16[16,2304]{1,0:T(8,128)(2,1)} custom-call(s32[12]{0:T(128)} %pad_add_fusion._.m.meta, bf16[3,16,512]{2,1,0:T(8,128)(2,1)} %get-tuple-element.170.refs_0_, bf16[3,16,512]{2,1,0:T(8,128)(2,1)} %get-tuple-element.171.refs_1_, bf16[3,512,768]{2,1,0:T(8,128)(2,1)} %get-tuple-element.166.refs_2_.refs_0_, ...), custom_call_target="tpu_custom_call" | custom-call | flops 75497472 | bytes 4718592 | tf_op jit(solution)/shard_map/self_second/pallas_call | solution.py:515
  322.6 8.1 %other_back.3.refs_4_ = bf16[256,1536]{1,0:T(8,128)(2,1)} custom-call(s32[12]{0:T(128)} %pad_add_fusion._.m.meta, bf16[3,512,768]{2,1,0:T(8,128)(2,1)} %get-tuple-element.167.refs_3_.refs_0_, bf16[3,1536,768]{2,1,0:T(8,128)(2,1)} %refs_1_.10, bf16[3,8,16,1536]{3,2,1,0:T(8,128)(2,1)} %refs_2_.8, bf16[3,8,16,768]{3,2,1,0:T(8,128)(2,1)} %refs_3_.8, ...), custom_call_target="tpu_custom_call" | custom-call | flops 1811939328 | bytes 9830400 | tf_op jit(solution)/shard_map/other_back/pallas_call | solution.py:515
  332.3 8.2 %other_back.2 = bf16[256,1536]{1,0:T(8,128)(2,1)} custom-call(s32[12]{0:T(128)} %pad_add_fusion._.m.meta, bf16[3,512,768]{2,1,0:T(8,128)(2,1)} %get-tuple-element.167.refs_3_.refs_0_, bf16[3,1536,768]{2,1,0:T(8,128)(2,1)} %refs_1_.10, bf16[3,8,16,1536]{3,2,1,0:T(8,128)(2,1)} %refs_2_.8, bf16[3,8,16,768]{3,2,1,0:T(8,128)(2,1)} %refs_3_.8, ...), custom_call_target="tpu_custom_call" | custom-call | flops 1811939328 | bytes 9830400 | tf_op jit(solution)/shard_map/other_back/pallas_call | solution.py:515
  341.8 5.5 %text_back.1 = f32[64,1536]{1,0:T(8,128)} custom-call(s32[12]{0:T(128)} %pad_add_fusion._.m.meta, bf16[2,64,768]{2,1,0:T(8,128)(2,1)} %fusion.1.refs_0_, bf16[2,1536,768]{2,1,0:T(8,128)(2,1)} %refs_1_.11, bf16[3,8,16,1536]{3,2,1,0:T(8,128)(2,1)} %refs_2_.9, bf16[3,8,16,768]{3,2,1,0:T(8,128)(2,1)} %refs_3_.9, bf16[256,1536]{1,0:T(8,128)(2,1)} %other_back.3.refs_4_), custom_call_target="tpu_custom_call" | custom-call | flops 301989888 | bytes 5308416 | tf_op jit(solution)/shard_map/text_back/pallas_call | solution.py:515
  349.8 11.8 %own_back.1.refs_2_.refs_1_ = f32[512,1536]{1,0:T(8,128)} custom-call(s32[12]{0:T(128)} %pad_add_fusion._.m.meta, bf16[3,512,768]{2,1,0:T(8,128)(2,1)} %get-tuple-element.166.refs_2_.refs_0_, bf16[3,1536,768]{2,1,0:T(8,128)(2,1)} %refs_1_.10, bf16[3,8,16,1536]{3,2,1,0:T(8,128)(2,1)} %refs_2_.8, bf16[3,8,16,768]{3,2,1,0:T(8,128)(2,1)} %refs_3_.8, ...), custom_call_target="tpu_custom_call" | custom-call | flops 3623878656 | bytes 12582912 | tf_op jit(solution)/shard_map/own_back/pallas_call | solution.py:515
  361.6 7.3 %early_slots.1 = (f32[1,8,16,768]{3,2,1,0:T(8,128)}, f32[1,8,16,768]{3,2,1,0:T(8,128)}, f32[2,8,16,768]{3,2,1,0:T(8,128)}, f32[2,8,16,768]{3,2,1,0:T(8,128)}, f3...) custom-call(s32[12]{0:T(128)} %pad_add_fusion._.m.meta, ...), custom_call_target="tpu_custom_call" | custom-call | bytes 6356992 | tf_op jit(solution)/shard_map/early_slots/pallas_call | solution.py:515
  372.7 10.8 %last_norm.1 = (f32[512,1536]{1,0:T(8,128)}, f32[3,8,16,768]{3,2,1,0:T(8,128)}, f32[3,8,16,768]{3,2,1,0:T(8,128)}, f32[3,8,16,768]{3,2,1,0:T(8,128)}, f32[3,8,16,768]{3,2,1,0:T(8,128)}) custom-call(s32[12]{0:T(128)} %pad_add_fusion._.m.meta, bf16[512,1536]{1,0:T(8,128)(2,1)} %bitcast.37, f32[512,1536]{1,0:T(8,128)} %own_back.1.refs_2_.refs_1_, ...), custom_call_target="tpu_custom_call" | custom-call | flops 15728640 | bytes 12582912 | tf_op jit(solution)/shard_map/last_norm/pallas_call | solution.py:515
  (123 shorter events, 56.3 us)
Async XLA Ops:
  7.2 113.7 %all-gather.9.cloned.1.call-start = ((), (), s32[]{:S(2)}) async-start(), calls=%async_computation | async-start | bytes 7520256 | tf_op jit(solution)/shard_map/all_gather | solution.py:2057
  8.3 12.4 %collective-permute-start.2 = (bf16[96,768]{1,0:T(8,128)(2,1)S(1)}, bf16[96,768]{1,0:T(8,128)(2,1)S(1)}, u32[]{:S(2)}, u32[]{:S(2)}) collective-permute-start(bf16[96,768]{1,0:T(8,128)(2,1)S(1)} %bitcast.50), channel_id=1, source_target_pairs={{0,1},{1,0},{2,3},{3,2},{4,5},{5,4},{6,7},{7,6},{8,9},{9,8},{10,11... | collective-permute-start | bytes 442376 | tf_op jit(solution)/shard_map/ppermute | solution.py:2040
  11.4 9.3 %collective-permute-start = (bf16[96,768]{1,0:T(8,128)(2,1)S(1)}, bf16[96,768]{1,0:T(8,128)(2,1)S(1)}, u32[]{:S(2)}, u32[]{:S(2)}) collective-permute-start(bf16[96,768]{1,0:T(8,128)(2,1)S(1)} %bitcast.51), channel_id=1, source_target_pairs={{0,1},{1,0},{2,3},{3,2},{4,5},{5,4},{6,7},{7,6},{8,9},{9,8},{10,11... | collective-permute-start | bytes 442376 | tf_op jit(solution)/shard_map/ppermute | solution.py:2040
  12.4 9.1 %collective-permute-start.1 = (bf16[96,768]{1,0:T(8,128)(2,1)S(1)}, bf16[96,768]{1,0:T(8,128)(2,1)S(1)}, u32[]{:S(2)}, u32[]{:S(2)}) collective-permute-start(bf16[96,768]{1,0:T(8,128)(2,1)S(1)} %constant_dynamic-slice_fusion.1), channel_id=1, source_target_pairs={{0,1},{1,0},{2,3},{3,2},{4,5},{5,4},{6,7},{7,6},{8,9},{9,8},{10,11... | collective-permute-start | bytes 442376 | tf_op jit(solution)/shard_map/ppermute | solution.py:2040
  22.3 169.5 %all-gather.11.cloned.1.call-start = ((), (), s32[]{:S(2)}) async-start(), calls=%async_computation.1 | async-start | bytes 20054016 | tf_op jit(solution)/shard_map/all_gather | solution.py:2091
  22.4 35.9 %collective-permute-start.3 = (bf16[512,1536]{1,0:T(8,128)(2,1)}, bf16[512,1536]{1,0:T(8,128)(2,1)S(1)}, u32[]{:S(2)}, u32[]{:S(2)}) collective-permute-start(bf16[512,1536]{1,0:T(8,128)(2,1)} %first_norm.1.act_ref.refs_0_), channel_id=1, source_target_pairs={{0,1},{1,0},{2,3},{3,2},{4,5},{5,4},{6,7},{7,6},{8,9},{9,8},{10,11... | collective-permute-start | bytes 4718600 | tf_op jit(solution)/shard_map/ppermute | solution.py:2040
  63.7 27.8 %collective-permute-start.4 = (bf16[4,96,1536]{2,1,0:T(8,128)(2,1)}, bf16[4,96,1536]{2,1,0:T(8,128)(2,1)S(1)}, u32[]{:S(2)}, u32[]{:S(2)}) collective-permute-start(bf16[4,96,1536]{2,1,0:T(8,128)(2,1)} %feed_share.1.refs_0_), channel_id=1, source_target_pairs={{0,1},{1,0},{2,3},{3,2},{4,5},{5,4},{6,7},{7,6},{8,9},{9,8},{10,11... | collective-permute-start | bytes 3538952 | tf_op jit(solution)/shard_map/ppermute | solution.py:2040
  92.5 230.1 %all-gather.13.cloned.1.call-start = ((), (), s32[]{:S(2)}) async-start(), calls=%async_computation.2 | async-start | bytes 6754304 | tf_op jit(solution)/shard_map/all_gather | solution.py:2137
  92.5 28.3 %collective-permute-start.5 = (bf16[512,768]{1,0:T(8,128)(2,1)}, bf16[512,768]{1,0:T(8,128)(2,1)S(1)}, u32[]{:S(2)}, u32[]{:S(2)}) collective-permute-start(bf16[512,768]{1,0:T(8,128)(2,1)} %get-tuple-element.117.refs_8_), channel_id=1, source_target_pairs={{0,1},{1,0},{2,3},{3,2},{4,5},{5,4},{6,7},{7,6},{8,9},{9,8},{10,11... | collective-permute-start | bytes 2359304 | tf_op jit(solution)/shard_map/ppermute | solution.py:2040
  93.0 24.4 %collective-permute-start.7 = (bf16[2,64,768]{2,1,0:T(8,128)(2,1)S(1)}, bf16[2,64,768]{2,1,0:T(8,128)(2,1)S(1)}, u32[]{:S(2)}, u32[]{:S(2)}) collective-permute-start(bf16[2,64,768]{2,1,0:T(8,128)(2,1)S(1)} %copy-done.9), channel_id=1, source_target_pairs={{0,1},{1,0},{2,3},{3,2},{4,5},{5,4},{6,7},{7,6},{8,9},{9,8},{10,11... | collective-permute-start | bytes 589832 | tf_op jit(solution)/shard_map/ppermute | solution.py:2040
  94.6 26.2 %collective-permute-start.6 = (bf16[16,9984]{1,0:T(8,128)(2,1)S(1)}, bf16[16,9984]{1,0:T(8,128)(2,1)S(1)}, u32[]{:S(2)}, u32[]{:S(2)}) collective-permute-start(bf16[16,9984]{1,0:T(8,128)(2,1)S(1)} %copy-done.3), channel_id=1, source_target_pairs={{0,1},{1,0},{2,3},{3,2},{4,5},{5,4},{6,7},{7,6},{8,9},{9,8},{10,11... | collective-permute-start | bytes 958472 | tf_op jit(solution)/shard_map/ppermute | solution.py:2040
  226.3 27.0 %collective-permute-start.8 = (bf16[16,7680]{1,0:T(8,128)(2,1)}, bf16[16,7680]{1,0:T(8,128)(2,1)S(1)}, u32[]{:S(2)}, u32[]{:S(2)}) collective-permute-start(bf16[16,7680]{1,0:T(8,128)(2,1)} %get-tuple-element.129), channel_id=1, source_target_pairs={{0,1},{1,0},{2,3},{3,2},{4,5},{5,4},{6,7},{7,6},{8,9},{9,8},{10,11... | collective-permute-start | bytes 737288 | tf_op jit(solution)/shard_map/ppermute | solution.py:2040
  227.9 26.1 %copy-start.13 = (f32[16,3072]{1,0:T(8,128)S(1)}, f32[16,3072]{1,0:T(8,128)}, u32[]{:S(2)}) copy-start(f32[16,3072]{1,0:T(8,128)} %get-tuple-element.164) | copy-start | bytes 589828
  227.9 26.1 %copy-start.14 = (f32[16,3072]{1,0:T(8,128)S(1)}, f32[16,3072]{1,0:T(8,128)}, u32[]{:S(2)}) copy-start(f32[16,3072]{1,0:T(8,128)} %get-tuple-element.163) | copy-start | bytes 589828
  227.9 26.1 %copy-start.16 = (f32[16,1536]{1,0:T(8,128)S(1)}, f32[16,1536]{1,0:T(8,128)}, u32[]{:S(2)}) copy-start(f32[16,1536]{1,0:T(8,128)} %get-tuple-element.161) | copy-start | bytes 294916
  253.4 6.0 %collective-permute-start.12 = (bf16[16,4608]{1,0:T(8,128)(2,1)}, bf16[16,4608]{1,0:T(8,128)(2,1)S(1)}, u32[]{:S(2)}, u32[]{:S(2)}) collective-permute-start(bf16[16,4608]{1,0:T(8,128)(2,1)} %get-tuple-element.160), channel_id=1, source_target_pairs={{0,1},{1,0},{2,3},{3,2},{4,5},{5,4},{6,7},{7,6},{8,9},{9,8},{10,11... | collective-permute-start | bytes 442376 | tf_op jit(solution)/shard_map/ppermute | solution.py:2040
  261.2 111.5 %all-gather.15.cloned.1.call-start = ((), (), s32[]{:S(2)}) async-start(), calls=%async_computation.3 | async-start | bytes 4177920 | tf_op jit(solution)/shard_map/all_gather | solution.py:2166
  261.3 16.8 %collective-permute-start.10 = (bf16[256,768]{1,0:T(8,128)(2,1)S(1)}, bf16[256,768]{1,0:T(8,128)(2,1)S(1)}, u32[]{:S(2)}, u32[]{:S(2)}) collective-permute-start(bf16[256,768]{1,0:T(8,128)(2,1)S(1)} %copy-done.21), channel_id=1, source_target_pairs={{0,1},{1,0},{2,3},{3,2},{4,5},{5,4},{6,7},{7,6},{8,9},{9,8},{10,11... | collective-permute-start | bytes 1179656 | tf_op jit(solution)/shard_map/ppermute | solution.py:2040
  261.9 18.0 %collective-permute-start.9 = (bf16[256,768]{1,0:T(8,128)(2,1)S(1)}, bf16[256,768]{1,0:T(8,128)(2,1)S(1)}, u32[]{:S(2)}, u32[]{:S(2)}) collective-permute-start(bf16[256,768]{1,0:T(8,128)(2,1)S(1)} %copy-done.20), channel_id=1, source_target_pairs={{0,1},{1,0},{2,3},{3,2},{4,5},{5,4},{6,7},{7,6},{8,9},{9,8},{10,11... | collective-permute-start | bytes 1179656 | tf_op jit(solution)/shard_map/ppermute | solution.py:2040
  279.9 25.5 %collective-permute-start.11 = (bf16[192,768]{1,0:T(8,128)(2,1)S(1)}, bf16[192,768]{1,0:T(8,128)(2,1)S(1)}, u32[]{:S(2)}, u32[]{:S(2)}) collective-permute-start(bf16[192,768]{1,0:T(8,128)(2,1)S(1)} %copy-done.24), channel_id=1, source_target_pairs={{0,1},{1,0},{2,3},{3,2},{4,5},{5,4},{6,7},{7,6},{8,9},{9,8},{10,11... | collective-permute-start | bytes 884744 | tf_op jit(solution)/shard_map/ppermute | solution.py:2040
  311.8 6.6 %collective-permute-start.13 = (bf16[16,2304]{1,0:T(8,128)(2,1)}, bf16[16,2304]{1,0:T(8,128)(2,1)S(1)}, u32[]{:S(2)}, u32[]{:S(2)}) collective-permute-start(bf16[16,2304]{1,0:T(8,128)(2,1)} %get-tuple-element.169.refs_4_), channel_id=1, source_target_pairs={{0,1},{1,0},{2,3},{3,2},{4,5},{5,4},{6,7},{7,6},{8,9},{9,8},{10,11... | collective-permute-start | bytes 221192 | tf_op jit(solution)/shard_map/ppermute | solution.py:2040
  330.8 38.9 %collective-permute-start.15 = (bf16[256,1536]{1,0:T(8,128)(2,1)}, bf16[256,1536]{1,0:T(8,128)(2,1)S(1)}, u32[]{:S(2)}, u32[]{:S(2)}) collective-permute-start(bf16[256,1536]{1,0:T(8,128)(2,1)} %other_back.3.refs_4_), channel_id=1, source_target_pairs={{0,1},{1,0},{2,3},{3,2},{4,5},{5,4},{6,7},{7,6},{8,9},{9,8},{10,11... | collective-permute-start | bytes 2359304 | tf_op jit(solution)/shard_map/ppermute | solution.py:2040
  340.4 29.2 %collective-permute-start.14 = (bf16[256,1536]{1,0:T(8,128)(2,1)}, bf16[256,1536]{1,0:T(8,128)(2,1)S(1)}, u32[]{:S(2)}, u32[]{:S(2)}) collective-permute-start(bf16[256,1536]{1,0:T(8,128)(2,1)} %other_back.2), channel_id=1, source_target_pairs={{0,1},{1,0},{2,3},{3,2},{4,5},{5,4},{6,7},{7,6},{8,9},{9,8},{10,11... | collective-permute-start | bytes 2359304 | tf_op jit(solution)/shard_map/ppermute | solution.py:2040
  348.3 21.4 %collective-permute-start.16 = (bf16[64,768]{1,0:T(8,128)(2,1)S(1)}, bf16[64,768]{1,0:T(8,128)(2,1)S(1)}, u32[]{:S(2)}, u32[]{:S(2)}) collective-permute-start(bf16[64,768]{1,0:T(8,128)(2,1)S(1)} %select_convert_fusion), channel_id=1, source_target_pairs={{0,1},{1,0},{2,3},{3,2},{4,5},{5,4},{6,7},{7,6},{8,9},{9,8},{10,11... | collective-permute-start | bytes 294920 | tf_op jit(solution)/shard_map/ppermute | solution.py:2040
  (23 other events, 207.5 us)
Sparse Core Ops, SparseCore 0:
  22.5 68.1 all-gather.8
  92.8 99.0 all-gather.10
  261.4 61.1 all-gather.12
  325.3 47.3 all-gather.14

commit v7 on v6

--- a/solution.py
+++ b/solution.py
@@ -846,7 +846,7 @@
     ]
 
 
-def slot_work(plan, slots, carried, everyone_ref, label_ref, earlier, out_refs, scratch):
+def slot_work(plan, slots, carried, everyone_ref, label_ref, earlier, out_refs, scratch, wait=True):
     names, arrived, totals, in_sems, out_sems = scratch
     clips, rank, unit = arrived.shape[1:]
     incoming = slot_copies(unit, len(plan), everyone_ref, arrived, in_sems)
@@ -866,8 +866,17 @@
         copy = pltpu.make_async_copy(totals.at[number], target, out_sems.at[number])
         copy.start()
         outgoing.append(copy)
-    for copy in outgoing:
-        copy.wait()
+    if wait:
+        for copy in outgoing:
+            copy.wait()
+
+
+def slot_wait(plan, unit, carried, earlier, out_refs, scratch):
+    totals, out_sems = scratch[2], scratch[4]
+    for number, (which, ref) in enumerate(zip(carried, earlier)):
+        pltpu.make_async_copy(ref.at[0], out_refs[which].at[0], out_sems.at[len(plan) + number]).wait()
+    for number, (_, which, place) in enumerate(plan):
+        pltpu.make_async_copy(totals.at[number], out_refs[which].at[place], out_sems.at[number]).wait()
 
 
 def slot_scratch(everyone, plan, slots, unit, carried):
@@ -1965,9 +1974,13 @@
     total = own_ref[...] + other
     out_ref[...] = grad_ref[...] + norm_back(total, gain_ref[...], normed, inverse)
 
+    @pl.when(step == 0)
+    def _():
+        slot_work(plan, slots, carried, everyone_ref, label_ref, earlier, refs[-5 - outs : -5], scratch, False)
+
     @pl.when(step == 2 * half - 1)
     def _():
-        slot_work(plan, slots, carried, everyone_ref, label_ref, earlier, refs[-5 - outs : -5], scratch)
+        slot_wait(plan, scratch[1].shape[3], carried, earlier, refs[-5 - outs : -5], scratch)
 
 
 def last_norm(meta, x, own, received, grad, gain, everyone, labelled, plan, outs, slots, unit, carried, after):

time: 397 us -> 397 us (level)
  no operation moved by 1% of the time
where the time goes in v7:
time: 397 us; the launch traced here: 390 us
  Pallas kernels  279 us (70%)
  waiting for transfers between devices  57.7 us (15%)
  starting transfers between devices  20.8 us (5%)
  between operations  14.6 us (4%)
  other arithmetic  9.6 us (2%)
  local copies, waits for them, and re-layouts  8.03 us (2%)
    pallas_call x22, Pallas kernels, call(): pl.pallas_call(body, grid_spec=pltpu.PrefetchScalarGridSpec(num_scalar_pr...  279 us
    ppermute x17, waiting for transfers between devices, swap(): return lax.ppermute(array, 'tensor', [(0, 1), (1, 0)])  39.5 us
    ppermute x17, starting transfers between devices, swap(): return lax.ppermute(array, 'tensor', [(0, 1), (1, 0)])  20.6 us
    all_gather x1, waiting for transfers between devices, on_pair(): gathered_two = lax.all_gather(share_two, 'dp', axis=0)  13.3 us
  transfers between devices with their start and end apart: 21, of which 10 were waited for; matrix products, arithmetic and copies ran while one was open for 3% of the time, Pallas kernels for 60%

profile of v7, /device:TPU:0, one launch (start us, length us, event | category | flops | bytes accessed | tf_op | source)
XLA Modules:
  0.0 390.1 jit_solution(3235914403077923099)
XLA Ops:
  26.6 4.8 %text_heads.1 = (bf16[2,64,768]{2,1,0:T(8,128)(2,1)}, bf16[2,16,64]{2,1,0:T(8,128)(2,1)}) custom-call(s32[12]{0:T(128)} %pad_add_fusion._.m.meta, bf16[64,1536]{1,0:T(8,128)(2,1)} %bitcast.39, bf16[2,1536,768]{2,1,0:T(8,128)(2,1)} %refs_1_.11, bf16[3,8,16,1536]{3,2,1,0:T(8,128)(2,1)} %refs_2_.9, bf16[3,8,16,768]{3,2,1,0:T(8,128)(2,1)} %refs_3_.9), custom_call_target="tpu_custom_call" | custom-call | flops 301989888 | bytes 5111808 | tf_op jit(solution)/shard_map/text_heads/pallas_call | solution.py:515
  31.4 10.6 %own_heads.1 = (bf16[3,512,768]{2,1,0:T(8,128)(2,1)}, bf16[3,16,512]{2,1,0:T(8,128)(2,1)}) custom-call(s32[12]{0:T(128)} %pad_add_fusion._.m.meta, bf16[512,1536]{1,0:T(8,128)(2,1)} %first_norm.1.act_ref.refs_0_, bf16[3,1536,768]{2,1,0:T(8,128)(2,1)} %refs_1_.10, bf16[3,8,16,1536]{3,2,1,0:T(8,128)(2,1)} %refs_2_.8, bf16[3,8,16,768]{3,2,1,0:T(8,128)(2,1)} %refs_3_.8), custom_call_target="tpu_custom_call" | custom-call | flops 3623878656 | bytes 11010048 | tf_op jit(solution)/shard_map/own_heads/pallas_call | solution.py:515
  42.1 8.5 %self_forward_own.1.refs_2_.part_ref = f32[6,2,88,512]{3,2,1,0:T(8,128)} custom-call(s32[12]{0:T(128)} %pad_add_fusion._.m.meta, bf16[3,512,768]{2,1,0:T(8,128)(2,1)} %get-tuple-element.112.own_ref, bf16[16,9984]{1,0:T(8,128)(2,1)} %picked_factors.1.after_ref), custom_call_target="tpu_custom_call" | custom-call | flops 805306368 | bytes 3932160 | tf_op jit(solution)/shard_map/self_forward_own/pallas_call | solution.py:515
  50.6 7.7 %collective-permute-done.3.refs_4_.act_ref.refs_1_ = bf16[512,1536]{1,0:T(8,128)(2,1)S(1)} collective-permute-done((bf16[512,1536]{1,0:T(8,128)(2,1)}, bf16[512,1536]{1,0:T(8,128)(2,1)S(1)}, u32[]{:S(2)}, u32[]{:S(2)}) %collective-permute-start.3) | collective-permute-done | bytes 1572896 | tf_op jit(solution)/shard_map/ppermute | solution.py:2053
  59.4 4.3 %feed_share.1.refs_0_ = bf16[4,96,1536]{2,1,0:T(8,128)(2,1)} custom-call(s32[12]{0:T(128)} %pad_add_fusion._.m.meta, bf16[3072,1536]{1,0:T(8,128)(2,1)} %down_weight_ref.1, bf16[1536,3072]{1,0:T(8,128)(2,1)} %up_weight_ref.1, f32[6,2,88,512]{3,2,1,0:T(8,128)} %self_forward_own.1.refs_2_.part_ref, ...), custom_call_target="tpu_custom_call" | custom-call | bytes 2359296 | tf_op jit(solution)/shard_map/feed_share/pallas_call | solution.py:515
  65.1 10.5 %other_heads.1 = (bf16[3,512,768]{2,1,0:T(8,128)(2,1)}, bf16[3,16,512]{2,1,0:T(8,128)(2,1)}) custom-call(s32[12]{0:T(128)} %pad_add_fusion._.m.meta, bf16[512,1536]{1,0:T(8,128)(2,1)} %copy-done.1, bf16[3,1536,768]{2,1,0:T(8,128)(2,1)} %refs_1_.10, bf16[3,8,16,1536]{3,2,1,0:T(8,128)(2,1)} %refs_2_.8, bf16[3,8,16,768]{3,2,1,0:T(8,128)(2,1)} %refs_3_.8, ...), custom_call_target="tpu_custom_call" | custom-call | flops 3623878656 | bytes 11010048 | tf_op jit(solution)/shard_map/other_heads/pallas_call | solution.py:515
  75.6 15.8 %self_forward.1 = (bf16[512,768]{1,0:T(8,128)(2,1)}, bf16[512,768]{1,0:T(8,128)(2,1)}, f32[512,768]{1,0:T(8,128)}, f32[512,768]{1,0:T(8,128)}) custom-call(s32[12]{0:T(128)} %pad_add_fusion._.m.meta, f32[6,2,88,512]{3,2,1,0:T(8,128)} %self_forward_own.1.refs_2_.part_ref, bf16[3,512,768]{2,1,0:T(8,128)(2,1)} %get-tuple-element.112.own_ref, ...), custom_call_target="tpu_custom_call" | custom-call | flops 2415919104 | bytes 7864320 | tf_op jit(solution)/shard_map/self_forward/pallas_call | solution.py:515
  97.7 19.7 %collective-permute-done.7.text_other_ref.refs_22_ = bf16[2,64,768]{2,1,0:T(8,128)(2,1)S(1)} collective-permute-done((bf16[2,64,768]{2,1,0:T(8,128)(2,1)S(1)}, bf16[2,64,768]{2,1,0:T(8,128)(2,1)S(1)}, u32[]{:S(2)}, u32[]{:S(2)}) %collective-permute-start.7) | collective-permute-done | bytes 196640 | tf_op jit(solution)/shard_map/ppermute | solution.py:2053
  121.8 23.6 %middle_forward.1 = (f32[512,1536]{1,0:T(8,128)}, f32[512,1536]{1,0:T(8,128)}, bf16[512,1536]{1,0:T(8,128)(2,1)}, bf16[512,768]{1,0:T(8,128)(2,1)}, bf16[512,768...) custom-call(s32[12]{0:T(128)} %pad_add_fusion._.m.meta, ...), custom_call_target="tpu_custom_call" | custom-call | flops 7247757312 | bytes 29884416 | tf_op jit(solution)/shard_map/middle_forward/pallas_call | solution.py:515
  145.4 33.1 %feed_own.1 = (f32[512,1536]{1,0:T(8,128)}, f32[512,1536]{1,0:T(8,128)}, f32[16,512]{1,0:T(8,128)}, f32[16,512]{1,0:T(8,128)}, bf16[16,512]{1,0:T(8,128)(2,1)}, ...) custom-call(s32[12]{0:T(128)} %pad_add_fusion._.m.meta, ...), custom_call_target="tpu_custom_call" | custom-call | flops 19327352832 | bytes 28311552 | tf_op jit(solution)/shard_map/feed_own/pallas_call | solution.py:515
  178.5 13.3 %all-gather.11.cloned.1.call-done = bf16[64,96,1536]{2,1,0:T(8,128)(2,1)} async-done(((bf16[4,96,1536]{2,1,0:T(8,128)(2,1)}), bf16[64,96,1536]{2,1,0:T(8,128)(2,1)}) %all-gather.11.cloned.1.call-update) | async-done | bytes 18874384 | tf_op jit(solution)/shard_map/all_gather | solution.py:2104
  191.8 34.5 %feed_other.1 = (bf16[512,1536]{1,0:T(8,128)(2,1)}, f32[512,1536]{1,0:T(8,128)}, f32[16,1536]{1,0:T(8,128)}, bf16[16,7680]{1,0:T(8,128)(2,1)}) custom-call(s32[12]{0:T(128)} %pad_add_fusion._.m.meta, bf16[512,1536]{1,0:T(8,128)(2,1)} %get-tuple-element.119.rows_ref.refs_0_, bf16[512,1536]{1,0:T(8,128)(2,1)} %bitcast.57, bf16[16,4,96,1536]{3,2,1,0:T(8,128)(2,1)} %bitcast.53, ...), custom_call_target="tpu_custom_call" | custom-call | flops 19327352832 | bytes 37748736 | tf_op jit(solution)/shard_map/feed_other/pallas_call | solution.py:515
  227.9 25.4 %middle_back.1 = (f32[512,1536]{1,0:T(8,128)}, bf16[512,768]{1,0:T(8,128)(2,1)}, bf16[256,768]{1,0:T(8,128)(2,1)}, bf16[256,768]{1,0:T(8,128)(2,1)}, f32[2,64,76...) custom-call(s32[12]{0:T(128)} %pad_add_fusion._.m.meta, ...), custom_call_target="tpu_custom_call" | custom-call | flops 7247757312 | bytes 33030144 | tf_op jit(solution)/shard_map/middle_back/pallas_call | solution.py:515
  254.1 5.3 %collective-permute-done.12 = bf16[16,4608]{1,0:T(8,128)(2,1)S(1)} collective-permute-done((bf16[16,4608]{1,0:T(8,128)(2,1)}, bf16[16,4608]{1,0:T(8,128)(2,1)S(1)}, u32[]{:S(2)}, u32[]{:S(2)}) %collective-permute-start.12) | collective-permute-done | bytes 147488 | tf_op jit(solution)/shard_map/ppermute | solution.py:2053
  263.4 14.7 %self_back_own.1 = (f32[3,768,512]{2,1,0:T(8,128)}, bf16[1,768,512]{2,1,0:T(8,128)(2,1)}, bf16[1,768,512]{2,1,0:T(8,128)(2,1)}, bf16[1,768,512]{2,1,0:T(8,128)(2...) custom-call(s32[12]{0:T(128)} %pad_add_fusion._.m.meta, ...), custom_call_target="tpu_custom_call" | custom-call | flops 20132659200 | bytes 19660800 | tf_op jit(solution)/shard_map/self_back_own/pallas_call | solution.py:515
  280.7 24.8 %self_back.1 = (bf16[3,512,768]{2,1,0:T(8,128)(2,1)}, bf16[3,512,768]{2,1,0:T(8,128)(2,1)}) custom-call(s32[12]{0:T(128)} %pad_add_fusion._.m.meta, f32[3,768,512]{2,1,0:T(8,128)} %get-tuple-element.148.part_ref, bf16[1,768,512]{2,1,0:T(8,128)(2,1)} %get-tuple-element.149.refs_0_, bf16[1,768,512]{2,1,0:T(8,128)(2,1)} %get-tuple-element.150.refs_1_, ...), custom_call_target="tpu_custom_call" | custom-call | flops 40265318400 | bytes 23592960 | tf_op jit(solution)/shard_map/self_back/pallas_call | solution.py:515
  305.5 6.3 %self_first.1 = (f32[16,2304]{1,0:T(8,128)}, bf16[16,2304]{1,0:T(8,128)(2,1)}) custom-call(s32[12]{0:T(128)} %pad_add_fusion._.m.meta, bf16[512,1536]{1,0:T(8,128)(2,1)} %first_norm.1.act_ref.refs_0_, bf16[512,1536]{1,0:T(8,128)(2,1)} %copy-done.1, bf16[3,512,768]{2,1,0:T(8,128)(2,1)} %get-tuple-element.166.refs_2_.refs_0_, ...), custom_call_target="tpu_custom_call" | custom-call | flops 452984832 | bytes 7864320 | tf_op jit(solution)/shard_map/self_first/pallas_call | solution.py:515
  313.3 5.1 %self_second.1.refs_4_ = bf16[16,2304]{1,0:T(8,128)(2,1)} custom-call(s32[12]{0:T(128)} %pad_add_fusion._.m.meta, bf16[3,16,512]{2,1,0:T(8,128)(2,1)} %get-tuple-element.170.refs_0_, bf16[3,16,512]{2,1,0:T(8,128)(2,1)} %get-tuple-element.171.refs_1_, bf16[3,512,768]{2,1,0:T(8,128)(2,1)} %get-tuple-element.166.refs_2_.refs_0_, ...), custom_call_target="tpu_custom_call" | custom-call | flops 75497472 | bytes 4718592 | tf_op jit(solution)/shard_map/self_second/pallas_call | solution.py:515
  322.6 8.1 %other_back.3.refs_4_ = bf16[256,1536]{1,0:T(8,128)(2,1)} custom-call(s32[12]{0:T(128)} %pad_add_fusion._.m.meta, bf16[3,512,768]{2,1,0:T(8,128)(2,1)} %get-tuple-element.167.refs_3_.refs_0_, bf16[3,1536,768]{2,1,0:T(8,128)(2,1)} %refs_1_.10, bf16[3,8,16,1536]{3,2,1,0:T(8,128)(2,1)} %refs_2_.8, bf16[3,8,16,768]{3,2,1,0:T(8,128)(2,1)} %refs_3_.8, ...), custom_call_target="tpu_custom_call" | custom-call | flops 1811939328 | bytes 9830400 | tf_op jit(solution)/shard_map/other_back/pallas_call | solution.py:515
  332.3 8.2 %other_back.2 = bf16[256,1536]{1,0:T(8,128)(2,1)} custom-call(s32[12]{0:T(128)} %pad_add_fusion._.m.meta, bf16[3,512,768]{2,1,0:T(8,128)(2,1)} %get-tuple-element.167.refs_3_.refs_0_, bf16[3,1536,768]{2,1,0:T(8,128)(2,1)} %refs_1_.10, bf16[3,8,16,1536]{3,2,1,0:T(8,128)(2,1)} %refs_2_.8, bf16[3,8,16,768]{3,2,1,0:T(8,128)(2,1)} %refs_3_.8, ...), custom_call_target="tpu_custom_call" | custom-call | flops 1811939328 | bytes 9830400 | tf_op jit(solution)/shard_map/other_back/pallas_call | solution.py:515
  341.8 5.5 %text_back.1 = f32[64,1536]{1,0:T(8,128)} custom-call(s32[12]{0:T(128)} %pad_add_fusion._.m.meta, bf16[2,64,768]{2,1,0:T(8,128)(2,1)} %fusion.1.refs_0_, bf16[2,1536,768]{2,1,0:T(8,128)(2,1)} %refs_1_.11, bf16[3,8,16,1536]{3,2,1,0:T(8,128)(2,1)} %refs_2_.9, bf16[3,8,16,768]{3,2,1,0:T(8,128)(2,1)} %refs_3_.9, bf16[256,1536]{1,0:T(8,128)(2,1)} %other_back.3.refs_4_), custom_call_target="tpu_custom_call" | custom-call | flops 301989888 | bytes 5308416 | tf_op jit(solution)/shard_map/text_back/pallas_call | solution.py:515
  349.8 11.8 %own_back.1.refs_2_.refs_1_ = f32[512,1536]{1,0:T(8,128)} custom-call(s32[12]{0:T(128)} %pad_add_fusion._.m.meta, bf16[3,512,768]{2,1,0:T(8,128)(2,1)} %get-tuple-element.166.refs_2_.refs_0_, bf16[3,1536,768]{2,1,0:T(8,128)(2,1)} %refs_1_.10, bf16[3,8,16,1536]{3,2,1,0:T(8,128)(2,1)} %refs_2_.8, bf16[3,8,16,768]{3,2,1,0:T(8,128)(2,1)} %refs_3_.8, ...), custom_call_target="tpu_custom_call" | custom-call | flops 3623878656 | bytes 12582912 | tf_op jit(solution)/shard_map/own_back/pallas_call | solution.py:515
  361.6 7.3 %early_slots.1 = (f32[1,8,16,768]{3,2,1,0:T(8,128)}, f32[1,8,16,768]{3,2,1,0:T(8,128)}, f32[2,8,16,768]{3,2,1,0:T(8,128)}, f32[2,8,16,768]{3,2,1,0:T(8,128)}, f3...) custom-call(s32[12]{0:T(128)} %pad_add_fusion._.m.meta, ...), custom_call_target="tpu_custom_call" | custom-call | bytes 6356992 | tf_op jit(solution)/shard_map/early_slots/pallas_call | solution.py:515
  372.7 10.3 %last_norm.1 = (f32[512,1536]{1,0:T(8,128)}, f32[3,8,16,768]{3,2,1,0:T(8,128)}, f32[3,8,16,768]{3,2,1,0:T(8,128)}, f32[3,8,16,768]{3,2,1,0:T(8,128)}, f32[3,8,16,768]{3,2,1,0:T(8,128)}) custom-call(s32[12]{0:T(128)} %pad_add_fusion._.m.meta, bf16[512,1536]{1,0:T(8,128)(2,1)} %bitcast.37, f32[512,1536]{1,0:T(8,128)} %own_back.1.refs_2_.refs_1_, ...), custom_call_target="tpu_custom_call" | custom-call | flops 15728640 | bytes 12582912 | tf_op jit(solution)/shard_map/last_norm/pallas_call | solution.py:515
  (123 shorter events, 56.3 us)
Async XLA Ops:
  7.2 113.7 %all-gather.9.cloned.1.call-start = ((), (), s32[]{:S(2)}) async-start(), calls=%async_computation | async-start | bytes 7520256 | tf_op jit(solution)/shard_map/all_gather | solution.py:2070
  8.3 12.4 %collective-permute-start.2 = (bf16[96,768]{1,0:T(8,128)(2,1)S(1)}, bf16[96,768]{1,0:T(8,128)(2,1)S(1)}, u32[]{:S(2)}, u32[]{:S(2)}) collective-permute-start(bf16[96,768]{1,0:T(8,128)(2,1)S(1)} %bitcast.50), channel_id=1, source_target_pairs={{0,1},{1,0},{2,3},{3,2},{4,5},{5,4},{6,7},{7,6},{8,9},{9,8},{10,11... | collective-permute-start | bytes 442376 | tf_op jit(solution)/shard_map/ppermute | solution.py:2053
  11.4 9.3 %collective-permute-start = (bf16[96,768]{1,0:T(8,128)(2,1)S(1)}, bf16[96,768]{1,0:T(8,128)(2,1)S(1)}, u32[]{:S(2)}, u32[]{:S(2)}) collective-permute-start(bf16[96,768]{1,0:T(8,128)(2,1)S(1)} %bitcast.51), channel_id=1, source_target_pairs={{0,1},{1,0},{2,3},{3,2},{4,5},{5,4},{6,7},{7,6},{8,9},{9,8},{10,11... | collective-permute-start | bytes 442376 | tf_op jit(solution)/shard_map/ppermute | solution.py:2053
  12.4 9.1 %collective-permute-start.1 = (bf16[96,768]{1,0:T(8,128)(2,1)S(1)}, bf16[96,768]{1,0:T(8,128)(2,1)S(1)}, u32[]{:S(2)}, u32[]{:S(2)}) collective-permute-start(bf16[96,768]{1,0:T(8,128)(2,1)S(1)} %constant_dynamic-slice_fusion.1), channel_id=1, source_target_pairs={{0,1},{1,0},{2,3},{3,2},{4,5},{5,4},{6,7},{7,6},{8,9},{9,8},{10,11... | collective-permute-start | bytes 442376 | tf_op jit(solution)/shard_map/ppermute | solution.py:2053
  22.3 169.5 %all-gather.11.cloned.1.call-start = ((), (), s32[]{:S(2)}) async-start(), calls=%async_computation.1 | async-start | bytes 20054016 | tf_op jit(solution)/shard_map/all_gather | solution.py:2104
  22.4 35.9 %collective-permute-start.3 = (bf16[512,1536]{1,0:T(8,128)(2,1)}, bf16[512,1536]{1,0:T(8,128)(2,1)S(1)}, u32[]{:S(2)}, u32[]{:S(2)}) collective-permute-start(bf16[512,1536]{1,0:T(8,128)(2,1)} %first_norm.1.act_ref.refs_0_), channel_id=1, source_target_pairs={{0,1},{1,0},{2,3},{3,2},{4,5},{5,4},{6,7},{7,6},{8,9},{9,8},{10,11... | collective-permute-start | bytes 4718600 | tf_op jit(solution)/shard_map/ppermute | solution.py:2053
  63.7 27.8 %collective-permute-start.4 = (bf16[4,96,1536]{2,1,0:T(8,128)(2,1)}, bf16[4,96,1536]{2,1,0:T(8,128)(2,1)S(1)}, u32[]{:S(2)}, u32[]{:S(2)}) collective-permute-start(bf16[4,96,1536]{2,1,0:T(8,128)(2,1)} %feed_share.1.refs_0_), channel_id=1, source_target_pairs={{0,1},{1,0},{2,3},{3,2},{4,5},{5,4},{6,7},{7,6},{8,9},{9,8},{10,11... | collective-permute-start | bytes 3538952 | tf_op jit(solution)/shard_map/ppermute | solution.py:2053
  92.5 230.1 %all-gather.13.cloned.1.call-start = ((), (), s32[]{:S(2)}) async-start(), calls=%async_computation.2 | async-start | bytes 6754304 | tf_op jit(solution)/shard_map/all_gather | solution.py:2150
  92.5 28.3 %collective-permute-start.5 = (bf16[512,768]{1,0:T(8,128)(2,1)}, bf16[512,768]{1,0:T(8,128)(2,1)S(1)}, u32[]{:S(2)}, u32[]{:S(2)}) collective-permute-start(bf16[512,768]{1,0:T(8,128)(2,1)} %get-tuple-element.117.refs_8_), channel_id=1, source_target_pairs={{0,1},{1,0},{2,3},{3,2},{4,5},{5,4},{6,7},{7,6},{8,9},{9,8},{10,11... | collective-permute-start | bytes 2359304 | tf_op jit(solution)/shard_map/ppermute | solution.py:2053
  93.0 24.4 %collective-permute-start.7 = (bf16[2,64,768]{2,1,0:T(8,128)(2,1)S(1)}, bf16[2,64,768]{2,1,0:T(8,128)(2,1)S(1)}, u32[]{:S(2)}, u32[]{:S(2)}) collective-permute-start(bf16[2,64,768]{2,1,0:T(8,128)(2,1)S(1)} %copy-done.9), channel_id=1, source_target_pairs={{0,1},{1,0},{2,3},{3,2},{4,5},{5,4},{6,7},{7,6},{8,9},{9,8},{10,11... | collective-permute-start | bytes 589832 | tf_op jit(solution)/shard_map/ppermute | solution.py:2053
  94.6 26.2 %collective-permute-start.6 = (bf16[16,9984]{1,0:T(8,128)(2,1)S(1)}, bf16[16,9984]{1,0:T(8,128)(2,1)S(1)}, u32[]{:S(2)}, u32[]{:S(2)}) collective-permute-start(bf16[16,9984]{1,0:T(8,128)(2,1)S(1)} %copy-done.3), channel_id=1, source_target_pairs={{0,1},{1,0},{2,3},{3,2},{4,5},{5,4},{6,7},{7,6},{8,9},{9,8},{10,11... | collective-permute-start | bytes 958472 | tf_op jit(solution)/shard_map/ppermute | solution.py:2053
  226.3 27.0 %collective-permute-start.8 = (bf16[16,7680]{1,0:T(8,128)(2,1)}, bf16[16,7680]{1,0:T(8,128)(2,1)S(1)}, u32[]{:S(2)}, u32[]{:S(2)}) collective-permute-start(bf16[16,7680]{1,0:T(8,128)(2,1)} %get-tuple-element.129), channel_id=1, source_target_pairs={{0,1},{1,0},{2,3},{3,2},{4,5},{5,4},{6,7},{7,6},{8,9},{9,8},{10,11... | collective-permute-start | bytes 737288 | tf_op jit(solution)/shard_map/ppermute | solution.py:2053
  227.9 26.1 %copy-start.13 = (f32[16,3072]{1,0:T(8,128)S(1)}, f32[16,3072]{1,0:T(8,128)}, u32[]{:S(2)}) copy-start(f32[16,3072]{1,0:T(8,128)} %get-tuple-element.164) | copy-start | bytes 589828
  227.9 26.1 %copy-start.14 = (f32[16,3072]{1,0:T(8,128)S(1)}, f32[16,3072]{1,0:T(8,128)}, u32[]{:S(2)}) copy-start(f32[16,3072]{1,0:T(8,128)} %get-tuple-element.163) | copy-start | bytes 589828
  227.9 26.1 %copy-start.16 = (f32[16,1536]{1,0:T(8,128)S(1)}, f32[16,1536]{1,0:T(8,128)}, u32[]{:S(2)}) copy-start(f32[16,1536]{1,0:T(8,128)} %get-tuple-element.161) | copy-start | bytes 294916
  253.4 6.0 %collective-permute-start.12 = (bf16[16,4608]{1,0:T(8,128)(2,1)}, bf16[16,4608]{1,0:T(8,128)(2,1)S(1)}, u32[]{:S(2)}, u32[]{:S(2)}) collective-permute-start(bf16[16,4608]{1,0:T(8,128)(2,1)} %get-tuple-element.160), channel_id=1, source_target_pairs={{0,1},{1,0},{2,3},{3,2},{4,5},{5,4},{6,7},{7,6},{8,9},{9,8},{10,11... | collective-permute-start | bytes 442376 | tf_op jit(solution)/shard_map/ppermute | solution.py:2053
  261.2 111.5 %all-gather.15.cloned.1.call-start = ((), (), s32[]{:S(2)}) async-start(), calls=%async_computation.3 | async-start | bytes 4177920 | tf_op jit(solution)/shard_map/all_gather | solution.py:2179
  261.3 16.8 %collective-permute-start.10 = (bf16[256,768]{1,0:T(8,128)(2,1)S(1)}, bf16[256,768]{1,0:T(8,128)(2,1)S(1)}, u32[]{:S(2)}, u32[]{:S(2)}) collective-permute-start(bf16[256,768]{1,0:T(8,128)(2,1)S(1)} %copy-done.21), channel_id=1, source_target_pairs={{0,1},{1,0},{2,3},{3,2},{4,5},{5,4},{6,7},{7,6},{8,9},{9,8},{10,11... | collective-permute-start | bytes 1179656 | tf_op jit(solution)/shard_map/ppermute | solution.py:2053
  261.9 18.0 %collective-permute-start.9 = (bf16[256,768]{1,0:T(8,128)(2,1)S(1)}, bf16[256,768]{1,0:T(8,128)(2,1)S(1)}, u32[]{:S(2)}, u32[]{:S(2)}) collective-permute-start(bf16[256,768]{1,0:T(8,128)(2,1)S(1)} %copy-done.20), channel_id=1, source_target_pairs={{0,1},{1,0},{2,3},{3,2},{4,5},{5,4},{6,7},{7,6},{8,9},{9,8},{10,11... | collective-permute-start | bytes 1179656 | tf_op jit(solution)/shard_map/ppermute | solution.py:2053
  279.9 25.5 %collective-permute-start.11 = (bf16[192,768]{1,0:T(8,128)(2,1)S(1)}, bf16[192,768]{1,0:T(8,128)(2,1)S(1)}, u32[]{:S(2)}, u32[]{:S(2)}) collective-permute-start(bf16[192,768]{1,0:T(8,128)(2,1)S(1)} %copy-done.24), channel_id=1, source_target_pairs={{0,1},{1,0},{2,3},{3,2},{4,5},{5,4},{6,7},{7,6},{8,9},{9,8},{10,11... | collective-permute-start | bytes 884744 | tf_op jit(solution)/shard_map/ppermute | solution.py:2053
  311.8 6.6 %collective-permute-start.13 = (bf16[16,2304]{1,0:T(8,128)(2,1)}, bf16[16,2304]{1,0:T(8,128)(2,1)S(1)}, u32[]{:S(2)}, u32[]{:S(2)}) collective-permute-start(bf16[16,2304]{1,0:T(8,128)(2,1)} %get-tuple-element.169.refs_4_), channel_id=1, source_target_pairs={{0,1},{1,0},{2,3},{3,2},{4,5},{5,4},{6,7},{7,6},{8,9},{9,8},{10,11... | collective-permute-start | bytes 221192 | tf_op jit(solution)/shard_map/ppermute | solution.py:2053
  330.8 38.9 %collective-permute-start.15 = (bf16[256,1536]{1,0:T(8,128)(2,1)}, bf16[256,1536]{1,0:T(8,128)(2,1)S(1)}, u32[]{:S(2)}, u32[]{:S(2)}) collective-permute-start(bf16[256,1536]{1,0:T(8,128)(2,1)} %other_back.3.refs_4_), channel_id=1, source_target_pairs={{0,1},{1,0},{2,3},{3,2},{4,5},{5,4},{6,7},{7,6},{8,9},{9,8},{10,11... | collective-permute-start | bytes 2359304 | tf_op jit(solution)/shard_map/ppermute | solution.py:2053
  340.4 29.2 %collective-permute-start.14 = (bf16[256,1536]{1,0:T(8,128)(2,1)}, bf16[256,1536]{1,0:T(8,128)(2,1)S(1)}, u32[]{:S(2)}, u32[]{:S(2)}) collective-permute-start(bf16[256,1536]{1,0:T(8,128)(2,1)} %other_back.2), channel_id=1, source_target_pairs={{0,1},{1,0},{2,3},{3,2},{4,5},{5,4},{6,7},{7,6},{8,9},{9,8},{10,11... | collective-permute-start | bytes 2359304 | tf_op jit(solution)/shard_map/ppermute | solution.py:2053
  348.3 21.4 %collective-permute-start.16 = (bf16[64,768]{1,0:T(8,128)(2,1)S(1)}, bf16[64,768]{1,0:T(8,128)(2,1)S(1)}, u32[]{:S(2)}, u32[]{:S(2)}) collective-permute-start(bf16[64,768]{1,0:T(8,128)(2,1)S(1)} %select_convert_fusion), channel_id=1, source_target_pairs={{0,1},{1,0},{2,3},{3,2},{4,5},{5,4},{6,7},{7,6},{8,9},{9,8},{10,11... | collective-permute-start | bytes 294920 | tf_op jit(solution)/shard_map/ppermute | solution.py:2053
  (23 other events, 207.5 us)
Sparse Core Ops, SparseCore 0:
  22.5 68.1 all-gather.8
  92.8 99.0 all-gather.10
  261.4 61.1 all-gather.12
  325.3 47.3 all-gather.14
